TPU v7x, 32 devices: a whole 2x2x4 slice. The times are simulated.
32 devices in a mesh: dom: 32 (over z, y, x, core).
Axes of the slice: x: 2, y: 2, z: 4, core: 2. Of those that a mesh axis runs over, the one named last changes fastest.
Arguments:
- a_blocks: bfloat16 [768, 64, 448], P('dom'), may hold values from -0.25 to 0.25
- p_blocks: bfloat16 [768, 64, 1728], P('dom'), may hold values from -0.59765625 to 0.59765625
- cols_a: int32 [768, 7], P('dom'), may hold values from 0 to 767, as said below
- cols_p: int32 [768, 27], P('dom'), may hold values from 0 to 95, as said below
Outputs:
- coarse_op: float32 [96, 64, 4032], P('dom')
Inputs may be any that keep to these rules, and one draw needn't show every extreme that they name: `cols_a`: row e lists e itself first, then 7 - 1 other distinct rows, all in the aggregates agg(e) - 1, agg(e) and agg(e) + 1, counted cyclically. `cols_p`: the 27 entries of a row are distinct aggregates within 15 of the row's own aggregate, counted cyclically.
All inputs are finite; a program needn't handle non-finite values.
Results may differ from a plain program's by a relative error of at most 0.0041.
Values may be sent and summed in bfloat16 or wider, within the bound.
No kernel may reach another device: no remote copies, remote signals or barrier semaphores. Data moves between devices by JAX's collectives and lax.ppermute only.
A program may use at most 192 MiB of HBM per device.

v0:
```python
import functools

import jax
import jax.numpy as jnp
from jax import lax
from jax.experimental import pallas as pl
from jax.experimental.pallas import tpu as pltpu
from jax.sharding import PartitionSpec as P

BS = 64
KA = 7
KP = 27
AGG = 8
H = 15
NC = 3
NB = 24
WIN = 31
WSLOT = 33
BAND = 63

QUAD = 4
LANES = QUAD * BS
EXT = NB + 2 * AGG
COLS = NC + 2 * H + 2
PAD = 4
WCOLS = 44
WINDOW = 40
FAR = 36
TILES = WINDOW // QUAD
GROUPS = 5
K = NB * BS
AW = AGG * BS
FRAME = 70
NT = (((1,), (1,)), ((), ()))
ROW_ORDER = [(j, i) for j in (0, 2, 1) for i in range(GROUPS)]


def eye(n):
    rows = lax.broadcasted_iota(jnp.int32, (n, n), 0)
    lanes = lax.broadcasted_iota(jnp.int32, (n, n), 1)
    return jnp.where(rows == lanes, 1.0, 0.0).astype(jnp.bfloat16)


def low_half():
    return lax.broadcasted_iota(jnp.int32, (BS, 2 * BS), 1) < BS


def transpose_quad(block, turned, width):
    for start in range(0, width, LANES):
        size = min(LANES, width - start)
        part = lax.dot_general(
            eye(size), block[:, start : start + size], NT, preferred_element_type=jnp.float32
        )
        turned[start // BS : (start + size) // BS] = part.astype(jnp.bfloat16).reshape(
            size // BS, BS, LANES
        )


def spread_quad(turned, index, first, store, count):
    half = low_half()

    def place(slot, carry):
        for pair in range(2):
            lanes = slice(pair * 2 * BS, (pair + 1) * 2 * BS)
            left = turned[index[first + 2 * pair, slot], :, lanes]
            right = turned[index[first + 2 * pair + 1, slot], :, lanes]
            store(slot, pair, jnp.where(half, left, right))
        return carry

    lax.fori_loop(0, count, place, 0)


def build_kernel(
    core, inv_p, inv_a, p_own, p_lo, p_hi, a_own, send, far, pt_rows, wt, ext, at, turned_p, turned_a, lhs
):
    s = core[0]
    turned_p[KP] = jnp.zeros((BS, LANES), jnp.bfloat16)
    turned_a[KA] = jnp.zeros((BS, LANES), jnp.bfloat16)

    def band_quad(source, source_row, quad):
        block = source[pl.ds(source_row, QUAD)].reshape(LANES, KP * BS)
        transpose_quad(block, turned_p, KP * BS)

        def store(slot, pair, value):
            lane = pl.multiple_of(quad * LANES + pair * 2 * BS, 2 * BS)
            ext[slot, :, pl.ds(lane, 2 * BS)] = value

        spread_quad(turned_p, inv_p, quad * QUAD, store, COLS)

    halo_quads = AGG // QUAD

    @pl.loop(0, halo_quads)
    def _(quad):
        band_quad(p_lo, quad * QUAD, quad)

    @pl.loop(0, NB // QUAD)
    def _(quad):
        band_quad(p_own, quad * QUAD, quad + halo_quads)

    @pl.loop(0, halo_quads)
    def _(quad):
        band_quad(p_hi, quad * QUAD, quad + halo_quads + NB // QUAD)

    @pl.loop(0, NB // QUAD)
    def _(quad):
        block = a_own[pl.ds(quad * QUAD, QUAD)].reshape(LANES, KA * BS)
        transpose_quad(block, turned_a, KA * BS)
        agg = quad // halo_quads

        def store(slot, pair, value):
            lane = pl.multiple_of((quad % halo_quads) * LANES + pair * 2 * BS, 2 * BS)
            at[agg, slot, :, pl.ds(lane, 2 * BS)] = value

        spread_quad(turned_a, inv_a, quad * QUAD, store, 3 * AGG)

    wt[0 : PAD + NC - 1] = jnp.zeros((PAD + NC - 1, BS, K), jnp.bfloat16)
    wt[PAD + WSLOT :] = jnp.zeros((WCOLS - PAD - WSLOT, BS, K), jnp.bfloat16)
    chunk = WSLOT // 3

    @pl.loop(0, NC)
    def _(agg):
        lane = pl.multiple_of(agg * AW, AW)

        @pl.loop(0, 3)
        def _(part):
            first = agg + part * chunk
            left = ext[pl.ds(first, chunk), :, pl.ds(lane, 3 * AW)].reshape(chunk * BS, 3 * AW)
            right = at[agg].reshape(3 * AW, AW)
            value = jnp.dot(left, right, preferred_element_type=jnp.float32)
            wt[pl.ds(PAD + first, chunk), :, pl.ds(lane, AW)] = value.astype(jnp.bfloat16).reshape(
                chunk, BS, AW
            )

    own_lanes = slice(AW, AW + K)
    for position, (j, i) in enumerate(ROW_ORDER):
        pt_rows[position] = ext[6 * i + 3 + j + 1, :, own_lanes]
    far_first = 30 * s
    for place, j in enumerate((0, 2, 1)):
        for i in range(GROUPS):
            lhs[place * 6 + i] = ext[6 * i + 6 * (1 - s) + j + 1, :, own_lanes]
        lhs[place * 6 + GROUPS] = ext[far_first + j + 1, :, own_lanes]

    def emit(place, count, first_col, tile):
        right = wt[pl.ds(first_col + QUAD * tile, QUAD)].reshape(LANES, K)
        left = lhs[6 * place : 6 * (place + count)].reshape(count * 6 * BS, K)
        value = lax.dot_general(left, right, NT, preferred_element_type=jnp.float32)
        value = value.astype(jnp.bfloat16).reshape(count * 6, BS, LANES)
        lane = pl.multiple_of(tile * LANES, LANES)
        for k in range(count):
            send[pl.ds((place + k) * GROUPS, GROUPS), :, pl.ds(lane, LANES)] = value[
                6 * k : 6 * k + GROUPS
            ]
        far_tile = tile - s

        @pl.when((far_tile >= 0) & (far_tile < FAR // QUAD))
        def _():
            far_lane = pl.multiple_of(far_tile * LANES, LANES)
            for k in range(count):
                far[(0, 2, 1)[place + k], :, pl.ds(far_lane, LANES)] = value[6 * k + GROUPS]

    @pl.loop(0, TILES)
    def _(tile):
        emit(0, 2, PAD - 4 * s, tile)
        emit(2, 1, PAD - 1 - 2 * s, tile)


def sum_kernel(core, pt_rows, wt, arrived, *outs):
    s = core[0]

    def emit(place, count, first_col, tile):
        right = wt[pl.ds(first_col + QUAD * tile, QUAD)].reshape(LANES, K)
        rows = pl.ds(place * GROUPS, count * GROUPS)
        left = pt_rows[rows].reshape(count * GROUPS * BS, K)
        value = lax.dot_general(left, right, NT, preferred_element_type=jnp.float32)
        lane = pl.multiple_of(tile * LANES, LANES)
        value = value.reshape(count * GROUPS, BS, LANES)
        value = value + arrived[rows, :, pl.ds(lane, LANES)].astype(jnp.float32)
        for k in range(count):
            for i in range(GROUPS):
                target = outs[i]
                target[(0, 2, 1)[place + k], :, pl.ds(lane, LANES)] = value[
                    k * GROUPS + i
                ].astype(target.dtype)

    @pl.loop(0, TILES)
    def _(tile):
        emit(0, 2, PAD - 1 - 2 * s, tile)
        emit(2, 1, PAD - 4 * s, tile)


def total_kernel(core, own, m0, m1, m3, m4, far, out, frame):
    s = core[0]
    j = pl.program_id(0)
    frame[...] = jnp.zeros_like(frame)

    def add(message, start, blocks):
        lane = pl.multiple_of((start + 2) * BS, 2 * BS)
        frame[:, pl.ds(lane, blocks * BS)] += message[0].astype(jnp.float32)

    top = 2 * ((27 - 3 * s - j) // 2)
    for i, message in enumerate((m0, m1, own, m3, m4)):
        add(message, top - 6 * i, WINDOW)
    far_start = jnp.where(s == 1, jnp.where(j == 0, 30, 28), jnp.where(j == 2, -2, 0))
    add(far, far_start, FAR)
    out[0] = frame[:, 2 * BS : (2 + BAND) * BS]


def permuted(block, pairs):
    return lax.ppermute(block, "dom", pairs)


def inverse_index(offset, slots, empty):
    order = jnp.arange(offset.shape[1], dtype=jnp.int32)[None, :, None]
    hit = offset[:, :, None] == jnp.arange(slots, dtype=jnp.int32)[None, None, :]
    return empty + jnp.sum(jnp.where(hit, order - empty, 0), axis=1)


def body(a_blocks, p_blocks, cols_a, cols_p):
    devices = lax.axis_size("dom")
    device = lax.axis_index("dom")
    count_agg = NC * devices
    count_rows = NB * devices
    first_agg = device * NC
    first_row = device * NB
    core = (device % 2).astype(jnp.int32).reshape(1)

    def shifted(distance):
        return [(i, (i + distance) % devices) for i in range(devices)]

    p_lo = permuted(p_blocks[NB - AGG :], shifted(1))
    p_hi = permuted(p_blocks[:AGG], shifted(-1))
    cols_lo = permuted(cols_p[NB - AGG :], shifted(1))
    cols_hi = permuted(cols_p[:AGG], shifted(-1))
    ext_cols = jnp.concatenate([cols_lo, cols_p, cols_hi])
    ext_agg = jnp.arange(EXT, dtype=jnp.int32)[:, None] // AGG
    slot = (ext_cols - first_agg - (ext_agg - 1) + H) % count_agg
    inv_p = inverse_index(slot + ext_agg, COLS, KP)
    own_agg = jnp.arange(NB, dtype=jnp.int32)[:, None] // AGG
    inv_a = inverse_index((cols_a - first_row - (own_agg - 1) * AGG) % count_rows, 3 * AGG, KA)

    smem = pl.BlockSpec(memory_space=pltpu.SMEM)
    vmem = pl.BlockSpec(memory_space=pltpu.VMEM)
    bf16 = jnp.bfloat16
    params = pltpu.CompilerParams(vmem_limit_bytes=60 * 1024 * 1024)
    send, far, pt_rows, wt = pl.pallas_call(
        build_kernel,
        out_shape=[
            jax.ShapeDtypeStruct((3 * GROUPS, BS, WINDOW * BS), bf16),
            jax.ShapeDtypeStruct((NC, BS, FAR * BS), bf16),
            jax.ShapeDtypeStruct((3 * GROUPS, BS, K), bf16),
            jax.ShapeDtypeStruct((WCOLS, BS, K), bf16),
        ],
        in_specs=[smem] * 3 + [vmem] * 4,
        out_specs=[vmem] * 4,
        scratch_shapes=[
            pltpu.VMEM((COLS, BS, EXT * BS), bf16),
            pltpu.VMEM((NC, 3 * AGG, BS, AW), bf16),
            pltpu.VMEM((KP + 1, BS, LANES), bf16),
            pltpu.VMEM((KA + 1, BS, LANES), bf16),
            pltpu.VMEM((18, BS, K), bf16),
        ],
        compiler_params=params,
        cost_estimate=pl.CostEstimate(flops=24 * 10**9, bytes_accessed=30 * 10**6, transcendentals=0),
        name="build",
    )(core, inv_p, inv_a, p_blocks, p_lo, p_hi, a_blocks)

    arrived = permuted(send, [(i, i ^ 1) for i in range(devices)])
    far = permuted(far, [(i, (i + (5 if i % 2 else -5)) % devices) for i in range(devices)])
    message = jax.ShapeDtypeStruct((NC, BS, WINDOW * BS), bf16)
    m0, m1, own, m3, m4 = pl.pallas_call(
        sum_kernel,
        out_shape=[message, message, jax.ShapeDtypeStruct(message.shape, jnp.float32), message, message],
        in_specs=[smem] + [vmem] * 3,
        out_specs=[vmem] * 5,
        compiler_params=params,
        cost_estimate=pl.CostEstimate(flops=8 * 10**9, bytes_accessed=25 * 10**6, transcendentals=0),
        name="add_core",
    )(core, pt_rows, wt, arrived)
    m0 = permuted(m0, shifted(-4))
    m4 = permuted(m4, shifted(4))
    m1 = permuted(m1, shifted(-2))
    m3 = permuted(m3, shifted(2))

    def row_block(blocks):
        return pl.BlockSpec((1, BS, blocks * BS), lambda j: (j, 0, 0))

    return pl.pallas_call(
        total_kernel,
        grid=(NC,),
        out_shape=jax.ShapeDtypeStruct((NC, BS, BAND * BS), jnp.float32),
        in_specs=[smem] + [row_block(WINDOW)] * 5 + [row_block(FAR)],
        out_specs=row_block(BAND),
        scratch_shapes=[pltpu.VMEM((BS, FRAME * BS), jnp.float32)],
        compiler_params=params,
        cost_estimate=pl.CostEstimate(flops=10**7, bytes_accessed=10**7, transcendentals=0),
        name="total",
    )(core, own, m0, m1, m3, m4, far)


def solution(mesh):
    in_specs = (P("dom", None, None), P("dom", None, None), P("dom", None), P("dom", None))
    out_specs = P("dom", None, None)
    return jax.shard_map(body, mesh=mesh, in_specs=in_specs, out_specs=out_specs, check_vma=False)
```

profile of v0, /device:TPU:4, one launch (start us, length us, event | category | flops | bytes accessed | tf_op | source)
XLA Modules:
  0.0 227.4 jit_solution(16722151901181891363)
XLA Ops:
  0.0 0.0 copy-start.5
  0.0 0.0 copy-start.6
  0.0 3.6 %fusion.6 = (bf16[8,64,1728]{2,1,0:T(8,128)(2,1)}, bf16[8,64,1728]{2,1,0:T(8,128)(2,1)S(1)}) fusion(bf16[24,64,1728]{2,1,0:T(8,128)(2,1)} %p_own.1), kind=kLoop, calls=%fused_computation.27 | loop fusion | bytes 7077888 | tf_op jit(solution)/shard_map/slice | solution.py:231
  3.6 0.9 collective-permute-start.3
  4.5 0.0 collective-permute-start.2
  4.5 0.0 copy-done.5
  4.5 0.1 copy.7
  4.6 0.1 fusion.7
  4.7 0.7 collective-permute-start
  5.4 2.0 collective-permute-start.1
  7.4 0.0 copy-done.6
  7.4 0.1 select_reduce_fusion.1
  7.5 0.6 broadcast_add_fusion.1.inv_a
  8.1 38.4 %collective-permute-done = s32[8,27]{0,1:T(8,128)S(1)} collective-permute-done((s32[8,27]{0,1:T(8,128)S(1)}, s32[8,27]{0,1:T(8,128)S(1)}, u32[]{:S(2)}, u32[]{:S(2)}) %collective-permute-start) | collective-permute-done | bytes 896 | tf_op jit(solution)/shard_map/ppermute | solution.py:209
  46.5 0.0 collective-permute-done.1
  46.5 0.1 fusion
  46.6 0.2 select_reduce_fusion
  46.8 0.6 broadcast_add_fusion.inv_p
  47.4 0.0 collective-permute-done.3.p_hi
  47.4 0.0 collective-permute-done.2.p_lo
  47.4 56.6 %build.1 = (bf16[15,64,2560]{2,1,0:T(8,128)(2,1)}, bf16[3,64,2304]{2,1,0:T(8,128)(2,1)}, bf16[15,64,1536]{2,1,0:T(8,128)(2,1)}, bf16[44,64,1536]{2,1,0:T(8,128)(2,1)}) custom-call(s32[1]{0:T(128)} %bitcast.core, s32[40,35]{1,0:T(8,128)} %broadcast_add_fusion.inv_p, s32[24,24]{1,0:T(8,128)} %broadcast_add_fusion.1.inv_a, bf16[24,64,1728]{2,1,0:T(8,128)(2,1)} %p_own.1, ...), custom_call_target="tpu_custom_call" | custom-call | flops 24000000000 | bytes 30000000 | tf_op jit(solution)/shard_map/build/pallas_call | solution.py:245
  104.1 0.1 collective-permute-start.4
  104.2 8.4 %collective-permute-done.4.arrived = bf16[15,64,2560]{2,1,0:T(8,128)(2,1)} collective-permute-done((bf16[15,64,2560]{2,1,0:T(8,128)(2,1)}, bf16[15,64,2560]{2,1,0:T(8,128)(2,1)}, u32[]{:S(2)}, u32[]{:S(2)}) %collective-permute-start.4) | collective-permute-done | bytes 4915232 | tf_op jit(solution)/shard_map/ppermute | solution.py:209
  112.6 17.9 %add_core.1 = (bf16[3,64,2560]{2,1,0:T(8,128)(2,1)}, bf16[3,64,2560]{2,1,0:T(8,128)(2,1)}, f32[3,64,2560]{2,1,0:T(8,128)}, bf16[3,64,2560]{2,1,0:T(8,128)(2,1)}, bf16[3,64,2560]{2,1,0:T(8,128)(2,1)}) custom-call(s32[1]{0:T(128)} %bitcast.core, bf16[15,64,1536]{2,1,0:T(8,128)(2,1)} %get-tuple-element.14.pt_rows, bf16[44,64,1536]{2,1,0:T(8,128)(2,1)} %get-tuple-element.15.wt, ...), custom_call_target="tpu_custom_call" | custom-call | flops 8000000000 | bytes 25000000 | tf_op jit(solution)/shard_map/add_core/pallas_call | solution.py:270
  130.5 0.0 collective-permute-start.5
  130.5 5.6 %collective-permute-start.6 = (bf16[3,64,2560]{2,1,0:T(8,128)(2,1)}, bf16[3,64,2560]{2,1,0:T(8,128)(2,1)S(1)}, u32[]{:S(2)}, u32[]{:S(2)}) collective-permute-start(bf16[3,64,2560]{2,1,0:T(8,128)(2,1)} %get-tuple-element.19), channel_id=1, source_target_pairs={{0,30},{1,31},{2,0},{3,1},{4,2},{5,3},{6,4},{7,5},{8,6},{9,7},{10,... | collective-permute-start | bytes 2949128 | tf_op jit(solution)/shard_map/ppermute | solution.py:209
  136.1 0.0 collective-permute-start.7
  136.1 0.0 collective-permute-start.8
  136.1 4.8 %collective-permute-start.9 = (bf16[3,64,2304]{2,1,0:T(8,128)(2,1)}, bf16[3,64,2304]{2,1,0:T(8,128)(2,1)S(1)}, u32[]{:S(2)}, u32[]{:S(2)}) collective-permute-start(bf16[3,64,2304]{2,1,0:T(8,128)(2,1)} %get-tuple-element.22), channel_id=1, source_target_pairs={{0,27},{1,6},{2,29},{3,8},{4,31},{5,10},{6,1},{7,12},{8,3},{9,14},... | collective-permute-start | bytes 2654216 | tf_op jit(solution)/shard_map/ppermute | solution.py:209
  140.9 78.3 %collective-permute-done.9.far = bf16[3,64,2304]{2,1,0:T(8,128)(2,1)S(1)} collective-permute-done((bf16[3,64,2304]{2,1,0:T(8,128)(2,1)}, bf16[3,64,2304]{2,1,0:T(8,128)(2,1)S(1)}, u32[]{:S(2)}, u32[]{:S(2)}) %collective-permute-start.9) | collective-permute-done | bytes 884768 | tf_op jit(solution)/shard_map/ppermute | solution.py:209
  219.2 0.0 copy-start.4
  219.2 0.0 collective-permute-done.5.m0
  219.2 0.0 copy-start
  219.2 0.0 collective-permute-done.6.m1
  219.2 0.0 copy-start.1
  219.2 0.0 collective-permute-done.7.m3
  219.2 0.0 copy-start.2
  219.2 0.0 collective-permute-done.8.m4
  219.2 0.9 copy-done.4
  220.1 0.0 copy-start.3
  220.1 0.3 copy-done
  220.4 0.3 copy-done.1
  220.8 0.3 copy-done.2
  221.0 0.3 copy-done.3
  221.3 6.1 %total.1 = f32[3,64,4032]{2,1,0:T(8,128)} custom-call(s32[1]{0:T(128)} %bitcast.core, f32[3,64,2560]{2,1,0:T(8,128)} %get-tuple-element.17.own, bf16[3,64,2560]{2,1,0:T(8,128)(2,1)} %copy-done, bf16[3,64,2560]{2,1,0:T(8,128)(2,1)} %copy-done.1, bf16[3,64,2560]{2,1,0:T(8,128)(2,1)} %copy-done.2, bf16[3,64,2560]{2,1,0:T(8,128)(2,1)} %copy-done.3, ...), custom_call_target="tpu_custom_call" | custom-call | flops 10000000 | bytes 10000000 | tf_op jit(solution)/shard_map/total/pallas_call | solution.py:287
  (5 shorter events, 0.0 us)
Async XLA Ops:
  0.0 4.5 %copy-start.5 = (s32[24,27]{1,0:T(8,128)S(1)}, s32[24,27]{1,0:T(8,128)}, u32[]{:S(2)}) copy-start(s32[24,27]{1,0:T(8,128)} %param.7) | copy-start | bytes 7780
  0.0 7.4 %copy-start.6 = (s32[24,7]{0,1:T(8,128)S(1)}, s32[24,7]{0,1:T(8,128)}, u32[]{:S(2)}) copy-start(s32[24,7]{0,1:T(8,128)} %param.6) | copy-start | bytes 2020
  3.6 43.8 %collective-permute-start.3 = (bf16[8,64,1728]{2,1,0:T(8,128)(2,1)}, bf16[8,64,1728]{2,1,0:T(8,128)(2,1)}, u32[]{:S(2)}, u32[]{:S(2)}) collective-permute-start(bf16[8,64,1728]{2,1,0:T(8,128)(2,1)} %get-tuple-element.23), channel_id=1, source_target_pairs={{0,31},{1,0},{2,1},{3,2},{4,3},{5,4},{6,5},{7,6},{8,7},{9,8},{10,9... | collective-permute-start | bytes 5308424 | tf_op jit(solution)/shard_map/ppermute | solution.py:209
  4.5 42.9 %collective-permute-start.2 = (bf16[8,64,1728]{2,1,0:T(8,128)(2,1)S(1)}, bf16[8,64,1728]{2,1,0:T(8,128)(2,1)}, u32[]{:S(2)}, u32[]{:S(2)}) collective-permute-start(bf16[8,64,1728]{2,1,0:T(8,128)(2,1)S(1)} %get-tuple-element.24), channel_id=1, source_target_pairs={{0,1},{1,2},{2,3},{3,4},{4,5},{5,6},{6,7},{7,8},{8,9},{9,10},{10,1... | collective-permute-start | bytes 5308424 | tf_op jit(solution)/shard_map/ppermute | solution.py:209
  4.7 41.8 %collective-permute-start = (s32[8,27]{0,1:T(8,128)S(1)}, s32[8,27]{0,1:T(8,128)S(1)}, u32[]{:S(2)}, u32[]{:S(2)}) collective-permute-start(s32[8,27]{0,1:T(8,128)S(1)} %get-tuple-element.25), channel_id=1, source_target_pairs={{0,1},{1,2},{2,3},{3,4},{4,5},{5,6},{6,7},{7,8},{8,9},{9,10},{10,1... | collective-permute-start | bytes 2600 | tf_op jit(solution)/shard_map/ppermute | solution.py:209
  5.4 41.1 %collective-permute-start.1 = (s32[8,27]{0,1:T(8,128)S(1)}, s32[8,27]{0,1:T(8,128)S(1)}, u32[]{:S(2)}, u32[]{:S(2)}) collective-permute-start(s32[8,27]{0,1:T(8,128)S(1)} %get-tuple-element.26), channel_id=1, source_target_pairs={{0,31},{1,0},{2,1},{3,2},{4,3},{5,4},{6,5},{7,6},{8,7},{9,8},{10,9... | collective-permute-start | bytes 2600 | tf_op jit(solution)/shard_map/ppermute | solution.py:209
  104.1 8.5 %collective-permute-start.4 = (bf16[15,64,2560]{2,1,0:T(8,128)(2,1)}, bf16[15,64,2560]{2,1,0:T(8,128)(2,1)}, u32[]{:S(2)}, u32[]{:S(2)}) collective-permute-start(bf16[15,64,2560]{2,1,0:T(8,128)(2,1)} %get-tuple-element.16), channel_id=1, source_target_pairs={{0,1},{1,0},{2,3},{3,2},{4,5},{5,4},{6,7},{7,6},{8,9},{9,8},{10,11... | collective-permute-start | bytes 14745608 | tf_op jit(solution)/shard_map/ppermute | solution.py:209
  130.5 88.7 %collective-permute-start.5 = (bf16[3,64,2560]{2,1,0:T(8,128)(2,1)}, bf16[3,64,2560]{2,1,0:T(8,128)(2,1)S(1)}, u32[]{:S(2)}, u32[]{:S(2)}) collective-permute-start(bf16[3,64,2560]{2,1,0:T(8,128)(2,1)} %get-tuple-element.18), channel_id=1, source_target_pairs={{0,28},{1,29},{2,30},{3,31},{4,0},{5,1},{6,2},{7,3},{8,4},{9,5},{1... | collective-permute-start | bytes 2949128 | tf_op jit(solution)/shard_map/ppermute | solution.py:209
  130.5 88.7 %collective-permute-start.6 = (bf16[3,64,2560]{2,1,0:T(8,128)(2,1)}, bf16[3,64,2560]{2,1,0:T(8,128)(2,1)S(1)}, u32[]{:S(2)}, u32[]{:S(2)}) collective-permute-start(bf16[3,64,2560]{2,1,0:T(8,128)(2,1)} %get-tuple-element.19), channel_id=1, source_target_pairs={{0,30},{1,31},{2,0},{3,1},{4,2},{5,3},{6,4},{7,5},{8,6},{9,7},{10,... | collective-permute-start | bytes 2949128 | tf_op jit(solution)/shard_map/ppermute | solution.py:209
  136.1 83.1 %collective-permute-start.7 = (bf16[3,64,2560]{2,1,0:T(8,128)(2,1)}, bf16[3,64,2560]{2,1,0:T(8,128)(2,1)S(1)}, u32[]{:S(2)}, u32[]{:S(2)}) collective-permute-start(bf16[3,64,2560]{2,1,0:T(8,128)(2,1)} %get-tuple-element.20), channel_id=1, source_target_pairs={{0,2},{1,3},{2,4},{3,5},{4,6},{5,7},{6,8},{7,9},{8,10},{9,11},{10,... | collective-permute-start | bytes 2949128 | tf_op jit(solution)/shard_map/ppermute | solution.py:209
  136.1 83.1 %collective-permute-start.8 = (bf16[3,64,2560]{2,1,0:T(8,128)(2,1)}, bf16[3,64,2560]{2,1,0:T(8,128)(2,1)S(1)}, u32[]{:S(2)}, u32[]{:S(2)}) collective-permute-start(bf16[3,64,2560]{2,1,0:T(8,128)(2,1)} %get-tuple-element.21), channel_id=1, source_target_pairs={{0,4},{1,5},{2,6},{3,7},{4,8},{5,9},{6,10},{7,11},{8,12},{9,13},{1... | collective-permute-start | bytes 2949128 | tf_op jit(solution)/shard_map/ppermute | solution.py:209
  136.1 83.1 %collective-permute-start.9 = (bf16[3,64,2304]{2,1,0:T(8,128)(2,1)}, bf16[3,64,2304]{2,1,0:T(8,128)(2,1)S(1)}, u32[]{:S(2)}, u32[]{:S(2)}) collective-permute-start(bf16[3,64,2304]{2,1,0:T(8,128)(2,1)} %get-tuple-element.22), channel_id=1, source_target_pairs={{0,27},{1,6},{2,29},{3,8},{4,31},{5,10},{6,1},{7,12},{8,3},{9,14},... | collective-permute-start | bytes 2654216 | tf_op jit(solution)/shard_map/ppermute | solution.py:209
  219.2 0.9 copy-start.4
  219.2 1.2 copy-start
  219.2 1.6 copy-start.1
  219.2 1.8 copy-start.2
  220.1 1.2 copy-start.3
where the time goes:
time: 228 us; the launch traced here: 227 us
  waiting for transfers between devices  125 us (55%)
  Pallas kernels  80.6 us (35%)
  starting transfers between devices  14.1 us (6%)
  local copies, waits for them, and re-layouts  5.85 us (3%)
    ppermute x10, waiting for transfers between devices, permuted(): return lax.ppermute(block, 'dom', pairs)  125 us
    pallas_call x1, Pallas kernels, body(): pl.pallas_call(build_kernel, out_shape=[jax.ShapeDtypeStruct((3 * GROUPS,...  56.6 us
    pallas_call x1, Pallas kernels, body(): pl.pallas_call(sum_kernel, out_shape=[message, message, jax.ShapeDtypeStr...  17.9 us
    ppermute x10, starting transfers between devices, permuted(): return lax.ppermute(block, 'dom', pairs)  14.1 us
    pallas_call x1, Pallas kernels, body(): pl.pallas_call(total_kernel, grid=(NC,), out_shape=jax.ShapeDtypeStruct((...  6.06 us
  transfers between devices with their start and end apart: 10, of which 3 were waited for; matrix products, arithmetic and copies ran while one was open for 1% of the time, Pallas kernels for 0%

commit v1 on v0

--- a/solution.py
+++ b/solution.py
@@ -24,15 +24,14 @@
 COLS = NC + 2 * H + 2
 PAD = 4
 WCOLS = 44
-WINDOW = 40
-FAR = 36
-TILES = WINDOW // QUAD
+WINDOW = 38
+TILES = 10
 GROUPS = 5
 K = NB * BS
 AW = AGG * BS
-FRAME = 70
+FRAME = 76
 NT = (((1,), (1,)), ((), ()))
-ROW_ORDER = [(j, i) for j in (0, 2, 1) for i in range(GROUPS)]
+ROWS = NC * GROUPS
 
 
 def eye(n):
@@ -56,7 +55,7 @@
         )
 
 
-def spread_quad(turned, index, first, store, count):
+def spread_quad(turned, index, first, store, count, unroll):
     half = low_half()
 
     def place(slot, carry):
@@ -67,7 +66,7 @@
             store(slot, pair, jnp.where(half, left, right))
         return carry
 
-    lax.fori_loop(0, count, place, 0)
+    lax.fori_loop(0, count, place, 0, unroll=unroll)
 
 
 def build_kernel(
@@ -85,7 +84,7 @@
             lane = pl.multiple_of(quad * LANES + pair * 2 * BS, 2 * BS)
             ext[slot, :, pl.ds(lane, 2 * BS)] = value
 
-        spread_quad(turned_p, inv_p, quad * QUAD, store, COLS)
+        spread_quad(turned_p, inv_p, quad * QUAD, store, COLS, 7)
 
     halo_quads = AGG // QUAD
 
@@ -111,7 +110,7 @@
             lane = pl.multiple_of((quad % halo_quads) * LANES + pair * 2 * BS, 2 * BS)
             at[agg, slot, :, pl.ds(lane, 2 * BS)] = value
 
-        spread_quad(turned_a, inv_a, quad * QUAD, store, 3 * AGG)
+        spread_quad(turned_a, inv_a, quad * QUAD, store, 3 * AGG, 8)
 
     wt[0 : PAD + NC - 1] = jnp.zeros((PAD + NC - 1, BS, K), jnp.bfloat16)
     wt[PAD + WSLOT :] = jnp.zeros((WCOLS - PAD - WSLOT, BS, K), jnp.bfloat16)
@@ -132,60 +131,48 @@
             )
 
     own_lanes = slice(AW, AW + K)
-    for position, (j, i) in enumerate(ROW_ORDER):
-        pt_rows[position] = ext[6 * i + 3 + j + 1, :, own_lanes]
-    far_first = 30 * s
-    for place, j in enumerate((0, 2, 1)):
-        for i in range(GROUPS):
-            lhs[place * 6 + i] = ext[6 * i + 6 * (1 - s) + j + 1, :, own_lanes]
-        lhs[place * 6 + GROUPS] = ext[far_first + j + 1, :, own_lanes]
-
-    def emit(place, count, first_col, tile):
-        right = wt[pl.ds(first_col + QUAD * tile, QUAD)].reshape(LANES, K)
-        left = lhs[6 * place : 6 * (place + count)].reshape(count * 6 * BS, K)
+    for i in range(GROUPS):
+        for j in range(NC):
+            pt_rows[NC * i + j] = ext[6 * i + 3 + j + 1, :, own_lanes]
+            lhs[NC * i + j] = ext[6 * i + 6 * (1 - s) + j + 1, :, own_lanes]
+    for j in range(NC):
+        lhs[ROWS + j] = ext[30 * s + j + 1, :, own_lanes]
+
+    def emit(tile, width):
+        right = wt[pl.ds(PAD - 3 * s + QUAD * tile, width // BS)].reshape(width, K)
+        left = lhs[...].reshape((ROWS + NC) * BS, K)
         value = lax.dot_general(left, right, NT, preferred_element_type=jnp.float32)
-        value = value.astype(jnp.bfloat16).reshape(count * 6, BS, LANES)
+        value = value.astype(jnp.bfloat16).reshape(ROWS + NC, BS, width)
         lane = pl.multiple_of(tile * LANES, LANES)
-        for k in range(count):
-            send[pl.ds((place + k) * GROUPS, GROUPS), :, pl.ds(lane, LANES)] = value[
-                6 * k : 6 * k + GROUPS
-            ]
-        far_tile = tile - s
-
-        @pl.when((far_tile >= 0) & (far_tile < FAR // QUAD))
-        def _():
-            far_lane = pl.multiple_of(far_tile * LANES, LANES)
-            for k in range(count):
-                far[(0, 2, 1)[place + k], :, pl.ds(far_lane, LANES)] = value[6 * k + GROUPS]
-
-    @pl.loop(0, TILES)
+        send[:, :, pl.ds(lane, width)] = value[:ROWS]
+        far[:, :, pl.ds(lane, width)] = value[ROWS:]
+
+    @pl.loop(0, TILES - 1)
     def _(tile):
-        emit(0, 2, PAD - 4 * s, tile)
-        emit(2, 1, PAD - 1 - 2 * s, tile)
+        emit(tile, LANES)
+
+    emit(TILES - 1, LANES // 2)
 
 
 def sum_kernel(core, pt_rows, wt, arrived, *outs):
     s = core[0]
 
-    def emit(place, count, first_col, tile):
-        right = wt[pl.ds(first_col + QUAD * tile, QUAD)].reshape(LANES, K)
-        rows = pl.ds(place * GROUPS, count * GROUPS)
-        left = pt_rows[rows].reshape(count * GROUPS * BS, K)
+    def emit(tile, width):
+        right = wt[pl.ds(PAD - 3 * s + QUAD * tile, width // BS)].reshape(width, K)
+        left = pt_rows[...].reshape(ROWS * BS, K)
         value = lax.dot_general(left, right, NT, preferred_element_type=jnp.float32)
         lane = pl.multiple_of(tile * LANES, LANES)
-        value = value.reshape(count * GROUPS, BS, LANES)
-        value = value + arrived[rows, :, pl.ds(lane, LANES)].astype(jnp.float32)
-        for k in range(count):
-            for i in range(GROUPS):
-                target = outs[i]
-                target[(0, 2, 1)[place + k], :, pl.ds(lane, LANES)] = value[
-                    k * GROUPS + i
-                ].astype(target.dtype)
-
-    @pl.loop(0, TILES)
+        value = value.reshape(ROWS, BS, width)
+        value = value + arrived[:, :, pl.ds(lane, width)].astype(jnp.float32)
+        for i in range(GROUPS):
+            part = value[NC * i : NC * (i + 1)]
+            outs[i][:, :, pl.ds(lane, width)] = part.astype(outs[i].dtype)
+
+    @pl.loop(0, TILES - 1)
     def _(tile):
-        emit(0, 2, PAD - 1 - 2 * s, tile)
-        emit(2, 1, PAD - 4 * s, tile)
+        emit(tile, LANES)
+
+    emit(TILES - 1, LANES // 2)
 
 
 def total_kernel(core, own, m0, m1, m3, m4, far, out, frame):
@@ -193,16 +180,16 @@
     j = pl.program_id(0)
     frame[...] = jnp.zeros_like(frame)
 
-    def add(message, start, blocks):
-        lane = pl.multiple_of((start + 2) * BS, 2 * BS)
-        frame[:, pl.ds(lane, blocks * BS)] += message[0].astype(jnp.float32)
-
-    top = 2 * ((27 - 3 * s - j) // 2)
+    def add(message, start):
+        odd = start & 1
+        lane = pl.multiple_of((start - odd + 6) * BS, 2 * BS)
+        frame[odd, :, pl.ds(lane, WINDOW * BS)] += message[0].astype(jnp.float32)
+
     for i, message in enumerate((m0, m1, own, m3, m4)):
-        add(message, top - 6 * i, WINDOW)
-    far_start = jnp.where(s == 1, jnp.where(j == 0, 30, 28), jnp.where(j == 2, -2, 0))
-    add(far, far_start, FAR)
-    out[0] = frame[:, 2 * BS : (2 + BAND) * BS]
+        add(message, 27 - 3 * s - j - 6 * i)
+    add(far, jnp.where(s == 1, 30 - j, -3 - j))
+    first, last = 6 * BS, (6 + BAND) * BS
+    out[0] = frame[0, :, first:last] + frame[1, :, first - BS : last - BS]
 
 
 def permuted(block, pairs):
@@ -245,9 +232,9 @@
     send, far, pt_rows, wt = pl.pallas_call(
         build_kernel,
         out_shape=[
-            jax.ShapeDtypeStruct((3 * GROUPS, BS, WINDOW * BS), bf16),
-            jax.ShapeDtypeStruct((NC, BS, FAR * BS), bf16),
-            jax.ShapeDtypeStruct((3 * GROUPS, BS, K), bf16),
+            jax.ShapeDtypeStruct((ROWS, BS, WINDOW * BS), bf16),
+            jax.ShapeDtypeStruct((NC, BS, WINDOW * BS), bf16),
+            jax.ShapeDtypeStruct((ROWS, BS, K), bf16),
             jax.ShapeDtypeStruct((WCOLS, BS, K), bf16),
         ],
         in_specs=[smem] * 3 + [vmem] * 4,
@@ -257,7 +244,7 @@
             pltpu.VMEM((NC, 3 * AGG, BS, AW), bf16),
             pltpu.VMEM((KP + 1, BS, LANES), bf16),
             pltpu.VMEM((KA + 1, BS, LANES), bf16),
-            pltpu.VMEM((18, BS, K), bf16),
+            pltpu.VMEM((ROWS + NC, BS, K), bf16),
         ],
         compiler_params=params,
         cost_estimate=pl.CostEstimate(flops=24 * 10**9, bytes_accessed=30 * 10**6, transcendentals=0),
@@ -288,9 +275,9 @@
         total_kernel,
         grid=(NC,),
         out_shape=jax.ShapeDtypeStruct((NC, BS, BAND * BS), jnp.float32),
-        in_specs=[smem] + [row_block(WINDOW)] * 5 + [row_block(FAR)],
+        in_specs=[smem] + [row_block(WINDOW)] * 6,
         out_specs=row_block(BAND),
-        scratch_shapes=[pltpu.VMEM((BS, FRAME * BS), jnp.float32)],
+        scratch_shapes=[pltpu.VMEM((2, BS, FRAME * BS), jnp.float32)],
         compiler_params=params,
         cost_estimate=pl.CostEstimate(flops=10**7, bytes_accessed=10**7, transcendentals=0),
         name="total",

time: 228 us -> 192 us (0.84)
  the two profiles are of different devices: /device:TPU:4 before, /device:TPU:0 now
where the time goes in v1:
time: 192 us; the launch traced here: 191 us
  waiting for transfers between devices  78 us (41%)
  Pallas kernels  69.2 us (36%)
  starting transfers between devices  36.6 us (19%)
  local copies, waits for them, and re-layouts  5.08 us (3%)
    ppermute x10, waiting for transfers between devices, permuted(): return lax.ppermute(block, 'dom', pairs)  78 us
    pallas_call x1, Pallas kernels, body(): pl.pallas_call(build_kernel, out_shape=[jax.ShapeDtypeStruct((ROWS, BS, W...  45.3 us
    ppermute x10, starting transfers between devices, permuted(): return lax.ppermute(block, 'dom', pairs)  36.6 us
    pallas_call x1, Pallas kernels, body(): pl.pallas_call(sum_kernel, out_shape=[message, message, jax.ShapeDtypeStr...  17.5 us
    pallas_call x1, Pallas kernels, body(): pl.pallas_call(total_kernel, grid=(NC,), out_shape=jax.ShapeDtypeStruct((...  6.44 us
  transfers between devices with their start and end apart: 10, of which 4 were waited for; matrix products, arithmetic and copies ran while one was open for 1% of the time, Pallas kernels for 9%

profile of v1, /device:TPU:0, one launch (start us, length us, event | category | flops | bytes accessed | tf_op | source)
XLA Modules:
  0.0 190.6 jit_solution(12538729572864329686)
XLA Ops:
  0.0 0.0 copy-start.4
  0.0 0.0 copy-start.5
  0.0 3.6 %fusion.6 = (bf16[8,64,1728]{2,1,0:T(8,128)(2,1)}, bf16[8,64,1728]{2,1,0:T(8,128)(2,1)S(1)}) fusion(bf16[24,64,1728]{2,1,0:T(8,128)(2,1)} %p_own.1), kind=kLoop, calls=%fused_computation.27 | loop fusion | bytes 7077888 | tf_op jit(solution)/shard_map/slice | solution.py:218
  3.6 6.4 %collective-permute-start.3 = (bf16[8,64,1728]{2,1,0:T(8,128)(2,1)}, bf16[8,64,1728]{2,1,0:T(8,128)(2,1)}, u32[]{:S(2)}, u32[]{:S(2)}) collective-permute-start(bf16[8,64,1728]{2,1,0:T(8,128)(2,1)} %get-tuple-element.23), channel_id=1, source_target_pairs={{0,31},{1,0},{2,1},{3,2},{4,3},{5,4},{6,5},{7,6},{8,7},{9,8},{10,9... | collective-permute-start | bytes 5308424 | tf_op jit(solution)/shard_map/ppermute | solution.py:196
  10.0 0.0 collective-permute-start.2
  10.0 0.0 copy-done.4
  10.0 0.1 copy.7
  10.1 0.1 fusion.7
  10.2 0.0 collective-permute-start
  10.2 5.4 %collective-permute-start.1 = (s32[8,27]{0,1:T(8,128)S(1)}, s32[8,27]{0,1:T(8,128)S(1)}, u32[]{:S(2)}, u32[]{:S(2)}) collective-permute-start(s32[8,27]{0,1:T(8,128)S(1)} %get-tuple-element.26), channel_id=1, source_target_pairs={{0,31},{1,0},{2,1},{3,2},{4,3},{5,4},{6,5},{7,6},{8,7},{9,8},{10,9... | collective-permute-start | bytes 2600 | tf_op jit(solution)/shard_map/ppermute | solution.py:196
  15.6 0.0 copy-done.5
  15.6 0.1 select_reduce_fusion.1
  15.7 0.6 broadcast_add_fusion.1.inv_a
  16.3 20.2 %collective-permute-done = s32[8,27]{0,1:T(8,128)S(1)} collective-permute-done((s32[8,27]{0,1:T(8,128)S(1)}, s32[8,27]{0,1:T(8,128)S(1)}, u32[]{:S(2)}, u32[]{:S(2)}) %collective-permute-start) | collective-permute-done | bytes 896 | tf_op jit(solution)/shard_map/ppermute | solution.py:196
  36.5 0.0 collective-permute-done.1
  36.5 0.1 fusion
  36.6 0.2 select_reduce_fusion
  36.9 0.6 broadcast_add_fusion.inv_p
  37.5 0.0 collective-permute-done.3.p_hi
  37.5 0.0 collective-permute-done.2.p_lo
  37.5 45.3 %build.1 = (bf16[15,64,2432]{2,1,0:T(8,128)(2,1)}, bf16[3,64,2432]{2,1,0:T(8,128)(2,1)}, bf16[15,64,1536]{2,1,0:T(8,128)(2,1)}, bf16[44,64,1536]{2,1,0:T(8,128)(2,1)}) custom-call(s32[1]{0:T(128)} %bitcast.core, s32[40,35]{1,0:T(8,128)} %broadcast_add_fusion.inv_p, s32[24,24]{1,0:T(8,128)} %broadcast_add_fusion.1.inv_a, bf16[24,64,1728]{2,1,0:T(8,128)(2,1)} %p_own.1, ...), custom_call_target="tpu_custom_call" | custom-call | flops 24000000000 | bytes 30000000 | tf_op jit(solution)/shard_map/build/pallas_call | solution.py:232
  82.7 10.3 %collective-permute-start.4 = (bf16[15,64,2432]{2,1,0:T(8,128)(2,1)}, bf16[15,64,2432]{2,1,0:T(8,128)(2,1)}, u32[]{:S(2)}, u32[]{:S(2)}) collective-permute-start(bf16[15,64,2432]{2,1,0:T(8,128)(2,1)} %get-tuple-element.16), channel_id=1, source_target_pairs={{0,1},{1,0},{2,3},{3,2},{4,5},{5,4},{6,7},{7,6},{8,9},{9,8},{10,11... | collective-permute-start | bytes 14008328 | tf_op jit(solution)/shard_map/ppermute | solution.py:196
  93.1 5.8 %collective-permute-start.9 = (bf16[3,64,2432]{2,1,0:T(8,128)(2,1)}, bf16[3,64,2432]{2,1,0:T(8,128)(2,1)S(1)}, u32[]{:S(2)}, u32[]{:S(2)}) collective-permute-start(bf16[3,64,2432]{2,1,0:T(8,128)(2,1)} %get-tuple-element.22), channel_id=1, source_target_pairs={{0,27},{1,6},{2,29},{3,8},{4,31},{5,10},{6,1},{7,12},{8,3},{9,14},... | collective-permute-start | bytes 2801672 | tf_op jit(solution)/shard_map/ppermute | solution.py:196
  98.9 2.0 %collective-permute-done.4.arrived = bf16[15,64,2432]{2,1,0:T(8,128)(2,1)} collective-permute-done((bf16[15,64,2432]{2,1,0:T(8,128)(2,1)}, bf16[15,64,2432]{2,1,0:T(8,128)(2,1)}, u32[]{:S(2)}, u32[]{:S(2)}) %collective-permute-start.4) | collective-permute-done | bytes 4669472 | tf_op jit(solution)/shard_map/ppermute | solution.py:196
  100.9 17.5 %add_core.1 = (bf16[3,64,2432]{2,1,0:T(8,128)(2,1)}, bf16[3,64,2432]{2,1,0:T(8,128)(2,1)}, f32[3,64,2432]{2,1,0:T(8,128)}, bf16[3,64,2432]{2,1,0:T(8,128)(2,1)}, bf16[3,64,2432]{2,1,0:T(8,128)(2,1)}) custom-call(s32[1]{0:T(128)} %bitcast.core, bf16[15,64,1536]{2,1,0:T(8,128)(2,1)} %get-tuple-element.14.pt_rows, bf16[44,64,1536]{2,1,0:T(8,128)(2,1)} %get-tuple-element.15.wt, ...), custom_call_target="tpu_custom_call" | custom-call | flops 8000000000 | bytes 25000000 | tf_op jit(solution)/shard_map/add_core/pallas_call | solution.py:257
  118.4 6.0 %collective-permute-start.5 = (bf16[3,64,2432]{2,1,0:T(8,128)(2,1)}, bf16[3,64,2432]{2,1,0:T(8,128)(2,1)S(1)}, u32[]{:S(2)}, u32[]{:S(2)}) collective-permute-start(bf16[3,64,2432]{2,1,0:T(8,128)(2,1)} %get-tuple-element.18), channel_id=1, source_target_pairs={{0,28},{1,29},{2,30},{3,31},{4,0},{5,1},{6,2},{7,3},{8,4},{9,5},{1... | collective-permute-start | bytes 2801672 | tf_op jit(solution)/shard_map/ppermute | solution.py:196
  124.4 1.6 collective-permute-start.6
  126.0 0.4 collective-permute-start.7
  126.4 0.6 collective-permute-start.8
  127.0 0.0 collective-permute-done.9.far
  127.0 0.0 copy-start
  127.0 55.6 %collective-permute-done.5.m0 = bf16[3,64,2432]{2,1,0:T(8,128)(2,1)S(1)} collective-permute-done((bf16[3,64,2432]{2,1,0:T(8,128)(2,1)}, bf16[3,64,2432]{2,1,0:T(8,128)(2,1)S(1)}, u32[]{:S(2)}, u32[]{:S(2)}) %collective-permute-start.5) | collective-permute-done | bytes 933920 | tf_op jit(solution)/shard_map/ppermute | solution.py:196
  182.6 0.0 copy-start.1
  182.6 0.0 collective-permute-done.6.m1
  182.6 0.0 copy-start.2
  182.6 0.0 collective-permute-done.7.m3
  182.6 0.0 copy-start.3
  182.6 0.2 collective-permute-done.8.m4
  182.9 0.0 copy-done
  182.9 0.7 copy-done.1
  183.5 0.3 copy-done.2
  183.8 0.3 copy-done.3
  184.2 6.4 %total.1 = f32[3,64,4032]{2,1,0:T(8,128)} custom-call(s32[1]{0:T(128)} %bitcast.core, f32[3,64,2432]{2,1,0:T(8,128)} %get-tuple-element.17.own, bf16[3,64,2432]{2,1,0:T(8,128)(2,1)} %copy-done.1, bf16[3,64,2432]{2,1,0:T(8,128)(2,1)} %copy-done.2, bf16[3,64,2432]{2,1,0:T(8,128)(2,1)} %copy-done.3, bf16[3,64,2432]{2,1,0:T(8,128)(2,1)} %collective-permute-done.8.m4, ...), custom_call_target="tpu_custom_call" | custom-call | flops 10000000 | bytes 10000000 | tf_op jit(solution)/shard_map/total/pallas_call | solution.py:274
  (5 shorter events, 0.0 us)
Async XLA Ops:
  0.0 10.0 %copy-start.4 = (s32[24,27]{1,0:T(8,128)S(1)}, s32[24,27]{1,0:T(8,128)}, u32[]{:S(2)}) copy-start(s32[24,27]{1,0:T(8,128)} %param.7) | copy-start | bytes 7780
  0.0 15.6 %copy-start.5 = (s32[24,7]{0,1:T(8,128)S(1)}, s32[24,7]{0,1:T(8,128)}, u32[]{:S(2)}) copy-start(s32[24,7]{0,1:T(8,128)} %param.6) | copy-start | bytes 2020
  3.6 33.9 %collective-permute-start.3 = (bf16[8,64,1728]{2,1,0:T(8,128)(2,1)}, bf16[8,64,1728]{2,1,0:T(8,128)(2,1)}, u32[]{:S(2)}, u32[]{:S(2)}) collective-permute-start(bf16[8,64,1728]{2,1,0:T(8,128)(2,1)} %get-tuple-element.23), channel_id=1, source_target_pairs={{0,31},{1,0},{2,1},{3,2},{4,3},{5,4},{6,5},{7,6},{8,7},{9,8},{10,9... | collective-permute-start | bytes 5308424 | tf_op jit(solution)/shard_map/ppermute | solution.py:196
  10.0 27.5 %collective-permute-start.2 = (bf16[8,64,1728]{2,1,0:T(8,128)(2,1)S(1)}, bf16[8,64,1728]{2,1,0:T(8,128)(2,1)}, u32[]{:S(2)}, u32[]{:S(2)}) collective-permute-start(bf16[8,64,1728]{2,1,0:T(8,128)(2,1)S(1)} %get-tuple-element.24), channel_id=1, source_target_pairs={{0,1},{1,2},{2,3},{3,4},{4,5},{5,6},{6,7},{7,8},{8,9},{9,10},{10,1... | collective-permute-start | bytes 5308424 | tf_op jit(solution)/shard_map/ppermute | solution.py:196
  10.2 26.4 %collective-permute-start = (s32[8,27]{0,1:T(8,128)S(1)}, s32[8,27]{0,1:T(8,128)S(1)}, u32[]{:S(2)}, u32[]{:S(2)}) collective-permute-start(s32[8,27]{0,1:T(8,128)S(1)} %get-tuple-element.25), channel_id=1, source_target_pairs={{0,1},{1,2},{2,3},{3,4},{4,5},{5,6},{6,7},{7,8},{8,9},{9,10},{10,1... | collective-permute-start | bytes 2600 | tf_op jit(solution)/shard_map/ppermute | solution.py:196
  10.2 26.4 %collective-permute-start.1 = (s32[8,27]{0,1:T(8,128)S(1)}, s32[8,27]{0,1:T(8,128)S(1)}, u32[]{:S(2)}, u32[]{:S(2)}) collective-permute-start(s32[8,27]{0,1:T(8,128)S(1)} %get-tuple-element.26), channel_id=1, source_target_pairs={{0,31},{1,0},{2,1},{3,2},{4,3},{5,4},{6,5},{7,6},{8,7},{9,8},{10,9... | collective-permute-start | bytes 2600 | tf_op jit(solution)/shard_map/ppermute | solution.py:196
  82.7 18.1 %collective-permute-start.4 = (bf16[15,64,2432]{2,1,0:T(8,128)(2,1)}, bf16[15,64,2432]{2,1,0:T(8,128)(2,1)}, u32[]{:S(2)}, u32[]{:S(2)}) collective-permute-start(bf16[15,64,2432]{2,1,0:T(8,128)(2,1)} %get-tuple-element.16), channel_id=1, source_target_pairs={{0,1},{1,0},{2,3},{3,2},{4,5},{5,4},{6,7},{7,6},{8,9},{9,8},{10,11... | collective-permute-start | bytes 14008328 | tf_op jit(solution)/shard_map/ppermute | solution.py:196
  93.1 33.9 %collective-permute-start.9 = (bf16[3,64,2432]{2,1,0:T(8,128)(2,1)}, bf16[3,64,2432]{2,1,0:T(8,128)(2,1)S(1)}, u32[]{:S(2)}, u32[]{:S(2)}) collective-permute-start(bf16[3,64,2432]{2,1,0:T(8,128)(2,1)} %get-tuple-element.22), channel_id=1, source_target_pairs={{0,27},{1,6},{2,29},{3,8},{4,31},{5,10},{6,1},{7,12},{8,3},{9,14},... | collective-permute-start | bytes 2801672 | tf_op jit(solution)/shard_map/ppermute | solution.py:196
  118.4 64.2 %collective-permute-start.5 = (bf16[3,64,2432]{2,1,0:T(8,128)(2,1)}, bf16[3,64,2432]{2,1,0:T(8,128)(2,1)S(1)}, u32[]{:S(2)}, u32[]{:S(2)}) collective-permute-start(bf16[3,64,2432]{2,1,0:T(8,128)(2,1)} %get-tuple-element.18), channel_id=1, source_target_pairs={{0,28},{1,29},{2,30},{3,31},{4,0},{5,1},{6,2},{7,3},{8,4},{9,5},{1... | collective-permute-start | bytes 2801672 | tf_op jit(solution)/shard_map/ppermute | solution.py:196
  124.4 58.2 %collective-permute-start.6 = (bf16[3,64,2432]{2,1,0:T(8,128)(2,1)}, bf16[3,64,2432]{2,1,0:T(8,128)(2,1)S(1)}, u32[]{:S(2)}, u32[]{:S(2)}) collective-permute-start(bf16[3,64,2432]{2,1,0:T(8,128)(2,1)} %get-tuple-element.19), channel_id=1, source_target_pairs={{0,30},{1,31},{2,0},{3,1},{4,2},{5,3},{6,4},{7,5},{8,6},{9,7},{10,... | collective-permute-start | bytes 2801672 | tf_op jit(solution)/shard_map/ppermute | solution.py:196
  126.0 56.6 %collective-permute-start.7 = (bf16[3,64,2432]{2,1,0:T(8,128)(2,1)}, bf16[3,64,2432]{2,1,0:T(8,128)(2,1)S(1)}, u32[]{:S(2)}, u32[]{:S(2)}) collective-permute-start(bf16[3,64,2432]{2,1,0:T(8,128)(2,1)} %get-tuple-element.20), channel_id=1, source_target_pairs={{0,2},{1,3},{2,4},{3,5},{4,6},{5,7},{6,8},{7,9},{8,10},{9,11},{10,... | collective-permute-start | bytes 2801672 | tf_op jit(solution)/shard_map/ppermute | solution.py:196
  126.4 56.4 %collective-permute-start.8 = (bf16[3,64,2432]{2,1,0:T(8,128)(2,1)}, bf16[3,64,2432]{2,1,0:T(8,128)(2,1)}, u32[]{:S(2)}, u32[]{:S(2)}) collective-permute-start(bf16[3,64,2432]{2,1,0:T(8,128)(2,1)} %get-tuple-element.21), channel_id=1, source_target_pairs={{0,4},{1,5},{2,6},{3,7},{4,8},{5,9},{6,10},{7,11},{8,12},{9,13},{1... | collective-permute-start | bytes 2801672 | tf_op jit(solution)/shard_map/ppermute | solution.py:196
  127.0 55.8 %copy-start = (bf16[3,64,2432]{2,1,0:T(8,128)(2,1)}, bf16[3,64,2432]{2,1,0:T(8,128)(2,1)S(1)}, u32[]{:S(2)}) copy-start(bf16[3,64,2432]{2,1,0:T(8,128)(2,1)S(1)} %collective-permute-done.9.far) | copy-start | bytes 2801668
  182.6 0.9 copy-start.1
  182.6 1.2 copy-start.2
  182.6 1.6 copy-start.3

commit v2 on v1

v2 whole, which is shorter than its diff:
```python
import jax
import jax.numpy as jnp
from jax import lax
from jax.experimental import pallas as pl
from jax.experimental.pallas import tpu as pltpu
from jax.sharding import PartitionSpec as P

BS = 64
KA = 7
KP = 27
AGG = 8
H = 15
NC = 3
NB = 24
WIN = 31
WSLOT = 33
BAND = 63

QUAD = 4
LANES = QUAD * BS
EXT = NB + 2 * AGG
COLS = NC + 2 * H + 2
WCOLS = 40
WINDOW = 38
TILES = 10
GROUPS = 5
K = NB * BS
AW = AGG * BS
FRAME = 76
NT = (((1,), (1,)), ((), ()))
ROWS = NC * GROUPS


def eye(n):
    rows = lax.broadcasted_iota(jnp.int32, (n, n), 0)
    lanes = lax.broadcasted_iota(jnp.int32, (n, n), 1)
    return jnp.where(rows == lanes, 1.0, 0.0).astype(jnp.bfloat16)


def low_half():
    return lax.broadcasted_iota(jnp.int32, (BS, 2 * BS), 1) < BS


def transpose_quad(block, turned, width):
    for start in range(0, width, LANES):
        size = min(LANES, width - start)
        part = lax.dot_general(
            eye(size), block[:, start : start + size], NT, preferred_element_type=jnp.float32
        )
        turned[start // BS : (start + size) // BS] = part.astype(jnp.bfloat16).reshape(
            size // BS, BS, LANES
        )


def spread_quad(turned, index, first, store, count, unroll):
    half = low_half()

    def place(slot, carry):
        for pair in range(2):
            lanes = slice(pair * 2 * BS, (pair + 1) * 2 * BS)
            left = turned[index[first + 2 * pair, slot], :, lanes]
            right = turned[index[first + 2 * pair + 1, slot], :, lanes]
            store(slot, pair, jnp.where(half, left, right))
        return carry

    lax.fori_loop(0, count, place, 0, unroll=unroll)


def fast_kernel(
    core,
    inv_own,
    inv_fast,
    inv_a,
    p_own,
    p_fast,
    a_own,
    send,
    far,
    pt_fast,
    pt_slow,
    pt_other,
    wt,
    rest,
    at_halo,
    p_buf,
    ext,
    at,
    turned_p,
    turned_a,
    lhs,
    send_buf,
    far_buf,
    fast_buf,
    slow_buf,
    other_buf,
    wt_buf,
    rest_buf,
    in_sems,
    out_sems,
):
    s = core[0]
    own_quads = NB // QUAD
    halo_quads = AGG // QUAD

    def load(quad):
        if quad < own_quads:
            source = p_own.at[quad * QUAD : (quad + 1) * QUAD]
        else:
            source = p_fast.at[(quad - own_quads) * QUAD : (quad - own_quads + 1) * QUAD]
        target = p_buf.at[quad * QUAD : (quad + 1) * QUAD]
        return pltpu.make_async_copy(source, target, in_sems.at[quad])

    for quad in range(own_quads + halo_quads):
        load(quad).start()

    turned_p[KP] = jnp.zeros((BS, LANES), jnp.bfloat16)
    turned_a[KA] = jnp.zeros((BS, LANES), jnp.bfloat16)

    @pl.loop(0, own_quads)
    def _(quad):
        block = a_own[pl.ds(quad * QUAD, QUAD)].reshape(LANES, KA * BS)
        transpose_quad(block, turned_a, KA * BS)
        agg = quad // halo_quads

        def store(slot, pair, value):
            lane = pl.multiple_of((quad % halo_quads) * LANES + pair * 2 * BS, 2 * BS)
            at[agg, slot, :, pl.ds(lane, 2 * BS)] = value

        spread_quad(turned_a, inv_a, quad * QUAD, store, 3 * AGG, 8)

    slow_agg = 2 * s
    halo_copy = pltpu.make_async_copy(at.at[slow_agg, pl.ds(16 * s, AGG)], at_halo, out_sems.at[0])
    halo_copy.start()

    def band_quad(source_row, index, index_row, first_lane):
        block = p_buf[pl.ds(source_row, QUAD)].reshape(LANES, KP * BS)
        transpose_quad(block, turned_p, KP * BS)

        def store(slot, pair, value):
            lane = pl.multiple_of(first_lane + pair * 2 * BS, 2 * BS)
            ext[slot, :, pl.ds(lane, 2 * BS)] = value

        spread_quad(turned_p, index, index_row, store, COLS, 7)

    for quad in range(own_quads + halo_quads):
        load(quad).wait()

    @pl.loop(0, own_quads)
    def _(quad):
        band_quad(quad * QUAD, inv_own, quad * QUAD, AW + quad * LANES)

    @pl.loop(0, halo_quads)
    def _(quad):
        first_lane = (AW + K) * (1 - s) + quad * LANES
        band_quad((own_quads + quad) * QUAD, inv_fast, quad * QUAD, first_lane)

    fast_lanes = pl.ds(pl.multiple_of(AW + (1 - s) * AW, AW), 2 * AW)
    slow_lanes = pl.ds(pl.multiple_of(AW + 2 * s * AW, AW), AW)
    for i in range(GROUPS):
        for j in range(NC):
            row = NC * i + j
            mine, other = 6 * i + 3 + j + 1, 6 * i + 6 * (1 - s) + j + 1
            fast_buf[row] = ext[mine, :, fast_lanes]
            slow_buf[row] = ext[mine, :, slow_lanes]
            other_buf[row] = ext[other, :, slow_lanes]
            lhs[row] = ext[other, :, fast_lanes]
    for j in range(NC):
        lhs[ROWS + j] = ext[30 * s + j + 1, :, fast_lanes]
        slow_buf[ROWS + j] = ext[30 * s + j + 1, :, slow_lanes]
    copies = [halo_copy]

    def write(source, target):
        copy = pltpu.make_async_copy(source, target, out_sems.at[len(copies)])
        copy.start()
        copies.append(copy)

    write(other_buf, pt_other)
    write(fast_buf, pt_fast)
    write(slow_buf, pt_slow)

    wt_buf[0:7] = jnp.zeros((7, BS, 2 * AW), jnp.bfloat16)
    wt_buf[33:] = jnp.zeros((WCOLS - 33, BS, 2 * AW), jnp.bfloat16)
    chunk = WSLOT // 3

    @pl.loop(0, 2)
    def _(place):
        agg = place + 1 - s
        lane = pl.multiple_of(agg * AW, AW)
        target = pl.multiple_of(place * AW, AW)

        @pl.loop(0, 3)
        def _(part):
            first = agg + part * chunk
            left = ext[pl.ds(first, chunk), :, pl.ds(lane, 3 * AW)].reshape(chunk * BS, 3 * AW)
            value = jnp.dot(
                left, at[agg].reshape(3 * AW, AW), preferred_element_type=jnp.float32
            )
            wt_buf[pl.ds(3 * s + first, chunk), :, pl.ds(target, AW)] = value.astype(
                jnp.bfloat16
            ).reshape(chunk, BS, AW)

    write(wt_buf, wt)

    @pl.loop(0, 3)
    def _(part):
        lane = pl.multiple_of(AW + s * AW, AW)
        left = ext[pl.ds(slow_agg + part * chunk, chunk), :, pl.ds(lane, 2 * AW)]
        right = at[slow_agg, pl.ds(AGG - AGG * s, 2 * AGG)].reshape(2 * AW, AW)
        value = jnp.dot(
            left.reshape(chunk * BS, 2 * AW), right, preferred_element_type=jnp.float32
        )
        rest_buf[pl.ds(part * chunk, chunk)] = value.reshape(chunk, BS, AW)

    write(rest_buf, rest)

    def emit(tile, width):
        right = wt_buf[pl.ds(QUAD * tile, width // BS)].reshape(width, 2 * AW)
        left = lhs[...].reshape((ROWS + NC) * BS, 2 * AW)
        value = lax.dot_general(left, right, NT, preferred_element_type=jnp.float32)
        value = value.astype(jnp.bfloat16).reshape(ROWS + NC, BS, width)
        lanes = pl.ds(pl.multiple_of(tile * LANES, LANES), width)
        send_buf[:, :, lanes] = value[:ROWS]
        far_buf[:, :, lanes] = value[ROWS:]

    half = TILES // 2

    @pl.loop(0, half)
    def _(tile):
        emit(tile, LANES)

    write(send_buf.at[:, :, : half * LANES], send.at[:, :, : half * LANES])

    @pl.loop(half, TILES - 1)
    def _(tile):
        emit(tile, LANES)

    emit(TILES - 1, LANES // 2)
    write(send_buf.at[:, :, half * LANES :], send.at[:, :, half * LANES :])
    write(far_buf, far)
    for copy in copies:
        copy.wait()


def mine_kernel(pt_fast, wt, out):
    right = wt[...].reshape(LANES, 2 * AW)
    left = pt_fast[...].reshape(ROWS * BS, 2 * AW)
    value = lax.dot_general(left, right, NT, preferred_element_type=jnp.float32)
    out[...] = value.astype(out.dtype).reshape(ROWS, BS, LANES)


def slow_kernel(core, inv_slow, p_slow, at_halo, rest, wt, turned_p, ext):
    s = core[0]
    turned_p[KP] = jnp.zeros((BS, LANES), jnp.bfloat16)

    @pl.loop(0, AGG // QUAD)
    def _(quad):
        block = p_slow[pl.ds(quad * QUAD, QUAD)].reshape(LANES, KP * BS)
        transpose_quad(block, turned_p, KP * BS)

        def store(slot, pair, value):
            lane = pl.multiple_of(quad * LANES + pair * 2 * BS, 2 * BS)
            ext[slot, :, pl.ds(lane, 2 * BS)] = value

        spread_quad(turned_p, inv_slow, quad * QUAD, store, WSLOT, 11)

    wt[0:5] = jnp.zeros((5, BS, AW), jnp.bfloat16)
    wt[WSLOT:] = jnp.zeros((WCOLS - WSLOT, BS, AW), jnp.bfloat16)
    chunk = WSLOT // 3

    @pl.loop(0, 3)
    def _(part):
        rows = pl.ds(part * chunk, chunk)
        value = jnp.dot(
            ext[rows].reshape(chunk * BS, AW),
            at_halo[...].reshape(AW, AW),
            preferred_element_type=jnp.float32,
        )
        value = value.reshape(chunk, BS, AW) + rest[rows]
        wt[pl.ds(5 * s + part * chunk, chunk)] = value.astype(jnp.bfloat16)


def join_kernel(pt_slow, pt_other, wt_slow, wt_other, mine, arrived, far_fast, *outs):
    right = wt_slow[...].reshape(LANES, AW)
    left = pt_slow[...].reshape((ROWS + NC) * BS, AW)
    value = lax.dot_general(left, right, NT, preferred_element_type=jnp.float32)
    value = value.reshape(ROWS + NC, BS, LANES)
    right = wt_other[...].reshape(LANES, AW)
    left = pt_other[...].reshape(ROWS * BS, AW)
    other = lax.dot_general(left, right, NT, preferred_element_type=jnp.float32)
    other = other.reshape(ROWS, BS, LANES) + mine[...].astype(jnp.float32)
    near = value[:ROWS] + (other + arrived[...].astype(jnp.float32))
    for i in range(GROUPS):
        outs[i][...] = near[NC * i : NC * (i + 1)].astype(outs[i].dtype)
    outs[GROUPS][...] = (value[ROWS:] + far_fast[...].astype(jnp.float32)).astype(jnp.bfloat16)


def total_kernel(core, own, m0, m1, m3, m4, far, out, frame):
    s = core[0]
    j = pl.program_id(0)
    frame[...] = jnp.zeros_like(frame)

    def add(message, start):
        odd = start & 1
        lane = pl.multiple_of((start - odd + 6) * BS, 2 * BS)
        frame[odd, :, pl.ds(lane, WINDOW * BS)] += message[0].astype(jnp.float32)

    for i, message in enumerate((m0, m1, own, m3, m4)):
        add(message, 27 - 3 * s - j - 6 * i)
    add(far, jnp.where(s == 1, 30 - j, -3 - j))
    first, last = 6 * BS, (6 + BAND) * BS
    out[0] = frame[0, :, first:last] + frame[1, :, first - BS : last - BS]


def permuted(block, pairs):
    return lax.ppermute(block, "dom", pairs)


def inverse_index(offset, slots, empty):
    order = jnp.arange(offset.shape[1], dtype=jnp.int32)[None, :, None]
    hit = offset[:, :, None] == jnp.arange(slots, dtype=jnp.int32)[None, None, :]
    return empty + jnp.sum(jnp.where(hit, order - empty, 0), axis=1)


def body(a_blocks, p_blocks, cols_a, cols_p):
    devices = lax.axis_size("dom")
    device = lax.axis_index("dom")
    count_agg = NC * devices
    count_rows = NB * devices
    first_agg = device * NC
    first_row = device * NB
    core = (device % 2).astype(jnp.int32).reshape(1)

    def shifted(distance):
        return [(i, (i + distance) % devices) for i in range(devices)]

    high = NB - AGG
    parity = device % 2

    def halo(array, first, pairs):
        return permuted(lax.dynamic_slice_in_dim(array, first, AGG), pairs)

    outward = [(i, (i + (1 if i % 2 else -1)) % devices) for i in range(devices)]
    inward = [(i, i ^ 1) for i in range(devices)]
    cols_slow = halo(cols_p, high * parity, outward)
    p_slow = halo(p_blocks, high * parity, outward)
    cols_fast = halo(cols_p, high * (1 - parity), inward)
    p_fast = halo(p_blocks, high * (1 - parity), inward)

    def slots(cols, agg):
        return (cols - agg + H) % count_agg

    own_agg = jnp.arange(NB, dtype=jnp.int32)[:, None] // AGG
    inv_own = inverse_index(slots(cols_p, first_agg + own_agg) + own_agg + 1, COLS, KP)
    fast_place = NC * (1 - parity) - parity
    inv_fast = inverse_index(slots(cols_fast, first_agg + fast_place) + fast_place + 1, COLS, KP)
    slow_place = NC * parity - (1 - parity)
    inv_slow = inverse_index(slots(cols_slow, first_agg + slow_place) + 2 * parity, WSLOT, KP)
    inv_a = inverse_index((cols_a - first_row - (own_agg - 1) * AGG) % count_rows, 3 * AGG, KA)

    smem = pl.BlockSpec(memory_space=pltpu.SMEM)
    vmem = pl.BlockSpec(memory_space=pltpu.VMEM)
    hbm = pl.BlockSpec(memory_space=pl.ANY)
    bf16 = jnp.bfloat16

    def params(mebibytes):
        return pltpu.CompilerParams(vmem_limit_bytes=mebibytes * 1024 * 1024)

    def cost(flops, size):
        return pl.CostEstimate(flops=flops, bytes_accessed=size, transcendentals=0)

    shapes = [
        (ROWS, BS, WINDOW * BS),
        (NC, BS, WINDOW * BS),
        (ROWS, BS, 2 * AW),
        (ROWS + NC, BS, AW),
        (ROWS, BS, AW),
        (WCOLS, BS, 2 * AW),
        (WSLOT, BS, AW),
        (AGG, BS, AW),
    ]
    kinds = [bf16] * 6 + [jnp.float32, bf16]
    send, far, pt_fast, pt_slow, pt_other, wt_fast, rest, at_halo = pl.pallas_call(
        fast_kernel,
        out_shape=[jax.ShapeDtypeStruct(shape, kind) for shape, kind in zip(shapes, kinds)],
        in_specs=[smem] * 4 + [hbm, hbm, vmem],
        out_specs=[hbm] * 8,
        scratch_shapes=[
            pltpu.VMEM((NB + AGG, BS, KP * BS), bf16),
            pltpu.VMEM((COLS, BS, EXT * BS), bf16),
            pltpu.VMEM((NC, 3 * AGG, BS, AW), bf16),
            pltpu.VMEM((KP + 1, BS, LANES), bf16),
            pltpu.VMEM((KA + 1, BS, LANES), bf16),
            pltpu.VMEM((ROWS + NC, BS, 2 * AW), bf16),
        ]
        + [pltpu.VMEM(shape, kind) for shape, kind in zip(shapes[:7], kinds[:7])]
        + [pltpu.SemaphoreType.DMA(((NB + AGG) // QUAD,)), pltpu.SemaphoreType.DMA((9,))],
        compiler_params=params(56),
        cost_estimate=cost(20 * 10**9, 30 * 10**6),
        name="fast",
    )(core, inv_own, inv_fast, inv_a, p_blocks, p_fast, a_blocks)

    arrived = permuted(send, inward)
    pt_other = permuted(pt_other, inward)

    def lane_tile(rows):
        return pl.BlockSpec((rows, BS, LANES), lambda n: (0, 0, n))

    def col_tile(width):
        return pl.BlockSpec((QUAD, BS, width), lambda n: (n, 0, 0))

    def whole(rows, width):
        return pl.BlockSpec((rows, BS, width), lambda n: (0, 0, 0))

    mine = pl.pallas_call(
        mine_kernel,
        grid=(TILES,),
        out_shape=jax.ShapeDtypeStruct((ROWS, BS, WINDOW * BS), bf16),
        in_specs=[whole(ROWS, 2 * AW), col_tile(2 * AW)],
        out_specs=lane_tile(ROWS),
        compiler_params=params(16),
        cost_estimate=cost(60 * 10**9, 120 * 10**6),
        name="mine",
    )(pt_fast, wt_fast)

    wt_slow = pl.pallas_call(
        slow_kernel,
        out_shape=jax.ShapeDtypeStruct((WCOLS, BS, AW), bf16),
        in_specs=[smem] * 2 + [vmem] * 3,
        out_specs=vmem,
        scratch_shapes=[
            pltpu.VMEM((KP + 1, BS, LANES), bf16),
            pltpu.VMEM((WSLOT, BS, AW), bf16),
        ],
        compiler_params=params(24),
        cost_estimate=cost(20 * 10**9, 120 * 10**6),
        name="slow",
    )(core, inv_slow, p_slow, at_halo, rest)
    wt_other = permuted(wt_slow, inward)

    message = jax.ShapeDtypeStruct((NC, BS, WINDOW * BS), bf16)
    m0, m1, own, m3, m4, far = pl.pallas_call(
        join_kernel,
        grid=(TILES,),
        out_shape=[message] * 2
        + [jax.ShapeDtypeStruct(message.shape, jnp.float32)]
        + [message] * 3,
        in_specs=[whole(ROWS + NC, AW), whole(ROWS, AW)]
        + [col_tile(AW)] * 2
        + [lane_tile(ROWS)] * 2
        + [lane_tile(NC)],
        out_specs=[lane_tile(NC)] * 6,
        compiler_params=params(24),
        cost_estimate=cost(5 * 10**9, 22 * 10**6),
        name="join",
    )(pt_slow, pt_other, wt_slow, wt_other, mine, arrived, far)
    far = permuted(far, [(i, (i + (5 if i % 2 else -5)) % devices) for i in range(devices)])
    m0 = permuted(m0, shifted(-4))
    m4 = permuted(m4, shifted(4))
    m1 = permuted(m1, shifted(-2))
    m3 = permuted(m3, shifted(2))

    def row_block(blocks):
        return pl.BlockSpec((1, BS, blocks * BS), lambda j: (j, 0, 0))

    return pl.pallas_call(
        total_kernel,
        grid=(NC,),
        out_shape=jax.ShapeDtypeStruct((NC, BS, BAND * BS), jnp.float32),
        in_specs=[smem] + [row_block(WINDOW)] * 6,
        out_specs=row_block(BAND),
        scratch_shapes=[pltpu.VMEM((2, BS, FRAME * BS), jnp.float32)],
        compiler_params=params(20),
        cost_estimate=pl.CostEstimate(flops=10**7, bytes_accessed=10**7, transcendentals=0),
        name="total",
    )(core, own, m0, m1, m3, m4, far)


def solution(mesh):
    in_specs = (P("dom", None, None), P("dom", None, None), P("dom", None), P("dom", None))
    out_specs = P("dom", None, None)
    return jax.shard_map(body, mesh=mesh, in_specs=in_specs, out_specs=out_specs, check_vma=False)
```

time: 192 us -> 170 us (0.89)
  the two profiles are of different devices: /device:TPU:0 before, /device:TPU:4 now
where the time goes in v2:
time: 170 us
  waiting for transfers between devices  81 us (48%)
  Pallas kernels  61.8 us (36%)
  starting transfers between devices  15.6 us (9%)
  local copies, waits for them, and re-layouts  8.49 us (5%)
  other arithmetic  2.46 us (1%)
    ppermute x12, waiting for transfers between devices, permuted(): return lax.ppermute(block, 'dom', pairs)  81 us
    pallas_call x1, Pallas kernels, body(): pl.pallas_call(fast_kernel, out_shape=[jax.ShapeDtypeStruct(shape, kind)...  34.5 us
    ppermute x12, starting transfers between devices, permuted(): return lax.ppermute(block, 'dom', pairs)  15.6 us
    pallas_call x1, Pallas kernels, body(): pl.pallas_call(join_kernel, grid=(TILES,), out_shape=[message] * 2 + [jax...  11.7 us
    pallas_call x1, Pallas kernels, body(): pl.pallas_call(mine_kernel, grid=(TILES,), out_shape=jax.ShapeDtypeStruct...  7.71 us
    dynamic_slice x2, local copies, waits for them, and re-layouts, halo(): return permuted(lax.dynamic_slice_in_dim(array, first, AGG), pairs)  4.94 us
    pallas_call x1, Pallas kernels, body(): pl.pallas_call(slow_kernel, out_shape=jax.ShapeDtypeStruct((WCOLS, BS, AW...  4.21 us
    pallas_call x1, Pallas kernels, body(): pl.pallas_call(total_kernel, grid=(NC,), out_shape=jax.ShapeDtypeStruct((...  3.74 us
  transfers between devices with their start and end apart: 12, of which 6 were waited for; matrix products, arithmetic and copies ran while one was open for 4% of the time, Pallas kernels for 27%

profile of v2, /device:TPU:4, one launch (start us, length us, event | category | flops | bytes accessed | tf_op | source)
XLA Modules:
  0.0 169.5 jit_solution(8512648535875935318)
XLA Ops:
  0.0 0.7 constant_dynamic-slice_fusion.1
  0.7 0.9 collective-permute-start.3
  1.6 0.7 collective-permute-start
  2.3 4.2 %constant_dynamic-slice_fusion.3 = (bf16[8,64,1728]{2,1,0:T(8,128)(2,1)}, bf16[8,64,1728]{2,1,0:T(8,128)(2,1)}) fusion(bf16[24,64,1728]{2,1,0:T(8,128)(2,1)} %p_own.1, s32[]{:T(128)S(6)} %select_n.84, s32[]{:T(128)S(6)} %select_n.79), kind=kLoop, calls=%fused_computation.32 | loop fusion | bytes 7077896 | tf_op jit(solution)/shard_map/dynamic_slice | solution.py:340
  6.5 1.1 collective-permute-start.4
  7.6 0.5 collective-permute-start.1
  8.2 0.0 copy-done.6
  8.2 0.1 fusion.1
  8.3 0.1 copy.6
  8.4 0.0 copy-done.7
  8.4 0.1 select_reduce_fusion.3
  8.5 0.2 select_reduce_fusion
  8.7 0.6 broadcast_add_fusion.inv_a
  9.3 0.6 broadcast_add_fusion.1.inv_own
  9.9 0.0 collective-permute-done.3
  9.9 0.1 copy.8
  10.0 0.0 collective-permute-done
  10.0 0.1 copy.7
  10.1 0.1 select_reduce_fusion.1
  10.2 0.1 select_reduce_fusion.2
  10.4 0.6 broadcast_add_fusion.3.inv_fast
  11.0 1.0 collective-permute-done.1.p_fast
  11.9 34.5 %fast.1 = (bf16[15,64,2432]{2,1,0:T(8,128)(2,1)}, bf16[3,64,2432]{2,1,0:T(8,128)(2,1)}, bf16[15,64,1024]{2,1,0:T(8,128)(2,1)}, bf16[18,64,512]{2,1,0:T(8,128)(2,...) custom-call(s32[1]{0:T(128)} %bitcast.core, ...), custom_call_target="tpu_custom_call" | custom-call | flops 20000000000 | bytes 30000000 | tf_op jit(solution)/shard_map/fast/pallas_call | solution.py:382
  46.4 0.4 collective-permute-start.2
  46.8 1.4 collective-permute-done.4.p_slow
  48.2 2.2 %copy-done.3 = f32[33,64,512]{2,1,0:T(8,128)S(1)} copy-done((f32[33,64,512]{2,1,0:T(8,128)S(1)}, f32[33,64,512]{2,1,0:T(8,128)}, u32[]{:S(2)}) %copy-start.3) | copy-done | bytes 4325400
  50.4 1.0 copy-done.5
  51.5 4.2 %slow.1.wt_slow = bf16[40,64,512]{2,1,0:T(8,128)(2,1)S(1)} custom-call(s32[1]{0:T(128)} %bitcast.core, s32[8,33]{1,0:T(8,128)S(1)} %broadcast_add_fusion.2.inv_slow, bf16[8,64,1728]{2,1,0:T(8,128)(2,1)S(1)} %collective-permute-done.4.p_slow, bf16[8,64,512]{2,1,0:T(8,128)(2,1)S(1)} %copy-done.5, f32[33,64,512]{2,1,0:T(8,128)S(1)} %copy-done.3), custom_call_target="tpu_custom_call" | custom-call | flops 20000000000 | bytes 120000000 | tf_op jit(solution)/shard_map/slow/pallas_call | solution.py:425
  55.7 1.0 collective-permute-start.5
  56.7 0.1 collective-permute-start.6
  56.7 0.0 copy-done.4
  56.8 7.7 %mine.1 = bf16[15,64,2432]{2,1,0:T(8,128)(2,1)S(1)} custom-call(bf16[15,64,1024]{2,1,0:T(8,128)(2,1)S(1)} %copy-done.4, bf16[40,64,1024]{2,1,0:T(8,128)(2,1)S(1)} %copy-done.2), custom_call_target="tpu_custom_call" | custom-call | flops 60000002048 | bytes 120000000 | tf_op jit(solution)/shard_map/mine/pallas_call | solution.py:414
  64.5 0.0 collective-permute-done.2.pt_other
  64.5 0.0 collective-permute-done.5.wt_other
  64.5 3.6 %collective-permute-done.6.arrived = bf16[15,64,2432]{2,1,0:T(8,128)(2,1)S(1)} collective-permute-done((bf16[15,64,2432]{2,1,0:T(8,128)(2,1)}, bf16[15,64,2432]{2,1,0:T(8,128)(2,1)S(1)}, u32[]{:S(2)}, u32[]{:S(2)}) %collective-permute-start.6) | collective-permute-done | bytes 4669472 | tf_op jit(solution)/shard_map/ppermute | solution.py:315
  68.1 0.0 copy-done.1
  68.1 11.7 %join.1 = (bf16[3,64,2432]{2,1,0:T(8,128)(2,1)S(1)}, bf16[3,64,2432]{2,1,0:T(8,128)(2,1)S(1)}, f32[3,64,2432]{2,1,0:T(8,128)S(1)}, bf16[3,64,2432]{2,1,0:T(8,128...) custom-call(bf16[18,64,512]{2,1,0:T(8,128)(2,1)S(1)} %copy-done, ...), custom_call_target="tpu_custom_call" | custom-call | flops 5000000000 | bytes 22000000 | tf_op jit(solution)/shard_map/join/pallas_call | solution.py:441
  79.8 1.8 %collective-permute-start.7 = (bf16[3,64,2432]{2,1,0:T(8,128)(2,1)S(1)}, bf16[3,64,2432]{2,1,0:T(8,128)(2,1)S(1)}, u32[]{:S(2)}, u32[]{:S(2)}) collective-permute-start(bf16[3,64,2432]{2,1,0:T(8,128)(2,1)S(1)} %get-tuple-element.28), channel_id=1, source_target_pairs={{0,28},{1,29},{2,30},{3,31},{4,0},{5,1},{6,2},{7,3},{8,4},{9,5},{1... | collective-permute-start | bytes 2801672 | tf_op jit(solution)/shard_map/ppermute | solution.py:315
  81.6 4.3 %collective-permute-start.8 = (bf16[3,64,2432]{2,1,0:T(8,128)(2,1)S(1)}, bf16[3,64,2432]{2,1,0:T(8,128)(2,1)S(1)}, u32[]{:S(2)}, u32[]{:S(2)}) collective-permute-start(bf16[3,64,2432]{2,1,0:T(8,128)(2,1)S(1)} %get-tuple-element.29), channel_id=1, source_target_pairs={{0,30},{1,31},{2,0},{3,1},{4,2},{5,3},{6,4},{7,5},{8,6},{9,7},{10,... | collective-permute-start | bytes 2801672 | tf_op jit(solution)/shard_map/ppermute | solution.py:315
  85.9 0.0 collective-permute-start.9
  85.9 0.7 collective-permute-start.10
  86.6 4.1 %collective-permute-start.11 = (bf16[3,64,2432]{2,1,0:T(8,128)(2,1)S(1)}, bf16[3,64,2432]{2,1,0:T(8,128)(2,1)S(1)}, u32[]{:S(2)}, u32[]{:S(2)}) collective-permute-start(bf16[3,64,2432]{2,1,0:T(8,128)(2,1)S(1)} %get-tuple-element.32), channel_id=1, source_target_pairs={{0,27},{1,6},{2,29},{3,8},{4,31},{5,10},{6,1},{7,12},{8,3},{9,14},... | collective-permute-start | bytes 2801672 | tf_op jit(solution)/shard_map/ppermute | solution.py:315
  90.7 61.4 %collective-permute-done.7.m0 = bf16[3,64,2432]{2,1,0:T(8,128)(2,1)S(1)} collective-permute-done((bf16[3,64,2432]{2,1,0:T(8,128)(2,1)S(1)}, bf16[3,64,2432]{2,1,0:T(8,128)(2,1)S(1)}, u32[]{:S(2)}, u32[]{:S(2)}) %collective-permute-start.7) | collective-permute-done | bytes 933920 | tf_op jit(solution)/shard_map/ppermute | solution.py:315
  152.2 0.0 collective-permute-done.8.m1
  152.2 0.0 collective-permute-done.9.m3
  152.2 1.6 collective-permute-done.10.m4
  153.8 12.0 %collective-permute-done.11.far = bf16[3,64,2432]{2,1,0:T(8,128)(2,1)S(1)} collective-permute-done((bf16[3,64,2432]{2,1,0:T(8,128)(2,1)S(1)}, bf16[3,64,2432]{2,1,0:T(8,128)(2,1)S(1)}, u32[]{:S(2)}, u32[]{:S(2)}) %collective-permute-start.11) | collective-permute-done | bytes 933920 | tf_op jit(solution)/shard_map/ppermute | solution.py:315
  165.8 3.7 %total.1 = f32[3,64,4032]{2,1,0:T(8,128)} custom-call(s32[1]{0:T(128)} %bitcast.core, f32[3,64,2432]{2,1,0:T(8,128)S(1)} %get-tuple-element.27.own, bf16[3,64,2432]{2,1,0:T(8,128)(2,1)S(1)} %collective-permute-done.7.m0, bf16[3,64,2432]{2,1,0:T(8,128)(2,1)S(1)} %collective-permute-done.8.m1, bf16[3,64,2432]{2,1,0:T(8,128)(2,1)S(1)} %collective-permute-done.9.m3, ...), custom_call_target="tpu_custom_call" | custom-call | flops 10000000 | bytes 10000000 | tf_op jit(solution)/shard_map/total/pallas_call | solution.py:465
  (18 shorter events, 0.1 us)
Async XLA Ops:
  0.7 9.2 %collective-permute-start.3 = (s32[8,27]{1,0:T(8,128)S(1)}, s32[8,27]{1,0:T(8,128)S(1)}, u32[]{:S(2)}, u32[]{:S(2)}) collective-permute-start(s32[8,27]{1,0:T(8,128)S(1)} %get-tuple-element.35), channel_id=1, source_target_pairs={{0,31},{1,2},{2,1},{3,4},{4,3},{5,6},{6,5},{7,8},{8,7},{9,10},{10,... | collective-permute-start | bytes 2600 | tf_op jit(solution)/shard_map/ppermute | solution.py:315
  1.6 6.6 %copy-start.6 = (s32[24,27]{1,0:T(8,128)S(1)}, s32[24,27]{1,0:T(8,128)}, u32[]{:S(2)}) copy-start(s32[24,27]{1,0:T(8,128)} %param.7) | copy-start | bytes 7780
  1.6 6.8 %copy-start.7 = (s32[24,7]{0,1:T(8,128)S(1)}, s32[24,7]{0,1:T(8,128)}, u32[]{:S(2)}) copy-start(s32[24,7]{0,1:T(8,128)} %param.6) | copy-start | bytes 2020
  1.6 8.4 %collective-permute-start = (s32[8,27]{1,0:T(8,128)S(1)}, s32[8,27]{1,0:T(8,128)S(1)}, u32[]{:S(2)}, u32[]{:S(2)}) collective-permute-start(s32[8,27]{1,0:T(8,128)S(1)} %get-tuple-element.36), channel_id=1, source_target_pairs={{0,1},{1,0},{2,3},{3,2},{4,5},{5,4},{6,7},{7,6},{8,9},{9,8},{10,11... | collective-permute-start | bytes 2600 | tf_op jit(solution)/shard_map/ppermute | solution.py:315
  6.5 41.6 %collective-permute-start.4 = (bf16[8,64,1728]{2,1,0:T(8,128)(2,1)}, bf16[8,64,1728]{2,1,0:T(8,128)(2,1)S(1)}, u32[]{:S(2)}, u32[]{:S(2)}) collective-permute-start(bf16[8,64,1728]{2,1,0:T(8,128)(2,1)} %get-tuple-element.33), channel_id=1, source_target_pairs={{0,31},{1,2},{2,1},{3,4},{4,3},{5,6},{6,5},{7,8},{8,7},{9,10},{10,... | collective-permute-start | bytes 5308424 | tf_op jit(solution)/shard_map/ppermute | solution.py:315
  7.6 4.3 %collective-permute-start.1 = (bf16[8,64,1728]{2,1,0:T(8,128)(2,1)}, bf16[8,64,1728]{2,1,0:T(8,128)(2,1)}, u32[]{:S(2)}, u32[]{:S(2)}) collective-permute-start(bf16[8,64,1728]{2,1,0:T(8,128)(2,1)} %get-tuple-element.34), channel_id=1, source_target_pairs={{0,1},{1,0},{2,3},{3,2},{4,5},{5,4},{6,7},{7,6},{8,9},{9,8},{10,11... | collective-permute-start | bytes 5308424 | tf_op jit(solution)/shard_map/ppermute | solution.py:315
  46.4 18.1 %collective-permute-start.2 = (bf16[15,64,512]{2,1,0:T(8,128)(2,1)}, bf16[15,64,512]{2,1,0:T(8,128)(2,1)S(1)}, u32[]{:S(2)}, u32[]{:S(2)}) collective-permute-start(bf16[15,64,512]{2,1,0:T(8,128)(2,1)} %get-tuple-element.20), channel_id=1, source_target_pairs={{0,1},{1,0},{2,3},{3,2},{4,5},{5,4},{6,7},{7,6},{8,9},{9,8},{10,11... | collective-permute-start | bytes 2949128 | tf_op jit(solution)/shard_map/ppermute | solution.py:315
  48.2 2.2 %copy-start.3 = (f32[33,64,512]{2,1,0:T(8,128)S(1)}, f32[33,64,512]{2,1,0:T(8,128)}, u32[]{:S(2)}) copy-start(f32[33,64,512]{2,1,0:T(8,128)} %get-tuple-element.22.rest) | copy-start | bytes 12976132
  50.4 1.0 copy-start.5
  51.5 5.3 %copy-start.2 = (bf16[40,64,1024]{2,1,0:T(8,128)(2,1)S(1)}, bf16[40,64,1024]{2,1,0:T(8,128)(2,1)}, u32[]{:S(2)}) copy-start(bf16[40,64,1024]{2,1,0:T(8,128)(2,1)} %get-tuple-element.24.wt) | copy-start | bytes 15728644
  51.5 5.3 %copy-start.4 = (bf16[15,64,1024]{2,1,0:T(8,128)(2,1)S(1)}, bf16[15,64,1024]{2,1,0:T(8,128)(2,1)}, u32[]{:S(2)}) copy-start(bf16[15,64,1024]{2,1,0:T(8,128)(2,1)} %get-tuple-element.23.pt_fast) | copy-start | bytes 5898244
  55.7 8.8 %collective-permute-start.5 = (bf16[40,64,512]{2,1,0:T(8,128)(2,1)S(1)}, bf16[40,64,512]{2,1,0:T(8,128)(2,1)S(1)}, u32[]{:S(2)}, u32[]{:S(2)}) collective-permute-start(bf16[40,64,512]{2,1,0:T(8,128)(2,1)S(1)} %slow.1.wt_slow), channel_id=1, source_target_pairs={{0,1},{1,0},{2,3},{3,2},{4,5},{5,4},{6,7},{7,6},{8,9},{9,8},{10,11... | collective-permute-start | bytes 7864328 | tf_op jit(solution)/shard_map/ppermute | solution.py:315
  56.7 11.4 %collective-permute-start.6 = (bf16[15,64,2432]{2,1,0:T(8,128)(2,1)}, bf16[15,64,2432]{2,1,0:T(8,128)(2,1)S(1)}, u32[]{:S(2)}, u32[]{:S(2)}) collective-permute-start(bf16[15,64,2432]{2,1,0:T(8,128)(2,1)} %get-tuple-element.25), channel_id=1, source_target_pairs={{0,1},{1,0},{2,3},{3,2},{4,5},{5,4},{6,7},{7,6},{8,9},{9,8},{10,11... | collective-permute-start | bytes 14008328 | tf_op jit(solution)/shard_map/ppermute | solution.py:315
  56.7 11.3 %copy-start = (bf16[18,64,512]{2,1,0:T(8,128)(2,1)S(1)}, bf16[18,64,512]{2,1,0:T(8,128)(2,1)}, u32[]{:S(2)}) copy-start(bf16[18,64,512]{2,1,0:T(8,128)(2,1)} %get-tuple-element.19.pt_slow) | copy-start | bytes 3538948
  56.7 11.3 %copy-start.1 = (bf16[3,64,2432]{2,1,0:T(8,128)(2,1)S(1)}, bf16[3,64,2432]{2,1,0:T(8,128)(2,1)}, u32[]{:S(2)}) copy-start(bf16[3,64,2432]{2,1,0:T(8,128)(2,1)} %get-tuple-element.26.far_fast) | copy-start | bytes 2801668
  79.8 72.4 %collective-permute-start.7 = (bf16[3,64,2432]{2,1,0:T(8,128)(2,1)S(1)}, bf16[3,64,2432]{2,1,0:T(8,128)(2,1)S(1)}, u32[]{:S(2)}, u32[]{:S(2)}) collective-permute-start(bf16[3,64,2432]{2,1,0:T(8,128)(2,1)S(1)} %get-tuple-element.28), channel_id=1, source_target_pairs={{0,28},{1,29},{2,30},{3,31},{4,0},{5,1},{6,2},{7,3},{8,4},{9,5},{1... | collective-permute-start | bytes 2801672 | tf_op jit(solution)/shard_map/ppermute | solution.py:315
  81.6 70.5 %collective-permute-start.8 = (bf16[3,64,2432]{2,1,0:T(8,128)(2,1)S(1)}, bf16[3,64,2432]{2,1,0:T(8,128)(2,1)S(1)}, u32[]{:S(2)}, u32[]{:S(2)}) collective-permute-start(bf16[3,64,2432]{2,1,0:T(8,128)(2,1)S(1)} %get-tuple-element.29), channel_id=1, source_target_pairs={{0,30},{1,31},{2,0},{3,1},{4,2},{5,3},{6,4},{7,5},{8,6},{9,7},{10,... | collective-permute-start | bytes 2801672 | tf_op jit(solution)/shard_map/ppermute | solution.py:315
  85.9 66.2 %collective-permute-start.9 = (bf16[3,64,2432]{2,1,0:T(8,128)(2,1)S(1)}, bf16[3,64,2432]{2,1,0:T(8,128)(2,1)S(1)}, u32[]{:S(2)}, u32[]{:S(2)}) collective-permute-start(bf16[3,64,2432]{2,1,0:T(8,128)(2,1)S(1)} %get-tuple-element.30), channel_id=1, source_target_pairs={{0,2},{1,3},{2,4},{3,5},{4,6},{5,7},{6,8},{7,9},{8,10},{9,11},{10,... | collective-permute-start | bytes 2801672 | tf_op jit(solution)/shard_map/ppermute | solution.py:315
  85.9 67.8 %collective-permute-start.10 = (bf16[3,64,2432]{2,1,0:T(8,128)(2,1)S(1)}, bf16[3,64,2432]{2,1,0:T(8,128)(2,1)S(1)}, u32[]{:S(2)}, u32[]{:S(2)}) collective-permute-start(bf16[3,64,2432]{2,1,0:T(8,128)(2,1)S(1)} %get-tuple-element.31), channel_id=1, source_target_pairs={{0,4},{1,5},{2,6},{3,7},{4,8},{5,9},{6,10},{7,11},{8,12},{9,13},{1... | collective-permute-start | bytes 2801672 | tf_op jit(solution)/shard_map/ppermute | solution.py:315
  86.6 79.2 %collective-permute-start.11 = (bf16[3,64,2432]{2,1,0:T(8,128)(2,1)S(1)}, bf16[3,64,2432]{2,1,0:T(8,128)(2,1)S(1)}, u32[]{:S(2)}, u32[]{:S(2)}) collective-permute-start(bf16[3,64,2432]{2,1,0:T(8,128)(2,1)S(1)} %get-tuple-element.32), channel_id=1, source_target_pairs={{0,27},{1,6},{2,29},{3,8},{4,31},{5,10},{6,1},{7,12},{8,3},{9,14},... | collective-permute-start | bytes 2801672 | tf_op jit(solution)/shard_map/ppermute | solution.py:315

commit v3 on v2

--- a/solution.py
+++ b/solution.py
@@ -1,3 +1,5 @@
+import functools
+
 import jax
 import jax.numpy as jnp
 from jax import lax
@@ -29,6 +31,9 @@
 FRAME = 76
 NT = (((1,), (1,)), ((), ()))
 ROWS = NC * GROUPS
+FIRST = 2 * NC
+REST = ROWS - FIRST
+ORDER = (0, 4, 1, 3, 2)
 
 
 def eye(n):
@@ -74,11 +79,16 @@
     p_own,
     p_fast,
     a_own,
-    send,
+    send_low,
+    send_high,
+    send_rest,
     far,
-    pt_fast,
-    pt_slow,
-    pt_other,
+    fast_first,
+    fast_rest,
+    slow_first,
+    slow_rest,
+    other_first,
+    other_rest,
     wt,
     rest,
     at_halo,
@@ -156,17 +166,17 @@
 
     fast_lanes = pl.ds(pl.multiple_of(AW + (1 - s) * AW, AW), 2 * AW)
     slow_lanes = pl.ds(pl.multiple_of(AW + 2 * s * AW, AW), AW)
-    for i in range(GROUPS):
+    for place, i in enumerate(ORDER):
         for j in range(NC):
-            row = NC * i + j
+            row = NC * place + j
             mine, other = 6 * i + 3 + j + 1, 6 * i + 6 * (1 - s) + j + 1
             fast_buf[row] = ext[mine, :, fast_lanes]
-            slow_buf[row] = ext[mine, :, slow_lanes]
+            slow_buf[row if place < 2 else row + NC] = ext[mine, :, slow_lanes]
             other_buf[row] = ext[other, :, slow_lanes]
             lhs[row] = ext[other, :, fast_lanes]
     for j in range(NC):
         lhs[ROWS + j] = ext[30 * s + j + 1, :, fast_lanes]
-        slow_buf[ROWS + j] = ext[30 * s + j + 1, :, slow_lanes]
+        slow_buf[FIRST + j] = ext[30 * s + j + 1, :, slow_lanes]
     copies = [halo_copy]
 
     def write(source, target):
@@ -174,9 +184,12 @@
         copy.start()
         copies.append(copy)
 
-    write(other_buf, pt_other)
-    write(fast_buf, pt_fast)
-    write(slow_buf, pt_slow)
+    write(other_buf.at[:FIRST], other_first)
+    write(other_buf.at[FIRST:], other_rest)
+    write(fast_buf.at[:FIRST], fast_first)
+    write(fast_buf.at[FIRST:], fast_rest)
+    write(slow_buf.at[: FIRST + NC], slow_first)
+    write(slow_buf.at[FIRST + NC :], slow_rest)
 
     wt_buf[0:7] = jnp.zeros((7, BS, 2 * AW), jnp.bfloat16)
     wt_buf[33:] = jnp.zeros((WCOLS - 33, BS, 2 * AW), jnp.bfloat16)
@@ -222,34 +235,40 @@
         send_buf[:, :, lanes] = value[:ROWS]
         far_buf[:, :, lanes] = value[ROWS:]
 
-    half = TILES // 2
-
-    @pl.loop(0, half)
+    @pl.loop(0, TILES - 1)
     def _(tile):
         emit(tile, LANES)
 
-    write(send_buf.at[:, :, : half * LANES], send.at[:, :, : half * LANES])
-
-    @pl.loop(half, TILES - 1)
-    def _(tile):
-        emit(tile, LANES)
-
     emit(TILES - 1, LANES // 2)
-    write(send_buf.at[:, :, half * LANES :], send.at[:, :, half * LANES :])
+    write(send_buf.at[:NC], send_low)
+    write(send_buf.at[NC:FIRST], send_high)
+    write(send_buf.at[FIRST:], send_rest)
     write(far_buf, far)
     for copy in copies:
         copy.wait()
 
 
-def mine_kernel(pt_fast, wt, out):
-    right = wt[...].reshape(LANES, 2 * AW)
-    left = pt_fast[...].reshape(ROWS * BS, 2 * AW)
+def tile_dot(rows, cols):
+    left = rows[...].reshape(rows.shape[0] * BS, rows.shape[2])
+    right = cols[...].reshape(LANES, cols.shape[2])
     value = lax.dot_general(left, right, NT, preferred_element_type=jnp.float32)
-    out[...] = value.astype(out.dtype).reshape(ROWS, BS, LANES)
-
-
-def slow_kernel(core, inv_slow, p_slow, at_halo, rest, wt, turned_p, ext):
+    return value.reshape(rows.shape[0], BS, LANES)
+
+
+def mine_kernel(pt_fast, wt_fast, low, high, out):
+    value = tile_dot(pt_fast, wt_fast)
+    out[:NC] = value[:NC] + low[...].astype(jnp.float32)
+    out[NC:] = value[NC:] + high[...].astype(jnp.float32)
+
+
+def slow_kernel(core, inv_slow, p_slow, at_halo, rest, wt, turned_p, ext, at_buf, rest_buf, sems):
     s = core[0]
+    copies = [
+        pltpu.make_async_copy(at_halo, at_buf, sems.at[0]),
+        pltpu.make_async_copy(rest, rest_buf, sems.at[1]),
+    ]
+    for copy in copies:
+        copy.start()
     turned_p[KP] = jnp.zeros((BS, LANES), jnp.bfloat16)
 
     @pl.loop(0, AGG // QUAD)
@@ -266,49 +285,86 @@
     wt[0:5] = jnp.zeros((5, BS, AW), jnp.bfloat16)
     wt[WSLOT:] = jnp.zeros((WCOLS - WSLOT, BS, AW), jnp.bfloat16)
     chunk = WSLOT // 3
+    for copy in copies:
+        copy.wait()
 
     @pl.loop(0, 3)
     def _(part):
         rows = pl.ds(part * chunk, chunk)
         value = jnp.dot(
             ext[rows].reshape(chunk * BS, AW),
-            at_halo[...].reshape(AW, AW),
+            at_buf[...].reshape(AW, AW),
             preferred_element_type=jnp.float32,
         )
-        value = value.reshape(chunk, BS, AW) + rest[rows]
+        value = value.reshape(chunk, BS, AW) + rest_buf[rows]
         wt[pl.ds(5 * s + part * chunk, chunk)] = value.astype(jnp.bfloat16)
 
 
-def join_kernel(pt_slow, pt_other, wt_slow, wt_other, mine, arrived, far_fast, *outs):
-    right = wt_slow[...].reshape(LANES, AW)
-    left = pt_slow[...].reshape((ROWS + NC) * BS, AW)
-    value = lax.dot_general(left, right, NT, preferred_element_type=jnp.float32)
-    value = value.reshape(ROWS + NC, BS, LANES)
-    right = wt_other[...].reshape(LANES, AW)
-    left = pt_other[...].reshape(ROWS * BS, AW)
-    other = lax.dot_general(left, right, NT, preferred_element_type=jnp.float32)
-    other = other.reshape(ROWS, BS, LANES) + mine[...].astype(jnp.float32)
-    near = value[:ROWS] + (other + arrived[...].astype(jnp.float32))
-    for i in range(GROUPS):
-        outs[i][...] = near[NC * i : NC * (i + 1)].astype(outs[i].dtype)
-    outs[GROUPS][...] = (value[ROWS:] + far_fast[...].astype(jnp.float32)).astype(jnp.bfloat16)
-
-
-def total_kernel(core, own, m0, m1, m3, m4, far, out, frame):
+def join_first_kernel(slow, other, wt_slow, wt_other, mine, far_fast, m0, m4, far):
+    value = tile_dot(slow, wt_slow)
+    near = value[:FIRST] + (tile_dot(other, wt_other) + mine[...])
+    m0[...] = near[:NC].astype(jnp.bfloat16)
+    m4[...] = near[NC:].astype(jnp.bfloat16)
+    far[...] = (value[FIRST:] + far_fast[...].astype(jnp.float32)).astype(jnp.bfloat16)
+
+
+def join_rest_kernel(fast, slow, other, wt_fast, wt_slow, wt_other, arrived, m1, m3, own):
+    value = tile_dot(fast, wt_fast) + tile_dot(slow, wt_slow) + tile_dot(other, wt_other)
+    value = value + arrived[...].astype(jnp.float32)
+    m1[...] = value[:NC].astype(jnp.bfloat16)
+    m3[...] = value[NC : 2 * NC].astype(jnp.bfloat16)
+    own[...] = value[2 * NC :]
+
+
+def frame_add(frame, message, start):
+    odd = start & 1
+    lane = pl.multiple_of((start - odd + 6) * BS, 2 * BS)
+    frame[odd, :, pl.ds(lane, WINDOW * BS)] += message[0].astype(jnp.float32)
+
+
+def frame_sum(frame):
+    first, last = 6 * BS, (6 + BAND) * BS
+    return frame[0, :, first:last] + frame[1, :, first - BS : last - BS]
+
+
+def early_kernel(core, own, m0, m4, far, out, frame):
     s = core[0]
     j = pl.program_id(0)
     frame[...] = jnp.zeros_like(frame)
-
-    def add(message, start):
-        odd = start & 1
-        lane = pl.multiple_of((start - odd + 6) * BS, 2 * BS)
-        frame[odd, :, pl.ds(lane, WINDOW * BS)] += message[0].astype(jnp.float32)
-
-    for i, message in enumerate((m0, m1, own, m3, m4)):
-        add(message, 27 - 3 * s - j - 6 * i)
-    add(far, jnp.where(s == 1, 30 - j, -3 - j))
-    first, last = 6 * BS, (6 + BAND) * BS
-    out[0] = frame[0, :, first:last] + frame[1, :, first - BS : last - BS]
+    top = 27 - 3 * s - j
+    frame_add(frame, m0, top)
+    frame_add(frame, own, top - 12)
+    frame_add(frame, m4, top - 24)
+    frame_add(frame, far, jnp.where(s == 1, 30 - j, -3 - j))
+    out[0] = frame_sum(frame)
+
+
+def total_kernel(core, early, m1, m3, out, frame):
+    s = core[0]
+    j = pl.program_id(0)
+    frame[...] = jnp.zeros_like(frame)
+    top = 27 - 3 * s - j
+    frame_add(frame, m1, top - 6)
+    frame_add(frame, m3, top - 18)
+    out[0] = early[0] + frame_sum(frame)
+
+
+def pick_kernel(core, source, out, sems, *, outer):
+    s = core[0]
+    first = (NB - AGG) * (s if outer else 1 - s)
+    step = AGG // 4
+    copies = [
+        pltpu.make_async_copy(
+            source.at[pl.ds(first + k * step, step)],
+            out.at[k * step : (k + 1) * step],
+            sems.at[k],
+        )
+        for k in range(4)
+    ]
+    for copy in copies:
+        copy.start()
+    for copy in copies:
+        copy.wait()
 
 
 def permuted(block, pairs):
@@ -333,18 +389,36 @@
     def shifted(distance):
         return [(i, (i + distance) % devices) for i in range(devices)]
 
-    high = NB - AGG
     parity = device % 2
-
-    def halo(array, first, pairs):
-        return permuted(lax.dynamic_slice_in_dim(array, first, AGG), pairs)
+    smem = pl.BlockSpec(memory_space=pltpu.SMEM)
+    vmem = pl.BlockSpec(memory_space=pltpu.VMEM)
+    hbm = pl.BlockSpec(memory_space=pltpu.HBM)
+    bf16 = jnp.bfloat16
+
+    def params(mebibytes):
+        return pltpu.CompilerParams(vmem_limit_bytes=mebibytes * 1024 * 1024)
+
+    def cost(flops, size):
+        return pl.CostEstimate(flops=flops, bytes_accessed=size, transcendentals=0)
+
+    def picked(outer):
+        return pl.pallas_call(
+            functools.partial(pick_kernel, outer=outer),
+            out_shape=jax.ShapeDtypeStruct((AGG,) + p_blocks.shape[1:], bf16),
+            in_specs=[smem, hbm],
+            out_specs=hbm,
+            scratch_shapes=[pltpu.SemaphoreType.DMA((4,))],
+            compiler_params=params(60),
+            name="pick_outer" if outer else "pick_inner",
+        )(core, p_blocks)
 
     outward = [(i, (i + (1 if i % 2 else -1)) % devices) for i in range(devices)]
     inward = [(i, i ^ 1) for i in range(devices)]
-    cols_slow = halo(cols_p, high * parity, outward)
-    p_slow = halo(p_blocks, high * parity, outward)
-    cols_fast = halo(cols_p, high * (1 - parity), inward)
-    p_fast = halo(p_blocks, high * (1 - parity), inward)
+    p_slow = permuted(picked(True), outward)
+    p_fast = permuted(picked(False), inward)
+    edge_cols = jnp.stack([cols_p[:AGG], cols_p[NB - AGG :]])
+    cols_slow = permuted(edge_cols[parity], outward)
+    cols_fast = permuted(edge_cols[1 - parity], inward)
 
     def slots(cols, agg):
         return (cols - agg + H) % count_agg
@@ -357,33 +431,44 @@
     inv_slow = inverse_index(slots(cols_slow, first_agg + slow_place) + 2 * parity, WSLOT, KP)
     inv_a = inverse_index((cols_a - first_row - (own_agg - 1) * AGG) % count_rows, 3 * AGG, KA)
 
-    smem = pl.BlockSpec(memory_space=pltpu.SMEM)
-    vmem = pl.BlockSpec(memory_space=pltpu.VMEM)
-    hbm = pl.BlockSpec(memory_space=pl.ANY)
-    bf16 = jnp.bfloat16
-
-    def params(mebibytes):
-        return pltpu.CompilerParams(vmem_limit_bytes=mebibytes * 1024 * 1024)
-
-    def cost(flops, size):
-        return pl.CostEstimate(flops=flops, bytes_accessed=size, transcendentals=0)
-
-    shapes = [
-        (ROWS, BS, WINDOW * BS),
-        (NC, BS, WINDOW * BS),
-        (ROWS, BS, 2 * AW),
-        (ROWS + NC, BS, AW),
-        (ROWS, BS, AW),
-        (WCOLS, BS, 2 * AW),
-        (WSLOT, BS, AW),
-        (AGG, BS, AW),
+    def block(rows, width, kind=bf16):
+        return jax.ShapeDtypeStruct((rows, BS, width), kind)
+
+    span = WINDOW * BS
+    outs = [
+        block(NC, span),
+        block(NC, span),
+        block(REST, span),
+        block(NC, span),
+        block(FIRST, 2 * AW),
+        block(REST, 2 * AW),
+        block(FIRST + NC, AW),
+        block(REST, AW),
+        block(FIRST, AW),
+        block(REST, AW),
+        block(WCOLS, 2 * AW),
+        block(WSLOT, AW, jnp.float32),
+        block(AGG, AW),
     ]
-    kinds = [bf16] * 6 + [jnp.float32, bf16]
-    send, far, pt_fast, pt_slow, pt_other, wt_fast, rest, at_halo = pl.pallas_call(
+    (
+        send_low,
+        send_high,
+        send_rest,
+        far,
+        fast_first,
+        fast_rest,
+        slow_first,
+        slow_rest,
+        other_first,
+        other_rest,
+        wt_fast,
+        rest,
+        at_halo,
+    ) = pl.pallas_call(
         fast_kernel,
-        out_shape=[jax.ShapeDtypeStruct(shape, kind) for shape, kind in zip(shapes, kinds)],
+        out_shape=outs,
         in_specs=[smem] * 4 + [hbm, hbm, vmem],
-        out_specs=[hbm] * 8,
+        out_specs=[hbm] * len(outs),
         scratch_shapes=[
             pltpu.VMEM((NB + AGG, BS, KP * BS), bf16),
             pltpu.VMEM((COLS, BS, EXT * BS), bf16),
@@ -391,16 +476,25 @@
             pltpu.VMEM((KP + 1, BS, LANES), bf16),
             pltpu.VMEM((KA + 1, BS, LANES), bf16),
             pltpu.VMEM((ROWS + NC, BS, 2 * AW), bf16),
-        ]
-        + [pltpu.VMEM(shape, kind) for shape, kind in zip(shapes[:7], kinds[:7])]
-        + [pltpu.SemaphoreType.DMA(((NB + AGG) // QUAD,)), pltpu.SemaphoreType.DMA((9,))],
+            pltpu.VMEM((ROWS, BS, span), bf16),
+            pltpu.VMEM((NC, BS, span), bf16),
+            pltpu.VMEM((ROWS, BS, 2 * AW), bf16),
+            pltpu.VMEM((ROWS + NC, BS, AW), bf16),
+            pltpu.VMEM((ROWS, BS, AW), bf16),
+            pltpu.VMEM((WCOLS, BS, 2 * AW), bf16),
+            pltpu.VMEM((WSLOT, BS, AW), jnp.float32),
+            pltpu.SemaphoreType.DMA(((NB + AGG) // QUAD,)),
+            pltpu.SemaphoreType.DMA((len(outs),)),
+        ],
         compiler_params=params(56),
         cost_estimate=cost(20 * 10**9, 30 * 10**6),
         name="fast",
     )(core, inv_own, inv_fast, inv_a, p_blocks, p_fast, a_blocks)
 
-    arrived = permuted(send, inward)
-    pt_other = permuted(pt_other, inward)
+    low = permuted(send_low, inward)
+    high = permuted(send_high, inward)
+    other_first = permuted(other_first, inward)
+    p_slow, low, high, other_first = lax.optimization_barrier((p_slow, low, high, other_first))
 
     def lane_tile(rows):
         return pl.BlockSpec((rows, BS, LANES), lambda n: (0, 0, n))
@@ -411,68 +505,87 @@
     def whole(rows, width):
         return pl.BlockSpec((rows, BS, width), lambda n: (0, 0, 0))
 
-    mine = pl.pallas_call(
-        mine_kernel,
-        grid=(TILES,),
-        out_shape=jax.ShapeDtypeStruct((ROWS, BS, WINDOW * BS), bf16),
-        in_specs=[whole(ROWS, 2 * AW), col_tile(2 * AW)],
-        out_specs=lane_tile(ROWS),
-        compiler_params=params(16),
-        cost_estimate=cost(60 * 10**9, 120 * 10**6),
-        name="mine",
-    )(pt_fast, wt_fast)
-
     wt_slow = pl.pallas_call(
         slow_kernel,
-        out_shape=jax.ShapeDtypeStruct((WCOLS, BS, AW), bf16),
-        in_specs=[smem] * 2 + [vmem] * 3,
+        out_shape=block(WCOLS, AW),
+        in_specs=[smem] * 2 + [vmem, hbm, hbm],
         out_specs=vmem,
         scratch_shapes=[
             pltpu.VMEM((KP + 1, BS, LANES), bf16),
             pltpu.VMEM((WSLOT, BS, AW), bf16),
+            pltpu.VMEM((AGG, BS, AW), bf16),
+            pltpu.VMEM((WSLOT, BS, AW), jnp.float32),
+            pltpu.SemaphoreType.DMA((2,)),
         ],
-        compiler_params=params(24),
-        cost_estimate=cost(20 * 10**9, 120 * 10**6),
+        compiler_params=params(60),
+        cost_estimate=cost(20 * 10**9, 200 * 10**6),
         name="slow",
     )(core, inv_slow, p_slow, at_halo, rest)
     wt_other = permuted(wt_slow, inward)
 
-    message = jax.ShapeDtypeStruct((NC, BS, WINDOW * BS), bf16)
-    m0, m1, own, m3, m4, far = pl.pallas_call(
-        join_kernel,
+    wt_slow, low, high = lax.optimization_barrier((wt_slow, low, high))
+    mine = pl.pallas_call(
+        mine_kernel,
         grid=(TILES,),
-        out_shape=[message] * 2
-        + [jax.ShapeDtypeStruct(message.shape, jnp.float32)]
-        + [message] * 3,
-        in_specs=[whole(ROWS + NC, AW), whole(ROWS, AW)]
+        out_shape=block(FIRST, span, jnp.float32),
+        in_specs=[whole(FIRST, 2 * AW), col_tile(2 * AW), lane_tile(NC), lane_tile(NC)],
+        out_specs=lane_tile(FIRST),
+        compiler_params=params(60),
+        cost_estimate=cost(10**10, 100 * 10**6),
+        name="mine",
+    )(fast_first, wt_fast, low, high)
+    mine, wt_other, send_rest, other_rest = lax.optimization_barrier(
+        (mine, wt_other, send_rest, other_rest)
+    )
+    arrived_rest = permuted(send_rest, inward)
+    other_rest = permuted(other_rest, inward)
+    m0, m4, far = pl.pallas_call(
+        join_first_kernel,
+        grid=(TILES,),
+        out_shape=[block(NC, span)] * 3,
+        in_specs=[whole(FIRST + NC, AW), whole(FIRST, AW)]
         + [col_tile(AW)] * 2
-        + [lane_tile(ROWS)] * 2
-        + [lane_tile(NC)],
-        out_specs=[lane_tile(NC)] * 6,
-        compiler_params=params(24),
-        cost_estimate=cost(5 * 10**9, 22 * 10**6),
-        name="join",
-    )(pt_slow, pt_other, wt_slow, wt_other, mine, arrived, far)
-    far = permuted(far, [(i, (i + (5 if i % 2 else -5)) % devices) for i in range(devices)])
+        + [lane_tile(FIRST), lane_tile(NC)],
+        out_specs=[lane_tile(NC)] * 3,
+        compiler_params=params(16),
+        cost_estimate=cost(3 * 10**9, 10**7),
+        name="join_first",
+    )(slow_first, other_first, wt_slow, wt_other, mine, far)
     m0 = permuted(m0, shifted(-4))
     m4 = permuted(m4, shifted(4))
+    far = permuted(far, [(i, (i + (5 if i % 2 else -5)) % devices) for i in range(devices)])
+    m1, m3, own = pl.pallas_call(
+        join_rest_kernel,
+        grid=(TILES,),
+        out_shape=[block(NC, span)] * 2 + [block(NC, span, jnp.float32)],
+        in_specs=[whole(REST, 2 * AW), whole(REST, AW), whole(REST, AW)]
+        + [col_tile(2 * AW), col_tile(AW), col_tile(AW), lane_tile(REST)],
+        out_specs=[lane_tile(NC)] * 3,
+        compiler_params=params(24),
+        cost_estimate=cost(40 * 10**9, 200 * 10**6),
+        name="join_rest",
+    )(fast_rest, slow_rest, other_rest, wt_fast, wt_slow, wt_other, arrived_rest)
     m1 = permuted(m1, shifted(-2))
     m3 = permuted(m3, shifted(2))
 
     def row_block(blocks):
         return pl.BlockSpec((1, BS, blocks * BS), lambda j: (j, 0, 0))
 
-    return pl.pallas_call(
-        total_kernel,
-        grid=(NC,),
-        out_shape=jax.ShapeDtypeStruct((NC, BS, BAND * BS), jnp.float32),
-        in_specs=[smem] + [row_block(WINDOW)] * 6,
-        out_specs=row_block(BAND),
-        scratch_shapes=[pltpu.VMEM((2, BS, FRAME * BS), jnp.float32)],
-        compiler_params=params(20),
-        cost_estimate=pl.CostEstimate(flops=10**7, bytes_accessed=10**7, transcendentals=0),
-        name="total",
-    )(core, own, m0, m1, m3, m4, far)
+    def summed(kernel, name, *terms):
+        return pl.pallas_call(
+            kernel,
+            grid=(NC,),
+            out_shape=block(NC, BAND * BS, jnp.float32),
+            in_specs=[smem] + [row_block(term.shape[2] // BS) for term in terms],
+            out_specs=row_block(BAND),
+            scratch_shapes=[pltpu.VMEM((2, BS, FRAME * BS), jnp.float32)],
+            compiler_params=params(20),
+            cost_estimate=cost(10**7, 10**7),
+            name=name,
+        )(core, *terms)
+
+    early = summed(early_kernel, "early", own, m0, m4, far)
+    return summed(total_kernel, "total", early, m1, m3)
 
 
 def solution(mesh):

time: 170 us -> 281 us (1.65)
  the two profiles are of different devices: /device:TPU:4 before, /device:TPU:0 now
where the time goes in v3:
time: 281 us; the launch traced here: 279 us
  Pallas kernels  191 us (68%)
  waiting for transfers between devices  64 us (23%)
  starting transfers between devices  15 us (5%)
  local copies, waits for them, and re-layouts  5.32 us (2%)
  other arithmetic  3.04 us (1%)
    pallas_call x2, Pallas kernels, picked(): pl.pallas_call(functools.partial(pick_kernel, outer=outer), out_shape=jax...  113 us
    ppermute x15, waiting for transfers between devices, permuted(): return lax.ppermute(block, 'dom', pairs)  64 us
    pallas_call x1, Pallas kernels, body(): pl.pallas_call(fast_kernel, out_shape=outs, in_specs=[smem] * 4 + [hbm, h...  35.2 us
    ppermute x15, starting transfers between devices, permuted(): return lax.ppermute(block, 'dom', pairs)  15 us
    pallas_call x1, Pallas kernels, body(): pl.pallas_call(join_rest_kernel, grid=(TILES,), out_shape=[block(NC, span...  10.8 us
    pallas_call x1, Pallas kernels, body(): pl.pallas_call(mine_kernel, grid=(TILES,), out_shape=block(FIRST, span, j...  10.1 us
    pallas_call x1, Pallas kernels, body(): pl.pallas_call(join_first_kernel, grid=(TILES,), out_shape=[block(NC, spa...  9.06 us
    pallas_call x1, Pallas kernels, body(): pl.pallas_call(slow_kernel, out_shape=block(WCOLS, AW), in_specs=[smem] *...  7.1 us
  transfers between devices with their start and end apart: 15, of which 3 were waited for; matrix products, arithmetic and copies ran while one was open for 1% of the time, Pallas kernels for 65%

profile of v3, /device:TPU:0, one launch (start us, length us, event | category | flops | bytes accessed | tf_op | source)
XLA Modules:
  0.0 278.7 jit_solution(17526966174414577780)
XLA Ops:
  0.0 0.7 slice_bitcast_fusion
  0.7 0.5 collective-permute-start
  1.2 56.7 %pick_outer.1 = bf16[8,64,1728]{2,1,0:T(8,128)(2,1)} custom-call(s32[1]{0:T(128)} %bitcast.core, bf16[24,64,1728]{2,1,0:T(8,128)(2,1)} %source.3), custom_call_target="tpu_custom_call" | custom-call | tf_op jit(solution)/shard_map/pick_outer/pallas_call | solution.py:405
  58.0 0.0 copy-start.7
  58.0 0.0 copy-start.8
  58.0 6.7 %collective-permute-start.3 = (bf16[8,64,1728]{2,1,0:T(8,128)(2,1)}, bf16[8,64,1728]{2,1,0:T(8,128)(2,1)S(1)}, u32[]{:S(2)}, u32[]{:S(2)}) collective-permute-start(bf16[8,64,1728]{2,1,0:T(8,128)(2,1)} %pick_outer.1), channel_id=1, source_target_pairs={{0,31},{1,2},{2,1},{3,4},{4,3},{5,6},{6,5},{7,8},{8,7},{9,10},{10,... | collective-permute-start | bytes 5308424 | tf_op jit(solution)/shard_map/ppermute | solution.py:371
  64.7 56.7 %pick_inner.1 = bf16[8,64,1728]{2,1,0:T(8,128)(2,1)} custom-call(s32[1]{0:T(128)} %bitcast.core, bf16[24,64,1728]{2,1,0:T(8,128)(2,1)} %source.3), custom_call_target="tpu_custom_call" | custom-call | tf_op jit(solution)/shard_map/pick_inner/pallas_call | solution.py:405
  121.4 0.1 collective-permute-start.1
  121.5 0.1 fusion.1
  121.6 0.1 copy.15
  121.7 0.1 select_reduce_fusion.3
  121.8 0.2 select_reduce_fusion
  122.0 0.6 broadcast_add_fusion.inv_a
  122.6 0.6 broadcast_add_fusion.1.inv_own
  123.2 0.1 copy.16
  123.3 0.1 select_reduce_fusion.2
  123.4 0.6 broadcast_add_fusion.3.inv_fast
  124.0 1.6 collective-permute-done.1.p_fast
  125.6 35.2 %fast.1 = (bf16[3,64,2432]{2,1,0:T(8,128)(2,1)}, bf16[3,64,2432]{2,1,0:T(8,128)(2,1)}, bf16[9,64,2432]{2,1,0:T(8,128)(2,1)}, bf16[3,64,2432]{2,1,0:T(8,128)(2,1)...) custom-call(s32[1]{0:T(128)} %bitcast.core, ...), custom_call_target="tpu_custom_call" | custom-call | flops 20000000000 | bytes 30000000 | tf_op jit(solution)/shard_map/fast/pallas_call | solution.py:467
  160.7 0.2 collective-permute-start.4
  161.0 0.4 collective-permute-start.5
  161.3 0.3 collective-permute-start.2
  161.6 6.3 %collective-permute-done.2 = s32[8,27]{1,0:T(8,128)S(1)} collective-permute-done((s32[8,27]{1,0:T(8,128)S(1)}, s32[8,27]{1,0:T(8,128)S(1)}, u32[]{:S(2)}, u32[]{:S(2)}) %collective-permute-start.2) | collective-permute-done | bytes 896 | tf_op jit(solution)/shard_map/ppermute | solution.py:371
  168.0 0.1 copy.17
  168.1 0.1 select_reduce_fusion.1
  168.2 0.6 broadcast_add_fusion.2.inv_slow
  168.8 0.0 collective-permute-done.3.p_slow
  168.8 0.0 collective-permute-done.6.other
  168.8 0.0 collective-permute-done.5.high
  168.8 1.2 copy-done.9
  170.0 7.1 %slow.1.wt_slow = bf16[40,64,512]{2,1,0:T(8,128)(2,1)} custom-call(s32[1]{0:T(128)} %bitcast.core, s32[8,33]{1,0:T(8,128)} %broadcast_add_fusion.2.inv_slow, bf16[8,64,1728]{2,1,0:T(8,128)(2,1)} %copy-done.9, bf16[8,64,512]{2,1,0:T(8,128)(2,1)} %get-tuple-element.43.at_halo, f32[33,64,512]{2,1,0:T(8,128)} %get-tuple-element.44.rest), custom_call_target="tpu_custom_call" | custom-call | flops 20000000000 | bytes 200000000 | tf_op jit(solution)/shard_map/slow/pallas_call | solution.py:508
  177.1 0.1 collective-permute-start.7
  177.2 10.1 %mine.1 = f32[6,64,2432]{2,1,0:T(8,128)} custom-call(bf16[6,64,1024]{2,1,0:T(8,128)(2,1)} %get-tuple-element.37.pt_fast, bf16[40,64,1024]{2,1,0:T(8,128)(2,1)} %get-tuple-element.38.wt_fast, bf16[3,64,2432]{2,1,0:T(8,128)(2,1)} %copy-done.10, bf16[3,64,2432]{2,1,0:T(8,128)(2,1)} %collective-permute-done.5.high), custom_call_target="tpu_custom_call" | custom-call | flops 10000000000 | bytes 100000000 | tf_op jit(solution)/shard_map/mine/pallas_call | solution.py:527
  187.3 0.0 collective-permute-done.7.wt_other
  187.3 0.4 collective-permute-start.9
  187.7 0.1 collective-permute-start.8
  187.8 2.1 copy-done.1
  189.9 1.1 copy-done.3
  190.9 9.1 %join_first.1 = (bf16[3,64,2432]{2,1,0:T(8,128)(2,1)S(1)}, bf16[3,64,2432]{2,1,0:T(8,128)(2,1)S(1)}, bf16[3,64,2432]{2,1,0:T(8,128)(2,1)S(1)}) custom-call(bf16[9,64,512]{2,1,0:T(8,128)(2,1)S(1)} %copy-done.3, bf16[6,64,512]{2,1,0:T(8,128)(2,1)S(1)} %collective-permute-done.6.other, bf16[40,64,512]{2,1,0:T(8,128)(2,1)S(1)} %copy-done, ...), custom_call_target="tpu_custom_call" | custom-call | flops 3000000000 | bytes 10000000 | tf_op jit(solution)/shard_map/join_first/pallas_call | solution.py:542
  200.0 0.1 collective-permute-start.10
  200.1 2.0 collective-permute-start.11
  202.1 0.0 collective-permute-start.12
  202.1 10.8 %join_rest.1 = (bf16[3,64,2432]{2,1,0:T(8,128)(2,1)S(1)}, bf16[3,64,2432]{2,1,0:T(8,128)(2,1)S(1)}, f32[3,64,2432]{2,1,0:T(8,128)S(1)}) custom-call(bf16[9,64,1024]{2,1,0:T(8,128)(2,1)S(1)} %copy-done.5, bf16[9,64,512]{2,1,0:T(8,128)(2,1)S(1)} %copy-done.6, bf16[9,64,512]{2,1,0:T(8,128)(2,1)S(1)} %collective-permute-done.8.other, ...), custom_call_target="tpu_custom_call" | custom-call | flops 40000000000 | bytes 200000000 | tf_op jit(solution)/shard_map/join_rest/pallas_call | solution.py:557
  212.9 3.4 %collective-permute-start.13 = (bf16[3,64,2432]{2,1,0:T(8,128)(2,1)S(1)}, bf16[3,64,2432]{2,1,0:T(8,128)(2,1)S(1)}, u32[]{:S(2)}, u32[]{:S(2)}) collective-permute-start(bf16[3,64,2432]{2,1,0:T(8,128)(2,1)S(1)} %get-tuple-element.63), channel_id=1, source_target_pairs={{0,30},{1,31},{2,0},{3,1},{4,2},{5,3},{6,4},{7,5},{8,6},{9,7},{10,... | collective-permute-start | bytes 2801672 | tf_op jit(solution)/shard_map/ppermute | solution.py:371
  216.3 0.8 collective-permute-start.14
  217.1 56.0 %collective-permute-done.10.m0 = bf16[3,64,2432]{2,1,0:T(8,128)(2,1)S(1)} collective-permute-done((bf16[3,64,2432]{2,1,0:T(8,128)(2,1)S(1)}, bf16[3,64,2432]{2,1,0:T(8,128)(2,1)S(1)}, u32[]{:S(2)}, u32[]{:S(2)}) %collective-permute-start.10) | collective-permute-done | bytes 933920 | tf_op jit(solution)/shard_map/ppermute | solution.py:371
  273.2 2.3 early.1
  275.5 3.2 %total.1 = f32[3,64,4032]{2,1,0:T(8,128)} custom-call(s32[1]{0:T(128)} %bitcast.core, f32[3,64,4032]{2,1,0:T(8,128)S(1)} %early.1, bf16[3,64,2432]{2,1,0:T(8,128)(2,1)S(1)} %collective-permute-done.13.m1, bf16[3,64,2432]{2,1,0:T(8,128)(2,1)S(1)} %collective-permute-done.14.m3), custom_call_target="tpu_custom_call" | custom-call | flops 10000000 | bytes 10000000 | tf_op jit(solution)/shard_map/total/pallas_call | solution.py:575
  (34 shorter events, 0.1 us)
Async XLA Ops:
  0.7 122.5 %collective-permute-start = (s32[8,27]{1,0:T(8,128)S(1)}, s32[8,27]{1,0:T(8,128)S(1)}, u32[]{:S(2)}, u32[]{:S(2)}) collective-permute-start(s32[8,27]{1,0:T(8,128)S(1)} %get-tuple-element.68), channel_id=1, source_target_pairs={{0,1},{1,0},{2,3},{3,2},{4,5},{5,4},{6,7},{7,6},{8,9},{9,8},{10,11... | collective-permute-start | bytes 2600 | tf_op jit(solution)/shard_map/ppermute | solution.py:371
  58.0 63.5 %copy-start.7 = (s32[24,27]{1,0:T(8,128)S(1)}, s32[24,27]{1,0:T(8,128)}, u32[]{:S(2)}) copy-start(s32[24,27]{1,0:T(8,128)} %param.7) | copy-start | bytes 7780
  58.0 63.7 %copy-start.8 = (s32[24,7]{0,1:T(8,128)S(1)}, s32[24,7]{0,1:T(8,128)}, u32[]{:S(2)}) copy-start(s32[24,7]{0,1:T(8,128)} %param.6) | copy-start | bytes 2020
  58.0 110.8 %collective-permute-start.3 = (bf16[8,64,1728]{2,1,0:T(8,128)(2,1)}, bf16[8,64,1728]{2,1,0:T(8,128)(2,1)S(1)}, u32[]{:S(2)}, u32[]{:S(2)}) collective-permute-start(bf16[8,64,1728]{2,1,0:T(8,128)(2,1)} %pick_outer.1), channel_id=1, source_target_pairs={{0,31},{1,2},{2,1},{3,4},{4,3},{5,6},{6,5},{7,8},{8,7},{9,10},{10,... | collective-permute-start | bytes 5308424 | tf_op jit(solution)/shard_map/ppermute | solution.py:371
  121.4 4.2 %collective-permute-start.1 = (bf16[8,64,1728]{2,1,0:T(8,128)(2,1)}, bf16[8,64,1728]{2,1,0:T(8,128)(2,1)}, u32[]{:S(2)}, u32[]{:S(2)}) collective-permute-start(bf16[8,64,1728]{2,1,0:T(8,128)(2,1)} %pick_inner.1), channel_id=1, source_target_pairs={{0,1},{1,0},{2,3},{3,2},{4,5},{5,4},{6,7},{7,6},{8,9},{9,8},{10,11... | collective-permute-start | bytes 5308424 | tf_op jit(solution)/shard_map/ppermute | solution.py:371
  160.7 8.0 %collective-permute-start.4 = (bf16[3,64,2432]{2,1,0:T(8,128)(2,1)}, bf16[3,64,2432]{2,1,0:T(8,128)(2,1)S(1)}, u32[]{:S(2)}, u32[]{:S(2)}) collective-permute-start(bf16[3,64,2432]{2,1,0:T(8,128)(2,1)} %get-tuple-element.39), channel_id=1, source_target_pairs={{0,1},{1,0},{2,3},{3,2},{4,5},{5,4},{6,7},{7,6},{8,9},{9,8},{10,11... | collective-permute-start | bytes 2801672 | tf_op jit(solution)/shard_map/ppermute | solution.py:371
  161.0 7.8 %collective-permute-start.5 = (bf16[3,64,2432]{2,1,0:T(8,128)(2,1)}, bf16[3,64,2432]{2,1,0:T(8,128)(2,1)}, u32[]{:S(2)}, u32[]{:S(2)}) collective-permute-start(bf16[3,64,2432]{2,1,0:T(8,128)(2,1)} %get-tuple-element.40), channel_id=1, source_target_pairs={{0,1},{1,0},{2,3},{3,2},{4,5},{5,4},{6,7},{7,6},{8,9},{9,8},{10,11... | collective-permute-start | bytes 2801672 | tf_op jit(solution)/shard_map/ppermute | solution.py:371
  161.3 6.6 %collective-permute-start.2 = (s32[8,27]{1,0:T(8,128)S(1)}, s32[8,27]{1,0:T(8,128)S(1)}, u32[]{:S(2)}, u32[]{:S(2)}) collective-permute-start(s32[8,27]{1,0:T(8,128)S(1)} %get-tuple-element.67), channel_id=1, source_target_pairs={{0,31},{1,2},{2,1},{3,4},{4,3},{5,6},{6,5},{7,8},{8,7},{9,10},{10,... | collective-permute-start | bytes 2600 | tf_op jit(solution)/shard_map/ppermute | solution.py:371
  161.6 7.2 %collective-permute-start.6 = (bf16[6,64,512]{2,1,0:T(8,128)(2,1)}, bf16[6,64,512]{2,1,0:T(8,128)(2,1)S(1)}, u32[]{:S(2)}, u32[]{:S(2)}) collective-permute-start(bf16[6,64,512]{2,1,0:T(8,128)(2,1)} %get-tuple-element.41), channel_id=1, source_target_pairs={{0,1},{1,0},{2,3},{3,2},{4,5},{5,4},{6,7},{7,6},{8,9},{9,8},{10,11... | collective-permute-start | bytes 1179656 | tf_op jit(solution)/shard_map/ppermute | solution.py:371
  168.8 1.2 copy-start.9
  168.8 8.3 %copy-start.10 = (bf16[3,64,2432]{2,1,0:T(8,128)(2,1)}, bf16[3,64,2432]{2,1,0:T(8,128)(2,1)S(1)}, u32[]{:S(2)}) copy-start(bf16[3,64,2432]{2,1,0:T(8,128)(2,1)S(1)} %collective-permute-done.4.low) | copy-start | bytes 2801668
  177.1 10.2 %collective-permute-start.7 = (bf16[40,64,512]{2,1,0:T(8,128)(2,1)}, bf16[40,64,512]{2,1,0:T(8,128)(2,1)}, u32[]{:S(2)}, u32[]{:S(2)}) collective-permute-start(bf16[40,64,512]{2,1,0:T(8,128)(2,1)} %slow.1.wt_slow), channel_id=1, source_target_pairs={{0,1},{1,0},{2,3},{3,2},{4,5},{5,4},{6,7},{7,6},{8,9},{9,8},{10,11... | collective-permute-start | bytes 7864328 | tf_op jit(solution)/shard_map/ppermute | solution.py:371
  177.2 10.6 %copy-start = (bf16[40,64,512]{2,1,0:T(8,128)(2,1)S(1)}, bf16[40,64,512]{2,1,0:T(8,128)(2,1)}, u32[]{:S(2)}) copy-start(bf16[40,64,512]{2,1,0:T(8,128)(2,1)} %slow.1.wt_slow) | copy-start | bytes 7864324
  177.2 10.6 %copy-start.2 = (bf16[3,64,2432]{2,1,0:T(8,128)(2,1)S(1)}, bf16[3,64,2432]{2,1,0:T(8,128)(2,1)}, u32[]{:S(2)}) copy-start(bf16[3,64,2432]{2,1,0:T(8,128)(2,1)} %get-tuple-element.59.far_fast) | copy-start | bytes 2801668
  187.3 14.8 %collective-permute-start.9 = (bf16[9,64,2432]{2,1,0:T(8,128)(2,1)}, bf16[9,64,2432]{2,1,0:T(8,128)(2,1)S(1)}, u32[]{:S(2)}, u32[]{:S(2)}) collective-permute-start(bf16[9,64,2432]{2,1,0:T(8,128)(2,1)} %get-tuple-element.54), channel_id=1, source_target_pairs={{0,1},{1,0},{2,3},{3,2},{4,5},{5,4},{6,7},{7,6},{8,9},{9,8},{10,11... | collective-permute-start | bytes 8405000 | tf_op jit(solution)/shard_map/ppermute | solution.py:371
  187.7 14.4 %collective-permute-start.8 = (bf16[9,64,512]{2,1,0:T(8,128)(2,1)}, bf16[9,64,512]{2,1,0:T(8,128)(2,1)S(1)}, u32[]{:S(2)}, u32[]{:S(2)}) collective-permute-start(bf16[9,64,512]{2,1,0:T(8,128)(2,1)} %get-tuple-element.51), channel_id=1, source_target_pairs={{0,1},{1,0},{2,3},{3,2},{4,5},{5,4},{6,7},{7,6},{8,9},{9,8},{10,11... | collective-permute-start | bytes 1769480 | tf_op jit(solution)/shard_map/ppermute | solution.py:371
  187.8 2.1 copy-start.1
  189.9 1.1 copy-start.3
  190.9 11.2 %copy-start.4 = (bf16[40,64,1024]{2,1,0:T(8,128)(2,1)S(1)}, bf16[40,64,1024]{2,1,0:T(8,128)(2,1)}, u32[]{:S(2)}) copy-start(bf16[40,64,1024]{2,1,0:T(8,128)(2,1)} %get-tuple-element.38.wt_fast) | copy-start | bytes 15728644
  190.9 11.2 %copy-start.5 = (bf16[9,64,1024]{2,1,0:T(8,128)(2,1)S(1)}, bf16[9,64,1024]{2,1,0:T(8,128)(2,1)}, u32[]{:S(2)}) copy-start(bf16[9,64,1024]{2,1,0:T(8,128)(2,1)} %get-tuple-element.35.fast) | copy-start | bytes 3538948
  190.9 11.2 %copy-start.6 = (bf16[9,64,512]{2,1,0:T(8,128)(2,1)S(1)}, bf16[9,64,512]{2,1,0:T(8,128)(2,1)}, u32[]{:S(2)}) copy-start(bf16[9,64,512]{2,1,0:T(8,128)(2,1)} %get-tuple-element.36.slow) | copy-start | bytes 1769476
  200.0 73.2 %collective-permute-start.10 = (bf16[3,64,2432]{2,1,0:T(8,128)(2,1)S(1)}, bf16[3,64,2432]{2,1,0:T(8,128)(2,1)S(1)}, u32[]{:S(2)}, u32[]{:S(2)}) collective-permute-start(bf16[3,64,2432]{2,1,0:T(8,128)(2,1)S(1)} %get-tuple-element.60), channel_id=1, source_target_pairs={{0,28},{1,29},{2,30},{3,31},{4,0},{5,1},{6,2},{7,3},{8,4},{9,5},{1... | collective-permute-start | bytes 2801672 | tf_op jit(solution)/shard_map/ppermute | solution.py:371
  200.1 73.1 %collective-permute-start.11 = (bf16[3,64,2432]{2,1,0:T(8,128)(2,1)S(1)}, bf16[3,64,2432]{2,1,0:T(8,128)(2,1)S(1)}, u32[]{:S(2)}, u32[]{:S(2)}) collective-permute-start(bf16[3,64,2432]{2,1,0:T(8,128)(2,1)S(1)} %get-tuple-element.61), channel_id=1, source_target_pairs={{0,4},{1,5},{2,6},{3,7},{4,8},{5,9},{6,10},{7,11},{8,12},{9,13},{1... | collective-permute-start | bytes 2801672 | tf_op jit(solution)/shard_map/ppermute | solution.py:371
  202.1 71.1 %collective-permute-start.12 = (bf16[3,64,2432]{2,1,0:T(8,128)(2,1)S(1)}, bf16[3,64,2432]{2,1,0:T(8,128)(2,1)S(1)}, u32[]{:S(2)}, u32[]{:S(2)}) collective-permute-start(bf16[3,64,2432]{2,1,0:T(8,128)(2,1)S(1)} %get-tuple-element.62), channel_id=1, source_target_pairs={{0,27},{1,6},{2,29},{3,8},{4,31},{5,10},{6,1},{7,12},{8,3},{9,14},... | collective-permute-start | bytes 2801672 | tf_op jit(solution)/shard_map/ppermute | solution.py:371
  212.9 62.5 %collective-permute-start.13 = (bf16[3,64,2432]{2,1,0:T(8,128)(2,1)S(1)}, bf16[3,64,2432]{2,1,0:T(8,128)(2,1)S(1)}, u32[]{:S(2)}, u32[]{:S(2)}) collective-permute-start(bf16[3,64,2432]{2,1,0:T(8,128)(2,1)S(1)} %get-tuple-element.63), channel_id=1, source_target_pairs={{0,30},{1,31},{2,0},{3,1},{4,2},{5,3},{6,4},{7,5},{8,6},{9,7},{10,... | collective-permute-start | bytes 2801672 | tf_op jit(solution)/shard_map/ppermute | solution.py:371
  216.3 59.1 %collective-permute-start.14 = (bf16[3,64,2432]{2,1,0:T(8,128)(2,1)S(1)}, bf16[3,64,2432]{2,1,0:T(8,128)(2,1)S(1)}, u32[]{:S(2)}, u32[]{:S(2)}) collective-permute-start(bf16[3,64,2432]{2,1,0:T(8,128)(2,1)S(1)} %get-tuple-element.64), channel_id=1, source_target_pairs={{0,2},{1,3},{2,4},{3,5},{4,6},{5,7},{6,8},{7,9},{8,10},{9,11},{10,... | collective-permute-start | bytes 2801672 | tf_op jit(solution)/shard_map/ppermute | solution.py:371

commit v4 on v3

--- a/solution.py
+++ b/solution.py
@@ -235,11 +235,7 @@
         send_buf[:, :, lanes] = value[:ROWS]
         far_buf[:, :, lanes] = value[ROWS:]
 
-    @pl.loop(0, TILES - 1)
-    def _(tile):
-        emit(tile, LANES)
-
-    emit(TILES - 1, LANES // 2)
+    each_tile(emit)
     write(send_buf.at[:NC], send_low)
     write(send_buf.at[NC:FIRST], send_high)
     write(send_buf.at[FIRST:], send_rest)
@@ -248,27 +244,41 @@
         copy.wait()
 
 
-def tile_dot(rows, cols):
+def each_tile(step):
+    @pl.loop(0, TILES - 1)
+    def _(tile):
+        step(tile, LANES)
+
+    step(TILES - 1, LANES // 2)
+
+
+def tile_dot(rows, cols, tile, width):
     left = rows[...].reshape(rows.shape[0] * BS, rows.shape[2])
-    right = cols[...].reshape(LANES, cols.shape[2])
+    right = cols[pl.ds(QUAD * tile, width // BS)].reshape(width, cols.shape[2])
     value = lax.dot_general(left, right, NT, preferred_element_type=jnp.float32)
-    return value.reshape(rows.shape[0], BS, LANES)
-
-
-def mine_kernel(pt_fast, wt_fast, low, high, out):
-    value = tile_dot(pt_fast, wt_fast)
-    out[:NC] = value[:NC] + low[...].astype(jnp.float32)
-    out[NC:] = value[NC:] + high[...].astype(jnp.float32)
-
-
-def slow_kernel(core, inv_slow, p_slow, at_halo, rest, wt, turned_p, ext, at_buf, rest_buf, sems):
+    return value.reshape(rows.shape[0], BS, width)
+
+
+def tile_lanes(tile, width):
+    return pl.ds(pl.multiple_of(tile * LANES, LANES), width)
+
+
+def mine_kernel(fast, slow, wt_fast, wt_slow, low, high, far_fast, out, far):
+    def step(tile, width):
+        lanes = tile_lanes(tile, width)
+        inner = tile_dot(fast, wt_fast, tile, width)
+        outer = tile_dot(slow, wt_slow, tile, width)
+        near = inner + outer[:FIRST]
+        out[:NC, :, lanes] = near[:NC] + low[:, :, lanes].astype(jnp.float32)
+        out[NC:, :, lanes] = near[NC:] + high[:, :, lanes].astype(jnp.float32)
+        tail = outer[FIRST:] + far_fast[:, :, lanes].astype(jnp.float32)
+        far[:, :, lanes] = tail.astype(jnp.bfloat16)
+
+    each_tile(step)
+
+
+def slow_kernel(core, inv_slow, p_slow, at_halo, rest, wt, turned_p, ext):
     s = core[0]
-    copies = [
-        pltpu.make_async_copy(at_halo, at_buf, sems.at[0]),
-        pltpu.make_async_copy(rest, rest_buf, sems.at[1]),
-    ]
-    for copy in copies:
-        copy.start()
     turned_p[KP] = jnp.zeros((BS, LANES), jnp.bfloat16)
 
     @pl.loop(0, AGG // QUAD)
@@ -285,35 +295,40 @@
     wt[0:5] = jnp.zeros((5, BS, AW), jnp.bfloat16)
     wt[WSLOT:] = jnp.zeros((WCOLS - WSLOT, BS, AW), jnp.bfloat16)
     chunk = WSLOT // 3
-    for copy in copies:
-        copy.wait()
 
     @pl.loop(0, 3)
     def _(part):
         rows = pl.ds(part * chunk, chunk)
         value = jnp.dot(
             ext[rows].reshape(chunk * BS, AW),
-            at_buf[...].reshape(AW, AW),
+            at_halo[...].reshape(AW, AW),
             preferred_element_type=jnp.float32,
         )
-        value = value.reshape(chunk, BS, AW) + rest_buf[rows]
+        value = value.reshape(chunk, BS, AW) + rest[rows]
         wt[pl.ds(5 * s + part * chunk, chunk)] = value.astype(jnp.bfloat16)
 
 
-def join_first_kernel(slow, other, wt_slow, wt_other, mine, far_fast, m0, m4, far):
-    value = tile_dot(slow, wt_slow)
-    near = value[:FIRST] + (tile_dot(other, wt_other) + mine[...])
-    m0[...] = near[:NC].astype(jnp.bfloat16)
-    m4[...] = near[NC:].astype(jnp.bfloat16)
-    far[...] = (value[FIRST:] + far_fast[...].astype(jnp.float32)).astype(jnp.bfloat16)
+def join_first_kernel(other, wt_other, mine, m0, m4):
+    def step(tile, width):
+        lanes = tile_lanes(tile, width)
+        value = tile_dot(other, wt_other, tile, width) + mine[:, :, lanes]
+        m0[:, :, lanes] = value[:NC].astype(jnp.bfloat16)
+        m4[:, :, lanes] = value[NC:].astype(jnp.bfloat16)
+
+    each_tile(step)
 
 
 def join_rest_kernel(fast, slow, other, wt_fast, wt_slow, wt_other, arrived, m1, m3, own):
-    value = tile_dot(fast, wt_fast) + tile_dot(slow, wt_slow) + tile_dot(other, wt_other)
-    value = value + arrived[...].astype(jnp.float32)
-    m1[...] = value[:NC].astype(jnp.bfloat16)
-    m3[...] = value[NC : 2 * NC].astype(jnp.bfloat16)
-    own[...] = value[2 * NC :]
+    def step(tile, width):
+        lanes = tile_lanes(tile, width)
+        value = tile_dot(fast, wt_fast, tile, width) + tile_dot(slow, wt_slow, tile, width)
+        value = value + tile_dot(other, wt_other, tile, width)
+        value = value + arrived[:, :, lanes].astype(jnp.float32)
+        m1[:, :, lanes] = value[:NC].astype(jnp.bfloat16)
+        m3[:, :, lanes] = value[NC : 2 * NC].astype(jnp.bfloat16)
+        own[:, :, lanes] = value[2 * NC :]
+
+    each_tile(step)
 
 
 def frame_add(frame, message, start):
@@ -406,7 +421,7 @@
             functools.partial(pick_kernel, outer=outer),
             out_shape=jax.ShapeDtypeStruct((AGG,) + p_blocks.shape[1:], bf16),
             in_specs=[smem, hbm],
-            out_specs=hbm,
+            out_specs=vmem,
             scratch_shapes=[pltpu.SemaphoreType.DMA((4,))],
             compiler_params=params(60),
             name="pick_outer" if outer else "pick_inner",
@@ -496,72 +511,54 @@
     other_first = permuted(other_first, inward)
     p_slow, low, high, other_first = lax.optimization_barrier((p_slow, low, high, other_first))
 
-    def lane_tile(rows):
-        return pl.BlockSpec((rows, BS, LANES), lambda n: (0, 0, n))
-
-    def col_tile(width):
-        return pl.BlockSpec((QUAD, BS, width), lambda n: (n, 0, 0))
-
-    def whole(rows, width):
-        return pl.BlockSpec((rows, BS, width), lambda n: (0, 0, 0))
-
     wt_slow = pl.pallas_call(
         slow_kernel,
         out_shape=block(WCOLS, AW),
-        in_specs=[smem] * 2 + [vmem, hbm, hbm],
+        in_specs=[smem] * 2 + [vmem] * 3,
         out_specs=vmem,
         scratch_shapes=[
             pltpu.VMEM((KP + 1, BS, LANES), bf16),
             pltpu.VMEM((WSLOT, BS, AW), bf16),
-            pltpu.VMEM((AGG, BS, AW), bf16),
-            pltpu.VMEM((WSLOT, BS, AW), jnp.float32),
-            pltpu.SemaphoreType.DMA((2,)),
         ],
-        compiler_params=params(60),
+        compiler_params=params(24),
         cost_estimate=cost(20 * 10**9, 200 * 10**6),
         name="slow",
     )(core, inv_slow, p_slow, at_halo, rest)
     wt_other = permuted(wt_slow, inward)
 
     wt_slow, low, high = lax.optimization_barrier((wt_slow, low, high))
-    mine = pl.pallas_call(
+    mine, far = pl.pallas_call(
         mine_kernel,
-        grid=(TILES,),
-        out_shape=block(FIRST, span, jnp.float32),
-        in_specs=[whole(FIRST, 2 * AW), col_tile(2 * AW), lane_tile(NC), lane_tile(NC)],
-        out_specs=lane_tile(FIRST),
-        compiler_params=params(60),
+        out_shape=[block(FIRST, span, jnp.float32), block(NC, span)],
+        in_specs=[vmem] * 7,
+        out_specs=[vmem] * 2,
+        compiler_params=params(24),
         cost_estimate=cost(10**10, 100 * 10**6),
         name="mine",
-    )(fast_first, wt_fast, low, high)
+    )(fast_first, slow_first, wt_fast, wt_slow, low, high, far)
+    far = permuted(far, [(i, (i + (5 if i % 2 else -5)) % devices) for i in range(devices)])
     mine, wt_other, send_rest, other_rest = lax.optimization_barrier(
         (mine, wt_other, send_rest, other_rest)
     )
     arrived_rest = permuted(send_rest, inward)
     other_rest = permuted(other_rest, inward)
-    m0, m4, far = pl.pallas_call(
+    m0, m4 = pl.pallas_call(
         join_first_kernel,
-        grid=(TILES,),
-        out_shape=[block(NC, span)] * 3,
-        in_specs=[whole(FIRST + NC, AW), whole(FIRST, AW)]
-        + [col_tile(AW)] * 2
-        + [lane_tile(FIRST), lane_tile(NC)],
-        out_specs=[lane_tile(NC)] * 3,
+        out_shape=[block(NC, span)] * 2,
+        in_specs=[vmem] * 3,
+        out_specs=[vmem] * 2,
         compiler_params=params(16),
         cost_estimate=cost(3 * 10**9, 10**7),
         name="join_first",
-    )(slow_first, other_first, wt_slow, wt_other, mine, far)
+    )(other_first, wt_other, mine)
     m0 = permuted(m0, shifted(-4))
     m4 = permuted(m4, shifted(4))
-    far = permuted(far, [(i, (i + (5 if i % 2 else -5)) % devices) for i in range(devices)])
     m1, m3, own = pl.pallas_call(
         join_rest_kernel,
-        grid=(TILES,),
         out_shape=[block(NC, span)] * 2 + [block(NC, span, jnp.float32)],
-        in_specs=[whole(REST, 2 * AW), whole(REST, AW), whole(REST, AW)]
-        + [col_tile(2 * AW), col_tile(AW), col_tile(AW), lane_tile(REST)],
-        out_specs=[lane_tile(NC)] * 3,
-        compiler_params=params(24),
+        in_specs=[vmem] * 7,
+        out_specs=[vmem] * 3,
+        compiler_params=params(30),
         cost_estimate=cost(40 * 10**9, 200 * 10**6),
         name="join_rest",
     )(fast_rest, slow_rest, other_rest, wt_fast, wt_slow, wt_other, arrived_rest)

time: 281 us -> 157 us (0.56)
  Pallas kernels: 191 us -> 68.3 us
  waiting for transfers between devices: 64 us -> 67.4 us
    pallas_call x2, Pallas kernels: 113 us -> 5.39 us  [picked(): pl.pallas_call(functools.partial(pick_kernel, outer=outer), out_shape=jax...]
    pallas_call x3, Pallas kernels: 29.9 us -> 18.1 us  [the longest x1 8.1 us: body(): pl.pallas_call(join_rest_kernel, out_shape=[block(NC, span)] * 2 + [block...]
    ppermute x15, waiting for transfers between devices: 64 us -> 67.4 us  [permuted(): return lax.ppermute(block, 'dom', pairs)]
    pallas_call x1, Pallas kernels: 7.1 us -> 4.2 us  [body(): pl.pallas_call(slow_kernel, out_shape=block(WCOLS, AW), in_specs=[smem] *...]
  transfers between devices with their start and end apart: 15 -> 15, of which waited for: 3 -> 5; matrix products, arithmetic and copies ran while one was open for 1% -> 2% of each run, Pallas kernels for 65% -> 39%
where the time goes in v4:
time: 157 us
  Pallas kernels  68.3 us (44%)
  waiting for transfers between devices  67.4 us (43%)
  starting transfers between devices  14.3 us (9%)
  local copies, waits for them, and re-layouts  4.28 us (3%)
  other arithmetic  2.47 us (2%)
    ppermute x15, waiting for transfers between devices, permuted(): return lax.ppermute(block, 'dom', pairs)  67.4 us
    pallas_call x1, Pallas kernels, body(): pl.pallas_call(fast_kernel, out_shape=outs, in_specs=[smem] * 4 + [hbm, h...  35.2 us
    ppermute x15, starting transfers between devices, permuted(): return lax.ppermute(block, 'dom', pairs)  14.3 us
    pallas_call x1, Pallas kernels, body(): pl.pallas_call(join_rest_kernel, out_shape=[block(NC, span)] * 2 + [block...  8.1 us
    pallas_call x1, Pallas kernels, body(): pl.pallas_call(mine_kernel, out_shape=[block(FIRST, span, jnp.float32), b...  7.04 us
    pallas_call x2, Pallas kernels, summed(): pl.pallas_call(kernel, grid=(NC,), out_shape=block(NC, BAND * BS, jnp.flo...  5.51 us
    pallas_call x2, Pallas kernels, picked(): pl.pallas_call(functools.partial(pick_kernel, outer=outer), out_shape=jax...  5.39 us
    pallas_call x1, Pallas kernels, body(): pl.pallas_call(slow_kernel, out_shape=block(WCOLS, AW), in_specs=[smem] *...  4.2 us
  transfers between devices with their start and end apart: 15, of which 5 were waited for; matrix products, arithmetic and copies ran while one was open for 2% of the time, Pallas kernels for 39%

profile of v4, /device:TPU:0, one launch (start us, length us, event | category | flops | bytes accessed | tf_op | source)
XLA Modules:
  0.0 157.1 jit_solution(14849160026284340873)
XLA Ops:
  0.0 0.7 slice_bitcast_fusion
  0.7 0.5 collective-permute-start
  1.2 2.7 %pick_outer.1 = bf16[8,64,1728]{2,1,0:T(8,128)(2,1)} custom-call(s32[1]{0:T(128)} %bitcast.core, bf16[24,64,1728]{2,1,0:T(8,128)(2,1)} %source.3), custom_call_target="tpu_custom_call" | custom-call | tf_op jit(solution)/shard_map/pick_outer/pallas_call | solution.py:420
  3.9 0.0 copy-start.8
  4.0 0.0 copy-start.9
  4.0 6.7 %collective-permute-start.3 = (bf16[8,64,1728]{2,1,0:T(8,128)(2,1)}, bf16[8,64,1728]{2,1,0:T(8,128)(2,1)S(1)}, u32[]{:S(2)}, u32[]{:S(2)}) collective-permute-start(bf16[8,64,1728]{2,1,0:T(8,128)(2,1)} %pick_outer.1), channel_id=1, source_target_pairs={{0,31},{1,2},{2,1},{3,4},{4,3},{5,6},{6,5},{7,8},{8,7},{9,10},{10,... | collective-permute-start | bytes 5308424 | tf_op jit(solution)/shard_map/ppermute | solution.py:386
  10.6 2.7 %pick_inner.1 = bf16[8,64,1728]{2,1,0:T(8,128)(2,1)} custom-call(s32[1]{0:T(128)} %bitcast.core, bf16[24,64,1728]{2,1,0:T(8,128)(2,1)} %source.3), custom_call_target="tpu_custom_call" | custom-call | tf_op jit(solution)/shard_map/pick_inner/pallas_call | solution.py:420
  13.3 0.1 collective-permute-start.1
  13.5 0.1 fusion.1
  13.5 0.1 copy.15
  13.7 0.1 select_reduce_fusion.3
  13.8 0.2 select_reduce_fusion
  13.9 0.6 broadcast_add_fusion.inv_a
  14.5 0.6 broadcast_add_fusion.1.inv_own
  15.2 0.1 copy.16
  15.2 0.1 select_reduce_fusion.2
  15.4 0.6 broadcast_add_fusion.3.inv_fast
  16.0 1.5 collective-permute-done.1.p_fast
  17.5 35.2 %fast.1 = (bf16[3,64,2432]{2,1,0:T(8,128)(2,1)}, bf16[3,64,2432]{2,1,0:T(8,128)(2,1)}, bf16[9,64,2432]{2,1,0:T(8,128)(2,1)}, bf16[3,64,2432]{2,1,0:T(8,128)(2,1)...) custom-call(s32[1]{0:T(128)} %bitcast.core, ...), custom_call_target="tpu_custom_call" | custom-call | flops 20000000000 | bytes 30000000 | tf_op jit(solution)/shard_map/fast/pallas_call | solution.py:482
  52.7 0.2 collective-permute-start.4
  52.9 0.4 collective-permute-start.5
  53.3 0.3 collective-permute-start.2
  53.5 0.0 collective-permute-start.6
  53.5 6.4 %collective-permute-done.2 = s32[8,27]{1,0:T(8,128)S(1)} collective-permute-done((s32[8,27]{1,0:T(8,128)S(1)}, s32[8,27]{1,0:T(8,128)S(1)}, u32[]{:S(2)}, u32[]{:S(2)}) %collective-permute-start.2) | collective-permute-done | bytes 896 | tf_op jit(solution)/shard_map/ppermute | solution.py:386
  59.9 0.1 copy.17
  60.0 0.1 select_reduce_fusion.1
  60.1 0.0 collective-permute-done.3.p_slow
  60.2 0.0 collective-permute-done.4.low
  60.2 0.0 collective-permute-done.5.high
  60.2 2.2 %copy-done.3 = f32[33,64,512]{2,1,0:T(8,128)S(1)} copy-done((f32[33,64,512]{2,1,0:T(8,128)S(1)}, f32[33,64,512]{2,1,0:T(8,128)}, u32[]{:S(2)}) %copy-start.3) | copy-done | bytes 4325400
  62.4 1.0 copy-done.7
  63.5 4.2 %slow.1.wt_slow = bf16[40,64,512]{2,1,0:T(8,128)(2,1)S(1)} custom-call(s32[1]{0:T(128)} %bitcast.core, s32[8,33]{1,0:T(8,128)S(1)} %broadcast_add_fusion.2.inv_slow, bf16[8,64,1728]{2,1,0:T(8,128)(2,1)S(1)} %collective-permute-done.3.p_slow, bf16[8,64,512]{2,1,0:T(8,128)(2,1)S(1)} %copy-done.7, f32[33,64,512]{2,1,0:T(8,128)S(1)} %copy-done.3), custom_call_target="tpu_custom_call" | custom-call | flops 20000000000 | bytes 200000000 | tf_op jit(solution)/shard_map/slow/pallas_call | solution.py:514
  67.7 0.1 collective-permute-start.7
  67.8 0.0 copy-start.10
  67.8 7.0 %mine.1 = (f32[6,64,2432]{2,1,0:T(8,128)S(1)}, bf16[3,64,2432]{2,1,0:T(8,128)(2,1)S(1)}) custom-call(bf16[6,64,1024]{2,1,0:T(8,128)(2,1)S(1)} %copy-done.2, bf16[9,64,512]{2,1,0:T(8,128)(2,1)S(1)} %copy-done.4, bf16[40,64,1024]{2,1,0:T(8,128)(2,1)S(1)} %copy-done, bf16[40,64,512]{2,1,0:T(8,128)(2,1)S(1)} %slow.1.wt_slow, ...), custom_call_target="tpu_custom_call" | custom-call | flops 10000000000 | bytes 100000000 | tf_op jit(solution)/shard_map/mine/pallas_call | solution.py:530
  74.9 0.5 collective-permute-start.9
  75.4 0.1 collective-permute-start.8
  75.5 0.1 collective-permute-start.12
  75.6 2.9 %join_first.1 = (bf16[3,64,2432]{2,1,0:T(8,128)(2,1)S(1)}, bf16[3,64,2432]{2,1,0:T(8,128)(2,1)S(1)}) custom-call(bf16[6,64,512]{2,1,0:T(8,128)(2,1)S(1)} %collective-permute-done.6.other, bf16[40,64,512]{2,1,0:T(8,128)(2,1)S(1)} %collective-permute-done.7.wt_other, f32[6,64,2432]{2,1,0:T(8,128)S(1)} %get-tuple-element.61.mine), custom_call_target="tpu_custom_call" | custom-call | flops 3000000000 | bytes 10000000 | tf_op jit(solution)/shard_map/join_first/pallas_call | solution.py:545
  78.5 0.1 collective-permute-start.10
  78.6 2.0 %collective-permute-start.11 = (bf16[3,64,2432]{2,1,0:T(8,128)(2,1)S(1)}, bf16[3,64,2432]{2,1,0:T(8,128)(2,1)S(1)}, u32[]{:S(2)}, u32[]{:S(2)}) collective-permute-start(bf16[3,64,2432]{2,1,0:T(8,128)(2,1)S(1)} %get-tuple-element.63), channel_id=1, source_target_pairs={{0,4},{1,5},{2,6},{3,7},{4,8},{5,9},{6,10},{7,11},{8,12},{9,13},{1... | collective-permute-start | bytes 2801672 | tf_op jit(solution)/shard_map/ppermute | solution.py:386
  80.6 0.5 collective-permute-done.8.other
  81.1 8.1 %join_rest.1 = (bf16[3,64,2432]{2,1,0:T(8,128)(2,1)S(1)}, bf16[3,64,2432]{2,1,0:T(8,128)(2,1)S(1)}, f32[3,64,2432]{2,1,0:T(8,128)S(1)}) custom-call(bf16[9,64,1024]{2,1,0:T(8,128)(2,1)S(1)} %copy-done.5, bf16[9,64,512]{2,1,0:T(8,128)(2,1)S(1)} %copy-done.6, bf16[9,64,512]{2,1,0:T(8,128)(2,1)S(1)} %collective-permute-done.8.other, ...), custom_call_target="tpu_custom_call" | custom-call | flops 40000000000 | bytes 200000000 | tf_op jit(solution)/shard_map/join_rest/pallas_call | solution.py:556
  89.2 3.4 %collective-permute-start.13 = (bf16[3,64,2432]{2,1,0:T(8,128)(2,1)S(1)}, bf16[3,64,2432]{2,1,0:T(8,128)(2,1)S(1)}, u32[]{:S(2)}, u32[]{:S(2)}) collective-permute-start(bf16[3,64,2432]{2,1,0:T(8,128)(2,1)S(1)} %get-tuple-element.65), channel_id=1, source_target_pairs={{0,30},{1,31},{2,0},{3,1},{4,2},{5,3},{6,4},{7,5},{8,6},{9,7},{10,... | collective-permute-start | bytes 2801672 | tf_op jit(solution)/shard_map/ppermute | solution.py:386
  92.6 8.9 %collective-permute-done.12.far = bf16[3,64,2432]{2,1,0:T(8,128)(2,1)S(1)} collective-permute-done((bf16[3,64,2432]{2,1,0:T(8,128)(2,1)S(1)}, bf16[3,64,2432]{2,1,0:T(8,128)(2,1)S(1)}, u32[]{:S(2)}, u32[]{:S(2)}) %collective-permute-start.12) | collective-permute-done | bytes 933920 | tf_op jit(solution)/shard_map/ppermute | solution.py:386
  101.5 50.0 %collective-permute-done.10.m0 = bf16[3,64,2432]{2,1,0:T(8,128)(2,1)S(1)} collective-permute-done((bf16[3,64,2432]{2,1,0:T(8,128)(2,1)S(1)}, bf16[3,64,2432]{2,1,0:T(8,128)(2,1)S(1)}, u32[]{:S(2)}, u32[]{:S(2)}) %collective-permute-start.10) | collective-permute-done | bytes 933920 | tf_op jit(solution)/shard_map/ppermute | solution.py:386
  151.5 2.3 %early.1 = f32[3,64,4032]{2,1,0:T(8,128)S(1)} custom-call(s32[1]{0:T(128)} %bitcast.core, f32[3,64,2432]{2,1,0:T(8,128)S(1)} %get-tuple-element.59.own, bf16[3,64,2432]{2,1,0:T(8,128)(2,1)S(1)} %collective-permute-done.10.m0, bf16[3,64,2432]{2,1,0:T(8,128)(2,1)S(1)} %collective-permute-done.11.m4, bf16[3,64,2432]{2,1,0:T(8,128)(2,1)S(1)} %collective-permute-done.12.far), custom_call_target="tpu_custom_call" | custom-call | flops 10000000 | bytes 10000000 | tf_op jit(solution)/shard_map/early/pallas_call | solution.py:572
  153.9 3.2 %total.1 = f32[3,64,4032]{2,1,0:T(8,128)} custom-call(s32[1]{0:T(128)} %bitcast.core, f32[3,64,4032]{2,1,0:T(8,128)S(1)} %early.1, bf16[3,64,2432]{2,1,0:T(8,128)(2,1)S(1)} %collective-permute-done.13.m1, bf16[3,64,2432]{2,1,0:T(8,128)(2,1)S(1)} %collective-permute-done.14.m3), custom_call_target="tpu_custom_call" | custom-call | flops 10000000 | bytes 10000000 | tf_op jit(solution)/shard_map/total/pallas_call | solution.py:572
  (41 shorter events, 0.1 us)
Async XLA Ops:
  0.7 14.4 %collective-permute-start = (s32[8,27]{1,0:T(8,128)S(1)}, s32[8,27]{1,0:T(8,128)S(1)}, u32[]{:S(2)}, u32[]{:S(2)}) collective-permute-start(s32[8,27]{1,0:T(8,128)S(1)} %get-tuple-element.70), channel_id=1, source_target_pairs={{0,1},{1,0},{2,3},{3,2},{4,5},{5,4},{6,7},{7,6},{8,9},{9,8},{10,11... | collective-permute-start | bytes 2600 | tf_op jit(solution)/shard_map/ppermute | solution.py:386
  3.9 9.5 %copy-start.8 = (s32[24,27]{1,0:T(8,128)S(1)}, s32[24,27]{1,0:T(8,128)}, u32[]{:S(2)}) copy-start(s32[24,27]{1,0:T(8,128)} %param.7) | copy-start | bytes 7780
  4.0 9.7 %copy-start.9 = (s32[24,7]{0,1:T(8,128)S(1)}, s32[24,7]{0,1:T(8,128)}, u32[]{:S(2)}) copy-start(s32[24,7]{0,1:T(8,128)} %param.6) | copy-start | bytes 2020
  4.0 56.2 %collective-permute-start.3 = (bf16[8,64,1728]{2,1,0:T(8,128)(2,1)}, bf16[8,64,1728]{2,1,0:T(8,128)(2,1)S(1)}, u32[]{:S(2)}, u32[]{:S(2)}) collective-permute-start(bf16[8,64,1728]{2,1,0:T(8,128)(2,1)} %pick_outer.1), channel_id=1, source_target_pairs={{0,31},{1,2},{2,1},{3,4},{4,3},{5,6},{6,5},{7,8},{8,7},{9,10},{10,... | collective-permute-start | bytes 5308424 | tf_op jit(solution)/shard_map/ppermute | solution.py:386
  13.3 4.2 %collective-permute-start.1 = (bf16[8,64,1728]{2,1,0:T(8,128)(2,1)}, bf16[8,64,1728]{2,1,0:T(8,128)(2,1)}, u32[]{:S(2)}, u32[]{:S(2)}) collective-permute-start(bf16[8,64,1728]{2,1,0:T(8,128)(2,1)} %pick_inner.1), channel_id=1, source_target_pairs={{0,1},{1,0},{2,3},{3,2},{4,5},{5,4},{6,7},{7,6},{8,9},{9,8},{10,11... | collective-permute-start | bytes 5308424 | tf_op jit(solution)/shard_map/ppermute | solution.py:386
  52.7 7.5 %collective-permute-start.4 = (bf16[3,64,2432]{2,1,0:T(8,128)(2,1)}, bf16[3,64,2432]{2,1,0:T(8,128)(2,1)S(1)}, u32[]{:S(2)}, u32[]{:S(2)}) collective-permute-start(bf16[3,64,2432]{2,1,0:T(8,128)(2,1)} %get-tuple-element.41), channel_id=1, source_target_pairs={{0,1},{1,0},{2,3},{3,2},{4,5},{5,4},{6,7},{7,6},{8,9},{9,8},{10,11... | collective-permute-start | bytes 2801672 | tf_op jit(solution)/shard_map/ppermute | solution.py:386
  52.9 7.3 %collective-permute-start.5 = (bf16[3,64,2432]{2,1,0:T(8,128)(2,1)}, bf16[3,64,2432]{2,1,0:T(8,128)(2,1)}, u32[]{:S(2)}, u32[]{:S(2)}) collective-permute-start(bf16[3,64,2432]{2,1,0:T(8,128)(2,1)} %get-tuple-element.42), channel_id=1, source_target_pairs={{0,1},{1,0},{2,3},{3,2},{4,5},{5,4},{6,7},{7,6},{8,9},{9,8},{10,11... | collective-permute-start | bytes 2801672 | tf_op jit(solution)/shard_map/ppermute | solution.py:386
  53.3 6.6 %collective-permute-start.2 = (s32[8,27]{1,0:T(8,128)S(1)}, s32[8,27]{1,0:T(8,128)S(1)}, u32[]{:S(2)}, u32[]{:S(2)}) collective-permute-start(s32[8,27]{1,0:T(8,128)S(1)} %get-tuple-element.69), channel_id=1, source_target_pairs={{0,31},{1,2},{2,1},{3,4},{4,3},{5,6},{6,5},{7,8},{8,7},{9,10},{10,... | collective-permute-start | bytes 2600 | tf_op jit(solution)/shard_map/ppermute | solution.py:386
  53.5 6.6 %collective-permute-start.6 = (bf16[6,64,512]{2,1,0:T(8,128)(2,1)}, bf16[6,64,512]{2,1,0:T(8,128)(2,1)S(1)}, u32[]{:S(2)}, u32[]{:S(2)}) collective-permute-start(bf16[6,64,512]{2,1,0:T(8,128)(2,1)} %get-tuple-element.43), channel_id=1, source_target_pairs={{0,1},{1,0},{2,3},{3,2},{4,5},{5,4},{6,7},{7,6},{8,9},{9,8},{10,11... | collective-permute-start | bytes 1179656 | tf_op jit(solution)/shard_map/ppermute | solution.py:386
  60.2 2.2 %copy-start.3 = (f32[33,64,512]{2,1,0:T(8,128)S(1)}, f32[33,64,512]{2,1,0:T(8,128)}, u32[]{:S(2)}) copy-start(f32[33,64,512]{2,1,0:T(8,128)} %get-tuple-element.46.rest) | copy-start | bytes 12976132
  62.4 1.0 copy-start.7
  63.5 4.3 %copy-start = (bf16[40,64,1024]{2,1,0:T(8,128)(2,1)S(1)}, bf16[40,64,1024]{2,1,0:T(8,128)(2,1)}, u32[]{:S(2)}) copy-start(bf16[40,64,1024]{2,1,0:T(8,128)(2,1)} %get-tuple-element.40.wt_fast) | copy-start | bytes 15728644
  63.5 4.3 %copy-start.1 = (bf16[3,64,2432]{2,1,0:T(8,128)(2,1)S(1)}, bf16[3,64,2432]{2,1,0:T(8,128)(2,1)}, u32[]{:S(2)}) copy-start(bf16[3,64,2432]{2,1,0:T(8,128)(2,1)} %get-tuple-element.52.far_fast) | copy-start | bytes 2801668
  63.5 4.3 %copy-start.2 = (bf16[6,64,1024]{2,1,0:T(8,128)(2,1)S(1)}, bf16[6,64,1024]{2,1,0:T(8,128)(2,1)}, u32[]{:S(2)}) copy-start(bf16[6,64,1024]{2,1,0:T(8,128)(2,1)} %get-tuple-element.38.fast) | copy-start | bytes 2359300
  63.5 4.3 %copy-start.4 = (bf16[9,64,512]{2,1,0:T(8,128)(2,1)S(1)}, bf16[9,64,512]{2,1,0:T(8,128)(2,1)}, u32[]{:S(2)}) copy-start(bf16[9,64,512]{2,1,0:T(8,128)(2,1)} %get-tuple-element.39.slow) | copy-start | bytes 1769476
  67.7 7.2 %collective-permute-start.7 = (bf16[40,64,512]{2,1,0:T(8,128)(2,1)S(1)}, bf16[40,64,512]{2,1,0:T(8,128)(2,1)S(1)}, u32[]{:S(2)}, u32[]{:S(2)}) collective-permute-start(bf16[40,64,512]{2,1,0:T(8,128)(2,1)S(1)} %slow.1.wt_slow), channel_id=1, source_target_pairs={{0,1},{1,0},{2,3},{3,2},{4,5},{5,4},{6,7},{7,6},{8,9},{9,8},{10,11... | collective-permute-start | bytes 7864328 | tf_op jit(solution)/shard_map/ppermute | solution.py:386
  67.8 7.1 %copy-start.10 = (bf16[9,64,2432]{2,1,0:T(8,128)(2,1)S(1)}, bf16[9,64,2432]{2,1,0:T(8,128)(2,1)}, u32[]{:S(2)}) copy-start(bf16[9,64,2432]{2,1,0:T(8,128)(2,1)} %get-tuple-element.58) | copy-start | bytes 8404996
  67.8 7.6 %copy-start.11 = (bf16[9,64,512]{2,1,0:T(8,128)(2,1)S(1)}, bf16[9,64,512]{2,1,0:T(8,128)(2,1)}, u32[]{:S(2)}) copy-start(bf16[9,64,512]{2,1,0:T(8,128)(2,1)} %get-tuple-element.56) | copy-start | bytes 1769476
  74.9 6.2 %collective-permute-start.9 = (bf16[9,64,2432]{2,1,0:T(8,128)(2,1)S(1)}, bf16[9,64,2432]{2,1,0:T(8,128)(2,1)S(1)}, u32[]{:S(2)}, u32[]{:S(2)}) collective-permute-start(bf16[9,64,2432]{2,1,0:T(8,128)(2,1)S(1)} %copy-done.10), channel_id=1, source_target_pairs={{0,1},{1,0},{2,3},{3,2},{4,5},{5,4},{6,7},{7,6},{8,9},{9,8},{10,11... | collective-permute-start | bytes 8405000 | tf_op jit(solution)/shard_map/ppermute | solution.py:386
  75.4 5.6 %collective-permute-start.8 = (bf16[9,64,512]{2,1,0:T(8,128)(2,1)S(1)}, bf16[9,64,512]{2,1,0:T(8,128)(2,1)S(1)}, u32[]{:S(2)}, u32[]{:S(2)}) collective-permute-start(bf16[9,64,512]{2,1,0:T(8,128)(2,1)S(1)} %copy-done.11), channel_id=1, source_target_pairs={{0,1},{1,0},{2,3},{3,2},{4,5},{5,4},{6,7},{7,6},{8,9},{9,8},{10,11... | collective-permute-start | bytes 1769480 | tf_op jit(solution)/shard_map/ppermute | solution.py:386
  75.5 5.6 %slice-start = ((s8[5242880]{0:T(1024)(128)(4,1)}), s8[4194304]{0:T(1024)(128)(4,1)S(1)}, s32[]{:S(2)}) async-start(s8[5242880]{0:T(1024)(128)(4,1)} %bitcast.9), calls=%async_computation | async-start | bytes 8388608
  75.5 5.6 %slice-start.1 = ((s8[5242880]{0:T(1024)(128)(4,1)}), s8[1048576]{0:T(1024)(128)(4,1)S(1)}, s32[]{:S(2)}) async-start(s8[5242880]{0:T(1024)(128)(4,1)} %bitcast.9), calls=%async_computation.1 | async-start | bytes 2097152
  75.5 5.6 %copy-start.5 = (bf16[9,64,1024]{2,1,0:T(8,128)(2,1)S(1)}, bf16[9,64,1024]{2,1,0:T(8,128)(2,1)}, u32[]{:S(2)}) copy-start(bf16[9,64,1024]{2,1,0:T(8,128)(2,1)} %get-tuple-element.36.fast) | copy-start | bytes 3538948
  75.5 5.6 %copy-start.6 = (bf16[9,64,512]{2,1,0:T(8,128)(2,1)S(1)}, bf16[9,64,512]{2,1,0:T(8,128)(2,1)}, u32[]{:S(2)}) copy-start(bf16[9,64,512]{2,1,0:T(8,128)(2,1)} %get-tuple-element.37.slow) | copy-start | bytes 1769476
  75.5 26.0 %collective-permute-start.12 = (bf16[3,64,2432]{2,1,0:T(8,128)(2,1)S(1)}, bf16[3,64,2432]{2,1,0:T(8,128)(2,1)S(1)}, u32[]{:S(2)}, u32[]{:S(2)}) collective-permute-start(bf16[3,64,2432]{2,1,0:T(8,128)(2,1)S(1)} %get-tuple-element.64), channel_id=1, source_target_pairs={{0,27},{1,6},{2,29},{3,8},{4,31},{5,10},{6,1},{7,12},{8,3},{9,14},... | collective-permute-start | bytes 2801672 | tf_op jit(solution)/shard_map/ppermute | solution.py:386
  78.5 73.0 %collective-permute-start.10 = (bf16[3,64,2432]{2,1,0:T(8,128)(2,1)S(1)}, bf16[3,64,2432]{2,1,0:T(8,128)(2,1)S(1)}, u32[]{:S(2)}, u32[]{:S(2)}) collective-permute-start(bf16[3,64,2432]{2,1,0:T(8,128)(2,1)S(1)} %get-tuple-element.62), channel_id=1, source_target_pairs={{0,28},{1,29},{2,30},{3,31},{4,0},{5,1},{6,2},{7,3},{8,4},{9,5},{1... | collective-permute-start | bytes 2801672 | tf_op jit(solution)/shard_map/ppermute | solution.py:386
  78.6 73.0 %collective-permute-start.11 = (bf16[3,64,2432]{2,1,0:T(8,128)(2,1)S(1)}, bf16[3,64,2432]{2,1,0:T(8,128)(2,1)S(1)}, u32[]{:S(2)}, u32[]{:S(2)}) collective-permute-start(bf16[3,64,2432]{2,1,0:T(8,128)(2,1)S(1)} %get-tuple-element.63), channel_id=1, source_target_pairs={{0,4},{1,5},{2,6},{3,7},{4,8},{5,9},{6,10},{7,11},{8,12},{9,13},{1... | collective-permute-start | bytes 2801672 | tf_op jit(solution)/shard_map/ppermute | solution.py:386
  89.2 64.7 %collective-permute-start.13 = (bf16[3,64,2432]{2,1,0:T(8,128)(2,1)S(1)}, bf16[3,64,2432]{2,1,0:T(8,128)(2,1)S(1)}, u32[]{:S(2)}, u32[]{:S(2)}) collective-permute-start(bf16[3,64,2432]{2,1,0:T(8,128)(2,1)S(1)} %get-tuple-element.65), channel_id=1, source_target_pairs={{0,30},{1,31},{2,0},{3,1},{4,2},{5,3},{6,4},{7,5},{8,6},{9,7},{10,... | collective-permute-start | bytes 2801672 | tf_op jit(solution)/shard_map/ppermute | solution.py:386
  92.6 61.3 %collective-permute-start.14 = (bf16[3,64,2432]{2,1,0:T(8,128)(2,1)S(1)}, bf16[3,64,2432]{2,1,0:T(8,128)(2,1)S(1)}, u32[]{:S(2)}, u32[]{:S(2)}) collective-permute-start(bf16[3,64,2432]{2,1,0:T(8,128)(2,1)S(1)} %get-tuple-element.66), channel_id=1, source_target_pairs={{0,2},{1,3},{2,4},{3,5},{4,6},{5,7},{6,8},{7,9},{8,10},{9,11},{10,... | collective-permute-start | bytes 2801672 | tf_op jit(solution)/shard_map/ppermute | solution.py:386

commit v5 on v4

--- a/solution.py
+++ b/solution.py
@@ -33,7 +33,7 @@
 ROWS = NC * GROUPS
 FIRST = 2 * NC
 REST = ROWS - FIRST
-ORDER = (0, 4, 1, 3, 2)
+MERGED = WINDOW + 6
 
 
 def eye(n):
@@ -83,7 +83,7 @@
     send_high,
     send_rest,
     far,
-    fast_first,
+    inner,
     fast_rest,
     slow_first,
     slow_rest,
@@ -100,6 +100,7 @@
     lhs,
     send_buf,
     far_buf,
+    inner_buf,
     fast_buf,
     slow_buf,
     other_buf,
@@ -166,11 +167,15 @@
 
     fast_lanes = pl.ds(pl.multiple_of(AW + (1 - s) * AW, AW), 2 * AW)
     slow_lanes = pl.ds(pl.multiple_of(AW + 2 * s * AW, AW), AW)
-    for place, i in enumerate(ORDER):
+    x = core[1]
+    for place, i in enumerate((1 + 2 * x, 4 * x, 4 - 4 * x, 3 - 2 * x, 2)):
         for j in range(NC):
             row = NC * place + j
             mine, other = 6 * i + 3 + j + 1, 6 * i + 6 * (1 - s) + j + 1
-            fast_buf[row] = ext[mine, :, fast_lanes]
+            if place < 2:
+                lhs[ROWS + NC + row] = ext[mine, :, fast_lanes]
+            else:
+                fast_buf[row - FIRST] = ext[mine, :, fast_lanes]
             slow_buf[row if place < 2 else row + NC] = ext[mine, :, slow_lanes]
             other_buf[row] = ext[other, :, slow_lanes]
             lhs[row] = ext[other, :, fast_lanes]
@@ -186,8 +191,7 @@
 
     write(other_buf.at[:FIRST], other_first)
     write(other_buf.at[FIRST:], other_rest)
-    write(fast_buf.at[:FIRST], fast_first)
-    write(fast_buf.at[FIRST:], fast_rest)
+    write(fast_buf, fast_rest)
     write(slow_buf.at[: FIRST + NC], slow_first)
     write(slow_buf.at[FIRST + NC :], slow_rest)
 
@@ -228,18 +232,20 @@
 
     def emit(tile, width):
         right = wt_buf[pl.ds(QUAD * tile, width // BS)].reshape(width, 2 * AW)
-        left = lhs[...].reshape((ROWS + NC) * BS, 2 * AW)
+        left = lhs[...].reshape((ROWS + NC + FIRST) * BS, 2 * AW)
         value = lax.dot_general(left, right, NT, preferred_element_type=jnp.float32)
-        value = value.astype(jnp.bfloat16).reshape(ROWS + NC, BS, width)
+        value = value.astype(jnp.bfloat16).reshape(ROWS + NC + FIRST, BS, width)
         lanes = pl.ds(pl.multiple_of(tile * LANES, LANES), width)
         send_buf[:, :, lanes] = value[:ROWS]
-        far_buf[:, :, lanes] = value[ROWS:]
+        far_buf[:, :, lanes] = value[ROWS : ROWS + NC]
+        inner_buf[:, :, lanes] = value[ROWS + NC :]
 
     each_tile(emit)
     write(send_buf.at[:NC], send_low)
     write(send_buf.at[NC:FIRST], send_high)
     write(send_buf.at[FIRST:], send_rest)
     write(far_buf, far)
+    write(inner_buf, inner)
     for copy in copies:
         copy.wait()
 
@@ -263,12 +269,11 @@
     return pl.ds(pl.multiple_of(tile * LANES, LANES), width)
 
 
-def mine_kernel(fast, slow, wt_fast, wt_slow, low, high, far_fast, out, far):
+def mine_kernel(slow, wt_slow, inner, low, high, far_fast, out, far):
     def step(tile, width):
         lanes = tile_lanes(tile, width)
-        inner = tile_dot(fast, wt_fast, tile, width)
         outer = tile_dot(slow, wt_slow, tile, width)
-        near = inner + outer[:FIRST]
+        near = outer[:FIRST] + inner[:, :, lanes].astype(jnp.float32)
         out[:NC, :, lanes] = near[:NC] + low[:, :, lanes].astype(jnp.float32)
         out[NC:, :, lanes] = near[NC:] + high[:, :, lanes].astype(jnp.float32)
         tail = outer[FIRST:] + far_fast[:, :, lanes].astype(jnp.float32)
@@ -308,60 +313,85 @@
         wt[pl.ds(5 * s + part * chunk, chunk)] = value.astype(jnp.bfloat16)
 
 
-def join_first_kernel(other, wt_other, mine, m0, m4):
+def join_first_kernel(other, wt_other, mine, relay, direct):
     def step(tile, width):
         lanes = tile_lanes(tile, width)
         value = tile_dot(other, wt_other, tile, width) + mine[:, :, lanes]
-        m0[:, :, lanes] = value[:NC].astype(jnp.bfloat16)
-        m4[:, :, lanes] = value[NC:].astype(jnp.bfloat16)
+        relay[:, :, lanes] = value[:NC].astype(jnp.bfloat16)
+        direct[:, :, lanes] = value[NC:].astype(jnp.bfloat16)
 
     each_tile(step)
 
 
-def join_rest_kernel(fast, slow, other, wt_fast, wt_slow, wt_other, arrived, m1, m3, own):
+def join_rest_kernel(fast, slow, other, wt_fast, wt_slow, wt_other, arrived, merge, pair, own):
     def step(tile, width):
         lanes = tile_lanes(tile, width)
         value = tile_dot(fast, wt_fast, tile, width) + tile_dot(slow, wt_slow, tile, width)
         value = value + tile_dot(other, wt_other, tile, width)
         value = value + arrived[:, :, lanes].astype(jnp.float32)
-        m1[:, :, lanes] = value[:NC].astype(jnp.bfloat16)
-        m3[:, :, lanes] = value[NC : 2 * NC].astype(jnp.bfloat16)
+        merge[:, :, lanes] = value[:NC]
+        pair[:, :, lanes] = value[NC : 2 * NC].astype(jnp.bfloat16)
         own[:, :, lanes] = value[2 * NC :]
 
     each_tile(step)
 
 
-def frame_add(frame, message, start):
-    odd = start & 1
-    lane = pl.multiple_of((start - odd + 6) * BS, 2 * BS)
-    frame[odd, :, pl.ds(lane, WINDOW * BS)] += message[0].astype(jnp.float32)
-
-
-def frame_sum(frame):
+def merge_kernel(core, rows, relay, out, frame):
+    x = core[1]
+    step = 6 * BS
+    for j in range(NC):
+        frame[...] = jnp.zeros_like(frame)
+        frame[:, pl.ds(pl.multiple_of(step * x, step), WINDOW * BS)] = rows[j]
+        lanes = pl.ds(pl.multiple_of(step * (1 - x), step), WINDOW * BS)
+        frame[:, lanes] += relay[j].astype(jnp.float32)
+        out[j] = frame[...].astype(jnp.bfloat16)
+
+
+def in_frame(s, j, frame, messages, store):
+    odd = (j + 1 - s) % 2
+    frame[...] = jnp.zeros_like(frame)
+    for message, start in messages:
+        lane = pl.multiple_of((start - odd + 6) * BS, 2 * BS)
+        frame[:, pl.ds(lane, message.shape[2])] += message[j].astype(jnp.float32)
     first, last = 6 * BS, (6 + BAND) * BS
-    return frame[0, :, first:last] + frame[1, :, first - BS : last - BS]
-
-
-def early_kernel(core, own, m0, m4, far, out, frame):
-    s = core[0]
-    j = pl.program_id(0)
-    frame[...] = jnp.zeros_like(frame)
-    top = 27 - 3 * s - j
-    frame_add(frame, m0, top)
-    frame_add(frame, own, top - 12)
-    frame_add(frame, m4, top - 24)
-    frame_add(frame, far, jnp.where(s == 1, 30 - j, -3 - j))
-    out[0] = frame_sum(frame)
-
-
-def total_kernel(core, early, m1, m3, out, frame):
-    s = core[0]
-    j = pl.program_id(0)
-    frame[...] = jnp.zeros_like(frame)
-    top = 27 - 3 * s - j
-    frame_add(frame, m1, top - 6)
-    frame_add(frame, m3, top - 18)
-    out[0] = early[0] + frame_sum(frame)
+
+    @pl.when(odd == 0)
+    def _():
+        store(frame[:, first:last])
+
+    @pl.when(odd == 1)
+    def _():
+        store(frame[:, first - BS : last - BS])
+
+
+def early_kernel(core, own, direct, out, frame):
+    s, x = core[0], core[1]
+    for j in range(NC):
+        top = 27 - 3 * s - j
+
+        def store(value, j=j):
+            out[j] = value
+
+        in_frame(s, j, frame, [(own, top - 12), (direct, top - 24 * x)], store)
+
+
+def total_kernel(core, early, pair, merged, far, out, frame, buf, sems):
+    s, x = core[0], core[1]
+    copies = []
+    for j in range(NC):
+        top = 27 - 3 * s - j
+        far_start = jnp.where(s == 1, 30 - j, -3 - j)
+
+        def store(value, j=j):
+            buf[j] = value + early[j]
+
+        messages = [(pair, top - 6 - 12 * x), (merged, top - 24 + 18 * x), (far, far_start)]
+        in_frame(s, j, frame, messages, store)
+        copy = pltpu.make_async_copy(buf.at[j], out.at[j], sems.at[j])
+        copy.start()
+        copies.append(copy)
+    for copy in copies:
+        copy.wait()
 
 
 def pick_kernel(core, source, out, sems, *, outer):
@@ -399,7 +429,7 @@
     count_rows = NB * devices
     first_agg = device * NC
     first_row = device * NB
-    core = (device % 2).astype(jnp.int32).reshape(1)
+    core = jnp.stack([device % 2, device // 2 % 2]).astype(jnp.int32)
 
     def shifted(distance):
         return [(i, (i + distance) % devices) for i in range(devices)]
@@ -455,7 +485,7 @@
         block(NC, span),
         block(REST, span),
         block(NC, span),
-        block(FIRST, 2 * AW),
+        block(FIRST, span),
         block(REST, 2 * AW),
         block(FIRST + NC, AW),
         block(REST, AW),
@@ -470,7 +500,7 @@
         send_high,
         send_rest,
         far,
-        fast_first,
+        inner,
         fast_rest,
         slow_first,
         slow_rest,
@@ -490,10 +520,11 @@
             pltpu.VMEM((NC, 3 * AGG, BS, AW), bf16),
             pltpu.VMEM((KP + 1, BS, LANES), bf16),
             pltpu.VMEM((KA + 1, BS, LANES), bf16),
-            pltpu.VMEM((ROWS + NC, BS, 2 * AW), bf16),
+            pltpu.VMEM((ROWS + NC + FIRST, BS, 2 * AW), bf16),
             pltpu.VMEM((ROWS, BS, span), bf16),
             pltpu.VMEM((NC, BS, span), bf16),
-            pltpu.VMEM((ROWS, BS, 2 * AW), bf16),
+            pltpu.VMEM((FIRST, BS, span), bf16),
+            pltpu.VMEM((REST, BS, 2 * AW), bf16),
             pltpu.VMEM((ROWS + NC, BS, AW), bf16),
             pltpu.VMEM((ROWS, BS, AW), bf16),
             pltpu.VMEM((WCOLS, BS, 2 * AW), bf16),
@@ -530,19 +561,18 @@
     mine, far = pl.pallas_call(
         mine_kernel,
         out_shape=[block(FIRST, span, jnp.float32), block(NC, span)],
-        in_specs=[vmem] * 7,
+        in_specs=[vmem] * 6,
         out_specs=[vmem] * 2,
         compiler_params=params(24),
         cost_estimate=cost(10**10, 100 * 10**6),
         name="mine",
-    )(fast_first, slow_first, wt_fast, wt_slow, low, high, far)
-    far = permuted(far, [(i, (i + (5 if i % 2 else -5)) % devices) for i in range(devices)])
+    )(slow_first, wt_slow, inner, low, high, far)
     mine, wt_other, send_rest, other_rest = lax.optimization_barrier(
         (mine, wt_other, send_rest, other_rest)
     )
     arrived_rest = permuted(send_rest, inward)
     other_rest = permuted(other_rest, inward)
-    m0, m4 = pl.pallas_call(
+    relay, direct = pl.pallas_call(
         join_first_kernel,
         out_shape=[block(NC, span)] * 2,
         in_specs=[vmem] * 3,
@@ -551,38 +581,60 @@
         cost_estimate=cost(3 * 10**9, 10**7),
         name="join_first",
     )(other_first, wt_other, mine)
-    m0 = permuted(m0, shifted(-4))
-    m4 = permuted(m4, shifted(4))
-    m1, m3, own = pl.pallas_call(
+    along_x = [(i, i ^ 2) for i in range(devices)]
+    x_sign = [1 if i // 2 % 2 else -1 for i in range(devices)]
+    relay = permuted(relay, along_x)
+    direct = permuted(direct, [(i, (i + 4 * x_sign[i]) % devices) for i in range(devices)])
+    merge, pair, own = pl.pallas_call(
         join_rest_kernel,
-        out_shape=[block(NC, span)] * 2 + [block(NC, span, jnp.float32)],
+        out_shape=[block(NC, span, jnp.float32), block(NC, span), block(NC, span, jnp.float32)],
         in_specs=[vmem] * 7,
         out_specs=[vmem] * 3,
         compiler_params=params(30),
         cost_estimate=cost(40 * 10**9, 200 * 10**6),
         name="join_rest",
     )(fast_rest, slow_rest, other_rest, wt_fast, wt_slow, wt_other, arrived_rest)
-    m1 = permuted(m1, shifted(-2))
-    m3 = permuted(m3, shifted(2))
-
-    def row_block(blocks):
-        return pl.BlockSpec((1, BS, blocks * BS), lambda j: (j, 0, 0))
-
-    def summed(kernel, name, *terms):
-        return pl.pallas_call(
-            kernel,
-            grid=(NC,),
-            out_shape=block(NC, BAND * BS, jnp.float32),
-            in_specs=[smem] + [row_block(term.shape[2] // BS) for term in terms],
-            out_specs=row_block(BAND),
-            scratch_shapes=[pltpu.VMEM((2, BS, FRAME * BS), jnp.float32)],
-            compiler_params=params(20),
-            cost_estimate=cost(10**7, 10**7),
-            name=name,
-        )(core, *terms)
-
-    early = summed(early_kernel, "early", own, m0, m4, far)
-    return summed(total_kernel, "total", early, m1, m3)
+    relay, direct, pair, far = lax.optimization_barrier((relay, direct, pair, far))
+    merged = pl.pallas_call(
+        merge_kernel,
+        out_shape=block(NC, MERGED * BS),
+        in_specs=[smem, vmem, vmem],
+        out_specs=vmem,
+        scratch_shapes=[pltpu.VMEM((BS, MERGED * BS), jnp.float32)],
+        compiler_params=params(16),
+        cost_estimate=cost(10**7, 10**7),
+        name="merge",
+    )(core, merge, relay)
+    merged = permuted(merged, [(i, (i - 4 * x_sign[i]) % devices) for i in range(devices)])
+    pair = permuted(pair, along_x)
+    far = permuted(far, [(i, (i + (5 if i % 2 else -5)) % devices) for i in range(devices)])
+
+    total = block(NC, BAND * BS, jnp.float32)
+    frame = pltpu.VMEM((BS, FRAME * BS), jnp.float32)
+    early = pl.pallas_call(
+        early_kernel,
+        out_shape=total,
+        in_specs=[smem, vmem, vmem],
+        out_specs=vmem,
+        scratch_shapes=[frame],
+        compiler_params=params(16),
+        cost_estimate=cost(10**7, 10**7),
+        name="early",
+    )(core, own, direct)
+    return pl.pallas_call(
+        total_kernel,
+        out_shape=total,
+        in_specs=[smem] + [vmem] * 4,
+        out_specs=hbm,
+        scratch_shapes=[
+            frame,
+            pltpu.VMEM(total.shape, jnp.float32),
+            pltpu.SemaphoreType.DMA((NC,)),
+        ],
+        compiler_params=params(20),
+        cost_estimate=cost(10**7, 10**7),
+        name="total",
+    )(core, early, pair, merged, far)
 
 
 def solution(mesh):

time: 157 us -> 155 us (0.987); the launches traced: 157 us -> 152 us
  waiting for transfers between devices: 67.4 us -> 58.1 us
  Pallas kernels: 68.3 us -> 71.3 us
    ppermute x15, waiting for transfers between devices: 67.4 us -> 58.1 us  [permuted(): return lax.ppermute(block, 'dom', pairs)]
    pallas_call x1, Pallas kernels: 35.2 us -> 37.7 us  [body(): pl.pallas_call(fast_kernel, out_shape=outs, in_specs=[smem] * 4 + [hbm, h...]
    pallas_call x1, Pallas kernels: 7.04 us -> 4.77 us  [body(): pl.pallas_call(mine_kernel, out_shape=[block(FIRST, span, jnp.float32), b...]
    pallas_call x3 -> x4, Pallas kernels: 13.6 us -> 14.8 us  [the longest x1 8.11 us: body(): pl.pallas_call(join_rest_kernel, out_shape=[block(NC, span, jnp.float32),...]
  transfers between devices with their start and end apart: 15 -> 15, of which waited for: 5 -> 8; matrix products, arithmetic and copies ran while one was open for 2% -> 2% of each run, Pallas kernels for 39% -> 41%
where the time goes in v5:
time: 155 us; the launch traced here: 152 us
  Pallas kernels  71.3 us (46%)
  waiting for transfers between devices  58.1 us (37%)
  starting transfers between devices  14.5 us (9%)
  local copies, waits for them, and re-layouts  4.28 us (3%)
  other arithmetic  3.12 us (2%)
    ppermute x15, waiting for transfers between devices, permuted(): return lax.ppermute(block, 'dom', pairs)  58.1 us
    pallas_call x1, Pallas kernels, body(): pl.pallas_call(fast_kernel, out_shape=outs, in_specs=[smem] * 4 + [hbm, h...  37.7 us
    ppermute x15, starting transfers between devices, permuted(): return lax.ppermute(block, 'dom', pairs)  14.5 us
    pallas_call x1, Pallas kernels, body(): pl.pallas_call(join_rest_kernel, out_shape=[block(NC, span, jnp.float32),...  8.11 us
    pallas_call x2, Pallas kernels, picked(): pl.pallas_call(functools.partial(pick_kernel, outer=outer), out_shape=jax...  6.83 us
    pallas_call x1, Pallas kernels, body(): pl.pallas_call(mine_kernel, out_shape=[block(FIRST, span, jnp.float32), b...  4.77 us
    pallas_call x1, Pallas kernels, body(): pl.pallas_call(slow_kernel, out_shape=block(WCOLS, AW), in_specs=[smem] *...  4.2 us
    pallas_call x1, Pallas kernels, body(): pl.pallas_call(total_kernel, out_shape=total, in_specs=[smem] + [vmem] *...  3.69 us
  transfers between devices with their start and end apart: 15, of which 8 were waited for; matrix products, arithmetic and copies ran while one was open for 2% of the time, Pallas kernels for 41%

profile of v5, /device:TPU:0, one launch (start us, length us, event | category | flops | bytes accessed | tf_op | source)
XLA Modules:
  0.0 151.7 jit_solution(10741840480507494170)
XLA Ops:
  0.0 0.7 slice_bitcast_fusion
  0.7 0.5 collective-permute-start
  1.2 0.6 pad_add_fusion.core
  1.9 3.5 %pick_outer.1 = bf16[8,64,1728]{2,1,0:T(8,128)(2,1)} custom-call(s32[2]{0:T(128)} %pad_add_fusion.core, bf16[24,64,1728]{2,1,0:T(8,128)(2,1)} %source.3), custom_call_target="tpu_custom_call" | custom-call | tf_op jit(solution)/shard_map/pick_outer/pallas_call | solution.py:450
  5.4 0.0 copy-start.8
  5.4 0.0 copy-start.9
  5.4 6.7 %collective-permute-start.3 = (bf16[8,64,1728]{2,1,0:T(8,128)(2,1)}, bf16[8,64,1728]{2,1,0:T(8,128)(2,1)S(1)}, u32[]{:S(2)}, u32[]{:S(2)}) collective-permute-start(bf16[8,64,1728]{2,1,0:T(8,128)(2,1)} %pick_outer.1), channel_id=1, source_target_pairs={{0,31},{1,2},{2,1},{3,4},{4,3},{5,6},{6,5},{7,8},{8,7},{9,10},{10,... | collective-permute-start | bytes 5308424 | tf_op jit(solution)/shard_map/ppermute | solution.py:416
  12.0 3.4 %pick_inner.1 = bf16[8,64,1728]{2,1,0:T(8,128)(2,1)} custom-call(s32[2]{0:T(128)} %pad_add_fusion.core, bf16[24,64,1728]{2,1,0:T(8,128)(2,1)} %source.3), custom_call_target="tpu_custom_call" | custom-call | tf_op jit(solution)/shard_map/pick_inner/pallas_call | solution.py:450
  15.4 0.1 collective-permute-start.1
  15.5 0.1 fusion.1
  15.6 0.1 copy.15
  15.7 0.1 select_reduce_fusion.3
  15.8 0.2 select_reduce_fusion
  16.0 0.6 broadcast_add_fusion.inv_a
  16.6 0.6 broadcast_add_fusion.1.inv_own
  17.2 0.1 copy.16
  17.3 0.1 select_reduce_fusion.2
  17.5 0.6 broadcast_add_fusion.3.inv_fast
  18.1 1.5 %collective-permute-done.1.p_fast = bf16[8,64,1728]{2,1,0:T(8,128)(2,1)} collective-permute-done((bf16[8,64,1728]{2,1,0:T(8,128)(2,1)}, bf16[8,64,1728]{2,1,0:T(8,128)(2,1)}, u32[]{:S(2)}, u32[]{:S(2)}) %collective-permute-start.1) | collective-permute-done | bytes 1769504 | tf_op jit(solution)/shard_map/ppermute | solution.py:416
  19.6 37.7 %fast.1 = (bf16[3,64,2432]{2,1,0:T(8,128)(2,1)}, bf16[3,64,2432]{2,1,0:T(8,128)(2,1)}, bf16[9,64,2432]{2,1,0:T(8,128)(2,1)}, bf16[3,64,2432]{2,1,0:T(8,128)(2,1)...) custom-call(s32[2]{0:T(128)} %pad_add_fusion.core, ...), custom_call_target="tpu_custom_call" | custom-call | flops 20000000000 | bytes 30000000 | tf_op jit(solution)/shard_map/fast/pallas_call | solution.py:512
  57.3 0.2 collective-permute-start.4
  57.5 0.4 collective-permute-start.5
  57.9 0.3 collective-permute-start.2
  58.2 6.3 %collective-permute-done.2 = s32[8,27]{1,0:T(8,128)S(1)} collective-permute-done((s32[8,27]{1,0:T(8,128)S(1)}, s32[8,27]{1,0:T(8,128)S(1)}, u32[]{:S(2)}, u32[]{:S(2)}) %collective-permute-start.2) | collective-permute-done | bytes 896 | tf_op jit(solution)/shard_map/ppermute | solution.py:416
  64.5 0.1 copy.17
  64.6 0.1 select_reduce_fusion.1
  64.8 2.2 %copy-done.3 = f32[33,64,512]{2,1,0:T(8,128)S(1)} copy-done((f32[33,64,512]{2,1,0:T(8,128)S(1)}, f32[33,64,512]{2,1,0:T(8,128)}, u32[]{:S(2)}) %copy-start.3) | copy-done | bytes 4325400
  67.0 1.0 copy-done.7
  68.1 4.2 %slow.1.wt_slow = bf16[40,64,512]{2,1,0:T(8,128)(2,1)S(1)} custom-call(s32[2]{0:T(128)S(1)} %copy-done, s32[8,33]{1,0:T(8,128)S(1)} %broadcast_add_fusion.2.inv_slow, bf16[8,64,1728]{2,1,0:T(8,128)(2,1)S(1)} %collective-permute-done.3.p_slow, bf16[8,64,512]{2,1,0:T(8,128)(2,1)S(1)} %copy-done.7, f32[33,64,512]{2,1,0:T(8,128)S(1)} %copy-done.3), custom_call_target="tpu_custom_call" | custom-call | flops 20000000000 | bytes 200000000 | tf_op jit(solution)/shard_map/slow/pallas_call | solution.py:545
  72.3 0.1 collective-permute-start.7
  72.4 4.8 %mine.1 = (f32[6,64,2432]{2,1,0:T(8,128)S(1)}, bf16[3,64,2432]{2,1,0:T(8,128)(2,1)S(1)}) custom-call(bf16[9,64,512]{2,1,0:T(8,128)(2,1)S(1)} %copy-done.4, bf16[40,64,512]{2,1,0:T(8,128)(2,1)S(1)} %slow.1.wt_slow, bf16[6,64,2432]{2,1,0:T(8,128)(2,1)S(1)} %copy-done.1, bf16[3,64,2432]{2,1,0:T(8,128)(2,1)S(1)} %collective-permute-done.4.low, ...), custom_call_target="tpu_custom_call" | custom-call | flops 10000000000 | bytes 100000000 | tf_op jit(solution)/shard_map/mine/pallas_call | solution.py:561
  77.2 0.1 collective-permute-done.7.wt_other
  77.3 0.6 collective-permute-start.9
  77.9 0.1 collective-permute-start.8
  77.9 3.0 %join_first.1 = (bf16[3,64,2432]{2,1,0:T(8,128)(2,1)S(1)}, bf16[3,64,2432]{2,1,0:T(8,128)(2,1)S(1)}) custom-call(bf16[6,64,512]{2,1,0:T(8,128)(2,1)S(1)} %collective-permute-done.6.other, bf16[40,64,512]{2,1,0:T(8,128)(2,1)S(1)} %collective-permute-done.7.wt_other, f32[6,64,2432]{2,1,0:T(8,128)S(1)} %get-tuple-element.65.mine), custom_call_target="tpu_custom_call" | custom-call | flops 3000000000 | bytes 10000000 | tf_op jit(solution)/shard_map/join_first/pallas_call | solution.py:575
  80.9 0.1 collective-permute-start.10
  81.0 1.1 collective-permute-start.11
  82.1 1.4 collective-permute-done.8.other
  83.5 8.1 %join_rest.1 = (f32[3,64,2432]{2,1,0:T(8,128)S(1)}, bf16[3,64,2432]{2,1,0:T(8,128)(2,1)S(1)}, f32[3,64,2432]{2,1,0:T(8,128)S(1)}) custom-call(bf16[9,64,1024]{2,1,0:T(8,128)(2,1)S(1)} %copy-done.5, bf16[9,64,512]{2,1,0:T(8,128)(2,1)S(1)} %copy-done.6, bf16[9,64,512]{2,1,0:T(8,128)(2,1)S(1)} %collective-permute-done.8.other, ...), custom_call_target="tpu_custom_call" | custom-call | flops 40000000000 | bytes 200000000 | tf_op jit(solution)/shard_map/join_rest/pallas_call | solution.py:588
  91.6 12.3 %collective-permute-done.10.relay = bf16[3,64,2432]{2,1,0:T(8,128)(2,1)S(1)} collective-permute-done((bf16[3,64,2432]{2,1,0:T(8,128)(2,1)S(1)}, bf16[3,64,2432]{2,1,0:T(8,128)(2,1)S(1)}, u32[]{:S(2)}, u32[]{:S(2)}) %collective-permute-start.10) | collective-permute-done | bytes 933920 | tf_op jit(solution)/shard_map/ppermute | solution.py:416
  103.9 0.1 collective-permute-done.11.direct
  104.0 1.1 merge.1
  105.1 0.1 collective-permute-start.13
  105.2 4.4 %collective-permute-start.12 = (bf16[3,64,2432]{2,1,0:T(8,128)(2,1)S(1)}, bf16[3,64,2432]{2,1,0:T(8,128)(2,1)S(1)}, u32[]{:S(2)}, u32[]{:S(2)}) collective-permute-start(bf16[3,64,2432]{2,1,0:T(8,128)(2,1)S(1)} %get-tuple-element.71), channel_id=1, source_target_pairs={{0,2},{1,3},{2,0},{3,1},{4,6},{5,7},{6,4},{7,5},{8,10},{9,11},{10,... | collective-permute-start | bytes 2801672 | tf_op jit(solution)/shard_map/ppermute | solution.py:416
  109.6 1.9 %early.1 = f32[3,64,4032]{2,1,0:T(8,128)S(1)} custom-call(s32[2]{0:T(128)S(1)} %copy-done, f32[3,64,2432]{2,1,0:T(8,128)S(1)} %get-tuple-element.63.own, bf16[3,64,2432]{2,1,0:T(8,128)(2,1)S(1)} %collective-permute-done.11.direct), custom_call_target="tpu_custom_call" | custom-call | flops 10000000 | bytes 10000000 | tf_op jit(solution)/shard_map/early/pallas_call | solution.py:614
  111.6 29.1 %collective-permute-done.12.pair = bf16[3,64,2432]{2,1,0:T(8,128)(2,1)S(1)} collective-permute-done((bf16[3,64,2432]{2,1,0:T(8,128)(2,1)S(1)}, bf16[3,64,2432]{2,1,0:T(8,128)(2,1)S(1)}, u32[]{:S(2)}, u32[]{:S(2)}) %collective-permute-start.12) | collective-permute-done | bytes 933920 | tf_op jit(solution)/shard_map/ppermute | solution.py:416
  140.7 7.3 %collective-permute-done.14.far = bf16[3,64,2432]{2,1,0:T(8,128)(2,1)S(1)} collective-permute-done((bf16[3,64,2432]{2,1,0:T(8,128)(2,1)S(1)}, bf16[3,64,2432]{2,1,0:T(8,128)(2,1)S(1)}, u32[]{:S(2)}, u32[]{:S(2)}) %collective-permute-start.14) | collective-permute-done | bytes 933920 | tf_op jit(solution)/shard_map/ppermute | solution.py:416
  148.0 3.7 %total.1 = f32[3,64,4032]{2,1,0:T(8,128)} custom-call(s32[2]{0:T(128)S(1)} %copy-done, f32[3,64,4032]{2,1,0:T(8,128)S(1)} %early.1, bf16[3,64,2432]{2,1,0:T(8,128)(2,1)S(1)} %collective-permute-done.12.pair, bf16[3,64,2816]{2,1,0:T(8,128)(2,1)S(1)} %collective-permute-done.13.merged, bf16[3,64,2432]{2,1,0:T(8,128)(2,1)S(1)} %collective-permute-done.14.far), custom_call_target="tpu_custom_call" | custom-call | flops 10000000 | bytes 10000000 | tf_op jit(solution)/shard_map/total/pallas_call | solution.py:624
  (43 shorter events, 0.2 us)
Async XLA Ops:
  0.7 16.5 %collective-permute-start = (s32[8,27]{1,0:T(8,128)S(1)}, s32[8,27]{1,0:T(8,128)S(1)}, u32[]{:S(2)}, u32[]{:S(2)}) collective-permute-start(s32[8,27]{1,0:T(8,128)S(1)} %get-tuple-element.78), channel_id=1, source_target_pairs={{0,1},{1,0},{2,3},{3,2},{4,5},{5,4},{6,7},{7,6},{8,9},{9,8},{10,11... | collective-permute-start | bytes 2600 | tf_op jit(solution)/shard_map/ppermute | solution.py:416
  5.4 10.2 %copy-start.8 = (s32[24,27]{1,0:T(8,128)S(1)}, s32[24,27]{1,0:T(8,128)}, u32[]{:S(2)}) copy-start(s32[24,27]{1,0:T(8,128)} %param.7) | copy-start | bytes 7780
  5.4 10.3 %copy-start.9 = (s32[24,7]{0,1:T(8,128)S(1)}, s32[24,7]{0,1:T(8,128)}, u32[]{:S(2)}) copy-start(s32[24,7]{0,1:T(8,128)} %param.6) | copy-start | bytes 2020
  5.4 59.4 %collective-permute-start.3 = (bf16[8,64,1728]{2,1,0:T(8,128)(2,1)}, bf16[8,64,1728]{2,1,0:T(8,128)(2,1)S(1)}, u32[]{:S(2)}, u32[]{:S(2)}) collective-permute-start(bf16[8,64,1728]{2,1,0:T(8,128)(2,1)} %pick_outer.1), channel_id=1, source_target_pairs={{0,31},{1,2},{2,1},{3,4},{4,3},{5,6},{6,5},{7,8},{8,7},{9,10},{10,... | collective-permute-start | bytes 5308424 | tf_op jit(solution)/shard_map/ppermute | solution.py:416
  15.4 4.2 %collective-permute-start.1 = (bf16[8,64,1728]{2,1,0:T(8,128)(2,1)}, bf16[8,64,1728]{2,1,0:T(8,128)(2,1)}, u32[]{:S(2)}, u32[]{:S(2)}) collective-permute-start(bf16[8,64,1728]{2,1,0:T(8,128)(2,1)} %pick_inner.1), channel_id=1, source_target_pairs={{0,1},{1,0},{2,3},{3,2},{4,5},{5,4},{6,7},{7,6},{8,9},{9,8},{10,11... | collective-permute-start | bytes 5308424 | tf_op jit(solution)/shard_map/ppermute | solution.py:416
  18.1 46.8 %copy-start = (s32[2]{0:T(128)S(1)}, s32[2]{0:T(128)}, u32[]{:S(2)}) copy-start(s32[2]{0:T(128)} %pad_add_fusion.core) | copy-start | bytes 28
  57.3 7.5 %collective-permute-start.4 = (bf16[3,64,2432]{2,1,0:T(8,128)(2,1)}, bf16[3,64,2432]{2,1,0:T(8,128)(2,1)S(1)}, u32[]{:S(2)}, u32[]{:S(2)}) collective-permute-start(bf16[3,64,2432]{2,1,0:T(8,128)(2,1)} %get-tuple-element.43), channel_id=1, source_target_pairs={{0,1},{1,0},{2,3},{3,2},{4,5},{5,4},{6,7},{7,6},{8,9},{9,8},{10,11... | collective-permute-start | bytes 2801672 | tf_op jit(solution)/shard_map/ppermute | solution.py:416
  57.5 7.3 %collective-permute-start.5 = (bf16[3,64,2432]{2,1,0:T(8,128)(2,1)}, bf16[3,64,2432]{2,1,0:T(8,128)(2,1)}, u32[]{:S(2)}, u32[]{:S(2)}) collective-permute-start(bf16[3,64,2432]{2,1,0:T(8,128)(2,1)} %get-tuple-element.44), channel_id=1, source_target_pairs={{0,1},{1,0},{2,3},{3,2},{4,5},{5,4},{6,7},{7,6},{8,9},{9,8},{10,11... | collective-permute-start | bytes 2801672 | tf_op jit(solution)/shard_map/ppermute | solution.py:416
  57.9 6.6 %collective-permute-start.2 = (s32[8,27]{1,0:T(8,128)S(1)}, s32[8,27]{1,0:T(8,128)S(1)}, u32[]{:S(2)}, u32[]{:S(2)}) collective-permute-start(s32[8,27]{1,0:T(8,128)S(1)} %get-tuple-element.77), channel_id=1, source_target_pairs={{0,31},{1,2},{2,1},{3,4},{4,3},{5,6},{6,5},{7,8},{8,7},{9,10},{10,... | collective-permute-start | bytes 2600 | tf_op jit(solution)/shard_map/ppermute | solution.py:416
  58.2 6.6 %collective-permute-start.6 = (bf16[6,64,512]{2,1,0:T(8,128)(2,1)}, bf16[6,64,512]{2,1,0:T(8,128)(2,1)S(1)}, u32[]{:S(2)}, u32[]{:S(2)}) collective-permute-start(bf16[6,64,512]{2,1,0:T(8,128)(2,1)} %get-tuple-element.45), channel_id=1, source_target_pairs={{0,1},{1,0},{2,3},{3,2},{4,5},{5,4},{6,7},{7,6},{8,9},{9,8},{10,11... | collective-permute-start | bytes 1179656 | tf_op jit(solution)/shard_map/ppermute | solution.py:416
  64.8 2.2 %copy-start.3 = (f32[33,64,512]{2,1,0:T(8,128)S(1)}, f32[33,64,512]{2,1,0:T(8,128)}, u32[]{:S(2)}) copy-start(f32[33,64,512]{2,1,0:T(8,128)} %get-tuple-element.48.rest) | copy-start | bytes 12976132
  67.0 1.0 copy-start.7
  68.1 4.3 %copy-start.1 = (bf16[6,64,2432]{2,1,0:T(8,128)(2,1)S(1)}, bf16[6,64,2432]{2,1,0:T(8,128)(2,1)}, u32[]{:S(2)}) copy-start(bf16[6,64,2432]{2,1,0:T(8,128)(2,1)} %get-tuple-element.52.inner) | copy-start | bytes 5603332
  68.1 4.3 %copy-start.2 = (bf16[3,64,2432]{2,1,0:T(8,128)(2,1)S(1)}, bf16[3,64,2432]{2,1,0:T(8,128)(2,1)}, u32[]{:S(2)}) copy-start(bf16[3,64,2432]{2,1,0:T(8,128)(2,1)} %get-tuple-element.55.far_fast) | copy-start | bytes 2801668
  68.1 4.3 %copy-start.4 = (bf16[9,64,512]{2,1,0:T(8,128)(2,1)S(1)}, bf16[9,64,512]{2,1,0:T(8,128)(2,1)}, u32[]{:S(2)}) copy-start(bf16[9,64,512]{2,1,0:T(8,128)(2,1)} %get-tuple-element.42.slow) | copy-start | bytes 1769476
  72.3 5.0 %collective-permute-start.7 = (bf16[40,64,512]{2,1,0:T(8,128)(2,1)S(1)}, bf16[40,64,512]{2,1,0:T(8,128)(2,1)S(1)}, u32[]{:S(2)}, u32[]{:S(2)}) collective-permute-start(bf16[40,64,512]{2,1,0:T(8,128)(2,1)S(1)} %slow.1.wt_slow), channel_id=1, source_target_pairs={{0,1},{1,0},{2,3},{3,2},{4,5},{5,4},{6,7},{7,6},{8,9},{9,8},{10,11... | collective-permute-start | bytes 7864328 | tf_op jit(solution)/shard_map/ppermute | solution.py:416
  72.4 4.9 %copy-start.10 = (bf16[9,64,2432]{2,1,0:T(8,128)(2,1)S(1)}, bf16[9,64,2432]{2,1,0:T(8,128)(2,1)}, u32[]{:S(2)}) copy-start(bf16[9,64,2432]{2,1,0:T(8,128)(2,1)} %get-tuple-element.62) | copy-start | bytes 8404996
  72.4 5.4 %copy-start.11 = (bf16[9,64,512]{2,1,0:T(8,128)(2,1)S(1)}, bf16[9,64,512]{2,1,0:T(8,128)(2,1)}, u32[]{:S(2)}) copy-start(bf16[9,64,512]{2,1,0:T(8,128)(2,1)} %get-tuple-element.59) | copy-start | bytes 1769476
  77.3 6.2 %slice-start = ((s8[5242880]{0:T(1024)(128)(4,1)}), s8[4194304]{0:T(1024)(128)(4,1)S(1)}, s32[]{:S(2)}) async-start(s8[5242880]{0:T(1024)(128)(4,1)} %bitcast.10), calls=%async_computation | async-start | bytes 8388608
  77.3 6.2 %slice-start.1 = ((s8[5242880]{0:T(1024)(128)(4,1)}), s8[1048576]{0:T(1024)(128)(4,1)S(1)}, s32[]{:S(2)}) async-start(s8[5242880]{0:T(1024)(128)(4,1)} %bitcast.10), calls=%async_computation.1 | async-start | bytes 2097152
  77.3 6.2 %copy-start.5 = (bf16[9,64,1024]{2,1,0:T(8,128)(2,1)S(1)}, bf16[9,64,1024]{2,1,0:T(8,128)(2,1)}, u32[]{:S(2)}) copy-start(bf16[9,64,1024]{2,1,0:T(8,128)(2,1)} %get-tuple-element.40.fast) | copy-start | bytes 3538948
  77.3 6.2 %copy-start.6 = (bf16[9,64,512]{2,1,0:T(8,128)(2,1)S(1)}, bf16[9,64,512]{2,1,0:T(8,128)(2,1)}, u32[]{:S(2)}) copy-start(bf16[9,64,512]{2,1,0:T(8,128)(2,1)} %get-tuple-element.41.slow) | copy-start | bytes 1769476
  77.3 6.2 %collective-permute-start.9 = (bf16[9,64,2432]{2,1,0:T(8,128)(2,1)S(1)}, bf16[9,64,2432]{2,1,0:T(8,128)(2,1)S(1)}, u32[]{:S(2)}, u32[]{:S(2)}) collective-permute-start(bf16[9,64,2432]{2,1,0:T(8,128)(2,1)S(1)} %copy-done.10), channel_id=1, source_target_pairs={{0,1},{1,0},{2,3},{3,2},{4,5},{5,4},{6,7},{7,6},{8,9},{9,8},{10,11... | collective-permute-start | bytes 8405000 | tf_op jit(solution)/shard_map/ppermute | solution.py:416
  77.9 5.6 %collective-permute-start.8 = (bf16[9,64,512]{2,1,0:T(8,128)(2,1)S(1)}, bf16[9,64,512]{2,1,0:T(8,128)(2,1)S(1)}, u32[]{:S(2)}, u32[]{:S(2)}) collective-permute-start(bf16[9,64,512]{2,1,0:T(8,128)(2,1)S(1)} %copy-done.11), channel_id=1, source_target_pairs={{0,1},{1,0},{2,3},{3,2},{4,5},{5,4},{6,7},{7,6},{8,9},{9,8},{10,11... | collective-permute-start | bytes 1769480 | tf_op jit(solution)/shard_map/ppermute | solution.py:416
  80.9 23.0 %collective-permute-start.10 = (bf16[3,64,2432]{2,1,0:T(8,128)(2,1)S(1)}, bf16[3,64,2432]{2,1,0:T(8,128)(2,1)S(1)}, u32[]{:S(2)}, u32[]{:S(2)}) collective-permute-start(bf16[3,64,2432]{2,1,0:T(8,128)(2,1)S(1)} %get-tuple-element.66), channel_id=1, source_target_pairs={{0,2},{1,3},{2,0},{3,1},{4,6},{5,7},{6,4},{7,5},{8,10},{9,11},{10,... | collective-permute-start | bytes 2801672 | tf_op jit(solution)/shard_map/ppermute | solution.py:416
  81.0 23.0 %collective-permute-start.11 = (bf16[3,64,2432]{2,1,0:T(8,128)(2,1)S(1)}, bf16[3,64,2432]{2,1,0:T(8,128)(2,1)S(1)}, u32[]{:S(2)}, u32[]{:S(2)}) collective-permute-start(bf16[3,64,2432]{2,1,0:T(8,128)(2,1)S(1)} %get-tuple-element.67), channel_id=1, source_target_pairs={{0,28},{1,29},{2,6},{3,7},{4,0},{5,1},{6,10},{7,11},{8,4},{9,5},{1... | collective-permute-start | bytes 2801672 | tf_op jit(solution)/shard_map/ppermute | solution.py:416
  105.1 42.8 %collective-permute-start.13 = (bf16[3,64,2816]{2,1,0:T(8,128)(2,1)S(1)}, bf16[3,64,2816]{2,1,0:T(8,128)(2,1)S(1)}, u32[]{:S(2)}, u32[]{:S(2)}) collective-permute-start(bf16[3,64,2816]{2,1,0:T(8,128)(2,1)S(1)} %merge.1), channel_id=1, source_target_pairs={{0,4},{1,5},{2,30},{3,31},{4,8},{5,9},{6,2},{7,3},{8,12},{9,13},{1... | collective-permute-start | bytes 3244040 | tf_op jit(solution)/shard_map/ppermute | solution.py:416
  105.2 35.5 %collective-permute-start.12 = (bf16[3,64,2432]{2,1,0:T(8,128)(2,1)S(1)}, bf16[3,64,2432]{2,1,0:T(8,128)(2,1)S(1)}, u32[]{:S(2)}, u32[]{:S(2)}) collective-permute-start(bf16[3,64,2432]{2,1,0:T(8,128)(2,1)S(1)} %get-tuple-element.71), channel_id=1, source_target_pairs={{0,2},{1,3},{2,0},{3,1},{4,6},{5,7},{6,4},{7,5},{8,10},{9,11},{10,... | collective-permute-start | bytes 2801672 | tf_op jit(solution)/shard_map/ppermute | solution.py:416
  109.6 38.3 %collective-permute-start.14 = (bf16[3,64,2432]{2,1,0:T(8,128)(2,1)S(1)}, bf16[3,64,2432]{2,1,0:T(8,128)(2,1)S(1)}, u32[]{:S(2)}, u32[]{:S(2)}) collective-permute-start(bf16[3,64,2432]{2,1,0:T(8,128)(2,1)S(1)} %get-tuple-element.74), channel_id=1, source_target_pairs={{0,27},{1,6},{2,29},{3,8},{4,31},{5,10},{6,1},{7,12},{8,3},{9,14},... | collective-permute-start | bytes 2801672 | tf_op jit(solution)/shard_map/ppermute | solution.py:416

commit v6 on v5

--- a/solution.py
+++ b/solution.py
@@ -46,11 +46,14 @@
     return lax.broadcasted_iota(jnp.int32, (BS, 2 * BS), 1) < BS
 
 
-def transpose_quad(block, turned, width):
+def transpose_quad(unit, block, turned, width):
     for start in range(0, width, LANES):
         size = min(LANES, width - start)
         part = lax.dot_general(
-            eye(size), block[:, start : start + size], NT, preferred_element_type=jnp.float32
+            unit[:size, :size],
+            block[:, start : start + size],
+            NT,
+            preferred_element_type=jnp.float32,
         )
         turned[start // BS : (start + size) // BS] = part.astype(jnp.bfloat16).reshape(
             size // BS, BS, LANES
@@ -81,9 +84,9 @@
     a_own,
     send_low,
     send_high,
-    send_rest,
     far,
     inner,
+    send_rest,
     fast_rest,
     slow_first,
     slow_rest,
@@ -95,12 +98,11 @@
     p_buf,
     ext,
     at,
+    unit,
     turned_p,
     turned_a,
     lhs,
-    send_buf,
-    far_buf,
-    inner_buf,
+    rows_buf,
     fast_buf,
     slow_buf,
     other_buf,
@@ -124,13 +126,14 @@
     for quad in range(own_quads + halo_quads):
         load(quad).start()
 
+    unit[...] = eye(LANES)
     turned_p[KP] = jnp.zeros((BS, LANES), jnp.bfloat16)
     turned_a[KA] = jnp.zeros((BS, LANES), jnp.bfloat16)
 
     @pl.loop(0, own_quads)
     def _(quad):
         block = a_own[pl.ds(quad * QUAD, QUAD)].reshape(LANES, KA * BS)
-        transpose_quad(block, turned_a, KA * BS)
+        transpose_quad(unit, block, turned_a, KA * BS)
         agg = quad // halo_quads
 
         def store(slot, pair, value):
@@ -145,7 +148,7 @@
 
     def band_quad(source_row, index, index_row, first_lane):
         block = p_buf[pl.ds(source_row, QUAD)].reshape(LANES, KP * BS)
-        transpose_quad(block, turned_p, KP * BS)
+        transpose_quad(unit, block, turned_p, KP * BS)
 
         def store(slot, pair, value):
             lane = pl.multiple_of(first_lane + pair * 2 * BS, 2 * BS)
@@ -173,14 +176,15 @@
             row = NC * place + j
             mine, other = 6 * i + 3 + j + 1, 6 * i + 6 * (1 - s) + j + 1
             if place < 2:
-                lhs[ROWS + NC + row] = ext[mine, :, fast_lanes]
+                lhs[row] = ext[other, :, fast_lanes]
+                lhs[FIRST + NC + row] = ext[mine, :, fast_lanes]
             else:
+                lhs[ROWS + row - FIRST] = ext[other, :, fast_lanes]
                 fast_buf[row - FIRST] = ext[mine, :, fast_lanes]
             slow_buf[row if place < 2 else row + NC] = ext[mine, :, slow_lanes]
             other_buf[row] = ext[other, :, slow_lanes]
-            lhs[row] = ext[other, :, fast_lanes]
     for j in range(NC):
-        lhs[ROWS + j] = ext[30 * s + j + 1, :, fast_lanes]
+        lhs[FIRST + j] = ext[30 * s + j + 1, :, fast_lanes]
         slow_buf[FIRST + j] = ext[30 * s + j + 1, :, slow_lanes]
     copies = [halo_copy]
 
@@ -232,20 +236,32 @@
 
     def emit(tile, width):
         right = wt_buf[pl.ds(QUAD * tile, width // BS)].reshape(width, 2 * AW)
-        left = lhs[...].reshape((ROWS + NC + FIRST) * BS, 2 * AW)
+        left = lhs[...].reshape((ROWS + REST) * BS, 2 * AW)
         value = lax.dot_general(left, right, NT, preferred_element_type=jnp.float32)
-        value = value.astype(jnp.bfloat16).reshape(ROWS + NC + FIRST, BS, width)
-        lanes = pl.ds(pl.multiple_of(tile * LANES, LANES), width)
-        send_buf[:, :, lanes] = value[:ROWS]
-        far_buf[:, :, lanes] = value[ROWS : ROWS + NC]
-        inner_buf[:, :, lanes] = value[ROWS + NC :]
-
-    each_tile(emit)
-    write(send_buf.at[:NC], send_low)
-    write(send_buf.at[NC:FIRST], send_high)
-    write(send_buf.at[FIRST:], send_rest)
-    write(far_buf, far)
-    write(inner_buf, inner)
+        rows_buf[:, :, tile_lanes(tile, width)] = value.astype(jnp.bfloat16).reshape(
+            ROWS + REST, BS, width
+        )
+
+    parts = (
+        (send_low, 0),
+        (send_high, NC),
+        (far, FIRST),
+        (inner, FIRST + NC),
+        (send_rest, ROWS),
+    )
+    bounds = (0, 4, 8, TILES)
+    for first, last in zip(bounds[:-1], bounds[1:]):
+
+        @pl.loop(first, min(last, TILES - 1))
+        def _(tile):
+            emit(tile, LANES)
+
+        if last == TILES:
+            emit(TILES - 1, LANES // 2)
+        lanes = slice(first * LANES, min(last * LANES, WINDOW * BS))
+        for target, row in parts:
+            rows = slice(row, row + target.shape[0])
+            write(rows_buf.at[rows, :, lanes], target.at[:, :, lanes])
     for copy in copies:
         copy.wait()
 
@@ -282,14 +298,15 @@
     each_tile(step)
 
 
-def slow_kernel(core, inv_slow, p_slow, at_halo, rest, wt, turned_p, ext):
+def slow_kernel(core, inv_slow, p_slow, at_halo, rest, wt, unit, turned_p, ext):
     s = core[0]
+    unit[...] = eye(LANES)
     turned_p[KP] = jnp.zeros((BS, LANES), jnp.bfloat16)
 
     @pl.loop(0, AGG // QUAD)
     def _(quad):
         block = p_slow[pl.ds(quad * QUAD, QUAD)].reshape(LANES, KP * BS)
-        transpose_quad(block, turned_p, KP * BS)
+        transpose_quad(unit, block, turned_p, KP * BS)
 
         def store(slot, pair, value):
             lane = pl.multiple_of(quad * LANES + pair * 2 * BS, 2 * BS)
@@ -336,6 +353,17 @@
     each_tile(step)
 
 
+def stage_kernel(at_halo, rest, at_out, rest_out, sems):
+    copies = [
+        pltpu.make_async_copy(at_halo, at_out, sems.at[0]),
+        pltpu.make_async_copy(rest, rest_out, sems.at[1]),
+    ]
+    for copy in copies:
+        copy.start()
+    for copy in copies:
+        copy.wait()
+
+
 def merge_kernel(core, rows, relay, out, frame):
     x = core[1]
     step = 6 * BS
@@ -364,29 +392,29 @@
         store(frame[:, first - BS : last - BS])
 
 
-def early_kernel(core, own, direct, out, frame):
+def early_kernel(core, own, direct, pair, far, out, frame):
     s, x = core[0], core[1]
     for j in range(NC):
         top = 27 - 3 * s - j
+        far_start = jnp.where(s == 1, 30 - j, -3 - j)
+        messages = [(own, top - 12), (direct, top - 24 * x), (pair, top - 6 - 12 * x)]
+        messages.append((far, far_start))
 
         def store(value, j=j):
             out[j] = value
 
-        in_frame(s, j, frame, [(own, top - 12), (direct, top - 24 * x)], store)
-
-
-def total_kernel(core, early, pair, merged, far, out, frame, buf, sems):
+        in_frame(s, j, frame, messages, store)
+
+
+def total_kernel(core, early, merged, out, frame, buf, sems):
     s, x = core[0], core[1]
     copies = []
     for j in range(NC):
-        top = 27 - 3 * s - j
-        far_start = jnp.where(s == 1, 30 - j, -3 - j)
 
         def store(value, j=j):
             buf[j] = value + early[j]
 
-        messages = [(pair, top - 6 - 12 * x), (merged, top - 24 + 18 * x), (far, far_start)]
-        in_frame(s, j, frame, messages, store)
+        in_frame(s, j, frame, [(merged, 3 - 3 * s - j + 18 * x)], store)
         copy = pltpu.make_async_copy(buf.at[j], out.at[j], sems.at[j])
         copy.start()
         copies.append(copy)
@@ -394,18 +422,15 @@
         copy.wait()
 
 
-def pick_kernel(core, source, out, sems, *, outer):
+def pick_kernel(core, source, outer, inner, sems):
     s = core[0]
-    first = (NB - AGG) * (s if outer else 1 - s)
     step = AGG // 4
-    copies = [
-        pltpu.make_async_copy(
-            source.at[pl.ds(first + k * step, step)],
-            out.at[k * step : (k + 1) * step],
-            sems.at[k],
-        )
-        for k in range(4)
-    ]
+    copies = []
+    for target, side in ((outer, s), (inner, 1 - s)):
+        for k in range(4):
+            rows = pl.ds((NB - AGG) * side + k * step, step)
+            into = target.at[k * step : (k + 1) * step]
+            copies.append(pltpu.make_async_copy(source.at[rows], into, sems.at[len(copies)]))
     for copy in copies:
         copy.start()
     for copy in copies:
@@ -446,21 +471,20 @@
     def cost(flops, size):
         return pl.CostEstimate(flops=flops, bytes_accessed=size, transcendentals=0)
 
-    def picked(outer):
-        return pl.pallas_call(
-            functools.partial(pick_kernel, outer=outer),
-            out_shape=jax.ShapeDtypeStruct((AGG,) + p_blocks.shape[1:], bf16),
-            in_specs=[smem, hbm],
-            out_specs=vmem,
-            scratch_shapes=[pltpu.SemaphoreType.DMA((4,))],
-            compiler_params=params(60),
-            name="pick_outer" if outer else "pick_inner",
-        )(core, p_blocks)
-
+    edge = jax.ShapeDtypeStruct((AGG,) + p_blocks.shape[1:], bf16)
+    outer, inner = pl.pallas_call(
+        pick_kernel,
+        out_shape=[edge, edge],
+        in_specs=[smem, hbm],
+        out_specs=[vmem, vmem],
+        scratch_shapes=[pltpu.SemaphoreType.DMA((8,))],
+        compiler_params=params(60),
+        name="pick",
+    )(core, p_blocks)
     outward = [(i, (i + (1 if i % 2 else -1)) % devices) for i in range(devices)]
     inward = [(i, i ^ 1) for i in range(devices)]
-    p_slow = permuted(picked(True), outward)
-    p_fast = permuted(picked(False), inward)
+    p_slow = permuted(outer, outward)
+    p_fast = permuted(inner, inward)
     edge_cols = jnp.stack([cols_p[:AGG], cols_p[NB - AGG :]])
     cols_slow = permuted(edge_cols[parity], outward)
     cols_fast = permuted(edge_cols[1 - parity], inward)
@@ -474,6 +498,7 @@
     inv_fast = inverse_index(slots(cols_fast, first_agg + fast_place) + fast_place + 1, COLS, KP)
     slow_place = NC * parity - (1 - parity)
     inv_slow = inverse_index(slots(cols_slow, first_agg + slow_place) + 2 * parity, WSLOT, KP)
+    inv_fast, inv_slow = lax.optimization_barrier((inv_fast, inv_slow))
     inv_a = inverse_index((cols_a - first_row - (own_agg - 1) * AGG) % count_rows, 3 * AGG, KA)
 
     def block(rows, width, kind=bf16):
@@ -483,9 +508,9 @@
     outs = [
         block(NC, span),
         block(NC, span),
-        block(REST, span),
         block(NC, span),
         block(FIRST, span),
+        block(REST, span),
         block(REST, 2 * AW),
         block(FIRST + NC, AW),
         block(REST, AW),
@@ -498,9 +523,9 @@
     (
         send_low,
         send_high,
-        send_rest,
         far,
         inner,
+        send_rest,
         fast_rest,
         slow_first,
         slow_rest,
@@ -518,19 +543,18 @@
             pltpu.VMEM((NB + AGG, BS, KP * BS), bf16),
             pltpu.VMEM((COLS, BS, EXT * BS), bf16),
             pltpu.VMEM((NC, 3 * AGG, BS, AW), bf16),
+            pltpu.VMEM((LANES, LANES), bf16),
             pltpu.VMEM((KP + 1, BS, LANES), bf16),
             pltpu.VMEM((KA + 1, BS, LANES), bf16),
-            pltpu.VMEM((ROWS + NC + FIRST, BS, 2 * AW), bf16),
-            pltpu.VMEM((ROWS, BS, span), bf16),
-            pltpu.VMEM((NC, BS, span), bf16),
-            pltpu.VMEM((FIRST, BS, span), bf16),
+            pltpu.VMEM((ROWS + REST, BS, 2 * AW), bf16),
+            pltpu.VMEM((ROWS + REST, BS, span), bf16),
             pltpu.VMEM((REST, BS, 2 * AW), bf16),
             pltpu.VMEM((ROWS + NC, BS, AW), bf16),
             pltpu.VMEM((ROWS, BS, AW), bf16),
             pltpu.VMEM((WCOLS, BS, 2 * AW), bf16),
             pltpu.VMEM((WSLOT, BS, AW), jnp.float32),
             pltpu.SemaphoreType.DMA(((NB + AGG) // QUAD,)),
-            pltpu.SemaphoreType.DMA((len(outs),)),
+            pltpu.SemaphoreType.DMA((len(outs) + 10,)),
         ],
         compiler_params=params(56),
         cost_estimate=cost(20 * 10**9, 30 * 10**6),
@@ -540,6 +564,16 @@
     low = permuted(send_low, inward)
     high = permuted(send_high, inward)
     other_first = permuted(other_first, inward)
+    at_halo, rest = pl.pallas_call(
+        stage_kernel,
+        out_shape=[block(AGG, AW), block(WSLOT, AW, jnp.float32)],
+        in_specs=[hbm] * 2,
+        out_specs=[vmem] * 2,
+        scratch_shapes=[pltpu.SemaphoreType.DMA((2,))],
+        compiler_params=params(8),
+        cost_estimate=cost(10**6, 10**6),
+        name="stage",
+    )(at_halo, rest)
     p_slow, low, high, other_first = lax.optimization_barrier((p_slow, low, high, other_first))
 
     wt_slow = pl.pallas_call(
@@ -548,6 +582,7 @@
         in_specs=[smem] * 2 + [vmem] * 3,
         out_specs=vmem,
         scratch_shapes=[
+            pltpu.VMEM((LANES, LANES), bf16),
             pltpu.VMEM((KP + 1, BS, LANES), bf16),
             pltpu.VMEM((WSLOT, BS, AW), bf16),
         ],
@@ -558,6 +593,7 @@
     wt_other = permuted(wt_slow, inward)
 
     wt_slow, low, high = lax.optimization_barrier((wt_slow, low, high))
+    wt_slow, send_rest, other_rest = lax.optimization_barrier((wt_slow, send_rest, other_rest))
     mine, far = pl.pallas_call(
         mine_kernel,
         out_shape=[block(FIRST, span, jnp.float32), block(NC, span)],
@@ -594,7 +630,8 @@
         cost_estimate=cost(40 * 10**9, 200 * 10**6),
         name="join_rest",
     )(fast_rest, slow_rest, other_rest, wt_fast, wt_slow, wt_other, arrived_rest)
-    relay, direct, pair, far = lax.optimization_barrier((relay, direct, pair, far))
+    relay, direct = lax.optimization_barrier((relay, direct))
+    pair, far = lax.optimization_barrier((pair, far))
     merged = pl.pallas_call(
         merge_kernel,
         out_shape=block(NC, MERGED * BS),
@@ -614,17 +651,17 @@
     early = pl.pallas_call(
         early_kernel,
         out_shape=total,
-        in_specs=[smem, vmem, vmem],
+        in_specs=[smem] + [vmem] * 4,
         out_specs=vmem,
         scratch_shapes=[frame],
         compiler_params=params(16),
-        cost_estimate=cost(10**7, 10**7),
+        cost_estimate=cost(10**10, 100 * 10**6),
         name="early",
-    )(core, own, direct)
+    )(core, own, direct, pair, far)
     return pl.pallas_call(
         total_kernel,
         out_shape=total,
-        in_specs=[smem] + [vmem] * 4,
+        in_specs=[smem] + [vmem] * 2,
         out_specs=hbm,
         scratch_shapes=[
             frame,
@@ -634,7 +671,7 @@
         compiler_params=params(20),
         cost_estimate=cost(10**7, 10**7),
         name="total",
-    )(core, early, pair, merged, far)
+    )(core, early, merged)
 
 
 def solution(mesh):

time: 155 us -> 156 us (level); the launches traced: 152 us -> 156 us
  waiting for transfers between devices: 58.1 us -> 66.8 us
  Pallas kernels: 71.3 us -> 66.6 us
    ppermute x15, waiting for transfers between devices: 58.1 us -> 66.8 us  [permuted(): return lax.ppermute(block, 'dom', pairs)]
    pallas_call x1, Pallas kernels: 37.7 us -> 35.7 us  [body(): pl.pallas_call(fast_kernel, out_shape=outs, in_specs=[smem] * 4 + [hbm, h...]
  transfers between devices with their start and end apart: 15 -> 15, of which waited for: 8 -> 5; matrix products, arithmetic and copies ran while one was open for 2% -> 2% of each run, Pallas kernels for 41% -> 38%
where the time goes in v6:
time: 156 us
  waiting for transfers between devices  66.8 us (43%)
  Pallas kernels  66.6 us (43%)
  starting transfers between devices  14.4 us (9%)
  local copies, waits for them, and re-layouts  4.28 us (3%)
  other arithmetic  3.03 us (2%)
    ppermute x15, waiting for transfers between devices, permuted(): return lax.ppermute(block, 'dom', pairs)  66.8 us
    pallas_call x1, Pallas kernels, body(): pl.pallas_call(fast_kernel, out_shape=outs, in_specs=[smem] * 4 + [hbm, h...  35.7 us
    ppermute x15, starting transfers between devices, permuted(): return lax.ppermute(block, 'dom', pairs)  14.4 us
    pallas_call x1, Pallas kernels, body(): pl.pallas_call(join_rest_kernel, out_shape=[block(NC, span, jnp.float32),...  8.11 us
    pallas_call x1, Pallas kernels, body(): pl.pallas_call(pick_kernel, out_shape=[edge, edge], in_specs=[smem, hbm],...  4.68 us
    pallas_call x1, Pallas kernels, body(): pl.pallas_call(slow_kernel, out_shape=block(WCOLS, AW), in_specs=[smem] *...  4.24 us
    pallas_call x1, Pallas kernels, body(): pl.pallas_call(mine_kernel, out_shape=[block(FIRST, span, jnp.float32), b...  3.48 us
    pallas_call x1, Pallas kernels, body(): pl.pallas_call(total_kernel, out_shape=total, in_specs=[smem] + [vmem] *...  3.34 us
  transfers between devices with their start and end apart: 15, of which 5 were waited for; matrix products, arithmetic and copies ran while one was open for 2% of the time, Pallas kernels for 38%

profile of v6, /device:TPU:0, one launch (start us, length us, event | category | flops | bytes accessed | tf_op | source)
XLA Modules:
  0.0 155.6 jit_solution(5645506772191412782)
XLA Ops:
  0.0 0.7 slice_bitcast_fusion
  0.7 6.4 %collective-permute-start.1 = (s32[8,27]{1,0:T(8,128)S(1)}, s32[8,27]{1,0:T(8,128)S(1)}, u32[]{:S(2)}, u32[]{:S(2)}) collective-permute-start(s32[8,27]{1,0:T(8,128)S(1)} %get-tuple-element.95), channel_id=1, source_target_pairs={{0,31},{1,2},{2,1},{3,4},{4,3},{5,6},{6,5},{7,8},{8,7},{9,10},{10,... | collective-permute-start | bytes 2600 | tf_op jit(solution)/shard_map/ppermute | solution.py:441
  7.2 0.0 collective-permute-start
  7.2 0.6 pad_add_fusion.core
  7.7 4.7 %pick.1 = (bf16[8,64,1728]{2,1,0:T(8,128)(2,1)}, bf16[8,64,1728]{2,1,0:T(8,128)(2,1)}) custom-call(s32[2]{0:T(128)} %pad_add_fusion.core, bf16[24,64,1728]{2,1,0:T(8,128)(2,1)} %p_own.1), custom_call_target="tpu_custom_call" | custom-call | tf_op jit(solution)/shard_map/pick/pallas_call | solution.py:475
  12.4 0.6 collective-permute-start.2
  13.0 0.3 collective-permute-start.3
  13.3 0.1 fusion.1
  13.4 0.1 copy.15
  13.5 0.1 select_reduce_fusion.3
  13.6 0.2 select_reduce_fusion
  13.8 0.6 broadcast_add_fusion.inv_a
  14.4 0.6 broadcast_add_fusion.1.inv_own
  15.0 0.0 collective-permute-done.1
  15.0 0.1 copy.17
  15.2 0.1 copy.16
  15.2 0.1 select_reduce_fusion.1
  15.4 0.1 select_reduce_fusion.2
  15.5 0.6 broadcast_add_fusion.3.inv_fast
  16.1 0.6 collective-permute-done.2.p_fast
  16.7 35.7 %fast.1 = (bf16[3,64,2432]{2,1,0:T(8,128)(2,1)}, bf16[3,64,2432]{2,1,0:T(8,128)(2,1)}, bf16[3,64,2432]{2,1,0:T(8,128)(2,1)}, bf16[6,64,2432]{2,1,0:T(8,128)(2,1)...) custom-call(s32[2]{0:T(128)} %pad_add_fusion.core, ...), custom_call_target="tpu_custom_call" | custom-call | flops 20000000000 | bytes 30000000 | tf_op jit(solution)/shard_map/fast/pallas_call | solution.py:537
  52.5 0.4 collective-permute-start.4
  52.9 0.1 collective-permute-start.5
  53.1 0.4 collective-permute-start.6
  53.4 2.2 %copy-done = f32[33,64,512]{2,1,0:T(8,128)S(1)} copy-done((f32[33,64,512]{2,1,0:T(8,128)S(1)}, f32[33,64,512]{2,1,0:T(8,128)}, u32[]{:S(2)}) %copy-start) | copy-done | bytes 4325400
  55.7 1.0 copy-done.1
  56.7 0.5 stage.1
  57.2 0.0 collective-permute-done.6.other
  57.2 0.0 collective-permute-done.4.low
  57.3 4.2 %slow.1.wt_slow = bf16[40,64,512]{2,1,0:T(8,128)(2,1)S(1)} custom-call(s32[2]{0:T(128)S(1)} %copy-done.2, s32[8,33]{1,0:T(8,128)S(1)} %broadcast_add_fusion.2.inv_slow, bf16[8,64,1728]{2,1,0:T(8,128)(2,1)S(1)} %collective-permute-done.3.p_slow, bf16[8,64,512]{2,1,0:T(8,128)(2,1)S(1)} %get-tuple-element.62.at_halo, f32[33,64,512]{2,1,0:T(8,128)S(1)} %get-tuple-element.63.rest), custom_call_target="tpu_custom_call" | custom-call | flops 20000000000 | bytes 200000000 | tf_op jit(solution)/shard_map/slow/pallas_call | solution.py:579
  61.5 0.3 collective-permute-start.7
  61.9 3.5 %mine.1 = (f32[6,64,2432]{2,1,0:T(8,128)S(1)}, bf16[3,64,2432]{2,1,0:T(8,128)(2,1)S(1)}) custom-call(bf16[9,64,512]{2,1,0:T(8,128)(2,1)S(1)} %copy-done.5, bf16[40,64,512]{2,1,0:T(8,128)(2,1)S(1)} %slow.1.wt_slow, bf16[6,64,2432]{2,1,0:T(8,128)(2,1)S(1)} %copy-done.3, bf16[3,64,2432]{2,1,0:T(8,128)(2,1)S(1)} %collective-permute-done.4.low, ...), custom_call_target="tpu_custom_call" | custom-call | flops 10000000000 | bytes 100000000 | tf_op jit(solution)/shard_map/mine/pallas_call | solution.py:597
  65.4 1.1 collective-permute-done.7.wt_other
  66.5 0.3 collective-permute-start.9
  66.9 0.2 collective-permute-start.8
  67.1 2.9 %join_first.1 = (bf16[3,64,2432]{2,1,0:T(8,128)(2,1)S(1)}, bf16[3,64,2432]{2,1,0:T(8,128)(2,1)S(1)}) custom-call(bf16[6,64,512]{2,1,0:T(8,128)(2,1)S(1)} %collective-permute-done.6.other, bf16[40,64,512]{2,1,0:T(8,128)(2,1)S(1)} %collective-permute-done.7.wt_other, f32[6,64,2432]{2,1,0:T(8,128)S(1)} %get-tuple-element.83.mine), custom_call_target="tpu_custom_call" | custom-call | flops 3000000000 | bytes 10000000 | tf_op jit(solution)/shard_map/join_first/pallas_call | solution.py:611
  70.0 0.7 collective-permute-start.10
  70.8 4.3 %collective-permute-start.11 = (bf16[3,64,2432]{2,1,0:T(8,128)(2,1)S(1)}, bf16[3,64,2432]{2,1,0:T(8,128)(2,1)S(1)}, u32[]{:S(2)}, u32[]{:S(2)}) collective-permute-start(bf16[3,64,2432]{2,1,0:T(8,128)(2,1)S(1)} %get-tuple-element.85), channel_id=1, source_target_pairs={{0,28},{1,29},{2,6},{3,7},{4,0},{5,1},{6,10},{7,11},{8,4},{9,5},{1... | collective-permute-start | bytes 2801672 | tf_op jit(solution)/shard_map/ppermute | solution.py:441
  75.1 8.1 %join_rest.1 = (f32[3,64,2432]{2,1,0:T(8,128)S(1)}, bf16[3,64,2432]{2,1,0:T(8,128)(2,1)S(1)}, f32[3,64,2432]{2,1,0:T(8,128)S(1)}) custom-call(bf16[9,64,1024]{2,1,0:T(8,128)(2,1)S(1)} %copy-done.6, bf16[9,64,512]{2,1,0:T(8,128)(2,1)S(1)} %copy-done.7, bf16[9,64,512]{2,1,0:T(8,128)(2,1)S(1)} %collective-permute-done.8.other, ...), custom_call_target="tpu_custom_call" | custom-call | flops 40000000000 | bytes 200000000 | tf_op jit(solution)/shard_map/join_rest/pallas_call | solution.py:624
  83.2 0.1 collective-permute-start.12
  83.3 0.1 collective-permute-start.13
  83.4 30.2 %collective-permute-done.10.relay = bf16[3,64,2432]{2,1,0:T(8,128)(2,1)S(1)} collective-permute-done((bf16[3,64,2432]{2,1,0:T(8,128)(2,1)S(1)}, bf16[3,64,2432]{2,1,0:T(8,128)(2,1)S(1)}, u32[]{:S(2)}, u32[]{:S(2)}) %collective-permute-start.10) | collective-permute-done | bytes 933920 | tf_op jit(solution)/shard_map/ppermute | solution.py:441
  113.6 1.1 merge.1
  114.8 0.1 collective-permute-start.14
  114.8 18.2 %collective-permute-done.12.pair = bf16[3,64,2432]{2,1,0:T(8,128)(2,1)S(1)} collective-permute-done((bf16[3,64,2432]{2,1,0:T(8,128)(2,1)S(1)}, bf16[3,64,2432]{2,1,0:T(8,128)(2,1)S(1)}, u32[]{:S(2)}, u32[]{:S(2)}) %collective-permute-start.12) | collective-permute-done | bytes 933920 | tf_op jit(solution)/shard_map/ppermute | solution.py:441
  133.0 2.5 %early.1 = f32[3,64,4032]{2,1,0:T(8,128)S(1)} custom-call(s32[2]{0:T(128)S(1)} %copy-done.2, f32[3,64,2432]{2,1,0:T(8,128)S(1)} %get-tuple-element.81.own, bf16[3,64,2432]{2,1,0:T(8,128)(2,1)S(1)} %collective-permute-done.11.direct, bf16[3,64,2432]{2,1,0:T(8,128)(2,1)S(1)} %collective-permute-done.12.pair, bf16[3,64,2432]{2,1,0:T(8,128)(2,1)S(1)} %collective-permute-done.13.far), custom_call_target="tpu_custom_call" | custom-call | flops 10000000000 | bytes 100000000 | tf_op jit(solution)/shard_map/early/pallas_call | solution.py:651
  135.5 16.6 %collective-permute-done.14.merged = bf16[3,64,2816]{2,1,0:T(8,128)(2,1)S(1)} collective-permute-done((bf16[3,64,2816]{2,1,0:T(8,128)(2,1)S(1)}, bf16[3,64,2816]{2,1,0:T(8,128)(2,1)S(1)}, u32[]{:S(2)}, u32[]{:S(2)}) %collective-permute-start.14) | collective-permute-done | bytes 1081376 | tf_op jit(solution)/shard_map/ppermute | solution.py:441
  152.1 3.3 %total.1 = f32[3,64,4032]{2,1,0:T(8,128)} custom-call(s32[2]{0:T(128)S(1)} %copy-done.2, f32[3,64,4032]{2,1,0:T(8,128)S(1)} %early.1, bf16[3,64,2816]{2,1,0:T(8,128)(2,1)S(1)} %collective-permute-done.14.merged), custom_call_target="tpu_custom_call" | custom-call | flops 10000000 | bytes 10000000 | tf_op jit(solution)/shard_map/total/pallas_call | solution.py:661
  (43 shorter events, 0.1 us)
Async XLA Ops:
  0.7 14.3 %collective-permute-start.1 = (s32[8,27]{1,0:T(8,128)S(1)}, s32[8,27]{1,0:T(8,128)S(1)}, u32[]{:S(2)}, u32[]{:S(2)}) collective-permute-start(s32[8,27]{1,0:T(8,128)S(1)} %get-tuple-element.95), channel_id=1, source_target_pairs={{0,31},{1,2},{2,1},{3,4},{4,3},{5,6},{6,5},{7,8},{8,7},{9,10},{10,... | collective-permute-start | bytes 2600 | tf_op jit(solution)/shard_map/ppermute | solution.py:441
  7.2 8.0 %collective-permute-start = (s32[8,27]{1,0:T(8,128)S(1)}, s32[8,27]{1,0:T(8,128)S(1)}, u32[]{:S(2)}, u32[]{:S(2)}) collective-permute-start(s32[8,27]{1,0:T(8,128)S(1)} %get-tuple-element.96), channel_id=1, source_target_pairs={{0,1},{1,0},{2,3},{3,2},{4,5},{5,4},{6,7},{7,6},{8,9},{9,8},{10,11... | collective-permute-start | bytes 2600 | tf_op jit(solution)/shard_map/ppermute | solution.py:441
  7.7 5.6 %copy-start.8 = (s32[24,27]{1,0:T(8,128)S(1)}, s32[24,27]{1,0:T(8,128)}, u32[]{:S(2)}) copy-start(s32[24,27]{1,0:T(8,128)} %param.7) | copy-start | bytes 7780
  7.7 5.8 %copy-start.9 = (s32[24,7]{0,1:T(8,128)S(1)}, s32[24,7]{0,1:T(8,128)}, u32[]{:S(2)}) copy-start(s32[24,7]{0,1:T(8,128)} %param.6) | copy-start | bytes 2020
  12.4 4.3 %collective-permute-start.2 = (bf16[8,64,1728]{2,1,0:T(8,128)(2,1)}, bf16[8,64,1728]{2,1,0:T(8,128)(2,1)}, u32[]{:S(2)}, u32[]{:S(2)}) collective-permute-start(bf16[8,64,1728]{2,1,0:T(8,128)(2,1)} %get-tuple-element.50), channel_id=1, source_target_pairs={{0,1},{1,0},{2,3},{3,2},{4,5},{5,4},{6,7},{7,6},{8,9},{9,8},{10,11... | collective-permute-start | bytes 5308424 | tf_op jit(solution)/shard_map/ppermute | solution.py:441
  13.0 44.2 %collective-permute-start.3 = (bf16[8,64,1728]{2,1,0:T(8,128)(2,1)}, bf16[8,64,1728]{2,1,0:T(8,128)(2,1)S(1)}, u32[]{:S(2)}, u32[]{:S(2)}) collective-permute-start(bf16[8,64,1728]{2,1,0:T(8,128)(2,1)} %get-tuple-element.55), channel_id=1, source_target_pairs={{0,31},{1,2},{2,1},{3,4},{4,3},{5,6},{6,5},{7,8},{8,7},{9,10},{10,... | collective-permute-start | bytes 5308424 | tf_op jit(solution)/shard_map/ppermute | solution.py:441
  52.5 4.8 %copy-start.2 = (s32[2]{0:T(128)S(1)}, s32[2]{0:T(128)}, u32[]{:S(2)}) copy-start(s32[2]{0:T(128)} %pad_add_fusion.core) | copy-start | bytes 28
  52.5 4.8 %collective-permute-start.4 = (bf16[3,64,2432]{2,1,0:T(8,128)(2,1)}, bf16[3,64,2432]{2,1,0:T(8,128)(2,1)S(1)}, u32[]{:S(2)}, u32[]{:S(2)}) collective-permute-start(bf16[3,64,2432]{2,1,0:T(8,128)(2,1)} %get-tuple-element.56), channel_id=1, source_target_pairs={{0,1},{1,0},{2,3},{3,2},{4,5},{5,4},{6,7},{7,6},{8,9},{9,8},{10,11... | collective-permute-start | bytes 2801672 | tf_op jit(solution)/shard_map/ppermute | solution.py:441
  52.9 4.3 %collective-permute-start.5 = (bf16[3,64,2432]{2,1,0:T(8,128)(2,1)}, bf16[3,64,2432]{2,1,0:T(8,128)(2,1)S(1)}, u32[]{:S(2)}, u32[]{:S(2)}) collective-permute-start(bf16[3,64,2432]{2,1,0:T(8,128)(2,1)} %get-tuple-element.57), channel_id=1, source_target_pairs={{0,1},{1,0},{2,3},{3,2},{4,5},{5,4},{6,7},{7,6},{8,9},{9,8},{10,11... | collective-permute-start | bytes 2801672 | tf_op jit(solution)/shard_map/ppermute | solution.py:441
  53.1 4.2 %collective-permute-start.6 = (bf16[6,64,512]{2,1,0:T(8,128)(2,1)}, bf16[6,64,512]{2,1,0:T(8,128)(2,1)S(1)}, u32[]{:S(2)}, u32[]{:S(2)}) collective-permute-start(bf16[6,64,512]{2,1,0:T(8,128)(2,1)} %get-tuple-element.58), channel_id=1, source_target_pairs={{0,1},{1,0},{2,3},{3,2},{4,5},{5,4},{6,7},{7,6},{8,9},{9,8},{10,11... | collective-permute-start | bytes 1179656 | tf_op jit(solution)/shard_map/ppermute | solution.py:441
  53.4 2.2 %copy-start = (f32[33,64,512]{2,1,0:T(8,128)S(1)}, f32[33,64,512]{2,1,0:T(8,128)}, u32[]{:S(2)}) copy-start(f32[33,64,512]{2,1,0:T(8,128)} %get-tuple-element.61.rest) | copy-start | bytes 12976132
  55.7 1.0 copy-start.1
  57.3 4.6 %copy-start.3 = (bf16[6,64,2432]{2,1,0:T(8,128)(2,1)S(1)}, bf16[6,64,2432]{2,1,0:T(8,128)(2,1)}, u32[]{:S(2)}) copy-start(bf16[6,64,2432]{2,1,0:T(8,128)(2,1)} %get-tuple-element.70.inner) | copy-start | bytes 5603332
  57.3 4.6 %copy-start.4 = (bf16[3,64,2432]{2,1,0:T(8,128)(2,1)S(1)}, bf16[3,64,2432]{2,1,0:T(8,128)(2,1)}, u32[]{:S(2)}) copy-start(bf16[3,64,2432]{2,1,0:T(8,128)(2,1)} %get-tuple-element.73.far_fast) | copy-start | bytes 2801668
  57.3 4.6 %copy-start.5 = (bf16[9,64,512]{2,1,0:T(8,128)(2,1)S(1)}, bf16[9,64,512]{2,1,0:T(8,128)(2,1)}, u32[]{:S(2)}) copy-start(bf16[9,64,512]{2,1,0:T(8,128)(2,1)} %get-tuple-element.53.slow) | copy-start | bytes 1769476
  61.5 5.0 %collective-permute-start.7 = (bf16[40,64,512]{2,1,0:T(8,128)(2,1)S(1)}, bf16[40,64,512]{2,1,0:T(8,128)(2,1)S(1)}, u32[]{:S(2)}, u32[]{:S(2)}) collective-permute-start(bf16[40,64,512]{2,1,0:T(8,128)(2,1)S(1)} %slow.1.wt_slow), channel_id=1, source_target_pairs={{0,1},{1,0},{2,3},{3,2},{4,5},{5,4},{6,7},{7,6},{8,9},{9,8},{10,11... | collective-permute-start | bytes 7864328 | tf_op jit(solution)/shard_map/ppermute | solution.py:441
  61.9 4.6 %copy-start.10 = (bf16[9,64,2432]{2,1,0:T(8,128)(2,1)S(1)}, bf16[9,64,2432]{2,1,0:T(8,128)(2,1)}, u32[]{:S(2)}) copy-start(bf16[9,64,2432]{2,1,0:T(8,128)(2,1)} %get-tuple-element.80) | copy-start | bytes 8404996
  61.9 5.0 %copy-start.11 = (bf16[9,64,512]{2,1,0:T(8,128)(2,1)S(1)}, bf16[9,64,512]{2,1,0:T(8,128)(2,1)}, u32[]{:S(2)}) copy-start(bf16[9,64,512]{2,1,0:T(8,128)(2,1)} %get-tuple-element.77) | copy-start | bytes 1769476
  66.5 8.6 %slice-start = ((s8[5242880]{0:T(1024)(128)(4,1)}), s8[4194304]{0:T(1024)(128)(4,1)S(1)}, s32[]{:S(2)}) async-start(s8[5242880]{0:T(1024)(128)(4,1)} %bitcast.10), calls=%async_computation | async-start | bytes 8388608
  66.5 8.6 %slice-start.1 = ((s8[5242880]{0:T(1024)(128)(4,1)}), s8[1048576]{0:T(1024)(128)(4,1)S(1)}, s32[]{:S(2)}) async-start(s8[5242880]{0:T(1024)(128)(4,1)} %bitcast.10), calls=%async_computation.1 | async-start | bytes 2097152
  66.5 8.6 %copy-start.6 = (bf16[9,64,1024]{2,1,0:T(8,128)(2,1)S(1)}, bf16[9,64,1024]{2,1,0:T(8,128)(2,1)}, u32[]{:S(2)}) copy-start(bf16[9,64,1024]{2,1,0:T(8,128)(2,1)} %get-tuple-element.51.fast) | copy-start | bytes 3538948
  66.5 8.6 %copy-start.7 = (bf16[9,64,512]{2,1,0:T(8,128)(2,1)S(1)}, bf16[9,64,512]{2,1,0:T(8,128)(2,1)}, u32[]{:S(2)}) copy-start(bf16[9,64,512]{2,1,0:T(8,128)(2,1)} %get-tuple-element.52.slow) | copy-start | bytes 1769476
  66.5 8.5 %collective-permute-start.9 = (bf16[9,64,2432]{2,1,0:T(8,128)(2,1)S(1)}, bf16[9,64,2432]{2,1,0:T(8,128)(2,1)S(1)}, u32[]{:S(2)}, u32[]{:S(2)}) collective-permute-start(bf16[9,64,2432]{2,1,0:T(8,128)(2,1)S(1)} %copy-done.10), channel_id=1, source_target_pairs={{0,1},{1,0},{2,3},{3,2},{4,5},{5,4},{6,7},{7,6},{8,9},{9,8},{10,11... | collective-permute-start | bytes 8405000 | tf_op jit(solution)/shard_map/ppermute | solution.py:441
  66.9 8.2 %collective-permute-start.8 = (bf16[9,64,512]{2,1,0:T(8,128)(2,1)S(1)}, bf16[9,64,512]{2,1,0:T(8,128)(2,1)S(1)}, u32[]{:S(2)}, u32[]{:S(2)}) collective-permute-start(bf16[9,64,512]{2,1,0:T(8,128)(2,1)S(1)} %copy-done.11), channel_id=1, source_target_pairs={{0,1},{1,0},{2,3},{3,2},{4,5},{5,4},{6,7},{7,6},{8,9},{9,8},{10,11... | collective-permute-start | bytes 1769480 | tf_op jit(solution)/shard_map/ppermute | solution.py:441
  70.0 43.6 %collective-permute-start.10 = (bf16[3,64,2432]{2,1,0:T(8,128)(2,1)S(1)}, bf16[3,64,2432]{2,1,0:T(8,128)(2,1)S(1)}, u32[]{:S(2)}, u32[]{:S(2)}) collective-permute-start(bf16[3,64,2432]{2,1,0:T(8,128)(2,1)S(1)} %get-tuple-element.84), channel_id=1, source_target_pairs={{0,2},{1,3},{2,0},{3,1},{4,6},{5,7},{6,4},{7,5},{8,10},{9,11},{10,... | collective-permute-start | bytes 2801672 | tf_op jit(solution)/shard_map/ppermute | solution.py:441
  70.8 42.9 %collective-permute-start.11 = (bf16[3,64,2432]{2,1,0:T(8,128)(2,1)S(1)}, bf16[3,64,2432]{2,1,0:T(8,128)(2,1)S(1)}, u32[]{:S(2)}, u32[]{:S(2)}) collective-permute-start(bf16[3,64,2432]{2,1,0:T(8,128)(2,1)S(1)} %get-tuple-element.85), channel_id=1, source_target_pairs={{0,28},{1,29},{2,6},{3,7},{4,0},{5,1},{6,10},{7,11},{8,4},{9,5},{1... | collective-permute-start | bytes 2801672 | tf_op jit(solution)/shard_map/ppermute | solution.py:441
  83.2 49.8 %collective-permute-start.12 = (bf16[3,64,2432]{2,1,0:T(8,128)(2,1)S(1)}, bf16[3,64,2432]{2,1,0:T(8,128)(2,1)S(1)}, u32[]{:S(2)}, u32[]{:S(2)}) collective-permute-start(bf16[3,64,2432]{2,1,0:T(8,128)(2,1)S(1)} %get-tuple-element.89), channel_id=1, source_target_pairs={{0,2},{1,3},{2,0},{3,1},{4,6},{5,7},{6,4},{7,5},{8,10},{9,11},{10,... | collective-permute-start | bytes 2801672 | tf_op jit(solution)/shard_map/ppermute | solution.py:441
  83.3 49.7 %collective-permute-start.13 = (bf16[3,64,2432]{2,1,0:T(8,128)(2,1)S(1)}, bf16[3,64,2432]{2,1,0:T(8,128)(2,1)S(1)}, u32[]{:S(2)}, u32[]{:S(2)}) collective-permute-start(bf16[3,64,2432]{2,1,0:T(8,128)(2,1)S(1)} %get-tuple-element.90), channel_id=1, source_target_pairs={{0,27},{1,6},{2,29},{3,8},{4,31},{5,10},{6,1},{7,12},{8,3},{9,14},... | collective-permute-start | bytes 2801672 | tf_op jit(solution)/shard_map/ppermute | solution.py:441
  114.8 37.3 %collective-permute-start.14 = (bf16[3,64,2816]{2,1,0:T(8,128)(2,1)S(1)}, bf16[3,64,2816]{2,1,0:T(8,128)(2,1)S(1)}, u32[]{:S(2)}, u32[]{:S(2)}) collective-permute-start(bf16[3,64,2816]{2,1,0:T(8,128)(2,1)S(1)} %merge.1), channel_id=1, source_target_pairs={{0,4},{1,5},{2,30},{3,31},{4,8},{5,9},{6,2},{7,3},{8,12},{9,13},{1... | collective-permute-start | bytes 3244040 | tf_op jit(solution)/shard_map/ppermute | solution.py:441

commit v7 on v6

--- a/solution.py
+++ b/solution.py
@@ -44,6 +44,10 @@
 
 def low_half():
     return lax.broadcasted_iota(jnp.int32, (BS, 2 * BS), 1) < BS
+
+
+def places(device):
+    return device[0] % 2, device[0] // 2 % 2
 
 
 def transpose_quad(unit, block, turned, width):
@@ -111,7 +115,7 @@
     in_sems,
     out_sems,
 ):
-    s = core[0]
+    s, x = places(core)
     own_quads = NB // QUAD
     halo_quads = AGG // QUAD
 
@@ -170,7 +174,6 @@
 
     fast_lanes = pl.ds(pl.multiple_of(AW + (1 - s) * AW, AW), 2 * AW)
     slow_lanes = pl.ds(pl.multiple_of(AW + 2 * s * AW, AW), AW)
-    x = core[1]
     for place, i in enumerate((1 + 2 * x, 4 * x, 4 - 4 * x, 3 - 2 * x, 2)):
         for j in range(NC):
             row = NC * place + j
@@ -299,7 +302,7 @@
 
 
 def slow_kernel(core, inv_slow, p_slow, at_halo, rest, wt, unit, turned_p, ext):
-    s = core[0]
+    s, x = places(core)
     unit[...] = eye(LANES)
     turned_p[KP] = jnp.zeros((BS, LANES), jnp.bfloat16)
 
@@ -365,7 +368,7 @@
 
 
 def merge_kernel(core, rows, relay, out, frame):
-    x = core[1]
+    s, x = places(core)
     step = 6 * BS
     for j in range(NC):
         frame[...] = jnp.zeros_like(frame)
@@ -393,7 +396,7 @@
 
 
 def early_kernel(core, own, direct, pair, far, out, frame):
-    s, x = core[0], core[1]
+    s, x = places(core)
     for j in range(NC):
         top = 27 - 3 * s - j
         far_start = jnp.where(s == 1, 30 - j, -3 - j)
@@ -407,7 +410,7 @@
 
 
 def total_kernel(core, early, merged, out, frame, buf, sems):
-    s, x = core[0], core[1]
+    s, x = places(core)
     copies = []
     for j in range(NC):
 
@@ -422,18 +425,24 @@
         copy.wait()
 
 
-def pick_kernel(core, source, outer, inner, sems):
-    s = core[0]
+def pick_kernel(core, source, outer, inner, buf, in_sems, out_sems):
+    s, x = places(core)
     step = AGG // 4
-    copies = []
-    for target, side in ((outer, s), (inner, 1 - s)):
+    reads, writes = [], []
+    for side, (target, which) in enumerate(((outer, s), (inner, 1 - s))):
         for k in range(4):
-            rows = pl.ds((NB - AGG) * side + k * step, step)
+            n = len(reads)
+            rows = pl.ds((NB - AGG) * which + k * step, step)
+            part = buf.at[side, k * step : (k + 1) * step]
             into = target.at[k * step : (k + 1) * step]
-            copies.append(pltpu.make_async_copy(source.at[rows], into, sems.at[len(copies)]))
-    for copy in copies:
+            reads.append(pltpu.make_async_copy(source.at[rows], part, in_sems.at[n]))
+            writes.append(pltpu.make_async_copy(part, into, out_sems.at[n]))
+    for copy in reads:
         copy.start()
-    for copy in copies:
+    for read, write in zip(reads, writes):
+        read.wait()
+        write.start()
+    for copy in writes:
         copy.wait()
 
 
@@ -454,7 +463,7 @@
     count_rows = NB * devices
     first_agg = device * NC
     first_row = device * NB
-    core = jnp.stack([device % 2, device // 2 % 2]).astype(jnp.int32)
+    core = device.astype(jnp.int32).reshape(1)
 
     def shifted(distance):
         return [(i, (i + distance) % devices) for i in range(devices)]
@@ -476,16 +485,21 @@
         pick_kernel,
         out_shape=[edge, edge],
         in_specs=[smem, hbm],
-        out_specs=[vmem, vmem],
-        scratch_shapes=[pltpu.SemaphoreType.DMA((8,))],
+        out_specs=[hbm, hbm],
+        scratch_shapes=[
+            pltpu.VMEM((2,) + edge.shape, bf16),
+            pltpu.SemaphoreType.DMA((8,)),
+            pltpu.SemaphoreType.DMA((8,)),
+        ],
         compiler_params=params(60),
         name="pick",
     )(core, p_blocks)
     outward = [(i, (i + (1 if i % 2 else -1)) % devices) for i in range(devices)]
     inward = [(i, i ^ 1) for i in range(devices)]
+    outer, inner, edge_cols = lax.optimization_barrier((outer, inner, cols_p))
     p_slow = permuted(outer, outward)
     p_fast = permuted(inner, inward)
-    edge_cols = jnp.stack([cols_p[:AGG], cols_p[NB - AGG :]])
+    edge_cols = jnp.stack([edge_cols[:AGG], edge_cols[NB - AGG :]])
     cols_slow = permuted(edge_cols[parity], outward)
     cols_fast = permuted(edge_cols[1 - parity], inward)
 
@@ -630,8 +644,8 @@
         cost_estimate=cost(40 * 10**9, 200 * 10**6),
         name="join_rest",
     )(fast_rest, slow_rest, other_rest, wt_fast, wt_slow, wt_other, arrived_rest)
-    relay, direct = lax.optimization_barrier((relay, direct))
-    pair, far = lax.optimization_barrier((pair, far))
+    relay, pair, far = lax.optimization_barrier((relay, pair, far))
+    relay_in, direct = lax.optimization_barrier((relay, direct))
     merged = pl.pallas_call(
         merge_kernel,
         out_shape=block(NC, MERGED * BS),
@@ -641,7 +655,7 @@
         compiler_params=params(16),
         cost_estimate=cost(10**7, 10**7),
         name="merge",
-    )(core, merge, relay)
+    )(core, merge, relay_in)
     merged = permuted(merged, [(i, (i - 4 * x_sign[i]) % devices) for i in range(devices)])
     pair = permuted(pair, along_x)
     far = permuted(far, [(i, (i + (5 if i % 2 else -5)) % devices) for i in range(devices)])

time: 156 us -> 152 us (0.974)
  starting transfers between devices: 14.4 us -> 18 us
  Pallas kernels: 66.6 us -> 63.4 us
  waiting for transfers between devices: 66.8 us -> 64.2 us
    ppermute x15, starting transfers between devices: 14.4 us -> 18 us  [permuted(): return lax.ppermute(block, 'dom', pairs)]
    ppermute x15, waiting for transfers between devices: 66.8 us -> 64.2 us  [permuted(): return lax.ppermute(block, 'dom', pairs)]
    pallas_call x1, Pallas kernels: 4.68 us -> 3.08 us  [body(): pl.pallas_call(pick_kernel, out_shape=[edge, edge], in_specs=[smem, hbm],...]
    unnamed x28 -> x26, local copies, waits for them, and re-layouts: 3.31 us -> 3.31 us
  transfers between devices with their start and end apart: 15 -> 15, of which waited for: 5 -> 6; matrix products, arithmetic and copies ran while one was open for 2% -> 2% of each run, Pallas kernels for 38% -> 35%
where the time goes in v7:
time: 152 us
  waiting for transfers between devices  64.2 us (42%)
  Pallas kernels  63.4 us (42%)
  starting transfers between devices  18 us (12%)
  local copies, waits for them, and re-layouts  3.58 us (2%)
  other arithmetic  2.48 us (2%)
    ppermute x15, waiting for transfers between devices, permuted(): return lax.ppermute(block, 'dom', pairs)  64.2 us
    pallas_call x1, Pallas kernels, body(): pl.pallas_call(fast_kernel, out_shape=outs, in_specs=[smem] * 4 + [hbm, h...  35.7 us
    ppermute x15, starting transfers between devices, permuted(): return lax.ppermute(block, 'dom', pairs)  18 us
    pallas_call x1, Pallas kernels, body(): pl.pallas_call(join_rest_kernel, out_shape=[block(NC, span, jnp.float32),...  8.1 us
    pallas_call x1, Pallas kernels, body(): pl.pallas_call(slow_kernel, out_shape=block(WCOLS, AW), in_specs=[smem] *...  4.24 us
    pallas_call x1, Pallas kernels, body(): pl.pallas_call(mine_kernel, out_shape=[block(FIRST, span, jnp.float32), b...  3.41 us
    unnamed x26, local copies, waits for them, and re-layouts  3.31 us
    pallas_call x1, Pallas kernels, body(): pl.pallas_call(pick_kernel, out_shape=[edge, edge], in_specs=[smem, hbm],...  3.08 us
  transfers between devices with their start and end apart: 15, of which 6 were waited for; matrix products, arithmetic and copies ran while one was open for 2% of the time, Pallas kernels for 35%

profile of v7, /device:TPU:0, one launch (start us, length us, event | category | flops | bytes accessed | tf_op | source)
XLA Modules:
  0.0 152.1 jit_solution(11692787893008930728)
XLA Ops:
  0.0 3.1 %pick.1 = (bf16[8,64,1728]{2,1,0:T(8,128)(2,1)}, bf16[8,64,1728]{2,1,0:T(8,128)(2,1)}) custom-call(s32[1]{0:T(128)} %bitcast.core, bf16[24,64,1728]{2,1,0:T(8,128)(2,1)} %p_own.1), custom_call_target="tpu_custom_call" | custom-call | tf_op jit(solution)/shard_map/pick/pallas_call | solution.py:484
  3.2 6.4 %collective-permute-start.1 = (s32[8,27]{1,0:T(8,128)S(1)}, s32[8,27]{1,0:T(8,128)S(1)}, u32[]{:S(2)}, u32[]{:S(2)}) collective-permute-start(s32[8,27]{1,0:T(8,128)S(1)} %get-tuple-element.103), channel_id=1, source_target_pairs={{0,31},{1,2},{2,1},{3,4},{4,3},{5,6},{6,5},{7,8},{8,7},{9,10},{10,... | collective-permute-start | bytes 2600 | tf_op jit(solution)/shard_map/ppermute | solution.py:450
  9.6 0.0 collective-permute-start
  9.6 0.5 collective-permute-start.2
  10.1 0.3 collective-permute-start.3
  10.4 0.1 fusion.1
  10.5 0.1 copy.15
  10.6 0.1 select_reduce_fusion.3
  10.8 0.2 select_reduce_fusion
  10.9 0.6 broadcast_add_fusion.inv_a
  11.5 0.6 broadcast_add_fusion.1.inv_own
  12.2 0.1 copy.17
  12.3 0.1 copy.16
  12.4 0.1 select_reduce_fusion.1
  12.5 0.1 select_reduce_fusion.2
  12.6 0.6 broadcast_add_fusion.3.inv_fast
  13.2 0.6 collective-permute-done.2.p_fast
  13.9 35.7 %fast.1 = (bf16[3,64,2432]{2,1,0:T(8,128)(2,1)}, bf16[3,64,2432]{2,1,0:T(8,128)(2,1)}, bf16[3,64,2432]{2,1,0:T(8,128)(2,1)}, bf16[6,64,2432]{2,1,0:T(8,128)(2,1)...) custom-call(s32[1]{0:T(128)} %bitcast.core, ...), custom_call_target="tpu_custom_call" | custom-call | flops 20000000000 | bytes 30000000 | tf_op jit(solution)/shard_map/fast/pallas_call | solution.py:551
  49.6 0.4 collective-permute-start.4
  50.0 0.1 collective-permute-start.5
  50.2 0.4 collective-permute-start.6
  50.5 2.2 %copy-done = f32[33,64,512]{2,1,0:T(8,128)S(1)} copy-done((f32[33,64,512]{2,1,0:T(8,128)S(1)}, f32[33,64,512]{2,1,0:T(8,128)}, u32[]{:S(2)}) %copy-start) | copy-done | bytes 4325400
  52.8 1.0 copy-done.1
  53.8 0.5 stage.1
  54.3 0.0 collective-permute-done.3.p_slow
  54.3 0.0 collective-permute-done.6.other
  54.3 0.0 collective-permute-done.5.high
  54.4 4.2 %slow.1.wt_slow = bf16[40,64,512]{2,1,0:T(8,128)(2,1)S(1)} custom-call(s32[1]{0:T(128)} %bitcast.core, s32[8,33]{1,0:T(8,128)S(1)} %broadcast_add_fusion.2.inv_slow, bf16[8,64,1728]{2,1,0:T(8,128)(2,1)S(1)} %collective-permute-done.3.p_slow, bf16[8,64,512]{2,1,0:T(8,128)(2,1)S(1)} %get-tuple-element.69.at_halo, f32[33,64,512]{2,1,0:T(8,128)S(1)} %get-tuple-element.70.rest), custom_call_target="tpu_custom_call" | custom-call | flops 20000000000 | bytes 200000000 | tf_op jit(solution)/shard_map/slow/pallas_call | solution.py:593
  58.6 0.3 collective-permute-start.7
  59.0 3.4 %mine.1 = (f32[6,64,2432]{2,1,0:T(8,128)S(1)}, bf16[3,64,2432]{2,1,0:T(8,128)(2,1)S(1)}) custom-call(bf16[9,64,512]{2,1,0:T(8,128)(2,1)S(1)} %copy-done.4, bf16[40,64,512]{2,1,0:T(8,128)(2,1)S(1)} %slow.1.wt_slow, bf16[6,64,2432]{2,1,0:T(8,128)(2,1)S(1)} %copy-done.2, bf16[3,64,2432]{2,1,0:T(8,128)(2,1)S(1)} %collective-permute-done.4.low, ...), custom_call_target="tpu_custom_call" | custom-call | flops 10000000000 | bytes 100000000 | tf_op jit(solution)/shard_map/mine/pallas_call | solution.py:611
  62.4 1.2 collective-permute-done.7.wt_other
  63.6 0.3 collective-permute-start.9
  64.0 0.2 collective-permute-start.8
  64.2 3.0 %join_first.1 = (bf16[3,64,2432]{2,1,0:T(8,128)(2,1)S(1)}, bf16[3,64,2432]{2,1,0:T(8,128)(2,1)S(1)}) custom-call(bf16[6,64,512]{2,1,0:T(8,128)(2,1)S(1)} %collective-permute-done.6.other, bf16[40,64,512]{2,1,0:T(8,128)(2,1)S(1)} %collective-permute-done.7.wt_other, f32[6,64,2432]{2,1,0:T(8,128)S(1)} %get-tuple-element.90.mine), custom_call_target="tpu_custom_call" | custom-call | flops 3000000000 | bytes 10000000 | tf_op jit(solution)/shard_map/join_first/pallas_call | solution.py:625
  67.2 0.6 collective-permute-start.10
  67.8 4.5 %collective-permute-start.11 = (bf16[3,64,2432]{2,1,0:T(8,128)(2,1)S(1)}, bf16[3,64,2432]{2,1,0:T(8,128)(2,1)S(1)}, u32[]{:S(2)}, u32[]{:S(2)}) collective-permute-start(bf16[3,64,2432]{2,1,0:T(8,128)(2,1)S(1)} %get-tuple-element.95), channel_id=1, source_target_pairs={{0,28},{1,29},{2,6},{3,7},{4,0},{5,1},{6,10},{7,11},{8,4},{9,5},{1... | collective-permute-start | bytes 2801672 | tf_op jit(solution)/shard_map/ppermute | solution.py:450
  72.3 8.1 %join_rest.1 = (f32[3,64,2432]{2,1,0:T(8,128)S(1)}, bf16[3,64,2432]{2,1,0:T(8,128)(2,1)S(1)}, f32[3,64,2432]{2,1,0:T(8,128)S(1)}) custom-call(bf16[9,64,1024]{2,1,0:T(8,128)(2,1)S(1)} %copy-done.5, bf16[9,64,512]{2,1,0:T(8,128)(2,1)S(1)} %copy-done.6, bf16[9,64,512]{2,1,0:T(8,128)(2,1)S(1)} %collective-permute-done.8.other, ...), custom_call_target="tpu_custom_call" | custom-call | flops 40000000000 | bytes 200000000 | tf_op jit(solution)/shard_map/join_rest/pallas_call | solution.py:638
  80.4 9.7 %collective-permute-done.10.relay = bf16[3,64,2432]{2,1,0:T(8,128)(2,1)S(1)} collective-permute-done((bf16[3,64,2432]{2,1,0:T(8,128)(2,1)S(1)}, bf16[3,64,2432]{2,1,0:T(8,128)(2,1)S(1)}, u32[]{:S(2)}, u32[]{:S(2)}) %collective-permute-start.10) | collective-permute-done | bytes 933920 | tf_op jit(solution)/shard_map/ppermute | solution.py:450
  90.1 0.6 collective-permute-start.12
  90.7 0.9 collective-permute-start.13
  91.6 0.7 collective-permute-done.11.direct
  92.3 0.8 merge.1
  93.1 2.3 %collective-permute-start.14 = (bf16[3,64,2816]{2,1,0:T(8,128)(2,1)S(1)}, bf16[3,64,2816]{2,1,0:T(8,128)(2,1)S(1)}, u32[]{:S(2)}, u32[]{:S(2)}) collective-permute-start(bf16[3,64,2816]{2,1,0:T(8,128)(2,1)S(1)} %merge.1), channel_id=1, source_target_pairs={{0,4},{1,5},{2,30},{3,31},{4,8},{5,9},{6,2},{7,3},{8,12},{9,13},{1... | collective-permute-start | bytes 3244040 | tf_op jit(solution)/shard_map/ppermute | solution.py:450
  95.4 36.7 %collective-permute-done.12.pair = bf16[3,64,2432]{2,1,0:T(8,128)(2,1)S(1)} collective-permute-done((bf16[3,64,2432]{2,1,0:T(8,128)(2,1)S(1)}, bf16[3,64,2432]{2,1,0:T(8,128)(2,1)S(1)}, u32[]{:S(2)}, u32[]{:S(2)}) %collective-permute-start.12) | collective-permute-done | bytes 933920 | tf_op jit(solution)/shard_map/ppermute | solution.py:450
  132.1 0.0 collective-permute-done.13.far
  132.1 1.8 %early.1 = f32[3,64,4032]{2,1,0:T(8,128)S(1)} custom-call(s32[1]{0:T(128)} %bitcast.core, f32[3,64,2432]{2,1,0:T(8,128)S(1)} %get-tuple-element.88.own, bf16[3,64,2432]{2,1,0:T(8,128)(2,1)S(1)} %collective-permute-done.11.direct, bf16[3,64,2432]{2,1,0:T(8,128)(2,1)S(1)} %collective-permute-done.12.pair, bf16[3,64,2432]{2,1,0:T(8,128)(2,1)S(1)} %collective-permute-done.13.far), custom_call_target="tpu_custom_call" | custom-call | flops 10000000000 | bytes 100000000 | tf_op jit(solution)/shard_map/early/pallas_call | solution.py:665
  133.9 15.3 %collective-permute-done.14.merged = bf16[3,64,2816]{2,1,0:T(8,128)(2,1)S(1)} collective-permute-done((bf16[3,64,2816]{2,1,0:T(8,128)(2,1)S(1)}, bf16[3,64,2816]{2,1,0:T(8,128)(2,1)S(1)}, u32[]{:S(2)}, u32[]{:S(2)}) %collective-permute-start.14) | collective-permute-done | bytes 1081376 | tf_op jit(solution)/shard_map/ppermute | solution.py:450
  149.2 2.8 %total.1 = f32[3,64,4032]{2,1,0:T(8,128)} custom-call(s32[1]{0:T(128)} %bitcast.core, f32[3,64,4032]{2,1,0:T(8,128)S(1)} %early.1, bf16[3,64,2816]{2,1,0:T(8,128)(2,1)S(1)} %collective-permute-done.14.merged), custom_call_target="tpu_custom_call" | custom-call | flops 10000000 | bytes 10000000 | tf_op jit(solution)/shard_map/total/pallas_call | solution.py:675
  (40 shorter events, 0.1 us)
Async XLA Ops:
  0.0 3.1 %copy-start.7 = (s32[24,27]{1,0:T(8,128)S(1)}, s32[24,27]{1,0:T(8,128)}, u32[]{:S(2)}) copy-start(s32[24,27]{1,0:T(8,128)} %param.7) | copy-start | bytes 7780
  0.0 10.6 %copy-start.8 = (s32[24,7]{0,1:T(8,128)S(1)}, s32[24,7]{0,1:T(8,128)}, u32[]{:S(2)}) copy-start(s32[24,7]{0,1:T(8,128)} %param.6) | copy-start | bytes 2020
  3.2 9.0 %collective-permute-start.1 = (s32[8,27]{1,0:T(8,128)S(1)}, s32[8,27]{1,0:T(8,128)S(1)}, u32[]{:S(2)}, u32[]{:S(2)}) collective-permute-start(s32[8,27]{1,0:T(8,128)S(1)} %get-tuple-element.103), channel_id=1, source_target_pairs={{0,31},{1,2},{2,1},{3,4},{4,3},{5,6},{6,5},{7,8},{8,7},{9,10},{10,... | collective-permute-start | bytes 2600 | tf_op jit(solution)/shard_map/ppermute | solution.py:450
  9.6 2.7 %collective-permute-start = (s32[8,27]{1,0:T(8,128)S(1)}, s32[8,27]{1,0:T(8,128)S(1)}, u32[]{:S(2)}, u32[]{:S(2)}) collective-permute-start(s32[8,27]{1,0:T(8,128)S(1)} %get-tuple-element.104), channel_id=1, source_target_pairs={{0,1},{1,0},{2,3},{3,2},{4,5},{5,4},{6,7},{7,6},{8,9},{9,8},{10,11... | collective-permute-start | bytes 2600 | tf_op jit(solution)/shard_map/ppermute | solution.py:450
  9.6 4.3 %collective-permute-start.2 = (bf16[8,64,1728]{2,1,0:T(8,128)(2,1)}, bf16[8,64,1728]{2,1,0:T(8,128)(2,1)}, u32[]{:S(2)}, u32[]{:S(2)}) collective-permute-start(bf16[8,64,1728]{2,1,0:T(8,128)(2,1)} %get-tuple-element.57), channel_id=1, source_target_pairs={{0,1},{1,0},{2,3},{3,2},{4,5},{5,4},{6,7},{7,6},{8,9},{9,8},{10,11... | collective-permute-start | bytes 5308424 | tf_op jit(solution)/shard_map/ppermute | solution.py:450
  10.1 44.2 %collective-permute-start.3 = (bf16[8,64,1728]{2,1,0:T(8,128)(2,1)}, bf16[8,64,1728]{2,1,0:T(8,128)(2,1)S(1)}, u32[]{:S(2)}, u32[]{:S(2)}) collective-permute-start(bf16[8,64,1728]{2,1,0:T(8,128)(2,1)} %get-tuple-element.62), channel_id=1, source_target_pairs={{0,31},{1,2},{2,1},{3,4},{4,3},{5,6},{6,5},{7,8},{8,7},{9,10},{10,... | collective-permute-start | bytes 5308424 | tf_op jit(solution)/shard_map/ppermute | solution.py:450
  49.6 4.8 %collective-permute-start.4 = (bf16[3,64,2432]{2,1,0:T(8,128)(2,1)}, bf16[3,64,2432]{2,1,0:T(8,128)(2,1)S(1)}, u32[]{:S(2)}, u32[]{:S(2)}) collective-permute-start(bf16[3,64,2432]{2,1,0:T(8,128)(2,1)} %get-tuple-element.63), channel_id=1, source_target_pairs={{0,1},{1,0},{2,3},{3,2},{4,5},{5,4},{6,7},{7,6},{8,9},{9,8},{10,11... | collective-permute-start | bytes 2801672 | tf_op jit(solution)/shard_map/ppermute | solution.py:450
  50.0 4.3 %collective-permute-start.5 = (bf16[3,64,2432]{2,1,0:T(8,128)(2,1)}, bf16[3,64,2432]{2,1,0:T(8,128)(2,1)S(1)}, u32[]{:S(2)}, u32[]{:S(2)}) collective-permute-start(bf16[3,64,2432]{2,1,0:T(8,128)(2,1)} %get-tuple-element.64), channel_id=1, source_target_pairs={{0,1},{1,0},{2,3},{3,2},{4,5},{5,4},{6,7},{7,6},{8,9},{9,8},{10,11... | collective-permute-start | bytes 2801672 | tf_op jit(solution)/shard_map/ppermute | solution.py:450
  50.2 4.2 %collective-permute-start.6 = (bf16[6,64,512]{2,1,0:T(8,128)(2,1)}, bf16[6,64,512]{2,1,0:T(8,128)(2,1)S(1)}, u32[]{:S(2)}, u32[]{:S(2)}) collective-permute-start(bf16[6,64,512]{2,1,0:T(8,128)(2,1)} %get-tuple-element.65), channel_id=1, source_target_pairs={{0,1},{1,0},{2,3},{3,2},{4,5},{5,4},{6,7},{7,6},{8,9},{9,8},{10,11... | collective-permute-start | bytes 1179656 | tf_op jit(solution)/shard_map/ppermute | solution.py:450
  50.5 2.2 %copy-start = (f32[33,64,512]{2,1,0:T(8,128)S(1)}, f32[33,64,512]{2,1,0:T(8,128)}, u32[]{:S(2)}) copy-start(f32[33,64,512]{2,1,0:T(8,128)} %get-tuple-element.68.rest) | copy-start | bytes 12976132
  52.8 1.0 copy-start.1
  54.4 4.6 %copy-start.2 = (bf16[6,64,2432]{2,1,0:T(8,128)(2,1)S(1)}, bf16[6,64,2432]{2,1,0:T(8,128)(2,1)}, u32[]{:S(2)}) copy-start(bf16[6,64,2432]{2,1,0:T(8,128)(2,1)} %get-tuple-element.77.inner) | copy-start | bytes 5603332
  54.4 4.6 %copy-start.3 = (bf16[3,64,2432]{2,1,0:T(8,128)(2,1)S(1)}, bf16[3,64,2432]{2,1,0:T(8,128)(2,1)}, u32[]{:S(2)}) copy-start(bf16[3,64,2432]{2,1,0:T(8,128)(2,1)} %get-tuple-element.80.far_fast) | copy-start | bytes 2801668
  54.4 4.6 %copy-start.4 = (bf16[9,64,512]{2,1,0:T(8,128)(2,1)S(1)}, bf16[9,64,512]{2,1,0:T(8,128)(2,1)}, u32[]{:S(2)}) copy-start(bf16[9,64,512]{2,1,0:T(8,128)(2,1)} %get-tuple-element.60.slow) | copy-start | bytes 1769476
  58.6 5.0 %collective-permute-start.7 = (bf16[40,64,512]{2,1,0:T(8,128)(2,1)S(1)}, bf16[40,64,512]{2,1,0:T(8,128)(2,1)S(1)}, u32[]{:S(2)}, u32[]{:S(2)}) collective-permute-start(bf16[40,64,512]{2,1,0:T(8,128)(2,1)S(1)} %slow.1.wt_slow), channel_id=1, source_target_pairs={{0,1},{1,0},{2,3},{3,2},{4,5},{5,4},{6,7},{7,6},{8,9},{9,8},{10,11... | collective-permute-start | bytes 7864328 | tf_op jit(solution)/shard_map/ppermute | solution.py:450
  59.0 4.6 %copy-start.9 = (bf16[9,64,2432]{2,1,0:T(8,128)(2,1)S(1)}, bf16[9,64,2432]{2,1,0:T(8,128)(2,1)}, u32[]{:S(2)}) copy-start(bf16[9,64,2432]{2,1,0:T(8,128)(2,1)} %get-tuple-element.87) | copy-start | bytes 8404996
  59.0 5.0 %copy-start.10 = (bf16[9,64,512]{2,1,0:T(8,128)(2,1)S(1)}, bf16[9,64,512]{2,1,0:T(8,128)(2,1)}, u32[]{:S(2)}) copy-start(bf16[9,64,512]{2,1,0:T(8,128)(2,1)} %get-tuple-element.84) | copy-start | bytes 1769476
  63.6 8.6 %slice-start = ((s8[5242880]{0:T(1024)(128)(4,1)}), s8[4194304]{0:T(1024)(128)(4,1)S(1)}, s32[]{:S(2)}) async-start(s8[5242880]{0:T(1024)(128)(4,1)} %bitcast.9), calls=%async_computation | async-start | bytes 8388608
  63.6 8.6 %slice-start.1 = ((s8[5242880]{0:T(1024)(128)(4,1)}), s8[1048576]{0:T(1024)(128)(4,1)S(1)}, s32[]{:S(2)}) async-start(s8[5242880]{0:T(1024)(128)(4,1)} %bitcast.9), calls=%async_computation.1 | async-start | bytes 2097152
  63.6 8.6 %copy-start.5 = (bf16[9,64,1024]{2,1,0:T(8,128)(2,1)S(1)}, bf16[9,64,1024]{2,1,0:T(8,128)(2,1)}, u32[]{:S(2)}) copy-start(bf16[9,64,1024]{2,1,0:T(8,128)(2,1)} %get-tuple-element.58.fast) | copy-start | bytes 3538948
  63.6 8.6 %copy-start.6 = (bf16[9,64,512]{2,1,0:T(8,128)(2,1)S(1)}, bf16[9,64,512]{2,1,0:T(8,128)(2,1)}, u32[]{:S(2)}) copy-start(bf16[9,64,512]{2,1,0:T(8,128)(2,1)} %get-tuple-element.59.slow) | copy-start | bytes 1769476
  63.6 8.6 %collective-permute-start.9 = (bf16[9,64,2432]{2,1,0:T(8,128)(2,1)S(1)}, bf16[9,64,2432]{2,1,0:T(8,128)(2,1)S(1)}, u32[]{:S(2)}, u32[]{:S(2)}) collective-permute-start(bf16[9,64,2432]{2,1,0:T(8,128)(2,1)S(1)} %copy-done.9), channel_id=1, source_target_pairs={{0,1},{1,0},{2,3},{3,2},{4,5},{5,4},{6,7},{7,6},{8,9},{9,8},{10,11... | collective-permute-start | bytes 8405000 | tf_op jit(solution)/shard_map/ppermute | solution.py:450
  64.0 8.3 %collective-permute-start.8 = (bf16[9,64,512]{2,1,0:T(8,128)(2,1)S(1)}, bf16[9,64,512]{2,1,0:T(8,128)(2,1)S(1)}, u32[]{:S(2)}, u32[]{:S(2)}) collective-permute-start(bf16[9,64,512]{2,1,0:T(8,128)(2,1)S(1)} %copy-done.10), channel_id=1, source_target_pairs={{0,1},{1,0},{2,3},{3,2},{4,5},{5,4},{6,7},{7,6},{8,9},{9,8},{10,11... | collective-permute-start | bytes 1769480 | tf_op jit(solution)/shard_map/ppermute | solution.py:450
  67.2 22.9 %collective-permute-start.10 = (bf16[3,64,2432]{2,1,0:T(8,128)(2,1)S(1)}, bf16[3,64,2432]{2,1,0:T(8,128)(2,1)S(1)}, u32[]{:S(2)}, u32[]{:S(2)}) collective-permute-start(bf16[3,64,2432]{2,1,0:T(8,128)(2,1)S(1)} %get-tuple-element.91), channel_id=1, source_target_pairs={{0,2},{1,3},{2,0},{3,1},{4,6},{5,7},{6,4},{7,5},{8,10},{9,11},{10,... | collective-permute-start | bytes 2801672 | tf_op jit(solution)/shard_map/ppermute | solution.py:450
  67.8 24.5 %collective-permute-start.11 = (bf16[3,64,2432]{2,1,0:T(8,128)(2,1)S(1)}, bf16[3,64,2432]{2,1,0:T(8,128)(2,1)S(1)}, u32[]{:S(2)}, u32[]{:S(2)}) collective-permute-start(bf16[3,64,2432]{2,1,0:T(8,128)(2,1)S(1)} %get-tuple-element.95), channel_id=1, source_target_pairs={{0,28},{1,29},{2,6},{3,7},{4,0},{5,1},{6,10},{7,11},{8,4},{9,5},{1... | collective-permute-start | bytes 2801672 | tf_op jit(solution)/shard_map/ppermute | solution.py:450
  90.1 42.0 %collective-permute-start.12 = (bf16[3,64,2432]{2,1,0:T(8,128)(2,1)S(1)}, bf16[3,64,2432]{2,1,0:T(8,128)(2,1)S(1)}, u32[]{:S(2)}, u32[]{:S(2)}) collective-permute-start(bf16[3,64,2432]{2,1,0:T(8,128)(2,1)S(1)} %get-tuple-element.97), channel_id=1, source_target_pairs={{0,2},{1,3},{2,0},{3,1},{4,6},{5,7},{6,4},{7,5},{8,10},{9,11},{10,... | collective-permute-start | bytes 2801672 | tf_op jit(solution)/shard_map/ppermute | solution.py:450
  90.7 41.4 %collective-permute-start.13 = (bf16[3,64,2432]{2,1,0:T(8,128)(2,1)S(1)}, bf16[3,64,2432]{2,1,0:T(8,128)(2,1)S(1)}, u32[]{:S(2)}, u32[]{:S(2)}) collective-permute-start(bf16[3,64,2432]{2,1,0:T(8,128)(2,1)S(1)} %get-tuple-element.98), channel_id=1, source_target_pairs={{0,27},{1,6},{2,29},{3,8},{4,31},{5,10},{6,1},{7,12},{8,3},{9,14},... | collective-permute-start | bytes 2801672 | tf_op jit(solution)/shard_map/ppermute | solution.py:450
  93.1 56.1 %collective-permute-start.14 = (bf16[3,64,2816]{2,1,0:T(8,128)(2,1)S(1)}, bf16[3,64,2816]{2,1,0:T(8,128)(2,1)S(1)}, u32[]{:S(2)}, u32[]{:S(2)}) collective-permute-start(bf16[3,64,2816]{2,1,0:T(8,128)(2,1)S(1)} %merge.1), channel_id=1, source_target_pairs={{0,4},{1,5},{2,30},{3,31},{4,8},{5,9},{6,2},{7,3},{8,12},{9,13},{1... | collective-permute-start | bytes 3244040 | tf_op jit(solution)/shard_map/ppermute | solution.py:450

commit v8 on v7

--- a/solution.py
+++ b/solution.py
@@ -28,7 +28,7 @@
 GROUPS = 5
 K = NB * BS
 AW = AGG * BS
-FRAME = 76
+FRAME = 80
 NT = (((1,), (1,)), ((), ()))
 ROWS = NC * GROUPS
 FIRST = 2 * NC
@@ -94,6 +94,7 @@
     fast_rest,
     slow_first,
     slow_rest,
+    slow_far,
     other_first,
     other_rest,
     wt,
@@ -184,11 +185,11 @@
             else:
                 lhs[ROWS + row - FIRST] = ext[other, :, fast_lanes]
                 fast_buf[row - FIRST] = ext[mine, :, fast_lanes]
-            slow_buf[row if place < 2 else row + NC] = ext[mine, :, slow_lanes]
+            slow_buf[row] = ext[mine, :, slow_lanes]
             other_buf[row] = ext[other, :, slow_lanes]
     for j in range(NC):
         lhs[FIRST + j] = ext[30 * s + j + 1, :, fast_lanes]
-        slow_buf[FIRST + j] = ext[30 * s + j + 1, :, slow_lanes]
+        slow_buf[ROWS + j] = ext[30 * s + j + 1, :, slow_lanes]
     copies = [halo_copy]
 
     def write(source, target):
@@ -199,8 +200,9 @@
     write(other_buf.at[:FIRST], other_first)
     write(other_buf.at[FIRST:], other_rest)
     write(fast_buf, fast_rest)
-    write(slow_buf.at[: FIRST + NC], slow_first)
-    write(slow_buf.at[FIRST + NC :], slow_rest)
+    write(slow_buf.at[:FIRST], slow_first)
+    write(slow_buf.at[FIRST:ROWS], slow_rest)
+    write(slow_buf.at[ROWS:], slow_far)
 
     wt_buf[0:7] = jnp.zeros((7, BS, 2 * AW), jnp.bfloat16)
     wt_buf[33:] = jnp.zeros((WCOLS - 33, BS, 2 * AW), jnp.bfloat16)
@@ -288,15 +290,21 @@
     return pl.ds(pl.multiple_of(tile * LANES, LANES), width)
 
 
-def mine_kernel(slow, wt_slow, inner, low, high, far_fast, out, far):
+def far_kernel(slow, wt_slow, far_fast, far):
     def step(tile, width):
         lanes = tile_lanes(tile, width)
-        outer = tile_dot(slow, wt_slow, tile, width)
-        near = outer[:FIRST] + inner[:, :, lanes].astype(jnp.float32)
+        value = tile_dot(slow, wt_slow, tile, width) + far_fast[:, :, lanes].astype(jnp.float32)
+        far[:, :, lanes] = value.astype(jnp.bfloat16)
+
+    each_tile(step)
+
+
+def mine_kernel(slow, wt_slow, inner, low, high, out):
+    def step(tile, width):
+        lanes = tile_lanes(tile, width)
+        near = tile_dot(slow, wt_slow, tile, width) + inner[:, :, lanes].astype(jnp.float32)
         out[:NC, :, lanes] = near[:NC] + low[:, :, lanes].astype(jnp.float32)
         out[NC:, :, lanes] = near[NC:] + high[:, :, lanes].astype(jnp.float32)
-        tail = outer[FIRST:] + far_fast[:, :, lanes].astype(jnp.float32)
-        far[:, :, lanes] = tail.astype(jnp.bfloat16)
 
     each_tile(step)
 
@@ -338,7 +346,7 @@
         lanes = tile_lanes(tile, width)
         value = tile_dot(other, wt_other, tile, width) + mine[:, :, lanes]
         relay[:, :, lanes] = value[:NC].astype(jnp.bfloat16)
-        direct[:, :, lanes] = value[NC:].astype(jnp.bfloat16)
+        direct[:, :, lanes] = value[NC:]
 
     each_tile(step)
 
@@ -367,14 +375,14 @@
         copy.wait()
 
 
-def merge_kernel(core, rows, relay, out, frame):
+def merge_kernel(core, rows, other, out, frame):
     s, x = places(core)
     step = 6 * BS
     for j in range(NC):
         frame[...] = jnp.zeros_like(frame)
         frame[:, pl.ds(pl.multiple_of(step * x, step), WINDOW * BS)] = rows[j]
         lanes = pl.ds(pl.multiple_of(step * (1 - x), step), WINDOW * BS)
-        frame[:, lanes] += relay[j].astype(jnp.float32)
+        frame[:, lanes] += other[j].astype(jnp.float32)
         out[j] = frame[...].astype(jnp.bfloat16)
 
 
@@ -382,9 +390,9 @@
     odd = (j + 1 - s) % 2
     frame[...] = jnp.zeros_like(frame)
     for message, start in messages:
-        lane = pl.multiple_of((start - odd + 6) * BS, 2 * BS)
+        lane = pl.multiple_of((start - odd + 8) * BS, 2 * BS)
         frame[:, pl.ds(lane, message.shape[2])] += message[j].astype(jnp.float32)
-    first, last = 6 * BS, (6 + BAND) * BS
+    first, last = 8 * BS, (8 + BAND) * BS
 
     @pl.when(odd == 0)
     def _():
@@ -400,7 +408,7 @@
     for j in range(NC):
         top = 27 - 3 * s - j
         far_start = jnp.where(s == 1, 30 - j, -3 - j)
-        messages = [(own, top - 12), (direct, top - 24 * x), (pair, top - 6 - 12 * x)]
+        messages = [(own, top - 12), (direct, top - 30 * x), (pair, top - 6 - 12 * x)]
         messages.append((far, far_start))
 
         def store(value, j=j):
@@ -526,8 +534,9 @@
         block(FIRST, span),
         block(REST, span),
         block(REST, 2 * AW),
-        block(FIRST + NC, AW),
+        block(FIRST, AW),
         block(REST, AW),
+        block(NC, AW),
         block(FIRST, AW),
         block(REST, AW),
         block(WCOLS, 2 * AW),
@@ -543,6 +552,7 @@
         fast_rest,
         slow_first,
         slow_rest,
+        slow_far,
         other_first,
         other_rest,
         wt_fast,
@@ -607,33 +617,58 @@
     wt_other = permuted(wt_slow, inward)
 
     wt_slow, low, high = lax.optimization_barrier((wt_slow, low, high))
-    wt_slow, send_rest, other_rest = lax.optimization_barrier((wt_slow, send_rest, other_rest))
-    mine, far = pl.pallas_call(
+    far = pl.pallas_call(
+        far_kernel,
+        out_shape=block(NC, span),
+        in_specs=[vmem] * 3,
+        out_specs=vmem,
+        compiler_params=params(16),
+        cost_estimate=cost(10**9, 10**7),
+        name="far",
+    )(slow_far, wt_slow, far)
+    far, wt_slow = lax.optimization_barrier((far, wt_slow))
+    mine = pl.pallas_call(
         mine_kernel,
-        out_shape=[block(FIRST, span, jnp.float32), block(NC, span)],
-        in_specs=[vmem] * 6,
-        out_specs=[vmem] * 2,
+        out_shape=block(FIRST, span, jnp.float32),
+        in_specs=[vmem] * 5,
+        out_specs=vmem,
         compiler_params=params(24),
         cost_estimate=cost(10**10, 100 * 10**6),
         name="mine",
-    )(slow_first, wt_slow, inner, low, high, far)
-    mine, wt_other, send_rest, other_rest = lax.optimization_barrier(
-        (mine, wt_other, send_rest, other_rest)
+    )(slow_first, wt_slow, inner, low, high)
+    crossing = [i for i in range(devices) if i % 4 in (1, 2)]
+    far_near = permuted(far, [(i, i ^ 3) for i in crossing])
+    relay, direct = pl.pallas_call(
+        join_first_kernel,
+        out_shape=[block(NC, span), block(NC, span, jnp.float32)],
+        in_specs=[vmem] * 3,
+        out_specs=[vmem] * 2,
+        compiler_params=params(16),
+        cost_estimate=cost(10**6, 10**5),
+        name="join_first",
+    )(other_first, wt_other, mine)
+    relay, direct, send_rest, other_rest = lax.optimization_barrier(
+        (relay, direct, send_rest, other_rest)
     )
     arrived_rest = permuted(send_rest, inward)
     other_rest = permuted(other_rest, inward)
-    relay, direct = pl.pallas_call(
-        join_first_kernel,
-        out_shape=[block(NC, span)] * 2,
-        in_specs=[vmem] * 3,
-        out_specs=[vmem] * 2,
-        compiler_params=params(16),
-        cost_estimate=cost(3 * 10**9, 10**7),
-        name="join_first",
-    )(other_first, wt_other, mine)
     along_x = [(i, i ^ 2) for i in range(devices)]
     x_sign = [1 if i // 2 % 2 else -1 for i in range(devices)]
     relay = permuted(relay, along_x)
+
+    def merge_rows(rows, other, name):
+        return pl.pallas_call(
+            merge_kernel,
+            out_shape=block(NC, MERGED * BS),
+            in_specs=[smem, vmem, vmem],
+            out_specs=vmem,
+            scratch_shapes=[pltpu.VMEM((BS, MERGED * BS), jnp.float32)],
+            compiler_params=params(16),
+            cost_estimate=cost(10**7, 10**7),
+            name=name,
+        )(core, rows, other)
+
+    direct = merge_rows(direct, far_near, "merge_far")
     direct = permuted(direct, [(i, (i + 4 * x_sign[i]) % devices) for i in range(devices)])
     merge, pair, own = pl.pallas_call(
         join_rest_kernel,
@@ -646,19 +681,11 @@
     )(fast_rest, slow_rest, other_rest, wt_fast, wt_slow, wt_other, arrived_rest)
     relay, pair, far = lax.optimization_barrier((relay, pair, far))
     relay_in, direct = lax.optimization_barrier((relay, direct))
-    merged = pl.pallas_call(
-        merge_kernel,
-        out_shape=block(NC, MERGED * BS),
-        in_specs=[smem, vmem, vmem],
-        out_specs=vmem,
-        scratch_shapes=[pltpu.VMEM((BS, MERGED * BS), jnp.float32)],
-        compiler_params=params(16),
-        cost_estimate=cost(10**7, 10**7),
-        name="merge",
-    )(core, merge, relay_in)
+    merged = merge_rows(merge, relay_in, "merge")
     merged = permuted(merged, [(i, (i - 4 * x_sign[i]) % devices) for i in range(devices)])
     pair = permuted(pair, along_x)
-    far = permuted(far, [(i, (i + (5 if i % 2 else -5)) % devices) for i in range(devices)])
+    straight = [i for i in range(devices) if i % 4 in (0, 3)]
+    far = permuted(far, [(i, (i + (5 if i % 2 else -5)) % devices) for i in straight])
 
     total = block(NC, BAND * BS, jnp.float32)
     frame = pltpu.VMEM((BS, FRAME * BS), jnp.float32)

time: 152 us -> 146 us (0.961)
  waiting for transfers between devices: 64.2 us -> 50.9 us
  starting transfers between devices: 18 us -> 22.4 us
  Pallas kernels: 63.4 us -> 66.1 us
    ppermute x15 -> x16, waiting for transfers between devices: 64.2 us -> 50.9 us  [permuted(): return lax.ppermute(block, 'dom', pairs)]
    ppermute x15 -> x16, starting transfers between devices: 18 us -> 22.4 us  [permuted(): return lax.ppermute(block, 'dom', pairs)]
    pallas_call x3 -> x5, Pallas kernels: 7.17 us -> 9.84 us  [the longest x1 2.94 us: body(): pl.pallas_call(join_first_kernel, out_shape=[block(NC, span), block(NC, s...]
    unnamed x26 -> x28, local copies, waits for them, and re-layouts: 3.31 us -> 3.32 us
  transfers between devices with their start and end apart: 15 -> 16, of which waited for: 6 -> 4; matrix products, arithmetic and copies ran while one was open for 2% -> 2% of each run, Pallas kernels for 35% -> 36%
where the time goes in v8:
time: 146 us
  Pallas kernels  66.1 us (45%)
  waiting for transfers between devices  50.9 us (35%)
  starting transfers between devices  22.4 us (15%)
  local copies, waits for them, and re-layouts  3.59 us (2%)
  other arithmetic  2.49 us (2%)
    ppermute x16, waiting for transfers between devices, permuted(): return lax.ppermute(block, 'dom', pairs)  50.9 us
    pallas_call x1, Pallas kernels, body(): pl.pallas_call(fast_kernel, out_shape=outs, in_specs=[smem] * 4 + [hbm, h...  35.7 us
    ppermute x16, starting transfers between devices, permuted(): return lax.ppermute(block, 'dom', pairs)  22.4 us
    pallas_call x1, Pallas kernels, body(): pl.pallas_call(join_rest_kernel, out_shape=[block(NC, span, jnp.float32),...  8.11 us
    pallas_call x1, Pallas kernels, body(): pl.pallas_call(slow_kernel, out_shape=block(WCOLS, AW), in_specs=[smem] *...  4.24 us
    unnamed x28, local copies, waits for them, and re-layouts  3.32 us
    pallas_call x1, Pallas kernels, body(): pl.pallas_call(pick_kernel, out_shape=[edge, edge], in_specs=[smem, hbm],...  3.08 us
    pallas_call x1, Pallas kernels, body(): pl.pallas_call(join_first_kernel, out_shape=[block(NC, span), block(NC, s...  2.94 us
  transfers between devices with their start and end apart: 16, of which 4 were waited for; matrix products, arithmetic and copies ran while one was open for 2% of the time, Pallas kernels for 36%

profile of v8, /device:TPU:0, one launch (start us, length us, event | category | flops | bytes accessed | tf_op | source)
XLA Modules:
  0.0 146.0 jit_solution(620456937144746786)
XLA Ops:
  0.0 3.1 %pick.1 = (bf16[8,64,1728]{2,1,0:T(8,128)(2,1)}, bf16[8,64,1728]{2,1,0:T(8,128)(2,1)}) custom-call(s32[1]{0:T(128)} %bitcast.core, bf16[24,64,1728]{2,1,0:T(8,128)(2,1)} %p_own.1), custom_call_target="tpu_custom_call" | custom-call | tf_op jit(solution)/shard_map/pick/pallas_call | solution.py:492
  3.2 6.4 %collective-permute-start.1 = (s32[8,27]{1,0:T(8,128)S(1)}, s32[8,27]{1,0:T(8,128)S(1)}, u32[]{:S(2)}, u32[]{:S(2)}) collective-permute-start(s32[8,27]{1,0:T(8,128)S(1)} %get-tuple-element.99), channel_id=1, source_target_pairs={{0,31},{1,2},{2,1},{3,4},{4,3},{5,6},{6,5},{7,8},{8,7},{9,10},{10,... | collective-permute-start | bytes 2600 | tf_op jit(solution)/shard_map/ppermute | solution.py:458
  9.6 0.5 collective-permute-start.2
  10.1 0.3 collective-permute-start.3
  10.4 0.1 fusion.1
  10.5 0.1 copy.15
  10.6 0.1 select_reduce_fusion.3
  10.8 0.2 select_reduce_fusion
  10.9 0.6 broadcast_add_fusion.inv_a
  11.5 0.6 broadcast_add_fusion.1.inv_own
  12.1 0.0 collective-permute-done.1
  12.2 0.1 copy.17
  12.3 0.1 copy.16
  12.4 0.1 select_reduce_fusion.1
  12.5 0.1 select_reduce_fusion.2
  12.6 0.6 broadcast_add_fusion.3.inv_fast
  13.2 0.6 collective-permute-done.2.p_fast
  13.9 35.7 %fast.1 = (bf16[3,64,2432]{2,1,0:T(8,128)(2,1)}, bf16[3,64,2432]{2,1,0:T(8,128)(2,1)}, bf16[3,64,2432]{2,1,0:T(8,128)(2,1)}, bf16[6,64,2432]{2,1,0:T(8,128)(2,1)...) custom-call(s32[1]{0:T(128)} %bitcast.core, ...), custom_call_target="tpu_custom_call" | custom-call | flops 20000000000 | bytes 30000000 | tf_op jit(solution)/shard_map/fast/pallas_call | solution.py:561
  49.6 0.4 collective-permute-start.4
  50.0 0.1 collective-permute-start.5
  50.2 0.4 collective-permute-start.6
  50.5 2.2 %copy-done = f32[33,64,512]{2,1,0:T(8,128)S(1)} copy-done((f32[33,64,512]{2,1,0:T(8,128)S(1)}, f32[33,64,512]{2,1,0:T(8,128)}, u32[]{:S(2)}) %copy-start) | copy-done | bytes 4325400
  52.8 1.0 copy-done.2
  53.8 0.5 stage.1
  54.3 0.0 collective-permute-done.6.other
  54.3 0.0 collective-permute-done.4.low
  54.4 4.2 %slow.1.wt_slow = bf16[40,64,512]{2,1,0:T(8,128)(2,1)S(1)} custom-call(s32[1]{0:T(128)} %bitcast.core, s32[8,33]{1,0:T(8,128)S(1)} %broadcast_add_fusion.2.inv_slow, bf16[8,64,1728]{2,1,0:T(8,128)(2,1)S(1)} %collective-permute-done.3.p_slow, bf16[8,64,512]{2,1,0:T(8,128)(2,1)S(1)} %get-tuple-element.67.at_halo, f32[33,64,512]{2,1,0:T(8,128)S(1)} %get-tuple-element.68.rest), custom_call_target="tpu_custom_call" | custom-call | flops 20000000000 | bytes 200000000 | tf_op jit(solution)/shard_map/slow/pallas_call | solution.py:603
  58.6 0.3 collective-permute-start.7
  59.0 2.4 %far.1 = bf16[3,64,2432]{2,1,0:T(8,128)(2,1)S(1)} custom-call(bf16[3,64,512]{2,1,0:T(8,128)(2,1)S(1)} %copy-done.3, bf16[40,64,512]{2,1,0:T(8,128)(2,1)S(1)} %slow.1.wt_slow, bf16[3,64,2432]{2,1,0:T(8,128)(2,1)S(1)} %copy-done.1), custom_call_target="tpu_custom_call" | custom-call | flops 1000000000 | bytes 10000000 | tf_op jit(solution)/shard_map/far/pallas_call | solution.py:620
  61.4 2.9 %mine.1 = f32[6,64,2432]{2,1,0:T(8,128)S(1)} custom-call(bf16[6,64,512]{2,1,0:T(8,128)(2,1)S(1)} %copy-done.5, bf16[40,64,512]{2,1,0:T(8,128)(2,1)S(1)} %slow.1.wt_slow, bf16[6,64,2432]{2,1,0:T(8,128)(2,1)S(1)} %copy-done.4, bf16[3,64,2432]{2,1,0:T(8,128)(2,1)S(1)} %collective-permute-done.4.low, bf16[3,64,2432]{2,1,0:T(8,128)(2,1)S(1)} %collective-permute-done.5.high), custom_call_target="tpu_custom_call" | custom-call | flops 10000000000 | bytes 100000000 | tf_op jit(solution)/shard_map/mine/pallas_call | solution.py:630
  64.4 0.0 copy-start.10
  64.4 0.0 collective-permute-done.7.wt_other
  64.4 2.9 %join_first.1 = (bf16[3,64,2432]{2,1,0:T(8,128)(2,1)S(1)}, f32[3,64,2432]{2,1,0:T(8,128)S(1)}) custom-call(bf16[6,64,512]{2,1,0:T(8,128)(2,1)S(1)} %collective-permute-done.6.other, bf16[40,64,512]{2,1,0:T(8,128)(2,1)S(1)} %collective-permute-done.7.wt_other, f32[6,64,2432]{2,1,0:T(8,128)S(1)} %mine.1), custom_call_target="tpu_custom_call" | custom-call | flops 1000000 | bytes 100000 | tf_op jit(solution)/shard_map/join_first/pallas_call | solution.py:641
  67.4 0.3 collective-permute-start.9
  67.6 0.8 collective-permute-start.11
  68.5 2.0 %collective-permute-start.8 = (bf16[9,64,512]{2,1,0:T(8,128)(2,1)S(1)}, bf16[9,64,512]{2,1,0:T(8,128)(2,1)S(1)}, u32[]{:S(2)}, u32[]{:S(2)}) collective-permute-start(bf16[9,64,512]{2,1,0:T(8,128)(2,1)S(1)} %copy-done.11), channel_id=1, source_target_pairs={{0,1},{1,0},{2,3},{3,2},{4,5},{5,4},{6,7},{7,6},{8,9},{9,8},{10,11... | collective-permute-start | bytes 1769480 | tf_op jit(solution)/shard_map/ppermute | solution.py:458
  70.5 1.3 collective-permute-start.10
  71.8 0.8 merge_far.1
  72.6 3.1 %collective-permute-start.12 = (bf16[3,64,2816]{2,1,0:T(8,128)(2,1)S(1)}, bf16[3,64,2816]{2,1,0:T(8,128)(2,1)S(1)}, u32[]{:S(2)}, u32[]{:S(2)}) collective-permute-start(bf16[3,64,2816]{2,1,0:T(8,128)(2,1)S(1)} %merge_far.1), channel_id=1, source_target_pairs={{0,28},{1,29},{2,6},{3,7},{4,0},{5,1},{6,10},{7,11},{8,4},{9,5},{1... | collective-permute-start | bytes 3244040 | tf_op jit(solution)/shard_map/ppermute | solution.py:458
  75.7 8.1 %join_rest.1 = (f32[3,64,2432]{2,1,0:T(8,128)S(1)}, bf16[3,64,2432]{2,1,0:T(8,128)(2,1)S(1)}, f32[3,64,2432]{2,1,0:T(8,128)S(1)}) custom-call(bf16[9,64,1024]{2,1,0:T(8,128)(2,1)S(1)} %copy-done.6, bf16[9,64,512]{2,1,0:T(8,128)(2,1)S(1)} %copy-done.7, bf16[9,64,512]{2,1,0:T(8,128)(2,1)S(1)} %collective-permute-done.8.other, ...), custom_call_target="tpu_custom_call" | custom-call | flops 40000000000 | bytes 200000000 | tf_op jit(solution)/shard_map/join_rest/pallas_call | solution.py:673
  83.9 19.3 %collective-permute-done.10.other = bf16[3,64,2432]{2,1,0:T(8,128)(2,1)S(1)} collective-permute-done((bf16[3,64,2432]{2,1,0:T(8,128)(2,1)S(1)}, bf16[3,64,2432]{2,1,0:T(8,128)(2,1)S(1)}, u32[]{:S(2)}, u32[]{:S(2)}) %collective-permute-start.10) | collective-permute-done | bytes 933920 | tf_op jit(solution)/shard_map/ppermute | solution.py:458
  103.1 2.9 %collective-permute-start.14 = (bf16[3,64,2432]{2,1,0:T(8,128)(2,1)S(1)}, bf16[3,64,2432]{2,1,0:T(8,128)(2,1)S(1)}, u32[]{:S(2)}, u32[]{:S(2)}) collective-permute-start(bf16[3,64,2432]{2,1,0:T(8,128)(2,1)S(1)} %far.1), channel_id=1, source_target_pairs={{0,27},{3,8},{4,31},{7,12},{8,3},{11,16},{12,7},{15,20},{16,11},{1... | collective-permute-start | bytes 2801672 | tf_op jit(solution)/shard_map/ppermute | solution.py:458
  106.0 0.8 merge.1
  106.8 3.5 %collective-permute-start.15 = (bf16[3,64,2816]{2,1,0:T(8,128)(2,1)S(1)}, bf16[3,64,2816]{2,1,0:T(8,128)(2,1)S(1)}, u32[]{:S(2)}, u32[]{:S(2)}) collective-permute-start(bf16[3,64,2816]{2,1,0:T(8,128)(2,1)S(1)} %merge.1), channel_id=1, source_target_pairs={{0,4},{1,5},{2,30},{3,31},{4,8},{5,9},{6,2},{7,3},{8,12},{9,13},{1... | collective-permute-start | bytes 3244040 | tf_op jit(solution)/shard_map/ppermute | solution.py:458
  110.3 25.7 %collective-permute-done.13.pair = bf16[3,64,2432]{2,1,0:T(8,128)(2,1)S(1)} collective-permute-done((bf16[3,64,2432]{2,1,0:T(8,128)(2,1)S(1)}, bf16[3,64,2432]{2,1,0:T(8,128)(2,1)S(1)}, u32[]{:S(2)}, u32[]{:S(2)}) %collective-permute-start.13) | collective-permute-done | bytes 933920 | tf_op jit(solution)/shard_map/ppermute | solution.py:458
  136.0 1.8 %early.1 = f32[3,64,4032]{2,1,0:T(8,128)S(1)} custom-call(s32[1]{0:T(128)} %bitcast.core, f32[3,64,2432]{2,1,0:T(8,128)S(1)} %get-tuple-element.86.own, bf16[3,64,2816]{2,1,0:T(8,128)(2,1)S(1)} %collective-permute-done.12.direct, bf16[3,64,2432]{2,1,0:T(8,128)(2,1)S(1)} %collective-permute-done.13.pair, bf16[3,64,2432]{2,1,0:T(8,128)(2,1)S(1)} %collective-permute-done.14.far), custom_call_target="tpu_custom_call" | custom-call | flops 10000000000 | bytes 100000000 | tf_op jit(solution)/shard_map/early/pallas_call | solution.py:692
  137.9 5.2 %collective-permute-done.15.merged = bf16[3,64,2816]{2,1,0:T(8,128)(2,1)S(1)} collective-permute-done((bf16[3,64,2816]{2,1,0:T(8,128)(2,1)S(1)}, bf16[3,64,2816]{2,1,0:T(8,128)(2,1)S(1)}, u32[]{:S(2)}, u32[]{:S(2)}) %collective-permute-start.15) | collective-permute-done | bytes 1081376 | tf_op jit(solution)/shard_map/ppermute | solution.py:458
  143.1 2.8 %total.1 = f32[3,64,4032]{2,1,0:T(8,128)} custom-call(s32[1]{0:T(128)} %bitcast.core, f32[3,64,4032]{2,1,0:T(8,128)S(1)} %early.1, bf16[3,64,2816]{2,1,0:T(8,128)(2,1)S(1)} %collective-permute-done.15.merged), custom_call_target="tpu_custom_call" | custom-call | flops 10000000 | bytes 10000000 | tf_op jit(solution)/shard_map/total/pallas_call | solution.py:702
  (46 shorter events, 0.2 us)
Async XLA Ops:
  0.0 3.1 %copy-start.8 = (s32[24,27]{1,0:T(8,128)S(1)}, s32[24,27]{1,0:T(8,128)}, u32[]{:S(2)}) copy-start(s32[24,27]{1,0:T(8,128)} %param.7) | copy-start | bytes 7780
  0.0 10.6 %copy-start.9 = (s32[24,7]{0,1:T(8,128)S(1)}, s32[24,7]{0,1:T(8,128)}, u32[]{:S(2)}) copy-start(s32[24,7]{0,1:T(8,128)} %param.6) | copy-start | bytes 2020
  3.2 9.0 %collective-permute-start.1 = (s32[8,27]{1,0:T(8,128)S(1)}, s32[8,27]{1,0:T(8,128)S(1)}, u32[]{:S(2)}, u32[]{:S(2)}) collective-permute-start(s32[8,27]{1,0:T(8,128)S(1)} %get-tuple-element.99), channel_id=1, source_target_pairs={{0,31},{1,2},{2,1},{3,4},{4,3},{5,6},{6,5},{7,8},{8,7},{9,10},{10,... | collective-permute-start | bytes 2600 | tf_op jit(solution)/shard_map/ppermute | solution.py:458
  9.6 2.7 %collective-permute-start = (s32[8,27]{1,0:T(8,128)S(1)}, s32[8,27]{1,0:T(8,128)S(1)}, u32[]{:S(2)}, u32[]{:S(2)}) collective-permute-start(s32[8,27]{1,0:T(8,128)S(1)} %get-tuple-element.100), channel_id=1, source_target_pairs={{0,1},{1,0},{2,3},{3,2},{4,5},{5,4},{6,7},{7,6},{8,9},{9,8},{10,11... | collective-permute-start | bytes 2600 | tf_op jit(solution)/shard_map/ppermute | solution.py:458
  9.6 4.3 %collective-permute-start.2 = (bf16[8,64,1728]{2,1,0:T(8,128)(2,1)}, bf16[8,64,1728]{2,1,0:T(8,128)(2,1)}, u32[]{:S(2)}, u32[]{:S(2)}) collective-permute-start(bf16[8,64,1728]{2,1,0:T(8,128)(2,1)} %get-tuple-element.55), channel_id=1, source_target_pairs={{0,1},{1,0},{2,3},{3,2},{4,5},{5,4},{6,7},{7,6},{8,9},{9,8},{10,11... | collective-permute-start | bytes 5308424 | tf_op jit(solution)/shard_map/ppermute | solution.py:458
  10.1 44.2 %collective-permute-start.3 = (bf16[8,64,1728]{2,1,0:T(8,128)(2,1)}, bf16[8,64,1728]{2,1,0:T(8,128)(2,1)S(1)}, u32[]{:S(2)}, u32[]{:S(2)}) collective-permute-start(bf16[8,64,1728]{2,1,0:T(8,128)(2,1)} %get-tuple-element.58), channel_id=1, source_target_pairs={{0,31},{1,2},{2,1},{3,4},{4,3},{5,6},{6,5},{7,8},{8,7},{9,10},{10,... | collective-permute-start | bytes 5308424 | tf_op jit(solution)/shard_map/ppermute | solution.py:458
  49.6 4.8 %collective-permute-start.4 = (bf16[3,64,2432]{2,1,0:T(8,128)(2,1)}, bf16[3,64,2432]{2,1,0:T(8,128)(2,1)S(1)}, u32[]{:S(2)}, u32[]{:S(2)}) collective-permute-start(bf16[3,64,2432]{2,1,0:T(8,128)(2,1)} %get-tuple-element.59), channel_id=1, source_target_pairs={{0,1},{1,0},{2,3},{3,2},{4,5},{5,4},{6,7},{7,6},{8,9},{9,8},{10,11... | collective-permute-start | bytes 2801672 | tf_op jit(solution)/shard_map/ppermute | solution.py:458
  50.0 4.3 %collective-permute-start.5 = (bf16[3,64,2432]{2,1,0:T(8,128)(2,1)}, bf16[3,64,2432]{2,1,0:T(8,128)(2,1)S(1)}, u32[]{:S(2)}, u32[]{:S(2)}) collective-permute-start(bf16[3,64,2432]{2,1,0:T(8,128)(2,1)} %get-tuple-element.60), channel_id=1, source_target_pairs={{0,1},{1,0},{2,3},{3,2},{4,5},{5,4},{6,7},{7,6},{8,9},{9,8},{10,11... | collective-permute-start | bytes 2801672 | tf_op jit(solution)/shard_map/ppermute | solution.py:458
  50.2 4.2 %collective-permute-start.6 = (bf16[6,64,512]{2,1,0:T(8,128)(2,1)}, bf16[6,64,512]{2,1,0:T(8,128)(2,1)S(1)}, u32[]{:S(2)}, u32[]{:S(2)}) collective-permute-start(bf16[6,64,512]{2,1,0:T(8,128)(2,1)} %get-tuple-element.61), channel_id=1, source_target_pairs={{0,1},{1,0},{2,3},{3,2},{4,5},{5,4},{6,7},{7,6},{8,9},{9,8},{10,11... | collective-permute-start | bytes 1179656 | tf_op jit(solution)/shard_map/ppermute | solution.py:458
  50.5 2.2 %copy-start = (f32[33,64,512]{2,1,0:T(8,128)S(1)}, f32[33,64,512]{2,1,0:T(8,128)}, u32[]{:S(2)}) copy-start(f32[33,64,512]{2,1,0:T(8,128)} %get-tuple-element.66.rest) | copy-start | bytes 12976132
  52.8 1.0 copy-start.2
  54.4 4.6 %copy-start.1 = (bf16[3,64,2432]{2,1,0:T(8,128)(2,1)S(1)}, bf16[3,64,2432]{2,1,0:T(8,128)(2,1)}, u32[]{:S(2)}) copy-start(bf16[3,64,2432]{2,1,0:T(8,128)(2,1)} %get-tuple-element.74.far_fast) | copy-start | bytes 2801668
  54.4 4.6 %copy-start.3 = (bf16[3,64,512]{2,1,0:T(8,128)(2,1)S(1)}, bf16[3,64,512]{2,1,0:T(8,128)(2,1)}, u32[]{:S(2)}) copy-start(bf16[3,64,512]{2,1,0:T(8,128)(2,1)} %get-tuple-element.70.slow) | copy-start | bytes 589828
  54.4 7.0 %copy-start.5 = (bf16[6,64,512]{2,1,0:T(8,128)(2,1)S(1)}, bf16[6,64,512]{2,1,0:T(8,128)(2,1)}, u32[]{:S(2)}) copy-start(bf16[6,64,512]{2,1,0:T(8,128)(2,1)} %get-tuple-element.69.slow) | copy-start | bytes 1179652
  58.6 5.7 %collective-permute-start.7 = (bf16[40,64,512]{2,1,0:T(8,128)(2,1)S(1)}, bf16[40,64,512]{2,1,0:T(8,128)(2,1)S(1)}, u32[]{:S(2)}, u32[]{:S(2)}) collective-permute-start(bf16[40,64,512]{2,1,0:T(8,128)(2,1)S(1)} %slow.1.wt_slow), channel_id=1, source_target_pairs={{0,1},{1,0},{2,3},{3,2},{4,5},{5,4},{6,7},{7,6},{8,9},{9,8},{10,11... | collective-permute-start | bytes 7864328 | tf_op jit(solution)/shard_map/ppermute | solution.py:458
  59.0 2.4 %copy-start.4 = (bf16[6,64,2432]{2,1,0:T(8,128)(2,1)S(1)}, bf16[6,64,2432]{2,1,0:T(8,128)(2,1)}, u32[]{:S(2)}) copy-start(bf16[6,64,2432]{2,1,0:T(8,128)(2,1)} %get-tuple-element.76.inner) | copy-start | bytes 5603332
  59.0 16.7 %slice-start = ((s8[5242880]{0:T(1024)(128)(4,1)}), s8[4194304]{0:T(1024)(128)(4,1)S(1)}, s32[]{:S(2)}) async-start(s8[5242880]{0:T(1024)(128)(4,1)} %bitcast.9), calls=%async_computation | async-start | bytes 8388608
  61.4 14.3 %slice-start.1 = ((s8[5242880]{0:T(1024)(128)(4,1)}), s8[1048576]{0:T(1024)(128)(4,1)S(1)}, s32[]{:S(2)}) async-start(s8[5242880]{0:T(1024)(128)(4,1)} %bitcast.9), calls=%async_computation.1 | async-start | bytes 2097152
  64.4 3.0 %copy-start.10 = (bf16[9,64,2432]{2,1,0:T(8,128)(2,1)S(1)}, bf16[9,64,2432]{2,1,0:T(8,128)(2,1)}, u32[]{:S(2)}) copy-start(bf16[9,64,2432]{2,1,0:T(8,128)(2,1)} %get-tuple-element.85) | copy-start | bytes 8404996
  64.4 4.1 %copy-start.11 = (bf16[9,64,512]{2,1,0:T(8,128)(2,1)S(1)}, bf16[9,64,512]{2,1,0:T(8,128)(2,1)}, u32[]{:S(2)}) copy-start(bf16[9,64,512]{2,1,0:T(8,128)(2,1)} %get-tuple-element.83) | copy-start | bytes 1769476
  67.3 8.4 %copy-start.6 = (bf16[9,64,1024]{2,1,0:T(8,128)(2,1)S(1)}, bf16[9,64,1024]{2,1,0:T(8,128)(2,1)}, u32[]{:S(2)}) copy-start(bf16[9,64,1024]{2,1,0:T(8,128)(2,1)} %get-tuple-element.56.fast) | copy-start | bytes 3538948
  67.3 8.4 %copy-start.7 = (bf16[9,64,512]{2,1,0:T(8,128)(2,1)S(1)}, bf16[9,64,512]{2,1,0:T(8,128)(2,1)}, u32[]{:S(2)}) copy-start(bf16[9,64,512]{2,1,0:T(8,128)(2,1)} %get-tuple-element.57.slow) | copy-start | bytes 1769476
  67.4 8.3 %collective-permute-start.9 = (bf16[9,64,2432]{2,1,0:T(8,128)(2,1)S(1)}, bf16[9,64,2432]{2,1,0:T(8,128)(2,1)S(1)}, u32[]{:S(2)}, u32[]{:S(2)}) collective-permute-start(bf16[9,64,2432]{2,1,0:T(8,128)(2,1)S(1)} %copy-done.10), channel_id=1, source_target_pairs={{0,1},{1,0},{2,3},{3,2},{4,5},{5,4},{6,7},{7,6},{8,9},{9,8},{10,11... | collective-permute-start | bytes 8405000 | tf_op jit(solution)/shard_map/ppermute | solution.py:458
  67.6 4.1 %collective-permute-start.11 = (bf16[3,64,2432]{2,1,0:T(8,128)(2,1)S(1)}, bf16[3,64,2432]{2,1,0:T(8,128)(2,1)S(1)}, u32[]{:S(2)}, u32[]{:S(2)}) collective-permute-start(bf16[3,64,2432]{2,1,0:T(8,128)(2,1)S(1)} %far.1), channel_id=1, source_target_pairs={{1,2},{2,1},{5,6},{6,5},{9,10},{10,9},{13,14},{14,13},{17,18},{18,... | collective-permute-start | bytes 2801672 | tf_op jit(solution)/shard_map/ppermute | solution.py:458
  68.5 7.2 %collective-permute-start.8 = (bf16[9,64,512]{2,1,0:T(8,128)(2,1)S(1)}, bf16[9,64,512]{2,1,0:T(8,128)(2,1)S(1)}, u32[]{:S(2)}, u32[]{:S(2)}) collective-permute-start(bf16[9,64,512]{2,1,0:T(8,128)(2,1)S(1)} %copy-done.11), channel_id=1, source_target_pairs={{0,1},{1,0},{2,3},{3,2},{4,5},{5,4},{6,7},{7,6},{8,9},{9,8},{10,11... | collective-permute-start | bytes 1769480 | tf_op jit(solution)/shard_map/ppermute | solution.py:458
  70.5 32.7 %collective-permute-start.10 = (bf16[3,64,2432]{2,1,0:T(8,128)(2,1)S(1)}, bf16[3,64,2432]{2,1,0:T(8,128)(2,1)S(1)}, u32[]{:S(2)}, u32[]{:S(2)}) collective-permute-start(bf16[3,64,2432]{2,1,0:T(8,128)(2,1)S(1)} %get-tuple-element.87), channel_id=1, source_target_pairs={{0,2},{1,3},{2,0},{3,1},{4,6},{5,7},{6,4},{7,5},{8,10},{9,11},{10,... | collective-permute-start | bytes 2801672 | tf_op jit(solution)/shard_map/ppermute | solution.py:458
  72.6 33.5 %collective-permute-start.12 = (bf16[3,64,2816]{2,1,0:T(8,128)(2,1)S(1)}, bf16[3,64,2816]{2,1,0:T(8,128)(2,1)S(1)}, u32[]{:S(2)}, u32[]{:S(2)}) collective-permute-start(bf16[3,64,2816]{2,1,0:T(8,128)(2,1)S(1)} %merge_far.1), channel_id=1, source_target_pairs={{0,28},{1,29},{2,6},{3,7},{4,0},{5,1},{6,10},{7,11},{8,4},{9,5},{1... | collective-permute-start | bytes 3244040 | tf_op jit(solution)/shard_map/ppermute | solution.py:458
  103.1 32.9 %collective-permute-start.13 = (bf16[3,64,2432]{2,1,0:T(8,128)(2,1)S(1)}, bf16[3,64,2432]{2,1,0:T(8,128)(2,1)S(1)}, u32[]{:S(2)}, u32[]{:S(2)}) collective-permute-start(bf16[3,64,2432]{2,1,0:T(8,128)(2,1)S(1)} %get-tuple-element.93), channel_id=1, source_target_pairs={{0,2},{1,3},{2,0},{3,1},{4,6},{5,7},{6,4},{7,5},{8,10},{9,11},{10,... | collective-permute-start | bytes 2801672 | tf_op jit(solution)/shard_map/ppermute | solution.py:458
  103.1 32.9 %collective-permute-start.14 = (bf16[3,64,2432]{2,1,0:T(8,128)(2,1)S(1)}, bf16[3,64,2432]{2,1,0:T(8,128)(2,1)S(1)}, u32[]{:S(2)}, u32[]{:S(2)}) collective-permute-start(bf16[3,64,2432]{2,1,0:T(8,128)(2,1)S(1)} %far.1), channel_id=1, source_target_pairs={{0,27},{3,8},{4,31},{7,12},{8,3},{11,16},{12,7},{15,20},{16,11},{1... | collective-permute-start | bytes 2801672 | tf_op jit(solution)/shard_map/ppermute | solution.py:458
  106.8 36.3 %collective-permute-start.15 = (bf16[3,64,2816]{2,1,0:T(8,128)(2,1)S(1)}, bf16[3,64,2816]{2,1,0:T(8,128)(2,1)S(1)}, u32[]{:S(2)}, u32[]{:S(2)}) collective-permute-start(bf16[3,64,2816]{2,1,0:T(8,128)(2,1)S(1)} %merge.1), channel_id=1, source_target_pairs={{0,4},{1,5},{2,30},{3,31},{4,8},{5,9},{6,2},{7,3},{8,12},{9,13},{1... | collective-permute-start | bytes 3244040 | tf_op jit(solution)/shard_map/ppermute | solution.py:458

commit v9 on v8

--- a/solution.py
+++ b/solution.py
@@ -647,8 +647,8 @@
         cost_estimate=cost(10**6, 10**5),
         name="join_first",
     )(other_first, wt_other, mine)
-    relay, direct, send_rest, other_rest = lax.optimization_barrier(
-        (relay, direct, send_rest, other_rest)
+    relay, direct, far_near, send_rest, other_rest = lax.optimization_barrier(
+        (relay, direct, far_near, send_rest, other_rest)
     )
     arrived_rest = permuted(send_rest, inward)
     other_rest = permuted(other_rest, inward)

time: 146 us -> 144 us (0.986)
  waiting for transfers between devices: 50.9 us -> 44.5 us
  starting transfers between devices: 22.4 us -> 26.9 us
    ppermute x16, waiting for transfers between devices: 50.9 us -> 44.5 us  [permuted(): return lax.ppermute(block, 'dom', pairs)]
    ppermute x16, starting transfers between devices: 22.4 us -> 26.9 us  [permuted(): return lax.ppermute(block, 'dom', pairs)]
  transfers between devices with their start and end apart: 16 -> 16, of which waited for: 4 -> 5; matrix products, arithmetic and copies ran while one was open for 2% -> 2% of each run, Pallas kernels for 36% -> 39%
where the time goes in v9:
time: 144 us
  Pallas kernels  66.1 us (46%)
  waiting for transfers between devices  44.5 us (31%)
  starting transfers between devices  26.9 us (19%)
  local copies, waits for them, and re-layouts  3.59 us (2%)
  other arithmetic  2.49 us (2%)
    ppermute x16, waiting for transfers between devices, permuted(): return lax.ppermute(block, 'dom', pairs)  44.5 us
    pallas_call x1, Pallas kernels, body(): pl.pallas_call(fast_kernel, out_shape=outs, in_specs=[smem] * 4 + [hbm, h...  35.7 us
    ppermute x16, starting transfers between devices, permuted(): return lax.ppermute(block, 'dom', pairs)  26.9 us
    pallas_call x1, Pallas kernels, body(): pl.pallas_call(join_rest_kernel, out_shape=[block(NC, span, jnp.float32),...  8.11 us
    pallas_call x1, Pallas kernels, body(): pl.pallas_call(slow_kernel, out_shape=block(WCOLS, AW), in_specs=[smem] *...  4.22 us
    unnamed x28, local copies, waits for them, and re-layouts  3.32 us
    pallas_call x1, Pallas kernels, body(): pl.pallas_call(pick_kernel, out_shape=[edge, edge], in_specs=[smem, hbm],...  3.08 us
    pallas_call x1, Pallas kernels, body(): pl.pallas_call(join_first_kernel, out_shape=[block(NC, span), block(NC, s...  2.93 us
  transfers between devices with their start and end apart: 16, of which 5 were waited for; matrix products, arithmetic and copies ran while one was open for 2% of the time, Pallas kernels for 39%

profile of v9, /device:TPU:0, one launch (start us, length us, event | category | flops | bytes accessed | tf_op | source)
XLA Modules:
  0.0 144.1 jit_solution(14287263580024996240)
XLA Ops:
  0.0 3.1 %pick.1 = (bf16[8,64,1728]{2,1,0:T(8,128)(2,1)}, bf16[8,64,1728]{2,1,0:T(8,128)(2,1)}) custom-call(s32[1]{0:T(128)} %bitcast.core, bf16[24,64,1728]{2,1,0:T(8,128)(2,1)} %p_own.1), custom_call_target="tpu_custom_call" | custom-call | tf_op jit(solution)/shard_map/pick/pallas_call | solution.py:492
  3.2 6.4 %collective-permute-start.1 = (s32[8,27]{1,0:T(8,128)S(1)}, s32[8,27]{1,0:T(8,128)S(1)}, u32[]{:S(2)}, u32[]{:S(2)}) collective-permute-start(s32[8,27]{1,0:T(8,128)S(1)} %get-tuple-element.101), channel_id=1, source_target_pairs={{0,31},{1,2},{2,1},{3,4},{4,3},{5,6},{6,5},{7,8},{8,7},{9,10},{10,... | collective-permute-start | bytes 2600 | tf_op jit(solution)/shard_map/ppermute | solution.py:458
  9.6 0.5 collective-permute-start.2
  10.1 0.3 collective-permute-start.3
  10.4 0.1 fusion.1
  10.5 0.1 copy.15
  10.6 0.1 select_reduce_fusion.3
  10.8 0.2 select_reduce_fusion
  10.9 0.6 broadcast_add_fusion.inv_a
  11.5 0.6 broadcast_add_fusion.1.inv_own
  12.1 0.0 collective-permute-done.1
  12.2 0.1 copy.17
  12.3 0.1 copy.16
  12.4 0.1 select_reduce_fusion.1
  12.5 0.1 select_reduce_fusion.2
  12.6 0.6 broadcast_add_fusion.3.inv_fast
  13.2 0.6 collective-permute-done.2.p_fast
  13.9 35.7 %fast.1 = (bf16[3,64,2432]{2,1,0:T(8,128)(2,1)}, bf16[3,64,2432]{2,1,0:T(8,128)(2,1)}, bf16[3,64,2432]{2,1,0:T(8,128)(2,1)}, bf16[6,64,2432]{2,1,0:T(8,128)(2,1)...) custom-call(s32[1]{0:T(128)} %bitcast.core, ...), custom_call_target="tpu_custom_call" | custom-call | flops 20000000000 | bytes 30000000 | tf_op jit(solution)/shard_map/fast/pallas_call | solution.py:561
  49.6 0.4 collective-permute-start.4
  50.0 0.1 collective-permute-start.5
  50.2 0.4 collective-permute-start.6
  50.5 2.2 %copy-done = f32[33,64,512]{2,1,0:T(8,128)S(1)} copy-done((f32[33,64,512]{2,1,0:T(8,128)S(1)}, f32[33,64,512]{2,1,0:T(8,128)}, u32[]{:S(2)}) %copy-start) | copy-done | bytes 4325400
  52.8 1.0 copy-done.2
  53.8 0.5 stage.1
  54.3 0.0 collective-permute-done.6.other
  54.4 4.2 %slow.1.wt_slow = bf16[40,64,512]{2,1,0:T(8,128)(2,1)S(1)} custom-call(s32[1]{0:T(128)} %bitcast.core, s32[8,33]{1,0:T(8,128)S(1)} %broadcast_add_fusion.2.inv_slow, bf16[8,64,1728]{2,1,0:T(8,128)(2,1)S(1)} %collective-permute-done.3.p_slow, bf16[8,64,512]{2,1,0:T(8,128)(2,1)S(1)} %get-tuple-element.68.at_halo, f32[33,64,512]{2,1,0:T(8,128)S(1)} %get-tuple-element.69.rest), custom_call_target="tpu_custom_call" | custom-call | flops 20000000000 | bytes 200000000 | tf_op jit(solution)/shard_map/slow/pallas_call | solution.py:603
  58.6 0.3 collective-permute-start.7
  59.0 2.4 %far.1 = bf16[3,64,2432]{2,1,0:T(8,128)(2,1)S(1)} custom-call(bf16[3,64,512]{2,1,0:T(8,128)(2,1)S(1)} %copy-done.3, bf16[40,64,512]{2,1,0:T(8,128)(2,1)S(1)} %slow.1.wt_slow, bf16[3,64,2432]{2,1,0:T(8,128)(2,1)S(1)} %copy-done.1), custom_call_target="tpu_custom_call" | custom-call | flops 1000000000 | bytes 10000000 | tf_op jit(solution)/shard_map/far/pallas_call | solution.py:620
  61.4 0.7 collective-permute-start.8
  62.1 2.9 %mine.1 = f32[6,64,2432]{2,1,0:T(8,128)S(1)} custom-call(bf16[6,64,512]{2,1,0:T(8,128)(2,1)S(1)} %copy-done.5, bf16[40,64,512]{2,1,0:T(8,128)(2,1)S(1)} %slow.1.wt_slow, bf16[6,64,2432]{2,1,0:T(8,128)(2,1)S(1)} %copy-done.4, bf16[3,64,2432]{2,1,0:T(8,128)(2,1)S(1)} %collective-permute-done.4.low, bf16[3,64,2432]{2,1,0:T(8,128)(2,1)S(1)} %collective-permute-done.5.high), custom_call_target="tpu_custom_call" | custom-call | flops 10000000000 | bytes 100000000 | tf_op jit(solution)/shard_map/mine/pallas_call | solution.py:630
  65.1 0.0 copy-start.10
  65.1 2.9 %join_first.1 = (bf16[3,64,2432]{2,1,0:T(8,128)(2,1)S(1)}, f32[3,64,2432]{2,1,0:T(8,128)S(1)}) custom-call(bf16[6,64,512]{2,1,0:T(8,128)(2,1)S(1)} %collective-permute-done.6.other, bf16[40,64,512]{2,1,0:T(8,128)(2,1)S(1)} %collective-permute-done.7.wt_other, f32[6,64,2432]{2,1,0:T(8,128)S(1)} %mine.1), custom_call_target="tpu_custom_call" | custom-call | flops 1000000 | bytes 100000 | tf_op jit(solution)/shard_map/join_first/pallas_call | solution.py:641
  68.1 8.4 %collective-permute-start.10 = (bf16[9,64,2432]{2,1,0:T(8,128)(2,1)S(1)}, bf16[9,64,2432]{2,1,0:T(8,128)(2,1)S(1)}, u32[]{:S(2)}, u32[]{:S(2)}) collective-permute-start(bf16[9,64,2432]{2,1,0:T(8,128)(2,1)S(1)} %copy-done.10), channel_id=1, source_target_pairs={{0,1},{1,0},{2,3},{3,2},{4,5},{5,4},{6,7},{7,6},{8,9},{9,8},{10,11... | collective-permute-start | bytes 8405000 | tf_op jit(solution)/shard_map/ppermute | solution.py:458
  76.5 0.1 collective-permute-start.9
  76.6 0.8 collective-permute-start.11
  77.3 0.8 merge_far.1
  78.1 4.5 %collective-permute-start.12 = (bf16[3,64,2816]{2,1,0:T(8,128)(2,1)S(1)}, bf16[3,64,2816]{2,1,0:T(8,128)(2,1)S(1)}, u32[]{:S(2)}, u32[]{:S(2)}) collective-permute-start(bf16[3,64,2816]{2,1,0:T(8,128)(2,1)S(1)} %merge_far.1), channel_id=1, source_target_pairs={{0,28},{1,29},{2,6},{3,7},{4,0},{5,1},{6,10},{7,11},{8,4},{9,5},{1... | collective-permute-start | bytes 3244040 | tf_op jit(solution)/shard_map/ppermute | solution.py:458
  82.7 8.1 %join_rest.1 = (f32[3,64,2432]{2,1,0:T(8,128)S(1)}, bf16[3,64,2432]{2,1,0:T(8,128)(2,1)S(1)}, f32[3,64,2432]{2,1,0:T(8,128)S(1)}) custom-call(bf16[9,64,1024]{2,1,0:T(8,128)(2,1)S(1)} %copy-done.6, bf16[9,64,512]{2,1,0:T(8,128)(2,1)S(1)} %copy-done.7, bf16[9,64,512]{2,1,0:T(8,128)(2,1)S(1)} %collective-permute-done.9.other, ...), custom_call_target="tpu_custom_call" | custom-call | flops 40000000000 | bytes 200000000 | tf_op jit(solution)/shard_map/join_rest/pallas_call | solution.py:673
  90.8 8.9 %collective-permute-done.11.other = bf16[3,64,2432]{2,1,0:T(8,128)(2,1)S(1)} collective-permute-done((bf16[3,64,2432]{2,1,0:T(8,128)(2,1)S(1)}, bf16[3,64,2432]{2,1,0:T(8,128)(2,1)S(1)}, u32[]{:S(2)}, u32[]{:S(2)}) %collective-permute-start.11) | collective-permute-done | bytes 933920 | tf_op jit(solution)/shard_map/ppermute | solution.py:458
  99.6 0.4 collective-permute-start.13
  100.0 3.3 %collective-permute-start.14 = (bf16[3,64,2432]{2,1,0:T(8,128)(2,1)S(1)}, bf16[3,64,2432]{2,1,0:T(8,128)(2,1)S(1)}, u32[]{:S(2)}, u32[]{:S(2)}) collective-permute-start(bf16[3,64,2432]{2,1,0:T(8,128)(2,1)S(1)} %far.1), channel_id=1, source_target_pairs={{0,27},{3,8},{4,31},{7,12},{8,3},{11,16},{12,7},{15,20},{16,11},{1... | collective-permute-start | bytes 2801672 | tf_op jit(solution)/shard_map/ppermute | solution.py:458
  103.3 2.4 %collective-permute-done.12.direct = bf16[3,64,2816]{2,1,0:T(8,128)(2,1)S(1)} collective-permute-done((bf16[3,64,2816]{2,1,0:T(8,128)(2,1)S(1)}, bf16[3,64,2816]{2,1,0:T(8,128)(2,1)S(1)}, u32[]{:S(2)}, u32[]{:S(2)}) %collective-permute-start.12) | collective-permute-done | bytes 1081376 | tf_op jit(solution)/shard_map/ppermute | solution.py:458
  105.7 0.8 merge.1
  106.5 0.2 collective-permute-start.15
  106.7 25.2 %collective-permute-done.13.pair = bf16[3,64,2432]{2,1,0:T(8,128)(2,1)S(1)} collective-permute-done((bf16[3,64,2432]{2,1,0:T(8,128)(2,1)S(1)}, bf16[3,64,2432]{2,1,0:T(8,128)(2,1)S(1)}, u32[]{:S(2)}, u32[]{:S(2)}) %collective-permute-start.13) | collective-permute-done | bytes 933920 | tf_op jit(solution)/shard_map/ppermute | solution.py:458
  131.9 1.8 %early.1 = f32[3,64,4032]{2,1,0:T(8,128)S(1)} custom-call(s32[1]{0:T(128)} %bitcast.core, f32[3,64,2432]{2,1,0:T(8,128)S(1)} %get-tuple-element.88.own, bf16[3,64,2816]{2,1,0:T(8,128)(2,1)S(1)} %collective-permute-done.12.direct, bf16[3,64,2432]{2,1,0:T(8,128)(2,1)S(1)} %collective-permute-done.13.pair, bf16[3,64,2432]{2,1,0:T(8,128)(2,1)S(1)} %collective-permute-done.14.far), custom_call_target="tpu_custom_call" | custom-call | flops 10000000000 | bytes 100000000 | tf_op jit(solution)/shard_map/early/pallas_call | solution.py:692
  133.7 7.4 %collective-permute-done.15.merged = bf16[3,64,2816]{2,1,0:T(8,128)(2,1)S(1)} collective-permute-done((bf16[3,64,2816]{2,1,0:T(8,128)(2,1)S(1)}, bf16[3,64,2816]{2,1,0:T(8,128)(2,1)S(1)}, u32[]{:S(2)}, u32[]{:S(2)}) %collective-permute-start.15) | collective-permute-done | bytes 1081376 | tf_op jit(solution)/shard_map/ppermute | solution.py:458
  141.1 2.8 %total.1 = f32[3,64,4032]{2,1,0:T(8,128)} custom-call(s32[1]{0:T(128)} %bitcast.core, f32[3,64,4032]{2,1,0:T(8,128)S(1)} %early.1, bf16[3,64,2816]{2,1,0:T(8,128)(2,1)S(1)} %collective-permute-done.15.merged), custom_call_target="tpu_custom_call" | custom-call | flops 10000000 | bytes 10000000 | tf_op jit(solution)/shard_map/total/pallas_call | solution.py:702
  (46 shorter events, 0.2 us)
Async XLA Ops:
  0.0 3.1 %copy-start.8 = (s32[24,27]{1,0:T(8,128)S(1)}, s32[24,27]{1,0:T(8,128)}, u32[]{:S(2)}) copy-start(s32[24,27]{1,0:T(8,128)} %param.7) | copy-start | bytes 7780
  0.0 10.6 %copy-start.9 = (s32[24,7]{0,1:T(8,128)S(1)}, s32[24,7]{0,1:T(8,128)}, u32[]{:S(2)}) copy-start(s32[24,7]{0,1:T(8,128)} %param.6) | copy-start | bytes 2020
  3.2 9.0 %collective-permute-start.1 = (s32[8,27]{1,0:T(8,128)S(1)}, s32[8,27]{1,0:T(8,128)S(1)}, u32[]{:S(2)}, u32[]{:S(2)}) collective-permute-start(s32[8,27]{1,0:T(8,128)S(1)} %get-tuple-element.101), channel_id=1, source_target_pairs={{0,31},{1,2},{2,1},{3,4},{4,3},{5,6},{6,5},{7,8},{8,7},{9,10},{10,... | collective-permute-start | bytes 2600 | tf_op jit(solution)/shard_map/ppermute | solution.py:458
  9.6 2.7 %collective-permute-start = (s32[8,27]{1,0:T(8,128)S(1)}, s32[8,27]{1,0:T(8,128)S(1)}, u32[]{:S(2)}, u32[]{:S(2)}) collective-permute-start(s32[8,27]{1,0:T(8,128)S(1)} %get-tuple-element.102), channel_id=1, source_target_pairs={{0,1},{1,0},{2,3},{3,2},{4,5},{5,4},{6,7},{7,6},{8,9},{9,8},{10,11... | collective-permute-start | bytes 2600 | tf_op jit(solution)/shard_map/ppermute | solution.py:458
  9.6 4.3 %collective-permute-start.2 = (bf16[8,64,1728]{2,1,0:T(8,128)(2,1)}, bf16[8,64,1728]{2,1,0:T(8,128)(2,1)}, u32[]{:S(2)}, u32[]{:S(2)}) collective-permute-start(bf16[8,64,1728]{2,1,0:T(8,128)(2,1)} %get-tuple-element.56), channel_id=1, source_target_pairs={{0,1},{1,0},{2,3},{3,2},{4,5},{5,4},{6,7},{7,6},{8,9},{9,8},{10,11... | collective-permute-start | bytes 5308424 | tf_op jit(solution)/shard_map/ppermute | solution.py:458
  10.1 44.2 %collective-permute-start.3 = (bf16[8,64,1728]{2,1,0:T(8,128)(2,1)}, bf16[8,64,1728]{2,1,0:T(8,128)(2,1)S(1)}, u32[]{:S(2)}, u32[]{:S(2)}) collective-permute-start(bf16[8,64,1728]{2,1,0:T(8,128)(2,1)} %get-tuple-element.59), channel_id=1, source_target_pairs={{0,31},{1,2},{2,1},{3,4},{4,3},{5,6},{6,5},{7,8},{8,7},{9,10},{10,... | collective-permute-start | bytes 5308424 | tf_op jit(solution)/shard_map/ppermute | solution.py:458
  49.6 4.8 %collective-permute-start.4 = (bf16[3,64,2432]{2,1,0:T(8,128)(2,1)}, bf16[3,64,2432]{2,1,0:T(8,128)(2,1)S(1)}, u32[]{:S(2)}, u32[]{:S(2)}) collective-permute-start(bf16[3,64,2432]{2,1,0:T(8,128)(2,1)} %get-tuple-element.60), channel_id=1, source_target_pairs={{0,1},{1,0},{2,3},{3,2},{4,5},{5,4},{6,7},{7,6},{8,9},{9,8},{10,11... | collective-permute-start | bytes 2801672 | tf_op jit(solution)/shard_map/ppermute | solution.py:458
  50.0 4.3 %collective-permute-start.5 = (bf16[3,64,2432]{2,1,0:T(8,128)(2,1)}, bf16[3,64,2432]{2,1,0:T(8,128)(2,1)S(1)}, u32[]{:S(2)}, u32[]{:S(2)}) collective-permute-start(bf16[3,64,2432]{2,1,0:T(8,128)(2,1)} %get-tuple-element.61), channel_id=1, source_target_pairs={{0,1},{1,0},{2,3},{3,2},{4,5},{5,4},{6,7},{7,6},{8,9},{9,8},{10,11... | collective-permute-start | bytes 2801672 | tf_op jit(solution)/shard_map/ppermute | solution.py:458
  50.2 4.2 %collective-permute-start.6 = (bf16[6,64,512]{2,1,0:T(8,128)(2,1)}, bf16[6,64,512]{2,1,0:T(8,128)(2,1)S(1)}, u32[]{:S(2)}, u32[]{:S(2)}) collective-permute-start(bf16[6,64,512]{2,1,0:T(8,128)(2,1)} %get-tuple-element.62), channel_id=1, source_target_pairs={{0,1},{1,0},{2,3},{3,2},{4,5},{5,4},{6,7},{7,6},{8,9},{9,8},{10,11... | collective-permute-start | bytes 1179656 | tf_op jit(solution)/shard_map/ppermute | solution.py:458
  50.5 2.2 %copy-start = (f32[33,64,512]{2,1,0:T(8,128)S(1)}, f32[33,64,512]{2,1,0:T(8,128)}, u32[]{:S(2)}) copy-start(f32[33,64,512]{2,1,0:T(8,128)} %get-tuple-element.67.rest) | copy-start | bytes 12976132
  52.8 1.0 copy-start.2
  54.4 4.6 %copy-start.1 = (bf16[3,64,2432]{2,1,0:T(8,128)(2,1)S(1)}, bf16[3,64,2432]{2,1,0:T(8,128)(2,1)}, u32[]{:S(2)}) copy-start(bf16[3,64,2432]{2,1,0:T(8,128)(2,1)} %get-tuple-element.75.far_fast) | copy-start | bytes 2801668
  54.4 4.6 %copy-start.3 = (bf16[3,64,512]{2,1,0:T(8,128)(2,1)S(1)}, bf16[3,64,512]{2,1,0:T(8,128)(2,1)}, u32[]{:S(2)}) copy-start(bf16[3,64,512]{2,1,0:T(8,128)(2,1)} %get-tuple-element.71.slow) | copy-start | bytes 589828
  54.4 7.7 %copy-start.5 = (bf16[6,64,512]{2,1,0:T(8,128)(2,1)S(1)}, bf16[6,64,512]{2,1,0:T(8,128)(2,1)}, u32[]{:S(2)}) copy-start(bf16[6,64,512]{2,1,0:T(8,128)(2,1)} %get-tuple-element.70.slow) | copy-start | bytes 1179652
  58.6 6.5 %collective-permute-start.7 = (bf16[40,64,512]{2,1,0:T(8,128)(2,1)S(1)}, bf16[40,64,512]{2,1,0:T(8,128)(2,1)S(1)}, u32[]{:S(2)}, u32[]{:S(2)}) collective-permute-start(bf16[40,64,512]{2,1,0:T(8,128)(2,1)S(1)} %slow.1.wt_slow), channel_id=1, source_target_pairs={{0,1},{1,0},{2,3},{3,2},{4,5},{5,4},{6,7},{7,6},{8,9},{9,8},{10,11... | collective-permute-start | bytes 7864328 | tf_op jit(solution)/shard_map/ppermute | solution.py:458
  59.0 3.2 %copy-start.4 = (bf16[6,64,2432]{2,1,0:T(8,128)(2,1)S(1)}, bf16[6,64,2432]{2,1,0:T(8,128)(2,1)}, u32[]{:S(2)}) copy-start(bf16[6,64,2432]{2,1,0:T(8,128)(2,1)} %get-tuple-element.77.inner) | copy-start | bytes 5603332
  59.0 23.7 %slice-start = ((s8[5242880]{0:T(1024)(128)(4,1)}), s8[4194304]{0:T(1024)(128)(4,1)S(1)}, s32[]{:S(2)}) async-start(s8[5242880]{0:T(1024)(128)(4,1)} %bitcast.9), calls=%async_computation | async-start | bytes 8388608
  61.4 6.6 %collective-permute-start.8 = (bf16[3,64,2432]{2,1,0:T(8,128)(2,1)S(1)}, bf16[3,64,2432]{2,1,0:T(8,128)(2,1)S(1)}, u32[]{:S(2)}, u32[]{:S(2)}) collective-permute-start(bf16[3,64,2432]{2,1,0:T(8,128)(2,1)S(1)} %far.1), channel_id=1, source_target_pairs={{1,2},{2,1},{5,6},{6,5},{9,10},{10,9},{13,14},{14,13},{17,18},{18,... | collective-permute-start | bytes 2801672 | tf_op jit(solution)/shard_map/ppermute | solution.py:458
  62.1 20.5 %slice-start.1 = ((s8[5242880]{0:T(1024)(128)(4,1)}), s8[1048576]{0:T(1024)(128)(4,1)S(1)}, s32[]{:S(2)}) async-start(s8[5242880]{0:T(1024)(128)(4,1)} %bitcast.9), calls=%async_computation.1 | async-start | bytes 2097152
  65.1 3.0 %copy-start.10 = (bf16[9,64,2432]{2,1,0:T(8,128)(2,1)S(1)}, bf16[9,64,2432]{2,1,0:T(8,128)(2,1)}, u32[]{:S(2)}) copy-start(bf16[9,64,2432]{2,1,0:T(8,128)(2,1)} %get-tuple-element.87) | copy-start | bytes 8404996
  65.1 11.4 %copy-start.11 = (bf16[9,64,512]{2,1,0:T(8,128)(2,1)S(1)}, bf16[9,64,512]{2,1,0:T(8,128)(2,1)}, u32[]{:S(2)}) copy-start(bf16[9,64,512]{2,1,0:T(8,128)(2,1)} %get-tuple-element.85) | copy-start | bytes 1769476
  68.0 14.6 %copy-start.6 = (bf16[9,64,1024]{2,1,0:T(8,128)(2,1)S(1)}, bf16[9,64,1024]{2,1,0:T(8,128)(2,1)}, u32[]{:S(2)}) copy-start(bf16[9,64,1024]{2,1,0:T(8,128)(2,1)} %get-tuple-element.57.fast) | copy-start | bytes 3538948
  68.1 14.6 %copy-start.7 = (bf16[9,64,512]{2,1,0:T(8,128)(2,1)S(1)}, bf16[9,64,512]{2,1,0:T(8,128)(2,1)}, u32[]{:S(2)}) copy-start(bf16[9,64,512]{2,1,0:T(8,128)(2,1)} %get-tuple-element.58.slow) | copy-start | bytes 1769476
  68.1 14.6 %collective-permute-start.10 = (bf16[9,64,2432]{2,1,0:T(8,128)(2,1)S(1)}, bf16[9,64,2432]{2,1,0:T(8,128)(2,1)S(1)}, u32[]{:S(2)}, u32[]{:S(2)}) collective-permute-start(bf16[9,64,2432]{2,1,0:T(8,128)(2,1)S(1)} %copy-done.10), channel_id=1, source_target_pairs={{0,1},{1,0},{2,3},{3,2},{4,5},{5,4},{6,7},{7,6},{8,9},{9,8},{10,11... | collective-permute-start | bytes 8405000 | tf_op jit(solution)/shard_map/ppermute | solution.py:458
  76.5 6.1 %collective-permute-start.9 = (bf16[9,64,512]{2,1,0:T(8,128)(2,1)S(1)}, bf16[9,64,512]{2,1,0:T(8,128)(2,1)S(1)}, u32[]{:S(2)}, u32[]{:S(2)}) collective-permute-start(bf16[9,64,512]{2,1,0:T(8,128)(2,1)S(1)} %copy-done.11), channel_id=1, source_target_pairs={{0,1},{1,0},{2,3},{3,2},{4,5},{5,4},{6,7},{7,6},{8,9},{9,8},{10,11... | collective-permute-start | bytes 1769480 | tf_op jit(solution)/shard_map/ppermute | solution.py:458
  76.6 23.0 %collective-permute-start.11 = (bf16[3,64,2432]{2,1,0:T(8,128)(2,1)S(1)}, bf16[3,64,2432]{2,1,0:T(8,128)(2,1)S(1)}, u32[]{:S(2)}, u32[]{:S(2)}) collective-permute-start(bf16[3,64,2432]{2,1,0:T(8,128)(2,1)S(1)} %get-tuple-element.89), channel_id=1, source_target_pairs={{0,2},{1,3},{2,0},{3,1},{4,6},{5,7},{6,4},{7,5},{8,10},{9,11},{10,... | collective-permute-start | bytes 2801672 | tf_op jit(solution)/shard_map/ppermute | solution.py:458
  78.1 27.6 %collective-permute-start.12 = (bf16[3,64,2816]{2,1,0:T(8,128)(2,1)S(1)}, bf16[3,64,2816]{2,1,0:T(8,128)(2,1)S(1)}, u32[]{:S(2)}, u32[]{:S(2)}) collective-permute-start(bf16[3,64,2816]{2,1,0:T(8,128)(2,1)S(1)} %merge_far.1), channel_id=1, source_target_pairs={{0,28},{1,29},{2,6},{3,7},{4,0},{5,1},{6,10},{7,11},{8,4},{9,5},{1... | collective-permute-start | bytes 3244040 | tf_op jit(solution)/shard_map/ppermute | solution.py:458
  99.6 32.3 %collective-permute-start.13 = (bf16[3,64,2432]{2,1,0:T(8,128)(2,1)S(1)}, bf16[3,64,2432]{2,1,0:T(8,128)(2,1)S(1)}, u32[]{:S(2)}, u32[]{:S(2)}) collective-permute-start(bf16[3,64,2432]{2,1,0:T(8,128)(2,1)S(1)} %get-tuple-element.95), channel_id=1, source_target_pairs={{0,2},{1,3},{2,0},{3,1},{4,6},{5,7},{6,4},{7,5},{8,10},{9,11},{10,... | collective-permute-start | bytes 2801672 | tf_op jit(solution)/shard_map/ppermute | solution.py:458
  100.0 31.9 %collective-permute-start.14 = (bf16[3,64,2432]{2,1,0:T(8,128)(2,1)S(1)}, bf16[3,64,2432]{2,1,0:T(8,128)(2,1)S(1)}, u32[]{:S(2)}, u32[]{:S(2)}) collective-permute-start(bf16[3,64,2432]{2,1,0:T(8,128)(2,1)S(1)} %far.1), channel_id=1, source_target_pairs={{0,27},{3,8},{4,31},{7,12},{8,3},{11,16},{12,7},{15,20},{16,11},{1... | collective-permute-start | bytes 2801672 | tf_op jit(solution)/shard_map/ppermute | solution.py:458
  106.5 34.6 %collective-permute-start.15 = (bf16[3,64,2816]{2,1,0:T(8,128)(2,1)S(1)}, bf16[3,64,2816]{2,1,0:T(8,128)(2,1)S(1)}, u32[]{:S(2)}, u32[]{:S(2)}) collective-permute-start(bf16[3,64,2816]{2,1,0:T(8,128)(2,1)S(1)} %merge.1), channel_id=1, source_target_pairs={{0,4},{1,5},{2,30},{3,31},{4,8},{5,9},{6,2},{7,3},{8,12},{9,13},{1... | collective-permute-start | bytes 3244040 | tf_op jit(solution)/shard_map/ppermute | solution.py:458

commit v10 on v9

--- a/solution.py
+++ b/solution.py
@@ -98,21 +98,20 @@
     other_first,
     other_rest,
     wt,
-    rest,
+    rest_0,
+    rest_1,
+    rest_2,
     at_halo,
-    p_buf,
     ext,
     at,
     unit,
     turned_p,
     turned_a,
     lhs,
-    rows_buf,
     fast_buf,
     slow_buf,
     other_buf,
     wt_buf,
-    rest_buf,
     in_sems,
     out_sems,
 ):
@@ -120,59 +119,59 @@
     own_quads = NB // QUAD
     halo_quads = AGG // QUAD
 
-    def load(quad):
-        if quad < own_quads:
-            source = p_own.at[quad * QUAD : (quad + 1) * QUAD]
-        else:
-            source = p_fast.at[(quad - own_quads) * QUAD : (quad - own_quads + 1) * QUAD]
-        target = p_buf.at[quad * QUAD : (quad + 1) * QUAD]
-        return pltpu.make_async_copy(source, target, in_sems.at[quad])
-
-    for quad in range(own_quads + halo_quads):
-        load(quad).start()
-
-    unit[...] = eye(LANES)
-    turned_p[KP] = jnp.zeros((BS, LANES), jnp.bfloat16)
-    turned_a[KA] = jnp.zeros((BS, LANES), jnp.bfloat16)
-
-    @pl.loop(0, own_quads)
-    def _(quad):
-        block = a_own[pl.ds(quad * QUAD, QUAD)].reshape(LANES, KA * BS)
-        transpose_quad(unit, block, turned_a, KA * BS)
-        agg = quad // halo_quads
-
-        def store(slot, pair, value):
-            lane = pl.multiple_of((quad % halo_quads) * LANES + pair * 2 * BS, 2 * BS)
-            at[agg, slot, :, pl.ds(lane, 2 * BS)] = value
-
-        spread_quad(turned_a, inv_a, quad * QUAD, store, 3 * AGG, 8)
-
+    def band_phase(p_buf):
+        def load(quad):
+            if quad < own_quads:
+                source = p_own.at[quad * QUAD : (quad + 1) * QUAD]
+            else:
+                source = p_fast.at[(quad - own_quads) * QUAD : (quad - own_quads + 1) * QUAD]
+            target = p_buf.at[quad * QUAD : (quad + 1) * QUAD]
+            return pltpu.make_async_copy(source, target, in_sems.at[quad])
+
+        for quad in range(own_quads + halo_quads):
+            load(quad).start()
+
+        unit[...] = eye(LANES)
+        turned_p[KP] = jnp.zeros((BS, LANES), jnp.bfloat16)
+        turned_a[KA] = jnp.zeros((BS, LANES), jnp.bfloat16)
+
+        @pl.loop(0, own_quads)
+        def _(quad):
+            block = a_own[pl.ds(quad * QUAD, QUAD)].reshape(LANES, KA * BS)
+            transpose_quad(unit, block, turned_a, KA * BS)
+            agg = quad // halo_quads
+
+            def store(slot, pair, value):
+                lane = pl.multiple_of((quad % halo_quads) * LANES + pair * 2 * BS, 2 * BS)
+                at[agg, slot, :, pl.ds(lane, 2 * BS)] = value
+
+            spread_quad(turned_a, inv_a, quad * QUAD, store, 3 * AGG, 8)
+
+        def band_quad(source_row, index, index_row, first_lane):
+            block = p_buf[pl.ds(source_row, QUAD)].reshape(LANES, KP * BS)
+            transpose_quad(unit, block, turned_p, KP * BS)
+
+            def store(slot, pair, value):
+                lane = pl.multiple_of(first_lane + pair * 2 * BS, 2 * BS)
+                ext[slot, :, pl.ds(lane, 2 * BS)] = value
+
+            spread_quad(turned_p, index, index_row, store, COLS, 7)
+
+        for quad in range(own_quads + halo_quads):
+            load(quad).wait()
+
+        @pl.loop(0, own_quads)
+        def _(quad):
+            band_quad(quad * QUAD, inv_own, quad * QUAD, AW + quad * LANES)
+
+        @pl.loop(0, halo_quads)
+        def _(quad):
+            first_lane = (AW + K) * (1 - s) + quad * LANES
+            band_quad((own_quads + quad) * QUAD, inv_fast, quad * QUAD, first_lane)
+
+    pl.run_scoped(band_phase, pltpu.VMEM((NB + AGG, BS, KP * BS), jnp.bfloat16))
     slow_agg = 2 * s
-    halo_copy = pltpu.make_async_copy(at.at[slow_agg, pl.ds(16 * s, AGG)], at_halo, out_sems.at[0])
-    halo_copy.start()
-
-    def band_quad(source_row, index, index_row, first_lane):
-        block = p_buf[pl.ds(source_row, QUAD)].reshape(LANES, KP * BS)
-        transpose_quad(unit, block, turned_p, KP * BS)
-
-        def store(slot, pair, value):
-            lane = pl.multiple_of(first_lane + pair * 2 * BS, 2 * BS)
-            ext[slot, :, pl.ds(lane, 2 * BS)] = value
-
-        spread_quad(turned_p, index, index_row, store, COLS, 7)
-
-    for quad in range(own_quads + halo_quads):
-        load(quad).wait()
-
-    @pl.loop(0, own_quads)
-    def _(quad):
-        band_quad(quad * QUAD, inv_own, quad * QUAD, AW + quad * LANES)
-
-    @pl.loop(0, halo_quads)
-    def _(quad):
-        first_lane = (AW + K) * (1 - s) + quad * LANES
-        band_quad((own_quads + quad) * QUAD, inv_fast, quad * QUAD, first_lane)
-
+    at_halo[...] = at[slow_agg, pl.ds(16 * s, AGG)]
     fast_lanes = pl.ds(pl.multiple_of(AW + (1 - s) * AW, AW), 2 * AW)
     slow_lanes = pl.ds(pl.multiple_of(AW + 2 * s * AW, AW), AW)
     for place, i in enumerate((1 + 2 * x, 4 * x, 4 - 4 * x, 3 - 2 * x, 2)):
@@ -190,7 +189,7 @@
     for j in range(NC):
         lhs[FIRST + j] = ext[30 * s + j + 1, :, fast_lanes]
         slow_buf[ROWS + j] = ext[30 * s + j + 1, :, slow_lanes]
-    copies = [halo_copy]
+    copies = []
 
     def write(source, target):
         copy = pltpu.make_async_copy(source, target, out_sems.at[len(copies)])
@@ -227,48 +226,48 @@
 
     write(wt_buf, wt)
 
-    @pl.loop(0, 3)
-    def _(part):
+    for part, rest in enumerate((rest_0, rest_1, rest_2)):
         lane = pl.multiple_of(AW + s * AW, AW)
         left = ext[pl.ds(slow_agg + part * chunk, chunk), :, pl.ds(lane, 2 * AW)]
         right = at[slow_agg, pl.ds(AGG - AGG * s, 2 * AGG)].reshape(2 * AW, AW)
         value = jnp.dot(
             left.reshape(chunk * BS, 2 * AW), right, preferred_element_type=jnp.float32
         )
-        rest_buf[pl.ds(part * chunk, chunk)] = value.reshape(chunk, BS, AW)
-
-    write(rest_buf, rest)
-
-    def emit(tile, width):
-        right = wt_buf[pl.ds(QUAD * tile, width // BS)].reshape(width, 2 * AW)
-        left = lhs[...].reshape((ROWS + REST) * BS, 2 * AW)
-        value = lax.dot_general(left, right, NT, preferred_element_type=jnp.float32)
-        rows_buf[:, :, tile_lanes(tile, width)] = value.astype(jnp.bfloat16).reshape(
-            ROWS + REST, BS, width
+        rest[...] = value.reshape(chunk, BS, AW)
+
+    def send_phase(rows_buf):
+        def emit(tile, width):
+            right = wt_buf[pl.ds(QUAD * tile, width // BS)].reshape(width, 2 * AW)
+            left = lhs[...].reshape((ROWS + REST) * BS, 2 * AW)
+            value = lax.dot_general(left, right, NT, preferred_element_type=jnp.float32)
+            rows_buf[:, :, tile_lanes(tile, width)] = value.astype(jnp.bfloat16).reshape(
+                ROWS + REST, BS, width
+            )
+
+        parts = (
+            (send_low, 0),
+            (send_high, NC),
+            (far, FIRST),
+            (inner, FIRST + NC),
+            (send_rest, ROWS),
         )
-
-    parts = (
-        (send_low, 0),
-        (send_high, NC),
-        (far, FIRST),
-        (inner, FIRST + NC),
-        (send_rest, ROWS),
-    )
-    bounds = (0, 4, 8, TILES)
-    for first, last in zip(bounds[:-1], bounds[1:]):
-
-        @pl.loop(first, min(last, TILES - 1))
-        def _(tile):
-            emit(tile, LANES)
-
-        if last == TILES:
-            emit(TILES - 1, LANES // 2)
-        lanes = slice(first * LANES, min(last * LANES, WINDOW * BS))
-        for target, row in parts:
-            rows = slice(row, row + target.shape[0])
-            write(rows_buf.at[rows, :, lanes], target.at[:, :, lanes])
-    for copy in copies:
-        copy.wait()
+        bounds = (0, 4, 8, TILES)
+        for first, last in zip(bounds[:-1], bounds[1:]):
+
+            @pl.loop(first, min(last, TILES - 1))
+            def _(tile):
+                emit(tile, LANES)
+
+            if last == TILES:
+                emit(TILES - 1, LANES // 2)
+            lanes = slice(first * LANES, min(last * LANES, WINDOW * BS))
+            for target, row in parts:
+                rows = slice(row, row + target.shape[0])
+                write(rows_buf.at[rows, :, lanes], target.at[:, :, lanes])
+        for copy in copies:
+            copy.wait()
+
+    pl.run_scoped(send_phase, pltpu.VMEM((ROWS + REST, BS, WINDOW * BS), jnp.bfloat16))
 
 
 def each_tile(step):
@@ -309,7 +308,7 @@
     each_tile(step)
 
 
-def slow_kernel(core, inv_slow, p_slow, at_halo, rest, wt, unit, turned_p, ext):
+def slow_kernel(core, inv_slow, p_slow, at_halo, rest_0, rest_1, rest_2, wt, unit, turned_p, ext):
     s, x = places(core)
     unit[...] = eye(LANES)
     turned_p[KP] = jnp.zeros((BS, LANES), jnp.bfloat16)
@@ -329,15 +328,13 @@
     wt[WSLOT:] = jnp.zeros((WCOLS - WSLOT, BS, AW), jnp.bfloat16)
     chunk = WSLOT // 3
 
-    @pl.loop(0, 3)
-    def _(part):
-        rows = pl.ds(part * chunk, chunk)
+    for part, rest in enumerate((rest_0, rest_1, rest_2)):
         value = jnp.dot(
-            ext[rows].reshape(chunk * BS, AW),
+            ext[part * chunk : (part + 1) * chunk].reshape(chunk * BS, AW),
             at_halo[...].reshape(AW, AW),
             preferred_element_type=jnp.float32,
         )
-        value = value.reshape(chunk, BS, AW) + rest[rows]
+        value = value.reshape(chunk, BS, AW) + rest[...]
         wt[pl.ds(5 * s + part * chunk, chunk)] = value.astype(jnp.bfloat16)
 
 
@@ -362,17 +359,6 @@
         own[:, :, lanes] = value[2 * NC :]
 
     each_tile(step)
-
-
-def stage_kernel(at_halo, rest, at_out, rest_out, sems):
-    copies = [
-        pltpu.make_async_copy(at_halo, at_out, sems.at[0]),
-        pltpu.make_async_copy(rest, rest_out, sems.at[1]),
-    ]
-    for copy in copies:
-        copy.start()
-    for copy in copies:
-        copy.wait()
 
 
 def merge_kernel(core, rows, other, out, frame):
@@ -540,9 +526,8 @@
         block(FIRST, AW),
         block(REST, AW),
         block(WCOLS, 2 * AW),
-        block(WSLOT, AW, jnp.float32),
-        block(AGG, AW),
     ]
+    outs += [block(WSLOT // 3, AW, jnp.float32)] * 3 + [block(AGG, AW)]
     (
         send_low,
         send_high,
@@ -556,31 +541,28 @@
         other_first,
         other_rest,
         wt_fast,
-        rest,
+        *rest,
         at_halo,
     ) = pl.pallas_call(
         fast_kernel,
         out_shape=outs,
         in_specs=[smem] * 4 + [hbm, hbm, vmem],
-        out_specs=[hbm] * len(outs),
+        out_specs=[hbm] * (len(outs) - 4) + [vmem] * 4,
         scratch_shapes=[
-            pltpu.VMEM((NB + AGG, BS, KP * BS), bf16),
             pltpu.VMEM((COLS, BS, EXT * BS), bf16),
             pltpu.VMEM((NC, 3 * AGG, BS, AW), bf16),
             pltpu.VMEM((LANES, LANES), bf16),
             pltpu.VMEM((KP + 1, BS, LANES), bf16),
             pltpu.VMEM((KA + 1, BS, LANES), bf16),
             pltpu.VMEM((ROWS + REST, BS, 2 * AW), bf16),
-            pltpu.VMEM((ROWS + REST, BS, span), bf16),
             pltpu.VMEM((REST, BS, 2 * AW), bf16),
             pltpu.VMEM((ROWS + NC, BS, AW), bf16),
             pltpu.VMEM((ROWS, BS, AW), bf16),
             pltpu.VMEM((WCOLS, BS, 2 * AW), bf16),
-            pltpu.VMEM((WSLOT, BS, AW), jnp.float32),
             pltpu.SemaphoreType.DMA(((NB + AGG) // QUAD,)),
             pltpu.SemaphoreType.DMA((len(outs) + 10,)),
         ],
-        compiler_params=params(56),
+        compiler_params=params(44),
         cost_estimate=cost(20 * 10**9, 30 * 10**6),
         name="fast",
     )(core, inv_own, inv_fast, inv_a, p_blocks, p_fast, a_blocks)
@@ -588,22 +570,12 @@
     low = permuted(send_low, inward)
     high = permuted(send_high, inward)
     other_first = permuted(other_first, inward)
-    at_halo, rest = pl.pallas_call(
-        stage_kernel,
-        out_shape=[block(AGG, AW), block(WSLOT, AW, jnp.float32)],
-        in_specs=[hbm] * 2,
-        out_specs=[vmem] * 2,
-        scratch_shapes=[pltpu.SemaphoreType.DMA((2,))],
-        compiler_params=params(8),
-        cost_estimate=cost(10**6, 10**6),
-        name="stage",
-    )(at_halo, rest)
     p_slow, low, high, other_first = lax.optimization_barrier((p_slow, low, high, other_first))
 
     wt_slow = pl.pallas_call(
         slow_kernel,
         out_shape=block(WCOLS, AW),
-        in_specs=[smem] * 2 + [vmem] * 3,
+        in_specs=[smem] * 2 + [vmem] * 5,
         out_specs=vmem,
         scratch_shapes=[
             pltpu.VMEM((LANES, LANES), bf16),
@@ -613,7 +585,7 @@
         compiler_params=params(24),
         cost_estimate=cost(20 * 10**9, 200 * 10**6),
         name="slow",
-    )(core, inv_slow, p_slow, at_halo, rest)
+    )(core, inv_slow, p_slow, at_halo, *rest)
     wt_other = permuted(wt_slow, inward)
 
     wt_slow, low, high = lax.optimization_barrier((wt_slow, low, high))
@@ -680,8 +652,7 @@
         name="join_rest",
     )(fast_rest, slow_rest, other_rest, wt_fast, wt_slow, wt_other, arrived_rest)
     relay, pair, far = lax.optimization_barrier((relay, pair, far))
-    relay_in, direct = lax.optimization_barrier((relay, direct))
-    merged = merge_rows(merge, relay_in, "merge")
+    merged = merge_rows(merge, relay, "merge")
     merged = permuted(merged, [(i, (i - 4 * x_sign[i]) % devices) for i in range(devices)])
     pair = permuted(pair, along_x)
     straight = [i for i in range(devices) if i % 4 in (0, 3)]

time: 144 us -> 146 us (1.014)
  waiting for transfers between devices: 44.5 us -> 48.4 us
  local copies, waits for them, and re-layouts: 3.59 us -> 1.67 us
  other arithmetic: 2.49 us -> 0.71 us
  Pallas kernels: 66.1 us -> 67.8 us
    ppermute x16, waiting for transfers between devices: 44.5 us -> 48.4 us  [permuted(): return lax.ppermute(block, 'dom', pairs)]
    pallas_call x1, Pallas kernels: 35.7 us -> 38.2 us  [body(): pl.pallas_call(fast_kernel, out_shape=outs, in_specs=[smem] * 4 + [hbm, h...]
    unnamed x28 -> x18, local copies, waits for them, and re-layouts: 3.32 us -> 1.4 us
    add x4, other arithmetic: 1.79 us -> 0.02 us  [inverse_index(): return empty + jnp.sum(jnp.where(hit, order - empty, 0), axis=1)]
  transfers between devices with their start and end apart: 16 -> 16, of which waited for: 5 -> 6; matrix products, arithmetic and copies ran while one was open for 2% -> 1% of each run, Pallas kernels for 39% -> 40%
where the time goes in v10:
time: 146 us; the launch traced here: 145 us
  Pallas kernels  67.8 us (46%)
  waiting for transfers between devices  48.4 us (33%)
  starting transfers between devices  26.5 us (18%)
  local copies, waits for them, and re-layouts  1.67 us (1%)
    ppermute x16, waiting for transfers between devices, permuted(): return lax.ppermute(block, 'dom', pairs)  48.4 us
    pallas_call x1, Pallas kernels, body(): pl.pallas_call(fast_kernel, out_shape=outs, in_specs=[smem] * 4 + [hbm, h...  38.2 us
    ppermute x16, starting transfers between devices, permuted(): return lax.ppermute(block, 'dom', pairs)  26.5 us
    pallas_call x1, Pallas kernels, body(): pl.pallas_call(join_rest_kernel, out_shape=[block(NC, span, jnp.float32),...  8.12 us
    pallas_call x1, Pallas kernels, body(): pl.pallas_call(slow_kernel, out_shape=block(WCOLS, AW), in_specs=[smem] *...  3.81 us
    pallas_call x1, Pallas kernels, body(): pl.pallas_call(pick_kernel, out_shape=[edge, edge], in_specs=[smem, hbm],...  3.08 us
    pallas_call x1, Pallas kernels, body(): pl.pallas_call(mine_kernel, out_shape=block(FIRST, span, jnp.float32), in...  2.98 us
    pallas_call x1, Pallas kernels, body(): pl.pallas_call(join_first_kernel, out_shape=[block(NC, span), block(NC, s...  2.93 us
  transfers between devices with their start and end apart: 16, of which 6 were waited for; matrix products, arithmetic and copies ran while one was open for 1% of the time, Pallas kernels for 40%

profile of v10, /device:TPU:0, one launch (start us, length us, event | category | flops | bytes accessed | tf_op | source)
XLA Modules:
  0.0 145.4 jit_solution(15082965747203329937)
XLA Ops:
  0.0 3.1 %pick.1 = (bf16[8,64,1728]{2,1,0:T(8,128)(2,1)}, bf16[8,64,1728]{2,1,0:T(8,128)(2,1)}) custom-call(s32[1]{0:T(128)} %bitcast.core, bf16[24,64,1728]{2,1,0:T(8,128)(2,1)} %p_own.1), custom_call_target="tpu_custom_call" | custom-call | tf_op jit(solution)/shard_map/pick/pallas_call | solution.py:478
  3.2 6.4 %collective-permute-start.1 = (s32[8,27]{1,0:T(8,128)S(1)}, s32[8,27]{1,0:T(8,128)S(1)}, u32[]{:S(2)}, u32[]{:S(2)}) collective-permute-start(s32[8,27]{1,0:T(8,128)S(1)} %get-tuple-element.97), channel_id=1, source_target_pairs={{0,31},{1,2},{2,1},{3,4},{4,3},{5,6},{6,5},{7,8},{8,7},{9,10},{10,... | collective-permute-start | bytes 2600 | tf_op jit(solution)/shard_map/ppermute | solution.py:444
  9.6 0.0 collective-permute-start
  9.6 0.5 collective-permute-start.2
  10.1 0.3 collective-permute-start.3
  10.4 0.1 fusion.1
  10.5 0.1 copy.15
  10.6 0.1 select_reduce_fusion.3
  10.8 0.2 select_reduce_fusion
  11.0 0.0 collective-permute-done.1
  11.0 0.1 copy.17
  11.1 0.0 collective-permute-done
  11.1 0.1 copy.16
  11.2 0.1 select_reduce_fusion.1
  11.3 0.1 select_reduce_fusion.2
  11.5 2.4 %collective-permute-done.2.p_fast = bf16[8,64,1728]{2,1,0:T(8,128)(2,1)} collective-permute-done((bf16[8,64,1728]{2,1,0:T(8,128)(2,1)}, bf16[8,64,1728]{2,1,0:T(8,128)(2,1)}, u32[]{:S(2)}, u32[]{:S(2)}) %collective-permute-start.2) | collective-permute-done | bytes 1769504 | tf_op jit(solution)/shard_map/ppermute | solution.py:444
  13.9 38.2 %fast.1 = (bf16[3,64,2432]{2,1,0:T(8,128)(2,1)S(1)}, bf16[3,64,2432]{2,1,0:T(8,128)(2,1)S(1)}, bf16[3,64,2432]{2,1,0:T(8,128)(2,1)S(1)}, bf16[6,64,2432]{2,1,0:T...) custom-call(s32[1]{0:T(128)} %bitcast.core, ...), custom_call_target="tpu_custom_call" | custom-call | flops 20000000000 | bytes 30000000 | tf_op jit(solution)/shard_map/fast/pallas_call | solution.py:546
  52.1 0.5 collective-permute-start.4
  52.6 0.1 collective-permute-start.5
  52.7 0.4 collective-permute-start.6
  53.1 3.5 %collective-permute-done.6.other = bf16[6,64,512]{2,1,0:T(8,128)(2,1)S(1)} collective-permute-done((bf16[6,64,512]{2,1,0:T(8,128)(2,1)S(1)}, bf16[6,64,512]{2,1,0:T(8,128)(2,1)S(1)}, u32[]{:S(2)}, u32[]{:S(2)}) %collective-permute-start.6) | collective-permute-done | bytes 393248 | tf_op jit(solution)/shard_map/ppermute | solution.py:444
  56.6 0.0 collective-permute-done.5.high
  56.6 1.4 copy-done.1
  57.9 3.8 %slow.1.wt_slow = bf16[40,64,512]{2,1,0:T(8,128)(2,1)S(1)} custom-call(s32[1]{0:T(128)} %bitcast.core, s32[8,33]{1,0:T(8,128)S(1)} %broadcast_add_fusion.2.inv_slow, bf16[8,64,1728]{2,1,0:T(8,128)(2,1)S(1)} %collective-permute-done.3.p_slow, bf16[8,64,512]{2,1,0:T(8,128)(2,1)S(1)} %get-tuple-element.64.at_halo, f32[11,64,512]{2,1,0:T(8,128)S(1)} %get-tuple-element.65.rest_0, ...), custom_call_target="tpu_custom_call" | custom-call | flops 20000000000 | bytes 200000000 | tf_op jit(solution)/shard_map/slow/pallas_call | solution.py:575
  61.8 0.4 collective-permute-start.7
  62.2 2.4 %far.1 = bf16[3,64,2432]{2,1,0:T(8,128)(2,1)S(1)} custom-call(bf16[3,64,512]{2,1,0:T(8,128)(2,1)S(1)} %get-tuple-element.69.slow, bf16[40,64,512]{2,1,0:T(8,128)(2,1)S(1)} %slow.1.wt_slow, bf16[3,64,2432]{2,1,0:T(8,128)(2,1)S(1)} %get-tuple-element.73.far_fast), custom_call_target="tpu_custom_call" | custom-call | flops 1000000000 | bytes 10000000 | tf_op jit(solution)/shard_map/far/pallas_call | solution.py:592
  64.6 0.9 collective-permute-start.8
  65.6 0.0 slice-start.1
  65.6 3.0 %mine.1 = f32[6,64,2432]{2,1,0:T(8,128)S(1)} custom-call(bf16[6,64,512]{2,1,0:T(8,128)(2,1)S(1)} %get-tuple-element.68.slow, bf16[40,64,512]{2,1,0:T(8,128)(2,1)S(1)} %slow.1.wt_slow, bf16[6,64,2432]{2,1,0:T(8,128)(2,1)S(1)} %copy-done, bf16[3,64,2432]{2,1,0:T(8,128)(2,1)S(1)} %collective-permute-done.4.low, bf16[3,64,2432]{2,1,0:T(8,128)(2,1)S(1)} %collective-permute-done.5.high), custom_call_target="tpu_custom_call" | custom-call | flops 10000000000 | bytes 100000000 | tf_op jit(solution)/shard_map/mine/pallas_call | solution.py:602
  68.6 0.0 copy-start.6
  68.6 2.9 %join_first.1 = (bf16[3,64,2432]{2,1,0:T(8,128)(2,1)S(1)}, f32[3,64,2432]{2,1,0:T(8,128)S(1)}) custom-call(bf16[6,64,512]{2,1,0:T(8,128)(2,1)S(1)} %collective-permute-done.6.other, bf16[40,64,512]{2,1,0:T(8,128)(2,1)S(1)} %collective-permute-done.7.wt_other, f32[6,64,2432]{2,1,0:T(8,128)S(1)} %mine.1), custom_call_target="tpu_custom_call" | custom-call | flops 1000000 | bytes 100000 | tf_op jit(solution)/shard_map/join_first/pallas_call | solution.py:613
  71.5 8.1 %collective-permute-start.10 = (bf16[9,64,2432]{2,1,0:T(8,128)(2,1)S(1)}, bf16[9,64,2432]{2,1,0:T(8,128)(2,1)S(1)}, u32[]{:S(2)}, u32[]{:S(2)}) collective-permute-start(bf16[9,64,2432]{2,1,0:T(8,128)(2,1)S(1)} %copy-done.6), channel_id=1, source_target_pairs={{0,1},{1,0},{2,3},{3,2},{4,5},{5,4},{6,7},{7,6},{8,9},{9,8},{10,11... | collective-permute-start | bytes 8405000 | tf_op jit(solution)/shard_map/ppermute | solution.py:444
  79.7 0.1 collective-permute-start.9
  79.7 0.3 collective-permute-start.12
  80.1 0.8 merge_far.1
  80.9 3.6 %collective-permute-start.11 = (bf16[3,64,2816]{2,1,0:T(8,128)(2,1)S(1)}, bf16[3,64,2816]{2,1,0:T(8,128)(2,1)S(1)}, u32[]{:S(2)}, u32[]{:S(2)}) collective-permute-start(bf16[3,64,2816]{2,1,0:T(8,128)(2,1)S(1)} %merge_far.1), channel_id=1, source_target_pairs={{0,28},{1,29},{2,6},{3,7},{4,0},{5,1},{6,10},{7,11},{8,4},{9,5},{1... | collective-permute-start | bytes 3244040 | tf_op jit(solution)/shard_map/ppermute | solution.py:444
  84.5 0.8 collective-permute-done.9.other
  85.3 0.0 collective-permute-done.10.arrived
  85.3 8.1 %join_rest.1 = (f32[3,64,2432]{2,1,0:T(8,128)S(1)}, bf16[3,64,2432]{2,1,0:T(8,128)(2,1)S(1)}, f32[3,64,2432]{2,1,0:T(8,128)S(1)}) custom-call(bf16[9,64,1024]{2,1,0:T(8,128)(2,1)S(1)} %get-tuple-element.55.fast, bf16[9,64,512]{2,1,0:T(8,128)(2,1)S(1)} %copy-done.3, bf16[9,64,512]{2,1,0:T(8,128)(2,1)S(1)} %collective-permute-done.9.other, ...), custom_call_target="tpu_custom_call" | custom-call | flops 40000000000 | bytes 200000000 | tf_op jit(solution)/shard_map/join_rest/pallas_call | solution.py:645
  93.5 9.3 %collective-permute-done.12.other = bf16[3,64,2432]{2,1,0:T(8,128)(2,1)S(1)} collective-permute-done((bf16[3,64,2432]{2,1,0:T(8,128)(2,1)S(1)}, bf16[3,64,2432]{2,1,0:T(8,128)(2,1)S(1)}, u32[]{:S(2)}, u32[]{:S(2)}) %collective-permute-start.12) | collective-permute-done | bytes 933920 | tf_op jit(solution)/shard_map/ppermute | solution.py:444
  102.8 0.3 collective-permute-start.13
  103.1 2.5 %collective-permute-start.14 = (bf16[3,64,2432]{2,1,0:T(8,128)(2,1)S(1)}, bf16[3,64,2432]{2,1,0:T(8,128)(2,1)S(1)}, u32[]{:S(2)}, u32[]{:S(2)}) collective-permute-start(bf16[3,64,2432]{2,1,0:T(8,128)(2,1)S(1)} %far.1), channel_id=1, source_target_pairs={{0,27},{3,8},{4,31},{7,12},{8,3},{11,16},{12,7},{15,20},{16,11},{1... | collective-permute-start | bytes 2801672 | tf_op jit(solution)/shard_map/ppermute | solution.py:444
  105.6 0.8 merge.1
  106.4 2.0 %collective-permute-start.15 = (bf16[3,64,2816]{2,1,0:T(8,128)(2,1)S(1)}, bf16[3,64,2816]{2,1,0:T(8,128)(2,1)S(1)}, u32[]{:S(2)}, u32[]{:S(2)}) collective-permute-start(bf16[3,64,2816]{2,1,0:T(8,128)(2,1)S(1)} %merge.1), channel_id=1, source_target_pairs={{0,4},{1,5},{2,30},{3,31},{4,8},{5,9},{6,2},{7,3},{8,12},{9,13},{1... | collective-permute-start | bytes 3244040 | tf_op jit(solution)/shard_map/ppermute | solution.py:444
  108.3 26.7 %collective-permute-done.13.pair = bf16[3,64,2432]{2,1,0:T(8,128)(2,1)S(1)} collective-permute-done((bf16[3,64,2432]{2,1,0:T(8,128)(2,1)S(1)}, bf16[3,64,2432]{2,1,0:T(8,128)(2,1)S(1)}, u32[]{:S(2)}, u32[]{:S(2)}) %collective-permute-start.13) | collective-permute-done | bytes 933920 | tf_op jit(solution)/shard_map/ppermute | solution.py:444
  135.1 1.8 %early.1 = f32[3,64,4032]{2,1,0:T(8,128)S(1)} custom-call(s32[1]{0:T(128)} %bitcast.core, f32[3,64,2432]{2,1,0:T(8,128)S(1)} %get-tuple-element.86.own, bf16[3,64,2816]{2,1,0:T(8,128)(2,1)S(1)} %collective-permute-done.11.direct, bf16[3,64,2432]{2,1,0:T(8,128)(2,1)S(1)} %collective-permute-done.13.pair, bf16[3,64,2432]{2,1,0:T(8,128)(2,1)S(1)} %collective-permute-done.14.far), custom_call_target="tpu_custom_call" | custom-call | flops 10000000000 | bytes 100000000 | tf_op jit(solution)/shard_map/early/pallas_call | solution.py:663
  136.9 5.6 %collective-permute-done.15.merged = bf16[3,64,2816]{2,1,0:T(8,128)(2,1)S(1)} collective-permute-done((bf16[3,64,2816]{2,1,0:T(8,128)(2,1)S(1)}, bf16[3,64,2816]{2,1,0:T(8,128)(2,1)S(1)}, u32[]{:S(2)}, u32[]{:S(2)}) %collective-permute-start.15) | collective-permute-done | bytes 1081376 | tf_op jit(solution)/shard_map/ppermute | solution.py:444
  142.5 2.8 %total.1 = f32[3,64,4032]{2,1,0:T(8,128)} custom-call(s32[1]{0:T(128)} %bitcast.core, f32[3,64,4032]{2,1,0:T(8,128)S(1)} %early.1, bf16[3,64,2816]{2,1,0:T(8,128)(2,1)S(1)} %collective-permute-done.15.merged), custom_call_target="tpu_custom_call" | custom-call | flops 10000000 | bytes 10000000 | tf_op jit(solution)/shard_map/total/pallas_call | solution.py:673
  (35 shorter events, 0.1 us)
Async XLA Ops:
  0.0 3.1 %copy-start.4 = (s32[24,27]{1,0:T(8,128)S(1)}, s32[24,27]{1,0:T(8,128)}, u32[]{:S(2)}) copy-start(s32[24,27]{1,0:T(8,128)} %param.7) | copy-start | bytes 7780
  0.0 10.6 %copy-start.5 = (s32[24,7]{0,1:T(8,128)S(1)}, s32[24,7]{0,1:T(8,128)}, u32[]{:S(2)}) copy-start(s32[24,7]{0,1:T(8,128)} %param.6) | copy-start | bytes 2020
  3.2 7.8 %collective-permute-start.1 = (s32[8,27]{1,0:T(8,128)S(1)}, s32[8,27]{1,0:T(8,128)S(1)}, u32[]{:S(2)}, u32[]{:S(2)}) collective-permute-start(s32[8,27]{1,0:T(8,128)S(1)} %get-tuple-element.97), channel_id=1, source_target_pairs={{0,31},{1,2},{2,1},{3,4},{4,3},{5,6},{6,5},{7,8},{8,7},{9,10},{10,... | collective-permute-start | bytes 2600 | tf_op jit(solution)/shard_map/ppermute | solution.py:444
  9.6 1.5 %collective-permute-start = (s32[8,27]{1,0:T(8,128)S(1)}, s32[8,27]{1,0:T(8,128)S(1)}, u32[]{:S(2)}, u32[]{:S(2)}) collective-permute-start(s32[8,27]{1,0:T(8,128)S(1)} %get-tuple-element.98), channel_id=1, source_target_pairs={{0,1},{1,0},{2,3},{3,2},{4,5},{5,4},{6,7},{7,6},{8,9},{9,8},{10,11... | collective-permute-start | bytes 2600 | tf_op jit(solution)/shard_map/ppermute | solution.py:444
  9.6 4.3 %collective-permute-start.2 = (bf16[8,64,1728]{2,1,0:T(8,128)(2,1)}, bf16[8,64,1728]{2,1,0:T(8,128)(2,1)}, u32[]{:S(2)}, u32[]{:S(2)}) collective-permute-start(bf16[8,64,1728]{2,1,0:T(8,128)(2,1)} %get-tuple-element.54), channel_id=1, source_target_pairs={{0,1},{1,0},{2,3},{3,2},{4,5},{5,4},{6,7},{7,6},{8,9},{9,8},{10,11... | collective-permute-start | bytes 5308424 | tf_op jit(solution)/shard_map/ppermute | solution.py:444
  10.1 43.0 %collective-permute-start.3 = (bf16[8,64,1728]{2,1,0:T(8,128)(2,1)}, bf16[8,64,1728]{2,1,0:T(8,128)(2,1)S(1)}, u32[]{:S(2)}, u32[]{:S(2)}) collective-permute-start(bf16[8,64,1728]{2,1,0:T(8,128)(2,1)} %get-tuple-element.57), channel_id=1, source_target_pairs={{0,31},{1,2},{2,1},{3,4},{4,3},{5,6},{6,5},{7,8},{8,7},{9,10},{10,... | collective-permute-start | bytes 5308424 | tf_op jit(solution)/shard_map/ppermute | solution.py:444
  52.1 9.7 %copy-start.2 = (bf16[9,64,512]{2,1,0:T(8,128)(2,1)}, bf16[9,64,512]{2,1,0:T(8,128)(2,1)S(1)}, u32[]{:S(2)}) copy-start(bf16[9,64,512]{2,1,0:T(8,128)(2,1)S(1)} %get-tuple-element.56.slow) | copy-start | bytes 1769476
  52.1 4.5 %collective-permute-start.4 = (bf16[3,64,2432]{2,1,0:T(8,128)(2,1)S(1)}, bf16[3,64,2432]{2,1,0:T(8,128)(2,1)S(1)}, u32[]{:S(2)}, u32[]{:S(2)}) collective-permute-start(bf16[3,64,2432]{2,1,0:T(8,128)(2,1)S(1)} %get-tuple-element.58), channel_id=1, source_target_pairs={{0,1},{1,0},{2,3},{3,2},{4,5},{5,4},{6,7},{7,6},{8,9},{9,8},{10,11... | collective-permute-start | bytes 2801672 | tf_op jit(solution)/shard_map/ppermute | solution.py:444
  52.6 4.0 %collective-permute-start.5 = (bf16[3,64,2432]{2,1,0:T(8,128)(2,1)S(1)}, bf16[3,64,2432]{2,1,0:T(8,128)(2,1)S(1)}, u32[]{:S(2)}, u32[]{:S(2)}) collective-permute-start(bf16[3,64,2432]{2,1,0:T(8,128)(2,1)S(1)} %get-tuple-element.59), channel_id=1, source_target_pairs={{0,1},{1,0},{2,3},{3,2},{4,5},{5,4},{6,7},{7,6},{8,9},{9,8},{10,11... | collective-permute-start | bytes 2801672 | tf_op jit(solution)/shard_map/ppermute | solution.py:444
  52.7 3.9 %collective-permute-start.6 = (bf16[6,64,512]{2,1,0:T(8,128)(2,1)S(1)}, bf16[6,64,512]{2,1,0:T(8,128)(2,1)S(1)}, u32[]{:S(2)}, u32[]{:S(2)}) collective-permute-start(bf16[6,64,512]{2,1,0:T(8,128)(2,1)S(1)} %get-tuple-element.60), channel_id=1, source_target_pairs={{0,1},{1,0},{2,3},{3,2},{4,5},{5,4},{6,7},{7,6},{8,9},{9,8},{10,11... | collective-permute-start | bytes 1179656 | tf_op jit(solution)/shard_map/ppermute | solution.py:444
  56.6 1.4 copy-start.1
  61.8 6.8 %collective-permute-start.7 = (bf16[40,64,512]{2,1,0:T(8,128)(2,1)S(1)}, bf16[40,64,512]{2,1,0:T(8,128)(2,1)S(1)}, u32[]{:S(2)}, u32[]{:S(2)}) collective-permute-start(bf16[40,64,512]{2,1,0:T(8,128)(2,1)S(1)} %slow.1.wt_slow), channel_id=1, source_target_pairs={{0,1},{1,0},{2,3},{3,2},{4,5},{5,4},{6,7},{7,6},{8,9},{9,8},{10,11... | collective-permute-start | bytes 7864328 | tf_op jit(solution)/shard_map/ppermute | solution.py:444
  62.2 3.3 %copy-start = (bf16[6,64,2432]{2,1,0:T(8,128)(2,1)S(1)}, bf16[6,64,2432]{2,1,0:T(8,128)(2,1)}, u32[]{:S(2)}) copy-start(bf16[6,64,2432]{2,1,0:T(8,128)(2,1)} %get-tuple-element.75.inner) | copy-start | bytes 5603332
  62.2 23.1 %slice-start = ((s8[5242880]{0:T(1024)(128)(4,1)}), s8[4194304]{0:T(1024)(128)(4,1)S(1)}, s32[]{:S(2)}) async-start(s8[5242880]{0:T(1024)(128)(4,1)} %bitcast.9), calls=%async_computation | async-start | bytes 8388608
  64.6 6.9 %collective-permute-start.8 = (bf16[3,64,2432]{2,1,0:T(8,128)(2,1)S(1)}, bf16[3,64,2432]{2,1,0:T(8,128)(2,1)S(1)}, u32[]{:S(2)}, u32[]{:S(2)}) collective-permute-start(bf16[3,64,2432]{2,1,0:T(8,128)(2,1)S(1)} %far.1), channel_id=1, source_target_pairs={{1,2},{2,1},{5,6},{6,5},{9,10},{10,9},{13,14},{14,13},{17,18},{18,... | collective-permute-start | bytes 2801672 | tf_op jit(solution)/shard_map/ppermute | solution.py:444
  65.6 19.8 %slice-start.1 = ((s8[5242880]{0:T(1024)(128)(4,1)}), s8[1048576]{0:T(1024)(128)(4,1)S(1)}, s32[]{:S(2)}) async-start(s8[5242880]{0:T(1024)(128)(4,1)} %bitcast.9), calls=%async_computation.1 | async-start | bytes 2097152
  68.6 3.0 %copy-start.6 = (bf16[9,64,2432]{2,1,0:T(8,128)(2,1)S(1)}, bf16[9,64,2432]{2,1,0:T(8,128)(2,1)}, u32[]{:S(2)}) copy-start(bf16[9,64,2432]{2,1,0:T(8,128)(2,1)} %get-tuple-element.85) | copy-start | bytes 8404996
  71.5 13.8 %copy-start.3 = (bf16[9,64,512]{2,1,0:T(8,128)(2,1)S(1)}, bf16[9,64,512]{2,1,0:T(8,128)(2,1)}, u32[]{:S(2)}) copy-start(bf16[9,64,512]{2,1,0:T(8,128)(2,1)} %copy-done.2) | copy-start | bytes 1769476
  71.5 13.8 %collective-permute-start.10 = (bf16[9,64,2432]{2,1,0:T(8,128)(2,1)S(1)}, bf16[9,64,2432]{2,1,0:T(8,128)(2,1)S(1)}, u32[]{:S(2)}, u32[]{:S(2)}) collective-permute-start(bf16[9,64,2432]{2,1,0:T(8,128)(2,1)S(1)} %copy-done.6), channel_id=1, source_target_pairs={{0,1},{1,0},{2,3},{3,2},{4,5},{5,4},{6,7},{7,6},{8,9},{9,8},{10,11... | collective-permute-start | bytes 8405000 | tf_op jit(solution)/shard_map/ppermute | solution.py:444
  79.7 5.6 %collective-permute-start.9 = (bf16[9,64,512]{2,1,0:T(8,128)(2,1)S(1)}, bf16[9,64,512]{2,1,0:T(8,128)(2,1)S(1)}, u32[]{:S(2)}, u32[]{:S(2)}) collective-permute-start(bf16[9,64,512]{2,1,0:T(8,128)(2,1)S(1)} %get-tuple-element.83), channel_id=1, source_target_pairs={{0,1},{1,0},{2,3},{3,2},{4,5},{5,4},{6,7},{7,6},{8,9},{9,8},{10,11... | collective-permute-start | bytes 1769480 | tf_op jit(solution)/shard_map/ppermute | solution.py:444
  79.7 23.0 %collective-permute-start.12 = (bf16[3,64,2432]{2,1,0:T(8,128)(2,1)S(1)}, bf16[3,64,2432]{2,1,0:T(8,128)(2,1)S(1)}, u32[]{:S(2)}, u32[]{:S(2)}) collective-permute-start(bf16[3,64,2432]{2,1,0:T(8,128)(2,1)S(1)} %get-tuple-element.89), channel_id=1, source_target_pairs={{0,2},{1,3},{2,0},{3,1},{4,6},{5,7},{6,4},{7,5},{8,10},{9,11},{10,... | collective-permute-start | bytes 2801672 | tf_op jit(solution)/shard_map/ppermute | solution.py:444
  80.9 27.5 %collective-permute-start.11 = (bf16[3,64,2816]{2,1,0:T(8,128)(2,1)S(1)}, bf16[3,64,2816]{2,1,0:T(8,128)(2,1)S(1)}, u32[]{:S(2)}, u32[]{:S(2)}) collective-permute-start(bf16[3,64,2816]{2,1,0:T(8,128)(2,1)S(1)} %merge_far.1), channel_id=1, source_target_pairs={{0,28},{1,29},{2,6},{3,7},{4,0},{5,1},{6,10},{7,11},{8,4},{9,5},{1... | collective-permute-start | bytes 3244040 | tf_op jit(solution)/shard_map/ppermute | solution.py:444
  102.8 32.3 %collective-permute-start.13 = (bf16[3,64,2432]{2,1,0:T(8,128)(2,1)S(1)}, bf16[3,64,2432]{2,1,0:T(8,128)(2,1)S(1)}, u32[]{:S(2)}, u32[]{:S(2)}) collective-permute-start(bf16[3,64,2432]{2,1,0:T(8,128)(2,1)S(1)} %get-tuple-element.91), channel_id=1, source_target_pairs={{0,2},{1,3},{2,0},{3,1},{4,6},{5,7},{6,4},{7,5},{8,10},{9,11},{10,... | collective-permute-start | bytes 2801672 | tf_op jit(solution)/shard_map/ppermute | solution.py:444
  103.1 32.0 %collective-permute-start.14 = (bf16[3,64,2432]{2,1,0:T(8,128)(2,1)S(1)}, bf16[3,64,2432]{2,1,0:T(8,128)(2,1)S(1)}, u32[]{:S(2)}, u32[]{:S(2)}) collective-permute-start(bf16[3,64,2432]{2,1,0:T(8,128)(2,1)S(1)} %far.1), channel_id=1, source_target_pairs={{0,27},{3,8},{4,31},{7,12},{8,3},{11,16},{12,7},{15,20},{16,11},{1... | collective-permute-start | bytes 2801672 | tf_op jit(solution)/shard_map/ppermute | solution.py:444
  106.4 36.1 %collective-permute-start.15 = (bf16[3,64,2816]{2,1,0:T(8,128)(2,1)S(1)}, bf16[3,64,2816]{2,1,0:T(8,128)(2,1)S(1)}, u32[]{:S(2)}, u32[]{:S(2)}) collective-permute-start(bf16[3,64,2816]{2,1,0:T(8,128)(2,1)S(1)} %merge.1), channel_id=1, source_target_pairs={{0,4},{1,5},{2,30},{3,31},{4,8},{5,9},{6,2},{7,3},{8,12},{9,13},{1... | collective-permute-start | bytes 3244040 | tf_op jit(solution)/shard_map/ppermute | solution.py:444

commit v11 on v9

--- a/solution.py
+++ b/solution.py
@@ -64,24 +64,37 @@
         )
 
 
-def spread_quad(turned, index, first, store, count, unroll):
+def spread_quad(turned, index, first, store, count):
     half = low_half()
-
-    def place(slot, carry):
+    for slot in range(count):
         for pair in range(2):
             lanes = slice(pair * 2 * BS, (pair + 1) * 2 * BS)
             left = turned[index[first + 2 * pair, slot], :, lanes]
             right = turned[index[first + 2 * pair + 1, slot], :, lanes]
             store(slot, pair, jnp.where(half, left, right))
-        return carry
-
-    lax.fori_loop(0, count, place, 0, unroll=unroll)
+
+
+def turn_and_spread(count, turn, spread, buffers):
+    even, odd = buffers
+    turn(0, even)
+
+    def two(step):
+        turn(2 * step + 1, odd)
+        spread(2 * step, even)
+        turn(2 * step + 2, even)
+        spread(2 * step + 1, odd)
+
+    if count > 2:
+        pl.loop(0, count // 2 - 1)(two)
+
+    turn(count - 1, odd)
+    spread(count - 2, even)
+    spread(count - 1, odd)
 
 
 def fast_kernel(
     core,
-    inv_own,
-    inv_fast,
+    inv_p,
     inv_a,
     p_own,
     p_fast,
@@ -105,7 +118,9 @@
     at,
     unit,
     turned_p,
+    turned_p2,
     turned_a,
+    turned_a2,
     lhs,
     rows_buf,
     fast_buf,
@@ -132,46 +147,48 @@
         load(quad).start()
 
     unit[...] = eye(LANES)
-    turned_p[KP] = jnp.zeros((BS, LANES), jnp.bfloat16)
-    turned_a[KA] = jnp.zeros((BS, LANES), jnp.bfloat16)
-
-    @pl.loop(0, own_quads)
-    def _(quad):
+    for buffers, empty in (((turned_p, turned_p2), KP), ((turned_a, turned_a2), KA)):
+        for buffer in buffers:
+            buffer[empty] = jnp.zeros((BS, LANES), jnp.bfloat16)
+
+    def turn_a(quad, turned):
         block = a_own[pl.ds(quad * QUAD, QUAD)].reshape(LANES, KA * BS)
-        transpose_quad(unit, block, turned_a, KA * BS)
+        transpose_quad(unit, block, turned, KA * BS)
+
+    def spread_a(quad, turned):
         agg = quad // halo_quads
+        first_lane = (quad % halo_quads) * LANES
 
         def store(slot, pair, value):
-            lane = pl.multiple_of((quad % halo_quads) * LANES + pair * 2 * BS, 2 * BS)
+            lane = pl.multiple_of(first_lane + pair * 2 * BS, 2 * BS)
             at[agg, slot, :, pl.ds(lane, 2 * BS)] = value
 
-        spread_quad(turned_a, inv_a, quad * QUAD, store, 3 * AGG, 8)
+        spread_quad(turned, inv_a, quad * QUAD, store, 3 * AGG)
+
+    turn_and_spread(own_quads, turn_a, spread_a, (turned_a, turned_a2))
 
     slow_agg = 2 * s
     halo_copy = pltpu.make_async_copy(at.at[slow_agg, pl.ds(16 * s, AGG)], at_halo, out_sems.at[0])
     halo_copy.start()
 
-    def band_quad(source_row, index, index_row, first_lane):
-        block = p_buf[pl.ds(source_row, QUAD)].reshape(LANES, KP * BS)
-        transpose_quad(unit, block, turned_p, KP * BS)
+    def turn_p(quad, turned):
+        block = p_buf[pl.ds(quad * QUAD, QUAD)].reshape(LANES, KP * BS)
+        transpose_quad(unit, block, turned, KP * BS)
+
+    def spread_p(quad, turned):
+        own_lane = AW + quad * LANES
+        halo_lane = (AW + K) * (1 - s) + (quad - own_quads) * LANES
+        first_lane = jnp.where(quad < own_quads, own_lane, halo_lane)
 
         def store(slot, pair, value):
             lane = pl.multiple_of(first_lane + pair * 2 * BS, 2 * BS)
             ext[slot, :, pl.ds(lane, 2 * BS)] = value
 
-        spread_quad(turned_p, index, index_row, store, COLS, 7)
+        spread_quad(turned, inv_p, quad * QUAD, store, COLS)
 
     for quad in range(own_quads + halo_quads):
         load(quad).wait()
-
-    @pl.loop(0, own_quads)
-    def _(quad):
-        band_quad(quad * QUAD, inv_own, quad * QUAD, AW + quad * LANES)
-
-    @pl.loop(0, halo_quads)
-    def _(quad):
-        first_lane = (AW + K) * (1 - s) + quad * LANES
-        band_quad((own_quads + quad) * QUAD, inv_fast, quad * QUAD, first_lane)
+    turn_and_spread(own_quads + halo_quads, turn_p, spread_p, (turned_p, turned_p2))
 
     fast_lanes = pl.ds(pl.multiple_of(AW + (1 - s) * AW, AW), 2 * AW)
     slow_lanes = pl.ds(pl.multiple_of(AW + 2 * s * AW, AW), AW)
@@ -309,22 +326,24 @@
     each_tile(step)
 
 
-def slow_kernel(core, inv_slow, p_slow, at_halo, rest, wt, unit, turned_p, ext):
+def slow_kernel(core, inv_slow, p_slow, at_halo, rest, wt, unit, turned_p, turned_p2, ext):
     s, x = places(core)
     unit[...] = eye(LANES)
-    turned_p[KP] = jnp.zeros((BS, LANES), jnp.bfloat16)
-
-    @pl.loop(0, AGG // QUAD)
-    def _(quad):
-        block = p_slow[pl.ds(quad * QUAD, QUAD)].reshape(LANES, KP * BS)
-        transpose_quad(unit, block, turned_p, KP * BS)
-
+    for buffer in (turned_p, turned_p2):
+        buffer[KP] = jnp.zeros((BS, LANES), jnp.bfloat16)
+
+    def turn(quad, turned):
+        block = p_slow[quad * QUAD : (quad + 1) * QUAD].reshape(LANES, KP * BS)
+        transpose_quad(unit, block, turned, KP * BS)
+
+    def spread(quad, turned):
         def store(slot, pair, value):
-            lane = pl.multiple_of(quad * LANES + pair * 2 * BS, 2 * BS)
-            ext[slot, :, pl.ds(lane, 2 * BS)] = value
-
-        spread_quad(turned_p, inv_slow, quad * QUAD, store, WSLOT, 11)
-
+            lane = quad * LANES + pair * 2 * BS
+            ext[slot, :, lane : lane + 2 * BS] = value
+
+        spread_quad(turned, inv_slow, quad * QUAD, store, WSLOT)
+
+    turn_and_spread(AGG // QUAD, turn, spread, (turned_p, turned_p2))
     wt[0:5] = jnp.zeros((5, BS, AW), jnp.bfloat16)
     wt[WSLOT:] = jnp.zeros((WCOLS - WSLOT, BS, AW), jnp.bfloat16)
     chunk = WSLOT // 3
@@ -561,7 +580,7 @@
     ) = pl.pallas_call(
         fast_kernel,
         out_shape=outs,
-        in_specs=[smem] * 4 + [hbm, hbm, vmem],
+        in_specs=[smem] * 3 + [hbm, hbm, vmem],
         out_specs=[hbm] * len(outs),
         scratch_shapes=[
             pltpu.VMEM((NB + AGG, BS, KP * BS), bf16),
@@ -569,6 +588,8 @@
             pltpu.VMEM((NC, 3 * AGG, BS, AW), bf16),
             pltpu.VMEM((LANES, LANES), bf16),
             pltpu.VMEM((KP + 1, BS, LANES), bf16),
+            pltpu.VMEM((KP + 1, BS, LANES), bf16),
+            pltpu.VMEM((KA + 1, BS, LANES), bf16),
             pltpu.VMEM((KA + 1, BS, LANES), bf16),
             pltpu.VMEM((ROWS + REST, BS, 2 * AW), bf16),
             pltpu.VMEM((ROWS + REST, BS, span), bf16),
@@ -583,7 +604,7 @@
         compiler_params=params(56),
         cost_estimate=cost(20 * 10**9, 30 * 10**6),
         name="fast",
-    )(core, inv_own, inv_fast, inv_a, p_blocks, p_fast, a_blocks)
+    )(core, jnp.concatenate([inv_own, inv_fast]), inv_a, p_blocks, p_fast, a_blocks)
 
     low = permuted(send_low, inward)
     high = permuted(send_high, inward)
@@ -607,6 +628,7 @@
         out_specs=vmem,
         scratch_shapes=[
             pltpu.VMEM((LANES, LANES), bf16),
+            pltpu.VMEM((KP + 1, BS, LANES), bf16),
             pltpu.VMEM((KP + 1, BS, LANES), bf16),
             pltpu.VMEM((WSLOT, BS, AW), bf16),
         ],
@@ -647,8 +669,10 @@
         cost_estimate=cost(10**6, 10**5),
         name="join_first",
     )(other_first, wt_other, mine)
-    relay, direct, far_near, send_rest, other_rest = lax.optimization_barrier(
-        (relay, direct, far_near, send_rest, other_rest)
+    straight = [i for i in range(devices) if i % 4 in (0, 3)]
+    far = permuted(far, [(i, (i + (5 if i % 2 else -5)) % devices) for i in straight])
+    relay, direct, far_near, far, send_rest, other_rest = lax.optimization_barrier(
+        (relay, direct, far_near, far, send_rest, other_rest)
     )
     arrived_rest = permuted(send_rest, inward)
     other_rest = permuted(other_rest, inward)
@@ -679,13 +703,10 @@
         cost_estimate=cost(40 * 10**9, 200 * 10**6),
         name="join_rest",
     )(fast_rest, slow_rest, other_rest, wt_fast, wt_slow, wt_other, arrived_rest)
-    relay, pair, far = lax.optimization_barrier((relay, pair, far))
-    relay_in, direct = lax.optimization_barrier((relay, direct))
-    merged = merge_rows(merge, relay_in, "merge")
+    relay, pair = lax.optimization_barrier((relay, pair))
+    merged = merge_rows(merge, relay, "merge")
     merged = permuted(merged, [(i, (i - 4 * x_sign[i]) % devices) for i in range(devices)])
     pair = permuted(pair, along_x)
-    straight = [i for i in range(devices) if i % 4 in (0, 3)]
-    far = permuted(far, [(i, (i + (5 if i % 2 else -5)) % devices) for i in straight])
 
     total = block(NC, BAND * BS, jnp.float32)
     frame = pltpu.VMEM((BS, FRAME * BS), jnp.float32)

time: 144 us -> 139 us (0.965)
  Pallas kernels: 66.1 us -> 61.5 us
  waiting for transfers between devices: 44.5 us -> 42.6 us
  starting transfers between devices: 26.9 us -> 28.6 us
    pallas_call x1, Pallas kernels: 35.7 us -> 31.9 us  [body(): pl.pallas_call(fast_kernel, out_shape=outs, in_specs=[smem] * 3 + [hbm, h...]
    ppermute x16, waiting for transfers between devices: 44.5 us -> 42.6 us  [permuted(): return lax.ppermute(block, 'dom', pairs)]
    ppermute x16, starting transfers between devices: 26.9 us -> 28.6 us  [permuted(): return lax.ppermute(block, 'dom', pairs)]
  transfers between devices with their start and end apart: 16 -> 16, of which waited for: 5 -> 7; matrix products, arithmetic and copies ran while one was open for 2% -> 2% of each run, Pallas kernels for 39% -> 38%
where the time goes in v11:
time: 139 us
  Pallas kernels  61.5 us (44%)
  waiting for transfers between devices  42.6 us (31%)
  starting transfers between devices  28.6 us (21%)
  local copies, waits for them, and re-layouts  3.59 us (3%)
  other arithmetic  1.91 us (1%)
    ppermute x16, waiting for transfers between devices, permuted(): return lax.ppermute(block, 'dom', pairs)  42.6 us
    pallas_call x1, Pallas kernels, body(): pl.pallas_call(fast_kernel, out_shape=outs, in_specs=[smem] * 3 + [hbm, h...  31.9 us
    ppermute x16, starting transfers between devices, permuted(): return lax.ppermute(block, 'dom', pairs)  28.6 us
    pallas_call x1, Pallas kernels, body(): pl.pallas_call(join_rest_kernel, out_shape=[block(NC, span, jnp.float32),...  8.11 us
    pallas_call x1, Pallas kernels, body(): pl.pallas_call(slow_kernel, out_shape=block(WCOLS, AW), in_specs=[smem] *...  3.55 us
    unnamed x28, local copies, waits for them, and re-layouts  3.32 us
    pallas_call x1, Pallas kernels, body(): pl.pallas_call(pick_kernel, out_shape=[edge, edge], in_specs=[smem, hbm],...  3.08 us
    pallas_call x1, Pallas kernels, body(): pl.pallas_call(join_first_kernel, out_shape=[block(NC, span), block(NC, s...  2.93 us
  transfers between devices with their start and end apart: 16, of which 7 were waited for; matrix products, arithmetic and copies ran while one was open for 2% of the time, Pallas kernels for 38%

profile of v11, /device:TPU:0, one launch (start us, length us, event | category | flops | bytes accessed | tf_op | source)
XLA Modules:
  0.0 138.7 jit_solution(4000939663248096154)
XLA Ops:
  0.0 3.1 %pick.1 = (bf16[8,64,1728]{2,1,0:T(8,128)(2,1)}, bf16[8,64,1728]{2,1,0:T(8,128)(2,1)}) custom-call(s32[1]{0:T(128)} %bitcast.core, bf16[24,64,1728]{2,1,0:T(8,128)(2,1)} %p_own.1), custom_call_target="tpu_custom_call" | custom-call | tf_op jit(solution)/shard_map/pick/pallas_call | solution.py:511
  3.2 6.4 %collective-permute-start.1 = (s32[8,27]{1,0:T(8,128)S(1)}, s32[8,27]{1,0:T(8,128)S(1)}, u32[]{:S(2)}, u32[]{:S(2)}) collective-permute-start(s32[8,27]{1,0:T(8,128)S(1)} %get-tuple-element.97), channel_id=1, source_target_pairs={{0,31},{1,2},{2,1},{3,4},{4,3},{5,6},{6,5},{7,8},{8,7},{9,10},{10,... | collective-permute-start | bytes 2600 | tf_op jit(solution)/shard_map/ppermute | solution.py:477
  9.6 0.5 collective-permute-start.2
  10.1 0.3 collective-permute-start.3
  10.4 0.1 fusion.1
  10.5 0.1 copy.15
  10.6 0.2 select_reduce_fusion
  10.8 0.1 select_reduce_fusion.3
  10.9 0.6 broadcast_add_fusion.inv_a
  11.6 0.1 copy.17
  11.7 0.1 copy.16
  11.8 0.1 select_reduce_fusion.1
  11.9 0.1 select_reduce_fusion.2
  12.1 0.6 pad_add_fusion.inv_p
  12.7 1.2 collective-permute-done.2.p_fast
  13.9 31.9 %fast.1 = (bf16[3,64,2432]{2,1,0:T(8,128)(2,1)}, bf16[3,64,2432]{2,1,0:T(8,128)(2,1)}, bf16[3,64,2432]{2,1,0:T(8,128)(2,1)}, bf16[6,64,2432]{2,1,0:T(8,128)(2,1)...) custom-call(s32[1]{0:T(128)} %bitcast.core, ...), custom_call_target="tpu_custom_call" | custom-call | flops 20000000000 | bytes 30000000 | tf_op jit(solution)/shard_map/fast/pallas_call | solution.py:580
  45.7 0.5 collective-permute-start.4
  46.2 0.1 collective-permute-start.5
  46.3 0.4 collective-permute-start.6
  46.7 2.2 %copy-done = f32[33,64,512]{2,1,0:T(8,128)S(1)} copy-done((f32[33,64,512]{2,1,0:T(8,128)S(1)}, f32[33,64,512]{2,1,0:T(8,128)}, u32[]{:S(2)}) %copy-start) | copy-done | bytes 4325400
  48.9 1.0 copy-done.2
  50.0 0.5 stage.1
  50.5 0.0 collective-permute-done.3.p_slow
  50.6 3.5 %slow.1.wt_slow = bf16[40,64,512]{2,1,0:T(8,128)(2,1)S(1)} custom-call(s32[1]{0:T(128)} %bitcast.core, s32[8,33]{1,0:T(8,128)S(1)} %broadcast_add_fusion.2.inv_slow, bf16[8,64,1728]{2,1,0:T(8,128)(2,1)S(1)} %collective-permute-done.3.p_slow, bf16[8,64,512]{2,1,0:T(8,128)(2,1)S(1)} %get-tuple-element.66.at_halo, f32[33,64,512]{2,1,0:T(8,128)S(1)} %get-tuple-element.67.rest), custom_call_target="tpu_custom_call" | custom-call | flops 20000000000 | bytes 200000000 | tf_op jit(solution)/shard_map/slow/pallas_call | solution.py:624
  54.1 0.3 collective-permute-start.7
  54.5 2.4 %far.1 = bf16[3,64,2432]{2,1,0:T(8,128)(2,1)S(1)} custom-call(bf16[3,64,512]{2,1,0:T(8,128)(2,1)S(1)} %copy-done.3, bf16[40,64,512]{2,1,0:T(8,128)(2,1)S(1)} %slow.1.wt_slow, bf16[3,64,2432]{2,1,0:T(8,128)(2,1)S(1)} %copy-done.1), custom_call_target="tpu_custom_call" | custom-call | flops 1000000000 | bytes 10000000 | tf_op jit(solution)/shard_map/far/pallas_call | solution.py:642
  56.9 4.6 %collective-permute-start.9 = (bf16[3,64,2432]{2,1,0:T(8,128)(2,1)S(1)}, bf16[3,64,2432]{2,1,0:T(8,128)(2,1)S(1)}, u32[]{:S(2)}, u32[]{:S(2)}) collective-permute-start(bf16[3,64,2432]{2,1,0:T(8,128)(2,1)S(1)} %far.1), channel_id=1, source_target_pairs={{0,27},{3,8},{4,31},{7,12},{8,3},{11,16},{12,7},{15,20},{16,11},{1... | collective-permute-start | bytes 2801672 | tf_op jit(solution)/shard_map/ppermute | solution.py:477
  61.5 0.9 collective-permute-start.8
  62.4 2.9 %mine.1 = f32[6,64,2432]{2,1,0:T(8,128)S(1)} custom-call(bf16[6,64,512]{2,1,0:T(8,128)(2,1)S(1)} %copy-done.5, bf16[40,64,512]{2,1,0:T(8,128)(2,1)S(1)} %slow.1.wt_slow, bf16[6,64,2432]{2,1,0:T(8,128)(2,1)S(1)} %copy-done.4, bf16[3,64,2432]{2,1,0:T(8,128)(2,1)S(1)} %collective-permute-done.4.low, bf16[3,64,2432]{2,1,0:T(8,128)(2,1)S(1)} %collective-permute-done.5.high), custom_call_target="tpu_custom_call" | custom-call | flops 10000000000 | bytes 100000000 | tf_op jit(solution)/shard_map/mine/pallas_call | solution.py:652
  65.3 0.0 copy-start.10
  65.4 2.9 %join_first.1 = (bf16[3,64,2432]{2,1,0:T(8,128)(2,1)S(1)}, f32[3,64,2432]{2,1,0:T(8,128)S(1)}) custom-call(bf16[6,64,512]{2,1,0:T(8,128)(2,1)S(1)} %collective-permute-done.6.other, bf16[40,64,512]{2,1,0:T(8,128)(2,1)S(1)} %collective-permute-done.7.wt_other, f32[6,64,2432]{2,1,0:T(8,128)S(1)} %mine.1), custom_call_target="tpu_custom_call" | custom-call | flops 1000000 | bytes 100000 | tf_op jit(solution)/shard_map/join_first/pallas_call | solution.py:663
  68.3 6.3 %collective-permute-done.9.far = bf16[3,64,2432]{2,1,0:T(8,128)(2,1)S(1)} collective-permute-done((bf16[3,64,2432]{2,1,0:T(8,128)(2,1)S(1)}, bf16[3,64,2432]{2,1,0:T(8,128)(2,1)S(1)}, u32[]{:S(2)}, u32[]{:S(2)}) %collective-permute-start.9) | collective-permute-done | bytes 933920 | tf_op jit(solution)/shard_map/ppermute | solution.py:477
  74.6 8.2 %collective-permute-start.11 = (bf16[9,64,2432]{2,1,0:T(8,128)(2,1)S(1)}, bf16[9,64,2432]{2,1,0:T(8,128)(2,1)S(1)}, u32[]{:S(2)}, u32[]{:S(2)}) collective-permute-start(bf16[9,64,2432]{2,1,0:T(8,128)(2,1)S(1)} %copy-done.10), channel_id=1, source_target_pairs={{0,1},{1,0},{2,3},{3,2},{4,5},{5,4},{6,7},{7,6},{8,9},{9,8},{10,11... | collective-permute-start | bytes 8405000 | tf_op jit(solution)/shard_map/ppermute | solution.py:477
  82.7 0.1 collective-permute-start.10
  82.8 1.9 %collective-permute-start.13 = (bf16[3,64,2432]{2,1,0:T(8,128)(2,1)S(1)}, bf16[3,64,2432]{2,1,0:T(8,128)(2,1)S(1)}, u32[]{:S(2)}, u32[]{:S(2)}) collective-permute-start(bf16[3,64,2432]{2,1,0:T(8,128)(2,1)S(1)} %get-tuple-element.89), channel_id=1, source_target_pairs={{0,2},{1,3},{2,0},{3,1},{4,6},{5,7},{6,4},{7,5},{8,10},{9,11},{10,... | collective-permute-start | bytes 2801672 | tf_op jit(solution)/shard_map/ppermute | solution.py:477
  84.8 0.8 merge_far.1
  85.6 2.6 %collective-permute-start.12 = (bf16[3,64,2816]{2,1,0:T(8,128)(2,1)S(1)}, bf16[3,64,2816]{2,1,0:T(8,128)(2,1)S(1)}, u32[]{:S(2)}, u32[]{:S(2)}) collective-permute-start(bf16[3,64,2816]{2,1,0:T(8,128)(2,1)S(1)} %merge_far.1), channel_id=1, source_target_pairs={{0,28},{1,29},{2,6},{3,7},{4,0},{5,1},{6,10},{7,11},{8,4},{9,5},{1... | collective-permute-start | bytes 3244040 | tf_op jit(solution)/shard_map/ppermute | solution.py:477
  88.2 0.2 collective-permute-done.10.other
  88.4 8.1 %join_rest.1 = (f32[3,64,2432]{2,1,0:T(8,128)S(1)}, bf16[3,64,2432]{2,1,0:T(8,128)(2,1)S(1)}, f32[3,64,2432]{2,1,0:T(8,128)S(1)}) custom-call(bf16[9,64,1024]{2,1,0:T(8,128)(2,1)S(1)} %copy-done.6, bf16[9,64,512]{2,1,0:T(8,128)(2,1)S(1)} %copy-done.7, bf16[9,64,512]{2,1,0:T(8,128)(2,1)S(1)} %collective-permute-done.10.other, ...), custom_call_target="tpu_custom_call" | custom-call | flops 40000000000 | bytes 200000000 | tf_op jit(solution)/shard_map/join_rest/pallas_call | solution.py:697
  96.5 9.4 %collective-permute-done.13.other = bf16[3,64,2432]{2,1,0:T(8,128)(2,1)S(1)} collective-permute-done((bf16[3,64,2432]{2,1,0:T(8,128)(2,1)S(1)}, bf16[3,64,2432]{2,1,0:T(8,128)(2,1)S(1)}, u32[]{:S(2)}, u32[]{:S(2)}) %collective-permute-start.13) | collective-permute-done | bytes 933920 | tf_op jit(solution)/shard_map/ppermute | solution.py:477
  105.9 1.6 %collective-permute-start.14 = (bf16[3,64,2432]{2,1,0:T(8,128)(2,1)S(1)}, bf16[3,64,2432]{2,1,0:T(8,128)(2,1)S(1)}, u32[]{:S(2)}, u32[]{:S(2)}) collective-permute-start(bf16[3,64,2432]{2,1,0:T(8,128)(2,1)S(1)} %get-tuple-element.91), channel_id=1, source_target_pairs={{0,2},{1,3},{2,0},{3,1},{4,6},{5,7},{6,4},{7,5},{8,10},{9,11},{10,... | collective-permute-start | bytes 2801672 | tf_op jit(solution)/shard_map/ppermute | solution.py:477
  107.5 0.8 merge.1
  108.3 0.1 collective-permute-start.15
  108.3 3.0 %collective-permute-done.12.direct = bf16[3,64,2816]{2,1,0:T(8,128)(2,1)S(1)} collective-permute-done((bf16[3,64,2816]{2,1,0:T(8,128)(2,1)S(1)}, bf16[3,64,2816]{2,1,0:T(8,128)(2,1)S(1)}, u32[]{:S(2)}, u32[]{:S(2)}) %collective-permute-start.12) | collective-permute-done | bytes 1081376 | tf_op jit(solution)/shard_map/ppermute | solution.py:477
  111.3 16.8 %collective-permute-done.14.pair = bf16[3,64,2432]{2,1,0:T(8,128)(2,1)S(1)} collective-permute-done((bf16[3,64,2432]{2,1,0:T(8,128)(2,1)S(1)}, bf16[3,64,2432]{2,1,0:T(8,128)(2,1)S(1)}, u32[]{:S(2)}, u32[]{:S(2)}) %collective-permute-start.14) | collective-permute-done | bytes 933920 | tf_op jit(solution)/shard_map/ppermute | solution.py:477
  128.1 1.8 %early.1 = f32[3,64,4032]{2,1,0:T(8,128)S(1)} custom-call(s32[1]{0:T(128)} %bitcast.core, f32[3,64,2432]{2,1,0:T(8,128)S(1)} %get-tuple-element.86.own, bf16[3,64,2816]{2,1,0:T(8,128)(2,1)S(1)} %collective-permute-done.12.direct, bf16[3,64,2432]{2,1,0:T(8,128)(2,1)S(1)} %collective-permute-done.14.pair, bf16[3,64,2432]{2,1,0:T(8,128)(2,1)S(1)} %collective-permute-done.9.far), custom_call_target="tpu_custom_call" | custom-call | flops 10000000000 | bytes 100000000 | tf_op jit(solution)/shard_map/early/pallas_call | solution.py:713
  130.0 5.8 %collective-permute-done.15.merged = bf16[3,64,2816]{2,1,0:T(8,128)(2,1)S(1)} collective-permute-done((bf16[3,64,2816]{2,1,0:T(8,128)(2,1)S(1)}, bf16[3,64,2816]{2,1,0:T(8,128)(2,1)S(1)}, u32[]{:S(2)}, u32[]{:S(2)}) %collective-permute-start.15) | collective-permute-done | bytes 1081376 | tf_op jit(solution)/shard_map/ppermute | solution.py:477
  135.7 2.8 %total.1 = f32[3,64,4032]{2,1,0:T(8,128)} custom-call(s32[1]{0:T(128)} %bitcast.core, f32[3,64,4032]{2,1,0:T(8,128)S(1)} %early.1, bf16[3,64,2816]{2,1,0:T(8,128)(2,1)S(1)} %collective-permute-done.15.merged), custom_call_target="tpu_custom_call" | custom-call | flops 10000000 | bytes 10000000 | tf_op jit(solution)/shard_map/total/pallas_call | solution.py:723
  (47 shorter events, 0.2 us)
Async XLA Ops:
  0.0 3.1 %copy-start.8 = (s32[24,27]{1,0:T(8,128)S(1)}, s32[24,27]{1,0:T(8,128)}, u32[]{:S(2)}) copy-start(s32[24,27]{1,0:T(8,128)} %param.7) | copy-start | bytes 7780
  0.0 10.8 %copy-start.9 = (s32[24,7]{0,1:T(8,128)S(1)}, s32[24,7]{0,1:T(8,128)}, u32[]{:S(2)}) copy-start(s32[24,7]{0,1:T(8,128)} %param.6) | copy-start | bytes 2020
  3.2 8.4 %collective-permute-start.1 = (s32[8,27]{1,0:T(8,128)S(1)}, s32[8,27]{1,0:T(8,128)S(1)}, u32[]{:S(2)}, u32[]{:S(2)}) collective-permute-start(s32[8,27]{1,0:T(8,128)S(1)} %get-tuple-element.97), channel_id=1, source_target_pairs={{0,31},{1,2},{2,1},{3,4},{4,3},{5,6},{6,5},{7,8},{8,7},{9,10},{10,... | collective-permute-start | bytes 2600 | tf_op jit(solution)/shard_map/ppermute | solution.py:477
  9.6 2.1 %collective-permute-start = (s32[8,27]{1,0:T(8,128)S(1)}, s32[8,27]{1,0:T(8,128)S(1)}, u32[]{:S(2)}, u32[]{:S(2)}) collective-permute-start(s32[8,27]{1,0:T(8,128)S(1)} %get-tuple-element.98), channel_id=1, source_target_pairs={{0,1},{1,0},{2,3},{3,2},{4,5},{5,4},{6,7},{7,6},{8,9},{9,8},{10,11... | collective-permute-start | bytes 2600 | tf_op jit(solution)/shard_map/ppermute | solution.py:477
  9.6 4.3 %collective-permute-start.2 = (bf16[8,64,1728]{2,1,0:T(8,128)(2,1)}, bf16[8,64,1728]{2,1,0:T(8,128)(2,1)}, u32[]{:S(2)}, u32[]{:S(2)}) collective-permute-start(bf16[8,64,1728]{2,1,0:T(8,128)(2,1)} %get-tuple-element.54), channel_id=1, source_target_pairs={{0,1},{1,0},{2,3},{3,2},{4,5},{5,4},{6,7},{7,6},{8,9},{9,8},{10,11... | collective-permute-start | bytes 5308424 | tf_op jit(solution)/shard_map/ppermute | solution.py:477
  10.1 40.4 %collective-permute-start.3 = (bf16[8,64,1728]{2,1,0:T(8,128)(2,1)}, bf16[8,64,1728]{2,1,0:T(8,128)(2,1)S(1)}, u32[]{:S(2)}, u32[]{:S(2)}) collective-permute-start(bf16[8,64,1728]{2,1,0:T(8,128)(2,1)} %get-tuple-element.57), channel_id=1, source_target_pairs={{0,31},{1,2},{2,1},{3,4},{4,3},{5,6},{6,5},{7,8},{8,7},{9,10},{10,... | collective-permute-start | bytes 5308424 | tf_op jit(solution)/shard_map/ppermute | solution.py:477
  45.7 4.8 %collective-permute-start.4 = (bf16[3,64,2432]{2,1,0:T(8,128)(2,1)}, bf16[3,64,2432]{2,1,0:T(8,128)(2,1)S(1)}, u32[]{:S(2)}, u32[]{:S(2)}) collective-permute-start(bf16[3,64,2432]{2,1,0:T(8,128)(2,1)} %get-tuple-element.58), channel_id=1, source_target_pairs={{0,1},{1,0},{2,3},{3,2},{4,5},{5,4},{6,7},{7,6},{8,9},{9,8},{10,11... | collective-permute-start | bytes 2801672 | tf_op jit(solution)/shard_map/ppermute | solution.py:477
  46.2 4.3 %collective-permute-start.5 = (bf16[3,64,2432]{2,1,0:T(8,128)(2,1)}, bf16[3,64,2432]{2,1,0:T(8,128)(2,1)S(1)}, u32[]{:S(2)}, u32[]{:S(2)}) collective-permute-start(bf16[3,64,2432]{2,1,0:T(8,128)(2,1)} %get-tuple-element.59), channel_id=1, source_target_pairs={{0,1},{1,0},{2,3},{3,2},{4,5},{5,4},{6,7},{7,6},{8,9},{9,8},{10,11... | collective-permute-start | bytes 2801672 | tf_op jit(solution)/shard_map/ppermute | solution.py:477
  46.3 4.2 %collective-permute-start.6 = (bf16[6,64,512]{2,1,0:T(8,128)(2,1)}, bf16[6,64,512]{2,1,0:T(8,128)(2,1)S(1)}, u32[]{:S(2)}, u32[]{:S(2)}) collective-permute-start(bf16[6,64,512]{2,1,0:T(8,128)(2,1)} %get-tuple-element.60), channel_id=1, source_target_pairs={{0,1},{1,0},{2,3},{3,2},{4,5},{5,4},{6,7},{7,6},{8,9},{9,8},{10,11... | collective-permute-start | bytes 1179656 | tf_op jit(solution)/shard_map/ppermute | solution.py:477
  46.7 2.2 %copy-start = (f32[33,64,512]{2,1,0:T(8,128)S(1)}, f32[33,64,512]{2,1,0:T(8,128)}, u32[]{:S(2)}) copy-start(f32[33,64,512]{2,1,0:T(8,128)} %get-tuple-element.65.rest) | copy-start | bytes 12976132
  48.9 1.0 copy-start.2
  50.5 3.9 %copy-start.1 = (bf16[3,64,2432]{2,1,0:T(8,128)(2,1)S(1)}, bf16[3,64,2432]{2,1,0:T(8,128)(2,1)}, u32[]{:S(2)}) copy-start(bf16[3,64,2432]{2,1,0:T(8,128)(2,1)} %get-tuple-element.73.far_fast) | copy-start | bytes 2801668
  50.5 3.9 %copy-start.3 = (bf16[3,64,512]{2,1,0:T(8,128)(2,1)S(1)}, bf16[3,64,512]{2,1,0:T(8,128)(2,1)}, u32[]{:S(2)}) copy-start(bf16[3,64,512]{2,1,0:T(8,128)(2,1)} %get-tuple-element.69.slow) | copy-start | bytes 589828
  50.6 11.8 %copy-start.5 = (bf16[6,64,512]{2,1,0:T(8,128)(2,1)S(1)}, bf16[6,64,512]{2,1,0:T(8,128)(2,1)}, u32[]{:S(2)}) copy-start(bf16[6,64,512]{2,1,0:T(8,128)(2,1)} %get-tuple-element.68.slow) | copy-start | bytes 1179652
  54.1 11.2 %collective-permute-start.7 = (bf16[40,64,512]{2,1,0:T(8,128)(2,1)S(1)}, bf16[40,64,512]{2,1,0:T(8,128)(2,1)S(1)}, u32[]{:S(2)}, u32[]{:S(2)}) collective-permute-start(bf16[40,64,512]{2,1,0:T(8,128)(2,1)S(1)} %slow.1.wt_slow), channel_id=1, source_target_pairs={{0,1},{1,0},{2,3},{3,2},{4,5},{5,4},{6,7},{7,6},{8,9},{9,8},{10,11... | collective-permute-start | bytes 7864328 | tf_op jit(solution)/shard_map/ppermute | solution.py:477
  54.5 7.9 %copy-start.4 = (bf16[6,64,2432]{2,1,0:T(8,128)(2,1)S(1)}, bf16[6,64,2432]{2,1,0:T(8,128)(2,1)}, u32[]{:S(2)}) copy-start(bf16[6,64,2432]{2,1,0:T(8,128)(2,1)} %get-tuple-element.75.inner) | copy-start | bytes 5603332
  54.5 33.9 %slice-start = ((s8[5242880]{0:T(1024)(128)(4,1)}), s8[4194304]{0:T(1024)(128)(4,1)S(1)}, s32[]{:S(2)}) async-start(s8[5242880]{0:T(1024)(128)(4,1)} %bitcast.9), calls=%async_computation | async-start | bytes 8388608
  56.9 17.7 %collective-permute-start.9 = (bf16[3,64,2432]{2,1,0:T(8,128)(2,1)S(1)}, bf16[3,64,2432]{2,1,0:T(8,128)(2,1)S(1)}, u32[]{:S(2)}, u32[]{:S(2)}) collective-permute-start(bf16[3,64,2432]{2,1,0:T(8,128)(2,1)S(1)} %far.1), channel_id=1, source_target_pairs={{0,27},{3,8},{4,31},{7,12},{8,3},{11,16},{12,7},{15,20},{16,11},{1... | collective-permute-start | bytes 2801672 | tf_op jit(solution)/shard_map/ppermute | solution.py:477
  61.5 13.1 %collective-permute-start.8 = (bf16[3,64,2432]{2,1,0:T(8,128)(2,1)S(1)}, bf16[3,64,2432]{2,1,0:T(8,128)(2,1)S(1)}, u32[]{:S(2)}, u32[]{:S(2)}) collective-permute-start(bf16[3,64,2432]{2,1,0:T(8,128)(2,1)S(1)} %far.1), channel_id=1, source_target_pairs={{1,2},{2,1},{5,6},{6,5},{9,10},{10,9},{13,14},{14,13},{17,18},{18,... | collective-permute-start | bytes 2801672 | tf_op jit(solution)/shard_map/ppermute | solution.py:477
  62.4 26.0 %slice-start.1 = ((s8[5242880]{0:T(1024)(128)(4,1)}), s8[1048576]{0:T(1024)(128)(4,1)S(1)}, s32[]{:S(2)}) async-start(s8[5242880]{0:T(1024)(128)(4,1)} %bitcast.9), calls=%async_computation.1 | async-start | bytes 2097152
  65.3 9.2 %copy-start.10 = (bf16[9,64,2432]{2,1,0:T(8,128)(2,1)S(1)}, bf16[9,64,2432]{2,1,0:T(8,128)(2,1)}, u32[]{:S(2)}) copy-start(bf16[9,64,2432]{2,1,0:T(8,128)(2,1)} %get-tuple-element.85) | copy-start | bytes 8404996
  65.3 17.4 %copy-start.11 = (bf16[9,64,512]{2,1,0:T(8,128)(2,1)S(1)}, bf16[9,64,512]{2,1,0:T(8,128)(2,1)}, u32[]{:S(2)}) copy-start(bf16[9,64,512]{2,1,0:T(8,128)(2,1)} %get-tuple-element.83) | copy-start | bytes 1769476
  74.6 13.8 %copy-start.6 = (bf16[9,64,1024]{2,1,0:T(8,128)(2,1)S(1)}, bf16[9,64,1024]{2,1,0:T(8,128)(2,1)}, u32[]{:S(2)}) copy-start(bf16[9,64,1024]{2,1,0:T(8,128)(2,1)} %get-tuple-element.55.fast) | copy-start | bytes 3538948
  74.6 13.8 %copy-start.7 = (bf16[9,64,512]{2,1,0:T(8,128)(2,1)S(1)}, bf16[9,64,512]{2,1,0:T(8,128)(2,1)}, u32[]{:S(2)}) copy-start(bf16[9,64,512]{2,1,0:T(8,128)(2,1)} %get-tuple-element.56.slow) | copy-start | bytes 1769476
  74.6 13.8 %collective-permute-start.11 = (bf16[9,64,2432]{2,1,0:T(8,128)(2,1)S(1)}, bf16[9,64,2432]{2,1,0:T(8,128)(2,1)S(1)}, u32[]{:S(2)}, u32[]{:S(2)}) collective-permute-start(bf16[9,64,2432]{2,1,0:T(8,128)(2,1)S(1)} %copy-done.10), channel_id=1, source_target_pairs={{0,1},{1,0},{2,3},{3,2},{4,5},{5,4},{6,7},{7,6},{8,9},{9,8},{10,11... | collective-permute-start | bytes 8405000 | tf_op jit(solution)/shard_map/ppermute | solution.py:477
  82.7 5.6 %collective-permute-start.10 = (bf16[9,64,512]{2,1,0:T(8,128)(2,1)S(1)}, bf16[9,64,512]{2,1,0:T(8,128)(2,1)S(1)}, u32[]{:S(2)}, u32[]{:S(2)}) collective-permute-start(bf16[9,64,512]{2,1,0:T(8,128)(2,1)S(1)} %copy-done.11), channel_id=1, source_target_pairs={{0,1},{1,0},{2,3},{3,2},{4,5},{5,4},{6,7},{7,6},{8,9},{9,8},{10,11... | collective-permute-start | bytes 1769480 | tf_op jit(solution)/shard_map/ppermute | solution.py:477
  82.8 23.0 %collective-permute-start.13 = (bf16[3,64,2432]{2,1,0:T(8,128)(2,1)S(1)}, bf16[3,64,2432]{2,1,0:T(8,128)(2,1)S(1)}, u32[]{:S(2)}, u32[]{:S(2)}) collective-permute-start(bf16[3,64,2432]{2,1,0:T(8,128)(2,1)S(1)} %get-tuple-element.89), channel_id=1, source_target_pairs={{0,2},{1,3},{2,0},{3,1},{4,6},{5,7},{6,4},{7,5},{8,10},{9,11},{10,... | collective-permute-start | bytes 2801672 | tf_op jit(solution)/shard_map/ppermute | solution.py:477
  85.6 25.7 %collective-permute-start.12 = (bf16[3,64,2816]{2,1,0:T(8,128)(2,1)S(1)}, bf16[3,64,2816]{2,1,0:T(8,128)(2,1)S(1)}, u32[]{:S(2)}, u32[]{:S(2)}) collective-permute-start(bf16[3,64,2816]{2,1,0:T(8,128)(2,1)S(1)} %merge_far.1), channel_id=1, source_target_pairs={{0,28},{1,29},{2,6},{3,7},{4,0},{5,1},{6,10},{7,11},{8,4},{9,5},{1... | collective-permute-start | bytes 3244040 | tf_op jit(solution)/shard_map/ppermute | solution.py:477
  105.9 22.3 %collective-permute-start.14 = (bf16[3,64,2432]{2,1,0:T(8,128)(2,1)S(1)}, bf16[3,64,2432]{2,1,0:T(8,128)(2,1)S(1)}, u32[]{:S(2)}, u32[]{:S(2)}) collective-permute-start(bf16[3,64,2432]{2,1,0:T(8,128)(2,1)S(1)} %get-tuple-element.91), channel_id=1, source_target_pairs={{0,2},{1,3},{2,0},{3,1},{4,6},{5,7},{6,4},{7,5},{8,10},{9,11},{10,... | collective-permute-start | bytes 2801672 | tf_op jit(solution)/shard_map/ppermute | solution.py:477
  108.3 27.5 %collective-permute-start.15 = (bf16[3,64,2816]{2,1,0:T(8,128)(2,1)S(1)}, bf16[3,64,2816]{2,1,0:T(8,128)(2,1)S(1)}, u32[]{:S(2)}, u32[]{:S(2)}) collective-permute-start(bf16[3,64,2816]{2,1,0:T(8,128)(2,1)S(1)} %merge.1), channel_id=1, source_target_pairs={{0,4},{1,5},{2,30},{3,31},{4,8},{5,9},{6,2},{7,3},{8,12},{9,13},{1... | collective-permute-start | bytes 3244040 | tf_op jit(solution)/shard_map/ppermute | solution.py:477

commit v12 on v11

--- a/solution.py
+++ b/solution.py
@@ -669,11 +669,11 @@
         cost_estimate=cost(10**6, 10**5),
         name="join_first",
     )(other_first, wt_other, mine)
-    straight = [i for i in range(devices) if i % 4 in (0, 3)]
-    far = permuted(far, [(i, (i + (5 if i % 2 else -5)) % devices) for i in straight])
     relay, direct, far_near, far, send_rest, other_rest = lax.optimization_barrier(
         (relay, direct, far_near, far, send_rest, other_rest)
     )
+    straight = [i for i in range(devices) if i % 4 in (0, 3)]
+    far = permuted(far, [(i, (i + (5 if i % 2 else -5)) % devices) for i in straight])
     arrived_rest = permuted(send_rest, inward)
     other_rest = permuted(other_rest, inward)
     along_x = [(i, i ^ 2) for i in range(devices)]
@@ -703,7 +703,7 @@
         cost_estimate=cost(40 * 10**9, 200 * 10**6),
         name="join_rest",
     )(fast_rest, slow_rest, other_rest, wt_fast, wt_slow, wt_other, arrived_rest)
-    relay, pair = lax.optimization_barrier((relay, pair))
+    relay, pair, far = lax.optimization_barrier((relay, pair, far))
     merged = merge_rows(merge, relay, "merge")
     merged = permuted(merged, [(i, (i - 4 * x_sign[i]) % devices) for i in range(devices)])
     pair = permuted(pair, along_x)

time: 139 us -> 138 us (level)
  starting transfers between devices: 28.6 us -> 26.7 us
    ppermute x16, starting transfers between devices: 28.6 us -> 26.7 us  [permuted(): return lax.ppermute(block, 'dom', pairs)]
  transfers between devices with their start and end apart: 16 -> 16, of which waited for: 7 -> 5; matrix products, arithmetic and copies ran while one was open for 2% -> 2% of each run, Pallas kernels for 38% -> 38%
where the time goes in v12:
time: 138 us
  Pallas kernels  61.5 us (45%)
  waiting for transfers between devices  43.7 us (32%)
  starting transfers between devices  26.7 us (19%)
  local copies, waits for them, and re-layouts  3.59 us (3%)
  other arithmetic  1.91 us (1%)
    ppermute x16, waiting for transfers between devices, permuted(): return lax.ppermute(block, 'dom', pairs)  43.7 us
    pallas_call x1, Pallas kernels, body(): pl.pallas_call(fast_kernel, out_shape=outs, in_specs=[smem] * 3 + [hbm, h...  31.9 us
    ppermute x16, starting transfers between devices, permuted(): return lax.ppermute(block, 'dom', pairs)  26.7 us
    pallas_call x1, Pallas kernels, body(): pl.pallas_call(join_rest_kernel, out_shape=[block(NC, span, jnp.float32),...  8.1 us
    pallas_call x1, Pallas kernels, body(): pl.pallas_call(slow_kernel, out_shape=block(WCOLS, AW), in_specs=[smem] *...  3.55 us
    unnamed x28, local copies, waits for them, and re-layouts  3.32 us
    pallas_call x1, Pallas kernels, body(): pl.pallas_call(pick_kernel, out_shape=[edge, edge], in_specs=[smem, hbm],...  3.08 us
    pallas_call x1, Pallas kernels, body(): pl.pallas_call(join_first_kernel, out_shape=[block(NC, span), block(NC, s...  2.93 us
  transfers between devices with their start and end apart: 16, of which 5 were waited for; matrix products, arithmetic and copies ran while one was open for 2% of the time, Pallas kernels for 38%

profile of v12, /device:TPU:0, one launch (start us, length us, event | category | flops | bytes accessed | tf_op | source)
XLA Modules:
  0.0 137.9 jit_solution(6139576552788068009)
XLA Ops:
  0.0 3.1 %pick.1 = (bf16[8,64,1728]{2,1,0:T(8,128)(2,1)}, bf16[8,64,1728]{2,1,0:T(8,128)(2,1)}) custom-call(s32[1]{0:T(128)} %bitcast.core, bf16[24,64,1728]{2,1,0:T(8,128)(2,1)} %p_own.1), custom_call_target="tpu_custom_call" | custom-call | tf_op jit(solution)/shard_map/pick/pallas_call | solution.py:511
  3.2 6.4 %collective-permute-start.1 = (s32[8,27]{1,0:T(8,128)S(1)}, s32[8,27]{1,0:T(8,128)S(1)}, u32[]{:S(2)}, u32[]{:S(2)}) collective-permute-start(s32[8,27]{1,0:T(8,128)S(1)} %get-tuple-element.99), channel_id=1, source_target_pairs={{0,31},{1,2},{2,1},{3,4},{4,3},{5,6},{6,5},{7,8},{8,7},{9,10},{10,... | collective-permute-start | bytes 2600 | tf_op jit(solution)/shard_map/ppermute | solution.py:477
  9.6 0.0 collective-permute-start
  9.6 0.5 collective-permute-start.2
  10.1 0.3 collective-permute-start.3
  10.4 0.1 fusion.1
  10.5 0.1 copy.15
  10.6 0.2 select_reduce_fusion
  10.8 0.1 select_reduce_fusion.3
  10.9 0.6 broadcast_add_fusion.inv_a
  11.6 0.0 collective-permute-done.1
  11.6 0.1 copy.17
  11.7 0.0 collective-permute-done
  11.7 0.1 copy.16
  11.8 0.1 select_reduce_fusion.1
  11.9 0.1 select_reduce_fusion.2
  12.1 0.6 pad_add_fusion.inv_p
  12.7 1.2 collective-permute-done.2.p_fast
  13.9 31.9 %fast.1 = (bf16[3,64,2432]{2,1,0:T(8,128)(2,1)}, bf16[3,64,2432]{2,1,0:T(8,128)(2,1)}, bf16[3,64,2432]{2,1,0:T(8,128)(2,1)}, bf16[6,64,2432]{2,1,0:T(8,128)(2,1)...) custom-call(s32[1]{0:T(128)} %bitcast.core, ...), custom_call_target="tpu_custom_call" | custom-call | flops 20000000000 | bytes 30000000 | tf_op jit(solution)/shard_map/fast/pallas_call | solution.py:580
  45.7 0.5 collective-permute-start.4
  46.2 0.1 collective-permute-start.5
  46.3 0.4 collective-permute-start.6
  46.7 2.2 %copy-done = f32[33,64,512]{2,1,0:T(8,128)S(1)} copy-done((f32[33,64,512]{2,1,0:T(8,128)S(1)}, f32[33,64,512]{2,1,0:T(8,128)}, u32[]{:S(2)}) %copy-start) | copy-done | bytes 4325400
  48.9 1.0 copy-done.2
  50.0 0.5 stage.1
  50.6 3.5 %slow.1.wt_slow = bf16[40,64,512]{2,1,0:T(8,128)(2,1)S(1)} custom-call(s32[1]{0:T(128)} %bitcast.core, s32[8,33]{1,0:T(8,128)S(1)} %broadcast_add_fusion.2.inv_slow, bf16[8,64,1728]{2,1,0:T(8,128)(2,1)S(1)} %collective-permute-done.3.p_slow, bf16[8,64,512]{2,1,0:T(8,128)(2,1)S(1)} %get-tuple-element.67.at_halo, f32[33,64,512]{2,1,0:T(8,128)S(1)} %get-tuple-element.68.rest), custom_call_target="tpu_custom_call" | custom-call | flops 20000000000 | bytes 200000000 | tf_op jit(solution)/shard_map/slow/pallas_call | solution.py:624
  54.1 0.3 collective-permute-start.7
  54.5 2.4 %far.1 = bf16[3,64,2432]{2,1,0:T(8,128)(2,1)S(1)} custom-call(bf16[3,64,512]{2,1,0:T(8,128)(2,1)S(1)} %copy-done.3, bf16[40,64,512]{2,1,0:T(8,128)(2,1)S(1)} %slow.1.wt_slow, bf16[3,64,2432]{2,1,0:T(8,128)(2,1)S(1)} %copy-done.1), custom_call_target="tpu_custom_call" | custom-call | flops 1000000000 | bytes 10000000 | tf_op jit(solution)/shard_map/far/pallas_call | solution.py:642
  56.9 0.9 collective-permute-start.8
  57.8 2.9 %mine.1 = f32[6,64,2432]{2,1,0:T(8,128)S(1)} custom-call(bf16[6,64,512]{2,1,0:T(8,128)(2,1)S(1)} %copy-done.5, bf16[40,64,512]{2,1,0:T(8,128)(2,1)S(1)} %slow.1.wt_slow, bf16[6,64,2432]{2,1,0:T(8,128)(2,1)S(1)} %copy-done.4, bf16[3,64,2432]{2,1,0:T(8,128)(2,1)S(1)} %collective-permute-done.4.low, bf16[3,64,2432]{2,1,0:T(8,128)(2,1)S(1)} %collective-permute-done.5.high), custom_call_target="tpu_custom_call" | custom-call | flops 10000000000 | bytes 100000000 | tf_op jit(solution)/shard_map/mine/pallas_call | solution.py:652
  60.7 0.0 copy-start.10
  60.7 2.9 %join_first.1 = (bf16[3,64,2432]{2,1,0:T(8,128)(2,1)S(1)}, f32[3,64,2432]{2,1,0:T(8,128)S(1)}) custom-call(bf16[6,64,512]{2,1,0:T(8,128)(2,1)S(1)} %collective-permute-done.6.other, bf16[40,64,512]{2,1,0:T(8,128)(2,1)S(1)} %collective-permute-done.7.wt_other, f32[6,64,2432]{2,1,0:T(8,128)S(1)} %mine.1), custom_call_target="tpu_custom_call" | custom-call | flops 1000000 | bytes 100000 | tf_op jit(solution)/shard_map/join_first/pallas_call | solution.py:663
  63.7 8.3 %collective-permute-start.10 = (bf16[9,64,2432]{2,1,0:T(8,128)(2,1)S(1)}, bf16[9,64,2432]{2,1,0:T(8,128)(2,1)S(1)}, u32[]{:S(2)}, u32[]{:S(2)}) collective-permute-start(bf16[9,64,2432]{2,1,0:T(8,128)(2,1)S(1)} %copy-done.10), channel_id=1, source_target_pairs={{0,1},{1,0},{2,3},{3,2},{4,5},{5,4},{6,7},{7,6},{8,9},{9,8},{10,11... | collective-permute-start | bytes 8405000 | tf_op jit(solution)/shard_map/ppermute | solution.py:477
  72.0 0.1 collective-permute-start.9
  72.1 1.9 %collective-permute-start.12 = (bf16[3,64,2432]{2,1,0:T(8,128)(2,1)S(1)}, bf16[3,64,2432]{2,1,0:T(8,128)(2,1)S(1)}, u32[]{:S(2)}, u32[]{:S(2)}) collective-permute-start(bf16[3,64,2432]{2,1,0:T(8,128)(2,1)S(1)} %get-tuple-element.90), channel_id=1, source_target_pairs={{0,2},{1,3},{2,0},{3,1},{4,6},{5,7},{6,4},{7,5},{8,10},{9,11},{10,... | collective-permute-start | bytes 2801672 | tf_op jit(solution)/shard_map/ppermute | solution.py:477
  74.0 3.2 %collective-permute-start.13 = (bf16[3,64,2432]{2,1,0:T(8,128)(2,1)S(1)}, bf16[3,64,2432]{2,1,0:T(8,128)(2,1)S(1)}, u32[]{:S(2)}, u32[]{:S(2)}) collective-permute-start(bf16[3,64,2432]{2,1,0:T(8,128)(2,1)S(1)} %far.1), channel_id=1, source_target_pairs={{0,27},{3,8},{4,31},{7,12},{8,3},{11,16},{12,7},{15,20},{16,11},{1... | collective-permute-start | bytes 2801672 | tf_op jit(solution)/shard_map/ppermute | solution.py:477
  77.2 0.8 merge_far.1
  78.0 2.1 %collective-permute-start.11 = (bf16[3,64,2816]{2,1,0:T(8,128)(2,1)S(1)}, bf16[3,64,2816]{2,1,0:T(8,128)(2,1)S(1)}, u32[]{:S(2)}, u32[]{:S(2)}) collective-permute-start(bf16[3,64,2816]{2,1,0:T(8,128)(2,1)S(1)} %merge_far.1), channel_id=1, source_target_pairs={{0,28},{1,29},{2,6},{3,7},{4,0},{5,1},{6,10},{7,11},{8,4},{9,5},{1... | collective-permute-start | bytes 3244040 | tf_op jit(solution)/shard_map/ppermute | solution.py:477
  80.2 8.1 %join_rest.1 = (f32[3,64,2432]{2,1,0:T(8,128)S(1)}, bf16[3,64,2432]{2,1,0:T(8,128)(2,1)S(1)}, f32[3,64,2432]{2,1,0:T(8,128)S(1)}) custom-call(bf16[9,64,1024]{2,1,0:T(8,128)(2,1)S(1)} %copy-done.6, bf16[9,64,512]{2,1,0:T(8,128)(2,1)S(1)} %copy-done.7, bf16[9,64,512]{2,1,0:T(8,128)(2,1)S(1)} %collective-permute-done.9.other, ...), custom_call_target="tpu_custom_call" | custom-call | flops 40000000000 | bytes 200000000 | tf_op jit(solution)/shard_map/join_rest/pallas_call | solution.py:697
  88.3 16.9 %collective-permute-done.12.other = bf16[3,64,2432]{2,1,0:T(8,128)(2,1)S(1)} collective-permute-done((bf16[3,64,2432]{2,1,0:T(8,128)(2,1)S(1)}, bf16[3,64,2432]{2,1,0:T(8,128)(2,1)S(1)}, u32[]{:S(2)}, u32[]{:S(2)}) %collective-permute-start.12) | collective-permute-done | bytes 933920 | tf_op jit(solution)/shard_map/ppermute | solution.py:477
  105.2 1.6 %collective-permute-start.14 = (bf16[3,64,2432]{2,1,0:T(8,128)(2,1)S(1)}, bf16[3,64,2432]{2,1,0:T(8,128)(2,1)S(1)}, u32[]{:S(2)}, u32[]{:S(2)}) collective-permute-start(bf16[3,64,2432]{2,1,0:T(8,128)(2,1)S(1)} %get-tuple-element.93), channel_id=1, source_target_pairs={{0,2},{1,3},{2,0},{3,1},{4,6},{5,7},{6,4},{7,5},{8,10},{9,11},{10,... | collective-permute-start | bytes 2801672 | tf_op jit(solution)/shard_map/ppermute | solution.py:477
  106.7 0.8 merge.1
  107.5 0.1 collective-permute-start.15
  107.6 3.7 %collective-permute-done.11.direct = bf16[3,64,2816]{2,1,0:T(8,128)(2,1)S(1)} collective-permute-done((bf16[3,64,2816]{2,1,0:T(8,128)(2,1)S(1)}, bf16[3,64,2816]{2,1,0:T(8,128)(2,1)S(1)}, u32[]{:S(2)}, u32[]{:S(2)}) %collective-permute-start.11) | collective-permute-done | bytes 1081376 | tf_op jit(solution)/shard_map/ppermute | solution.py:477
  111.3 16.1 %collective-permute-done.14.pair = bf16[3,64,2432]{2,1,0:T(8,128)(2,1)S(1)} collective-permute-done((bf16[3,64,2432]{2,1,0:T(8,128)(2,1)S(1)}, bf16[3,64,2432]{2,1,0:T(8,128)(2,1)S(1)}, u32[]{:S(2)}, u32[]{:S(2)}) %collective-permute-start.14) | collective-permute-done | bytes 933920 | tf_op jit(solution)/shard_map/ppermute | solution.py:477
  127.4 1.8 %early.1 = f32[3,64,4032]{2,1,0:T(8,128)S(1)} custom-call(s32[1]{0:T(128)} %bitcast.core, f32[3,64,2432]{2,1,0:T(8,128)S(1)} %get-tuple-element.87.own, bf16[3,64,2816]{2,1,0:T(8,128)(2,1)S(1)} %collective-permute-done.11.direct, bf16[3,64,2432]{2,1,0:T(8,128)(2,1)S(1)} %collective-permute-done.14.pair, bf16[3,64,2432]{2,1,0:T(8,128)(2,1)S(1)} %collective-permute-done.13.far), custom_call_target="tpu_custom_call" | custom-call | flops 10000000000 | bytes 100000000 | tf_op jit(solution)/shard_map/early/pallas_call | solution.py:713
  129.3 5.7 %collective-permute-done.15.merged = bf16[3,64,2816]{2,1,0:T(8,128)(2,1)S(1)} collective-permute-done((bf16[3,64,2816]{2,1,0:T(8,128)(2,1)S(1)}, bf16[3,64,2816]{2,1,0:T(8,128)(2,1)S(1)}, u32[]{:S(2)}, u32[]{:S(2)}) %collective-permute-start.15) | collective-permute-done | bytes 1081376 | tf_op jit(solution)/shard_map/ppermute | solution.py:477
  135.0 2.8 %total.1 = f32[3,64,4032]{2,1,0:T(8,128)} custom-call(s32[1]{0:T(128)} %bitcast.core, f32[3,64,4032]{2,1,0:T(8,128)S(1)} %early.1, bf16[3,64,2816]{2,1,0:T(8,128)(2,1)S(1)} %collective-permute-done.15.merged), custom_call_target="tpu_custom_call" | custom-call | flops 10000000 | bytes 10000000 | tf_op jit(solution)/shard_map/total/pallas_call | solution.py:723
  (47 shorter events, 0.2 us)
Async XLA Ops:
  0.0 3.1 %copy-start.8 = (s32[24,27]{1,0:T(8,128)S(1)}, s32[24,27]{1,0:T(8,128)}, u32[]{:S(2)}) copy-start(s32[24,27]{1,0:T(8,128)} %param.7) | copy-start | bytes 7780
  0.0 10.8 %copy-start.9 = (s32[24,7]{0,1:T(8,128)S(1)}, s32[24,7]{0,1:T(8,128)}, u32[]{:S(2)}) copy-start(s32[24,7]{0,1:T(8,128)} %param.6) | copy-start | bytes 2020
  3.2 8.4 %collective-permute-start.1 = (s32[8,27]{1,0:T(8,128)S(1)}, s32[8,27]{1,0:T(8,128)S(1)}, u32[]{:S(2)}, u32[]{:S(2)}) collective-permute-start(s32[8,27]{1,0:T(8,128)S(1)} %get-tuple-element.99), channel_id=1, source_target_pairs={{0,31},{1,2},{2,1},{3,4},{4,3},{5,6},{6,5},{7,8},{8,7},{9,10},{10,... | collective-permute-start | bytes 2600 | tf_op jit(solution)/shard_map/ppermute | solution.py:477
  9.6 2.1 %collective-permute-start = (s32[8,27]{1,0:T(8,128)S(1)}, s32[8,27]{1,0:T(8,128)S(1)}, u32[]{:S(2)}, u32[]{:S(2)}) collective-permute-start(s32[8,27]{1,0:T(8,128)S(1)} %get-tuple-element.100), channel_id=1, source_target_pairs={{0,1},{1,0},{2,3},{3,2},{4,5},{5,4},{6,7},{7,6},{8,9},{9,8},{10,11... | collective-permute-start | bytes 2600 | tf_op jit(solution)/shard_map/ppermute | solution.py:477
  9.6 4.3 %collective-permute-start.2 = (bf16[8,64,1728]{2,1,0:T(8,128)(2,1)}, bf16[8,64,1728]{2,1,0:T(8,128)(2,1)}, u32[]{:S(2)}, u32[]{:S(2)}) collective-permute-start(bf16[8,64,1728]{2,1,0:T(8,128)(2,1)} %get-tuple-element.55), channel_id=1, source_target_pairs={{0,1},{1,0},{2,3},{3,2},{4,5},{5,4},{6,7},{7,6},{8,9},{9,8},{10,11... | collective-permute-start | bytes 5308424 | tf_op jit(solution)/shard_map/ppermute | solution.py:477
  10.1 40.4 %collective-permute-start.3 = (bf16[8,64,1728]{2,1,0:T(8,128)(2,1)}, bf16[8,64,1728]{2,1,0:T(8,128)(2,1)S(1)}, u32[]{:S(2)}, u32[]{:S(2)}) collective-permute-start(bf16[8,64,1728]{2,1,0:T(8,128)(2,1)} %get-tuple-element.58), channel_id=1, source_target_pairs={{0,31},{1,2},{2,1},{3,4},{4,3},{5,6},{6,5},{7,8},{8,7},{9,10},{10,... | collective-permute-start | bytes 5308424 | tf_op jit(solution)/shard_map/ppermute | solution.py:477
  45.7 4.8 %collective-permute-start.4 = (bf16[3,64,2432]{2,1,0:T(8,128)(2,1)}, bf16[3,64,2432]{2,1,0:T(8,128)(2,1)S(1)}, u32[]{:S(2)}, u32[]{:S(2)}) collective-permute-start(bf16[3,64,2432]{2,1,0:T(8,128)(2,1)} %get-tuple-element.59), channel_id=1, source_target_pairs={{0,1},{1,0},{2,3},{3,2},{4,5},{5,4},{6,7},{7,6},{8,9},{9,8},{10,11... | collective-permute-start | bytes 2801672 | tf_op jit(solution)/shard_map/ppermute | solution.py:477
  46.2 4.3 %collective-permute-start.5 = (bf16[3,64,2432]{2,1,0:T(8,128)(2,1)}, bf16[3,64,2432]{2,1,0:T(8,128)(2,1)S(1)}, u32[]{:S(2)}, u32[]{:S(2)}) collective-permute-start(bf16[3,64,2432]{2,1,0:T(8,128)(2,1)} %get-tuple-element.60), channel_id=1, source_target_pairs={{0,1},{1,0},{2,3},{3,2},{4,5},{5,4},{6,7},{7,6},{8,9},{9,8},{10,11... | collective-permute-start | bytes 2801672 | tf_op jit(solution)/shard_map/ppermute | solution.py:477
  46.3 4.2 %collective-permute-start.6 = (bf16[6,64,512]{2,1,0:T(8,128)(2,1)}, bf16[6,64,512]{2,1,0:T(8,128)(2,1)S(1)}, u32[]{:S(2)}, u32[]{:S(2)}) collective-permute-start(bf16[6,64,512]{2,1,0:T(8,128)(2,1)} %get-tuple-element.61), channel_id=1, source_target_pairs={{0,1},{1,0},{2,3},{3,2},{4,5},{5,4},{6,7},{7,6},{8,9},{9,8},{10,11... | collective-permute-start | bytes 1179656 | tf_op jit(solution)/shard_map/ppermute | solution.py:477
  46.7 2.2 %copy-start = (f32[33,64,512]{2,1,0:T(8,128)S(1)}, f32[33,64,512]{2,1,0:T(8,128)}, u32[]{:S(2)}) copy-start(f32[33,64,512]{2,1,0:T(8,128)} %get-tuple-element.66.rest) | copy-start | bytes 12976132
  48.9 1.0 copy-start.2
  50.5 3.9 %copy-start.1 = (bf16[3,64,2432]{2,1,0:T(8,128)(2,1)S(1)}, bf16[3,64,2432]{2,1,0:T(8,128)(2,1)}, u32[]{:S(2)}) copy-start(bf16[3,64,2432]{2,1,0:T(8,128)(2,1)} %get-tuple-element.74.far_fast) | copy-start | bytes 2801668
  50.5 3.9 %copy-start.3 = (bf16[3,64,512]{2,1,0:T(8,128)(2,1)S(1)}, bf16[3,64,512]{2,1,0:T(8,128)(2,1)}, u32[]{:S(2)}) copy-start(bf16[3,64,512]{2,1,0:T(8,128)(2,1)} %get-tuple-element.70.slow) | copy-start | bytes 589828
  50.6 7.2 %copy-start.5 = (bf16[6,64,512]{2,1,0:T(8,128)(2,1)S(1)}, bf16[6,64,512]{2,1,0:T(8,128)(2,1)}, u32[]{:S(2)}) copy-start(bf16[6,64,512]{2,1,0:T(8,128)(2,1)} %get-tuple-element.69.slow) | copy-start | bytes 1179652
  54.1 6.6 %collective-permute-start.7 = (bf16[40,64,512]{2,1,0:T(8,128)(2,1)S(1)}, bf16[40,64,512]{2,1,0:T(8,128)(2,1)S(1)}, u32[]{:S(2)}, u32[]{:S(2)}) collective-permute-start(bf16[40,64,512]{2,1,0:T(8,128)(2,1)S(1)} %slow.1.wt_slow), channel_id=1, source_target_pairs={{0,1},{1,0},{2,3},{3,2},{4,5},{5,4},{6,7},{7,6},{8,9},{9,8},{10,11... | collective-permute-start | bytes 7864328 | tf_op jit(solution)/shard_map/ppermute | solution.py:477
  54.5 3.3 %copy-start.4 = (bf16[6,64,2432]{2,1,0:T(8,128)(2,1)S(1)}, bf16[6,64,2432]{2,1,0:T(8,128)(2,1)}, u32[]{:S(2)}) copy-start(bf16[6,64,2432]{2,1,0:T(8,128)(2,1)} %get-tuple-element.76.inner) | copy-start | bytes 5603332
  54.5 25.7 %slice-start = ((s8[5242880]{0:T(1024)(128)(4,1)}), s8[4194304]{0:T(1024)(128)(4,1)S(1)}, s32[]{:S(2)}) async-start(s8[5242880]{0:T(1024)(128)(4,1)} %bitcast.9), calls=%async_computation | async-start | bytes 8388608
  56.9 6.8 %collective-permute-start.8 = (bf16[3,64,2432]{2,1,0:T(8,128)(2,1)S(1)}, bf16[3,64,2432]{2,1,0:T(8,128)(2,1)S(1)}, u32[]{:S(2)}, u32[]{:S(2)}) collective-permute-start(bf16[3,64,2432]{2,1,0:T(8,128)(2,1)S(1)} %far.1), channel_id=1, source_target_pairs={{1,2},{2,1},{5,6},{6,5},{9,10},{10,9},{13,14},{14,13},{17,18},{18,... | collective-permute-start | bytes 2801672 | tf_op jit(solution)/shard_map/ppermute | solution.py:477
  57.8 22.4 %slice-start.1 = ((s8[5242880]{0:T(1024)(128)(4,1)}), s8[1048576]{0:T(1024)(128)(4,1)S(1)}, s32[]{:S(2)}) async-start(s8[5242880]{0:T(1024)(128)(4,1)} %bitcast.9), calls=%async_computation.1 | async-start | bytes 2097152
  60.7 3.0 %copy-start.10 = (bf16[9,64,2432]{2,1,0:T(8,128)(2,1)S(1)}, bf16[9,64,2432]{2,1,0:T(8,128)(2,1)}, u32[]{:S(2)}) copy-start(bf16[9,64,2432]{2,1,0:T(8,128)(2,1)} %get-tuple-element.86) | copy-start | bytes 8404996
  60.7 11.3 %copy-start.11 = (bf16[9,64,512]{2,1,0:T(8,128)(2,1)S(1)}, bf16[9,64,512]{2,1,0:T(8,128)(2,1)}, u32[]{:S(2)}) copy-start(bf16[9,64,512]{2,1,0:T(8,128)(2,1)} %get-tuple-element.84) | copy-start | bytes 1769476
  63.7 16.5 %copy-start.6 = (bf16[9,64,1024]{2,1,0:T(8,128)(2,1)S(1)}, bf16[9,64,1024]{2,1,0:T(8,128)(2,1)}, u32[]{:S(2)}) copy-start(bf16[9,64,1024]{2,1,0:T(8,128)(2,1)} %get-tuple-element.56.fast) | copy-start | bytes 3538948
  63.7 16.5 %copy-start.7 = (bf16[9,64,512]{2,1,0:T(8,128)(2,1)S(1)}, bf16[9,64,512]{2,1,0:T(8,128)(2,1)}, u32[]{:S(2)}) copy-start(bf16[9,64,512]{2,1,0:T(8,128)(2,1)} %get-tuple-element.57.slow) | copy-start | bytes 1769476
  63.7 16.5 %collective-permute-start.10 = (bf16[9,64,2432]{2,1,0:T(8,128)(2,1)S(1)}, bf16[9,64,2432]{2,1,0:T(8,128)(2,1)S(1)}, u32[]{:S(2)}, u32[]{:S(2)}) collective-permute-start(bf16[9,64,2432]{2,1,0:T(8,128)(2,1)S(1)} %copy-done.10), channel_id=1, source_target_pairs={{0,1},{1,0},{2,3},{3,2},{4,5},{5,4},{6,7},{7,6},{8,9},{9,8},{10,11... | collective-permute-start | bytes 8405000 | tf_op jit(solution)/shard_map/ppermute | solution.py:477
  72.0 8.1 %collective-permute-start.9 = (bf16[9,64,512]{2,1,0:T(8,128)(2,1)S(1)}, bf16[9,64,512]{2,1,0:T(8,128)(2,1)S(1)}, u32[]{:S(2)}, u32[]{:S(2)}) collective-permute-start(bf16[9,64,512]{2,1,0:T(8,128)(2,1)S(1)} %copy-done.11), channel_id=1, source_target_pairs={{0,1},{1,0},{2,3},{3,2},{4,5},{5,4},{6,7},{7,6},{8,9},{9,8},{10,11... | collective-permute-start | bytes 1769480 | tf_op jit(solution)/shard_map/ppermute | solution.py:477
  72.1 33.1 %collective-permute-start.12 = (bf16[3,64,2432]{2,1,0:T(8,128)(2,1)S(1)}, bf16[3,64,2432]{2,1,0:T(8,128)(2,1)S(1)}, u32[]{:S(2)}, u32[]{:S(2)}) collective-permute-start(bf16[3,64,2432]{2,1,0:T(8,128)(2,1)S(1)} %get-tuple-element.90), channel_id=1, source_target_pairs={{0,2},{1,3},{2,0},{3,1},{4,6},{5,7},{6,4},{7,5},{8,10},{9,11},{10,... | collective-permute-start | bytes 2801672 | tf_op jit(solution)/shard_map/ppermute | solution.py:477
  74.0 31.1 %collective-permute-start.13 = (bf16[3,64,2432]{2,1,0:T(8,128)(2,1)S(1)}, bf16[3,64,2432]{2,1,0:T(8,128)(2,1)S(1)}, u32[]{:S(2)}, u32[]{:S(2)}) collective-permute-start(bf16[3,64,2432]{2,1,0:T(8,128)(2,1)S(1)} %far.1), channel_id=1, source_target_pairs={{0,27},{3,8},{4,31},{7,12},{8,3},{11,16},{12,7},{15,20},{16,11},{1... | collective-permute-start | bytes 2801672 | tf_op jit(solution)/shard_map/ppermute | solution.py:477
  78.0 33.3 %collective-permute-start.11 = (bf16[3,64,2816]{2,1,0:T(8,128)(2,1)S(1)}, bf16[3,64,2816]{2,1,0:T(8,128)(2,1)S(1)}, u32[]{:S(2)}, u32[]{:S(2)}) collective-permute-start(bf16[3,64,2816]{2,1,0:T(8,128)(2,1)S(1)} %merge_far.1), channel_id=1, source_target_pairs={{0,28},{1,29},{2,6},{3,7},{4,0},{5,1},{6,10},{7,11},{8,4},{9,5},{1... | collective-permute-start | bytes 3244040 | tf_op jit(solution)/shard_map/ppermute | solution.py:477
  105.2 22.3 %collective-permute-start.14 = (bf16[3,64,2432]{2,1,0:T(8,128)(2,1)S(1)}, bf16[3,64,2432]{2,1,0:T(8,128)(2,1)S(1)}, u32[]{:S(2)}, u32[]{:S(2)}) collective-permute-start(bf16[3,64,2432]{2,1,0:T(8,128)(2,1)S(1)} %get-tuple-element.93), channel_id=1, source_target_pairs={{0,2},{1,3},{2,0},{3,1},{4,6},{5,7},{6,4},{7,5},{8,10},{9,11},{10,... | collective-permute-start | bytes 2801672 | tf_op jit(solution)/shard_map/ppermute | solution.py:477
  107.5 27.5 %collective-permute-start.15 = (bf16[3,64,2816]{2,1,0:T(8,128)(2,1)S(1)}, bf16[3,64,2816]{2,1,0:T(8,128)(2,1)S(1)}, u32[]{:S(2)}, u32[]{:S(2)}) collective-permute-start(bf16[3,64,2816]{2,1,0:T(8,128)(2,1)S(1)} %merge.1), channel_id=1, source_target_pairs={{0,4},{1,5},{2,30},{3,31},{4,8},{5,9},{6,2},{7,3},{8,12},{9,13},{1... | collective-permute-start | bytes 3244040 | tf_op jit(solution)/shard_map/ppermute | solution.py:477

commit v13 on v11

--- a/solution.py
+++ b/solution.py
@@ -34,6 +34,7 @@
 FIRST = 2 * NC
 REST = ROWS - FIRST
 MERGED = WINDOW + 6
+FAR = 36
 
 
 def eye(n):
@@ -307,13 +308,17 @@
     return pl.ds(pl.multiple_of(tile * LANES, LANES), width)
 
 
-def far_kernel(slow, wt_slow, far_fast, far):
-    def step(tile, width):
-        lanes = tile_lanes(tile, width)
-        value = tile_dot(slow, wt_slow, tile, width) + far_fast[:, :, lanes].astype(jnp.float32)
-        far[:, :, lanes] = value.astype(jnp.bfloat16)
-
-    each_tile(step)
+def far_kernel(core, slow, wt_slow, far_fast, far):
+    s, x = places(core)
+
+    @pl.loop(0, FAR // QUAD)
+    def _(tile):
+        left = slow[...].reshape(NC * BS, AW)
+        right = wt_slow[pl.ds(QUAD * tile + 2 * s, QUAD)].reshape(LANES, AW)
+        value = lax.dot_general(left, right, NT, preferred_element_type=jnp.float32)
+        lanes = pl.ds(pl.multiple_of(tile * LANES + 2 * BS * s, 2 * BS), LANES)
+        value = value.reshape(NC, BS, LANES) + far_fast[:, :, lanes].astype(jnp.float32)
+        far[:, :, tile_lanes(tile, LANES)] = value.astype(jnp.bfloat16)
 
 
 def mine_kernel(slow, wt_slow, inner, low, high, out):
@@ -394,13 +399,14 @@
         copy.wait()
 
 
-def merge_kernel(core, rows, other, out, frame):
+def merge_kernel(core, rows, other, out, frame, *, shift):
     s, x = places(core)
     step = 6 * BS
     for j in range(NC):
         frame[...] = jnp.zeros_like(frame)
         frame[:, pl.ds(pl.multiple_of(step * x, step), WINDOW * BS)] = rows[j]
-        lanes = pl.ds(pl.multiple_of(step * (1 - x), step), WINDOW * BS)
+        lane = pl.multiple_of(step * (1 - x) + shift * BS * x, 2 * BS)
+        lanes = pl.ds(lane, other.shape[2])
         frame[:, lanes] += other[j].astype(jnp.float32)
         out[j] = frame[...].astype(jnp.bfloat16)
 
@@ -422,13 +428,11 @@
         store(frame[:, first - BS : last - BS])
 
 
-def early_kernel(core, own, direct, pair, far, out, frame):
+def early_kernel(core, own, direct, pair, out, frame):
     s, x = places(core)
     for j in range(NC):
         top = 27 - 3 * s - j
-        far_start = jnp.where(s == 1, 30 - j, -3 - j)
         messages = [(own, top - 12), (direct, top - 30 * x), (pair, top - 6 - 12 * x)]
-        messages.append((far, far_start))
 
         def store(value, j=j):
             out[j] = value
@@ -436,15 +440,16 @@
         in_frame(s, j, frame, messages, store)
 
 
-def total_kernel(core, early, merged, out, frame, buf, sems):
+def total_kernel(core, early, merged, far, out, frame, buf, sems):
     s, x = places(core)
     copies = []
     for j in range(NC):
+        far_start = jnp.where(s == 1, 30 - j, -1 - j)
 
         def store(value, j=j):
             buf[j] = value + early[j]
 
-        in_frame(s, j, frame, [(merged, 3 - 3 * s - j + 18 * x)], store)
+        in_frame(s, j, frame, [(merged, 3 - 3 * s - j + 18 * x), (far, far_start)], store)
         copy = pltpu.make_async_copy(buf.at[j], out.at[j], sems.at[j])
         copy.start()
         copies.append(copy)
@@ -641,13 +646,13 @@
     wt_slow, low, high = lax.optimization_barrier((wt_slow, low, high))
     far = pl.pallas_call(
         far_kernel,
-        out_shape=block(NC, span),
-        in_specs=[vmem] * 3,
+        out_shape=block(NC, FAR * BS),
+        in_specs=[smem] + [vmem] * 3,
         out_specs=vmem,
         compiler_params=params(16),
         cost_estimate=cost(10**9, 10**7),
         name="far",
-    )(slow_far, wt_slow, far)
+    )(core, slow_far, wt_slow, far)
     far, wt_slow = lax.optimization_barrier((far, wt_slow))
     mine = pl.pallas_call(
         mine_kernel,
@@ -669,10 +674,8 @@
         cost_estimate=cost(10**6, 10**5),
         name="join_first",
     )(other_first, wt_other, mine)
-    straight = [i for i in range(devices) if i % 4 in (0, 3)]
-    far = permuted(far, [(i, (i + (5 if i % 2 else -5)) % devices) for i in straight])
-    relay, direct, far_near, far, send_rest, other_rest = lax.optimization_barrier(
-        (relay, direct, far_near, far, send_rest, other_rest)
+    relay, direct, far_near, send_rest, other_rest = lax.optimization_barrier(
+        (relay, direct, far_near, send_rest, other_rest)
     )
     arrived_rest = permuted(send_rest, inward)
     other_rest = permuted(other_rest, inward)
@@ -680,9 +683,9 @@
     x_sign = [1 if i // 2 % 2 else -1 for i in range(devices)]
     relay = permuted(relay, along_x)
 
-    def merge_rows(rows, other, name):
+    def merge_rows(rows, other, shift, name):
         return pl.pallas_call(
-            merge_kernel,
+            functools.partial(merge_kernel, shift=shift),
             out_shape=block(NC, MERGED * BS),
             in_specs=[smem, vmem, vmem],
             out_specs=vmem,
@@ -692,7 +695,7 @@
             name=name,
         )(core, rows, other)
 
-    direct = merge_rows(direct, far_near, "merge_far")
+    direct = merge_rows(direct, far_near, 2, "merge_far")
     direct = permuted(direct, [(i, (i + 4 * x_sign[i]) % devices) for i in range(devices)])
     merge, pair, own = pl.pallas_call(
         join_rest_kernel,
@@ -704,26 +707,29 @@
         name="join_rest",
     )(fast_rest, slow_rest, other_rest, wt_fast, wt_slow, wt_other, arrived_rest)
     relay, pair = lax.optimization_barrier((relay, pair))
-    merged = merge_rows(merge, relay, "merge")
+    merged = merge_rows(merge, relay, 0, "merge")
     merged = permuted(merged, [(i, (i - 4 * x_sign[i]) % devices) for i in range(devices)])
     pair = permuted(pair, along_x)
+    pair, far = lax.optimization_barrier((pair, far))
+    straight = [i for i in range(devices) if i % 4 in (0, 3)]
+    far = permuted(far, [(i, (i + (5 if i % 2 else -5)) % devices) for i in straight])
 
     total = block(NC, BAND * BS, jnp.float32)
     frame = pltpu.VMEM((BS, FRAME * BS), jnp.float32)
     early = pl.pallas_call(
         early_kernel,
         out_shape=total,
-        in_specs=[smem] + [vmem] * 4,
+        in_specs=[smem] + [vmem] * 3,
         out_specs=vmem,
         scratch_shapes=[frame],
         compiler_params=params(16),
         cost_estimate=cost(10**10, 100 * 10**6),
         name="early",
-    )(core, own, direct, pair, far)
+    )(core, own, direct, pair)
     return pl.pallas_call(
         total_kernel,
         out_shape=total,
-        in_specs=[smem] + [vmem] * 2,
+        in_specs=[smem] + [vmem] * 3,
         out_specs=hbm,
         scratch_shapes=[
             frame,
@@ -733,7 +739,7 @@
         compiler_params=params(20),
         cost_estimate=cost(10**7, 10**7),
         name="total",
-    )(core, early, merged)
+    )(core, early, merged, far)
 
 
 def solution(mesh):

time: 139 us -> 137 us (0.986)
  starting transfers between devices: 28.6 us -> 25.4 us
  waiting for transfers between devices: 42.6 us -> 44.2 us
    ppermute x16, starting transfers between devices: 28.6 us -> 25.4 us  [permuted(): return lax.ppermute(block, 'dom', pairs)]
    ppermute x16, waiting for transfers between devices: 42.6 us -> 44.2 us  [permuted(): return lax.ppermute(block, 'dom', pairs)]
  transfers between devices with their start and end apart: 16 -> 16, of which waited for: 7 -> 6; matrix products, arithmetic and copies ran while one was open for 2% -> 2% of each run, Pallas kernels for 38% -> 38%
where the time goes in v13:
time: 137 us
  Pallas kernels  61.2 us (45%)
  waiting for transfers between devices  44.2 us (32%)
  starting transfers between devices  25.4 us (19%)
  local copies, waits for them, and re-layouts  3.59 us (3%)
  other arithmetic  1.91 us (1%)
    ppermute x16, waiting for transfers between devices, permuted(): return lax.ppermute(block, 'dom', pairs)  44.2 us
    pallas_call x1, Pallas kernels, body(): pl.pallas_call(fast_kernel, out_shape=outs, in_specs=[smem] * 3 + [hbm, h...  31.9 us
    ppermute x16, starting transfers between devices, permuted(): return lax.ppermute(block, 'dom', pairs)  25.4 us
    pallas_call x1, Pallas kernels, body(): pl.pallas_call(join_rest_kernel, out_shape=[block(NC, span, jnp.float32),...  8.11 us
    pallas_call x1, Pallas kernels, body(): pl.pallas_call(slow_kernel, out_shape=block(WCOLS, AW), in_specs=[smem] *...  3.53 us
    unnamed x28, local copies, waits for them, and re-layouts  3.32 us
    pallas_call x1, Pallas kernels, body(): pl.pallas_call(pick_kernel, out_shape=[edge, edge], in_specs=[smem, hbm],...  3.08 us
    pallas_call x1, Pallas kernels, body(): pl.pallas_call(mine_kernel, out_shape=block(FIRST, span, jnp.float32), in...  2.98 us
  transfers between devices with their start and end apart: 16, of which 6 were waited for; matrix products, arithmetic and copies ran while one was open for 2% of the time, Pallas kernels for 38%

profile of v13, /device:TPU:0, one launch (start us, length us, event | category | flops | bytes accessed | tf_op | source)
XLA Modules:
  0.0 136.8 jit_solution(16647988267175210903)
XLA Ops:
  0.0 3.1 %pick.1 = (bf16[8,64,1728]{2,1,0:T(8,128)(2,1)}, bf16[8,64,1728]{2,1,0:T(8,128)(2,1)}) custom-call(s32[1]{0:T(128)} %bitcast.core, bf16[24,64,1728]{2,1,0:T(8,128)(2,1)} %p_own.1), custom_call_target="tpu_custom_call" | custom-call | tf_op jit(solution)/shard_map/pick/pallas_call | solution.py:516
  3.2 6.4 %collective-permute-start.1 = (s32[8,27]{1,0:T(8,128)S(1)}, s32[8,27]{1,0:T(8,128)S(1)}, u32[]{:S(2)}, u32[]{:S(2)}) collective-permute-start(s32[8,27]{1,0:T(8,128)S(1)} %get-tuple-element.99), channel_id=1, source_target_pairs={{0,31},{1,2},{2,1},{3,4},{4,3},{5,6},{6,5},{7,8},{8,7},{9,10},{10,... | collective-permute-start | bytes 2600 | tf_op jit(solution)/shard_map/ppermute | solution.py:482
  9.6 0.0 collective-permute-start
  9.6 0.5 collective-permute-start.2
  10.1 0.3 collective-permute-start.3
  10.4 0.1 fusion.1
  10.5 0.1 copy.15
  10.6 0.2 select_reduce_fusion
  10.8 0.1 select_reduce_fusion.3
  10.9 0.6 broadcast_add_fusion.inv_a
  11.6 0.0 collective-permute-done.1
  11.6 0.1 copy.17
  11.7 0.1 copy.16
  11.8 0.1 select_reduce_fusion.1
  11.9 0.1 select_reduce_fusion.2
  12.1 0.6 pad_add_fusion.inv_p
  12.7 1.2 collective-permute-done.2.p_fast
  13.9 31.9 %fast.1 = (bf16[3,64,2432]{2,1,0:T(8,128)(2,1)}, bf16[3,64,2432]{2,1,0:T(8,128)(2,1)}, bf16[3,64,2432]{2,1,0:T(8,128)(2,1)}, bf16[6,64,2432]{2,1,0:T(8,128)(2,1)...) custom-call(s32[1]{0:T(128)} %bitcast.core, ...), custom_call_target="tpu_custom_call" | custom-call | flops 20000000000 | bytes 30000000 | tf_op jit(solution)/shard_map/fast/pallas_call | solution.py:585
  45.7 0.5 collective-permute-start.4
  46.2 0.1 collective-permute-start.5
  46.3 0.4 collective-permute-start.6
  46.7 2.2 %copy-done = f32[33,64,512]{2,1,0:T(8,128)S(1)} copy-done((f32[33,64,512]{2,1,0:T(8,128)S(1)}, f32[33,64,512]{2,1,0:T(8,128)}, u32[]{:S(2)}) %copy-start) | copy-done | bytes 4325400
  48.9 1.0 copy-done.2
  50.0 0.5 stage.1
  50.6 3.5 %slow.1.wt_slow = bf16[40,64,512]{2,1,0:T(8,128)(2,1)S(1)} custom-call(s32[1]{0:T(128)} %bitcast.core, s32[8,33]{1,0:T(8,128)S(1)} %broadcast_add_fusion.2.inv_slow, bf16[8,64,1728]{2,1,0:T(8,128)(2,1)S(1)} %collective-permute-done.3.p_slow, bf16[8,64,512]{2,1,0:T(8,128)(2,1)S(1)} %get-tuple-element.67.at_halo, f32[33,64,512]{2,1,0:T(8,128)S(1)} %get-tuple-element.68.rest), custom_call_target="tpu_custom_call" | custom-call | flops 20000000000 | bytes 200000000 | tf_op jit(solution)/shard_map/slow/pallas_call | solution.py:629
  54.1 0.3 collective-permute-start.7
  54.5 2.2 %far.1 = bf16[3,64,2304]{2,1,0:T(8,128)(2,1)S(1)} custom-call(s32[1]{0:T(128)} %bitcast.core, bf16[3,64,512]{2,1,0:T(8,128)(2,1)S(1)} %copy-done.3, bf16[40,64,512]{2,1,0:T(8,128)(2,1)S(1)} %slow.1.wt_slow, bf16[3,64,2432]{2,1,0:T(8,128)(2,1)S(1)} %copy-done.1), custom_call_target="tpu_custom_call" | custom-call | flops 1000000000 | bytes 10000000 | tf_op jit(solution)/shard_map/far/pallas_call | solution.py:647
  56.7 0.9 collective-permute-start.8
  57.6 3.0 %mine.1 = f32[6,64,2432]{2,1,0:T(8,128)S(1)} custom-call(bf16[6,64,512]{2,1,0:T(8,128)(2,1)S(1)} %copy-done.5, bf16[40,64,512]{2,1,0:T(8,128)(2,1)S(1)} %slow.1.wt_slow, bf16[6,64,2432]{2,1,0:T(8,128)(2,1)S(1)} %copy-done.4, bf16[3,64,2432]{2,1,0:T(8,128)(2,1)S(1)} %collective-permute-done.4.low, bf16[3,64,2432]{2,1,0:T(8,128)(2,1)S(1)} %collective-permute-done.5.high), custom_call_target="tpu_custom_call" | custom-call | flops 10000000000 | bytes 100000000 | tf_op jit(solution)/shard_map/mine/pallas_call | solution.py:657
  60.6 0.0 copy-start.10
  60.6 2.9 %join_first.1 = (bf16[3,64,2432]{2,1,0:T(8,128)(2,1)S(1)}, f32[3,64,2432]{2,1,0:T(8,128)S(1)}) custom-call(bf16[6,64,512]{2,1,0:T(8,128)(2,1)S(1)} %collective-permute-done.6.other, bf16[40,64,512]{2,1,0:T(8,128)(2,1)S(1)} %collective-permute-done.7.wt_other, f32[6,64,2432]{2,1,0:T(8,128)S(1)} %mine.1), custom_call_target="tpu_custom_call" | custom-call | flops 1000000 | bytes 100000 | tf_op jit(solution)/shard_map/join_first/pallas_call | solution.py:668
  63.6 7.7 %collective-permute-start.10 = (bf16[9,64,2432]{2,1,0:T(8,128)(2,1)S(1)}, bf16[9,64,2432]{2,1,0:T(8,128)(2,1)S(1)}, u32[]{:S(2)}, u32[]{:S(2)}) collective-permute-start(bf16[9,64,2432]{2,1,0:T(8,128)(2,1)S(1)} %copy-done.10), channel_id=1, source_target_pairs={{0,1},{1,0},{2,3},{3,2},{4,5},{5,4},{6,7},{7,6},{8,9},{9,8},{10,11... | collective-permute-start | bytes 8405000 | tf_op jit(solution)/shard_map/ppermute | solution.py:482
  71.3 0.1 collective-permute-start.9
  71.4 2.0 %collective-permute-start.12 = (bf16[3,64,2432]{2,1,0:T(8,128)(2,1)S(1)}, bf16[3,64,2432]{2,1,0:T(8,128)(2,1)S(1)}, u32[]{:S(2)}, u32[]{:S(2)}) collective-permute-start(bf16[3,64,2432]{2,1,0:T(8,128)(2,1)S(1)} %get-tuple-element.90), channel_id=1, source_target_pairs={{0,2},{1,3},{2,0},{3,1},{4,6},{5,7},{6,4},{7,5},{8,10},{9,11},{10,... | collective-permute-start | bytes 2801672 | tf_op jit(solution)/shard_map/ppermute | solution.py:482
  73.3 0.6 merge_far.1
  73.9 2.6 %collective-permute-start.11 = (bf16[3,64,2816]{2,1,0:T(8,128)(2,1)S(1)}, bf16[3,64,2816]{2,1,0:T(8,128)(2,1)S(1)}, u32[]{:S(2)}, u32[]{:S(2)}) collective-permute-start(bf16[3,64,2816]{2,1,0:T(8,128)(2,1)S(1)} %merge_far.1), channel_id=1, source_target_pairs={{0,28},{1,29},{2,6},{3,7},{4,0},{5,1},{6,10},{7,11},{8,4},{9,5},{1... | collective-permute-start | bytes 3244040 | tf_op jit(solution)/shard_map/ppermute | solution.py:482
  76.5 0.4 collective-permute-done.9.other
  77.0 8.1 %join_rest.1 = (f32[3,64,2432]{2,1,0:T(8,128)S(1)}, bf16[3,64,2432]{2,1,0:T(8,128)(2,1)S(1)}, f32[3,64,2432]{2,1,0:T(8,128)S(1)}) custom-call(bf16[9,64,1024]{2,1,0:T(8,128)(2,1)S(1)} %copy-done.6, bf16[9,64,512]{2,1,0:T(8,128)(2,1)S(1)} %copy-done.7, bf16[9,64,512]{2,1,0:T(8,128)(2,1)S(1)} %collective-permute-done.9.other, ...), custom_call_target="tpu_custom_call" | custom-call | flops 40000000000 | bytes 200000000 | tf_op jit(solution)/shard_map/join_rest/pallas_call | solution.py:700
  85.1 9.3 %collective-permute-done.12.other = bf16[3,64,2432]{2,1,0:T(8,128)(2,1)S(1)} collective-permute-done((bf16[3,64,2432]{2,1,0:T(8,128)(2,1)S(1)}, bf16[3,64,2432]{2,1,0:T(8,128)(2,1)S(1)}, u32[]{:S(2)}, u32[]{:S(2)}) %collective-permute-start.12) | collective-permute-done | bytes 933920 | tf_op jit(solution)/shard_map/ppermute | solution.py:482
  94.4 1.6 %collective-permute-start.13 = (bf16[3,64,2432]{2,1,0:T(8,128)(2,1)S(1)}, bf16[3,64,2432]{2,1,0:T(8,128)(2,1)S(1)}, u32[]{:S(2)}, u32[]{:S(2)}) collective-permute-start(bf16[3,64,2432]{2,1,0:T(8,128)(2,1)S(1)} %get-tuple-element.92), channel_id=1, source_target_pairs={{0,2},{1,3},{2,0},{3,1},{4,6},{5,7},{6,4},{7,5},{8,10},{9,11},{10,... | collective-permute-start | bytes 2801672 | tf_op jit(solution)/shard_map/ppermute | solution.py:482
  96.0 0.8 merge.1
  96.8 0.1 collective-permute-start.14
  96.9 19.8 %collective-permute-done.13.pair = bf16[3,64,2432]{2,1,0:T(8,128)(2,1)S(1)} collective-permute-done((bf16[3,64,2432]{2,1,0:T(8,128)(2,1)S(1)}, bf16[3,64,2432]{2,1,0:T(8,128)(2,1)S(1)}, u32[]{:S(2)}, u32[]{:S(2)}) %collective-permute-start.13) | collective-permute-done | bytes 933920 | tf_op jit(solution)/shard_map/ppermute | solution.py:482
  116.7 1.9 %collective-permute-start.15 = (bf16[3,64,2304]{2,1,0:T(8,128)(2,1)S(1)}, bf16[3,64,2304]{2,1,0:T(8,128)(2,1)S(1)}, u32[]{:S(2)}, u32[]{:S(2)}) collective-permute-start(bf16[3,64,2304]{2,1,0:T(8,128)(2,1)S(1)} %far.1), channel_id=1, source_target_pairs={{0,27},{3,8},{4,31},{7,12},{8,3},{11,16},{12,7},{15,20},{16,11},{1... | collective-permute-start | bytes 2654216 | tf_op jit(solution)/shard_map/ppermute | solution.py:482
  118.6 1.6 %early.1 = f32[3,64,4032]{2,1,0:T(8,128)S(1)} custom-call(s32[1]{0:T(128)} %bitcast.core, f32[3,64,2432]{2,1,0:T(8,128)S(1)} %get-tuple-element.87.own, bf16[3,64,2816]{2,1,0:T(8,128)(2,1)S(1)} %collective-permute-done.11.direct, bf16[3,64,2432]{2,1,0:T(8,128)(2,1)S(1)} %collective-permute-done.13.pair), custom_call_target="tpu_custom_call" | custom-call | flops 10000000000 | bytes 100000000 | tf_op jit(solution)/shard_map/early/pallas_call | solution.py:719
  120.2 4.2 %collective-permute-done.14.merged = bf16[3,64,2816]{2,1,0:T(8,128)(2,1)S(1)} collective-permute-done((bf16[3,64,2816]{2,1,0:T(8,128)(2,1)S(1)}, bf16[3,64,2816]{2,1,0:T(8,128)(2,1)S(1)}, u32[]{:S(2)}, u32[]{:S(2)}) %collective-permute-start.14) | collective-permute-done | bytes 1081376 | tf_op jit(solution)/shard_map/ppermute | solution.py:482
  124.4 9.3 %collective-permute-done.15.far = bf16[3,64,2304]{2,1,0:T(8,128)(2,1)S(1)} collective-permute-done((bf16[3,64,2304]{2,1,0:T(8,128)(2,1)S(1)}, bf16[3,64,2304]{2,1,0:T(8,128)(2,1)S(1)}, u32[]{:S(2)}, u32[]{:S(2)}) %collective-permute-start.15) | collective-permute-done | bytes 884768 | tf_op jit(solution)/shard_map/ppermute | solution.py:482
  133.7 3.0 %total.1 = f32[3,64,4032]{2,1,0:T(8,128)} custom-call(s32[1]{0:T(128)} %bitcast.core, f32[3,64,4032]{2,1,0:T(8,128)S(1)} %early.1, bf16[3,64,2816]{2,1,0:T(8,128)(2,1)S(1)} %collective-permute-done.14.merged, bf16[3,64,2304]{2,1,0:T(8,128)(2,1)S(1)} %collective-permute-done.15.far), custom_call_target="tpu_custom_call" | custom-call | flops 10000000 | bytes 10000000 | tf_op jit(solution)/shard_map/total/pallas_call | solution.py:729
  (47 shorter events, 0.2 us)
Async XLA Ops:
  0.0 3.1 %copy-start.8 = (s32[24,27]{1,0:T(8,128)S(1)}, s32[24,27]{1,0:T(8,128)}, u32[]{:S(2)}) copy-start(s32[24,27]{1,0:T(8,128)} %param.7) | copy-start | bytes 7780
  0.0 10.8 %copy-start.9 = (s32[24,7]{0,1:T(8,128)S(1)}, s32[24,7]{0,1:T(8,128)}, u32[]{:S(2)}) copy-start(s32[24,7]{0,1:T(8,128)} %param.6) | copy-start | bytes 2020
  3.2 8.4 %collective-permute-start.1 = (s32[8,27]{1,0:T(8,128)S(1)}, s32[8,27]{1,0:T(8,128)S(1)}, u32[]{:S(2)}, u32[]{:S(2)}) collective-permute-start(s32[8,27]{1,0:T(8,128)S(1)} %get-tuple-element.99), channel_id=1, source_target_pairs={{0,31},{1,2},{2,1},{3,4},{4,3},{5,6},{6,5},{7,8},{8,7},{9,10},{10,... | collective-permute-start | bytes 2600 | tf_op jit(solution)/shard_map/ppermute | solution.py:482
  9.6 2.1 %collective-permute-start = (s32[8,27]{1,0:T(8,128)S(1)}, s32[8,27]{1,0:T(8,128)S(1)}, u32[]{:S(2)}, u32[]{:S(2)}) collective-permute-start(s32[8,27]{1,0:T(8,128)S(1)} %get-tuple-element.100), channel_id=1, source_target_pairs={{0,1},{1,0},{2,3},{3,2},{4,5},{5,4},{6,7},{7,6},{8,9},{9,8},{10,11... | collective-permute-start | bytes 2600 | tf_op jit(solution)/shard_map/ppermute | solution.py:482
  9.6 4.3 %collective-permute-start.2 = (bf16[8,64,1728]{2,1,0:T(8,128)(2,1)}, bf16[8,64,1728]{2,1,0:T(8,128)(2,1)}, u32[]{:S(2)}, u32[]{:S(2)}) collective-permute-start(bf16[8,64,1728]{2,1,0:T(8,128)(2,1)} %get-tuple-element.55), channel_id=1, source_target_pairs={{0,1},{1,0},{2,3},{3,2},{4,5},{5,4},{6,7},{7,6},{8,9},{9,8},{10,11... | collective-permute-start | bytes 5308424 | tf_op jit(solution)/shard_map/ppermute | solution.py:482
  10.1 40.4 %collective-permute-start.3 = (bf16[8,64,1728]{2,1,0:T(8,128)(2,1)}, bf16[8,64,1728]{2,1,0:T(8,128)(2,1)S(1)}, u32[]{:S(2)}, u32[]{:S(2)}) collective-permute-start(bf16[8,64,1728]{2,1,0:T(8,128)(2,1)} %get-tuple-element.58), channel_id=1, source_target_pairs={{0,31},{1,2},{2,1},{3,4},{4,3},{5,6},{6,5},{7,8},{8,7},{9,10},{10,... | collective-permute-start | bytes 5308424 | tf_op jit(solution)/shard_map/ppermute | solution.py:482
  45.7 4.8 %collective-permute-start.4 = (bf16[3,64,2432]{2,1,0:T(8,128)(2,1)}, bf16[3,64,2432]{2,1,0:T(8,128)(2,1)S(1)}, u32[]{:S(2)}, u32[]{:S(2)}) collective-permute-start(bf16[3,64,2432]{2,1,0:T(8,128)(2,1)} %get-tuple-element.59), channel_id=1, source_target_pairs={{0,1},{1,0},{2,3},{3,2},{4,5},{5,4},{6,7},{7,6},{8,9},{9,8},{10,11... | collective-permute-start | bytes 2801672 | tf_op jit(solution)/shard_map/ppermute | solution.py:482
  46.2 4.3 %collective-permute-start.5 = (bf16[3,64,2432]{2,1,0:T(8,128)(2,1)}, bf16[3,64,2432]{2,1,0:T(8,128)(2,1)S(1)}, u32[]{:S(2)}, u32[]{:S(2)}) collective-permute-start(bf16[3,64,2432]{2,1,0:T(8,128)(2,1)} %get-tuple-element.60), channel_id=1, source_target_pairs={{0,1},{1,0},{2,3},{3,2},{4,5},{5,4},{6,7},{7,6},{8,9},{9,8},{10,11... | collective-permute-start | bytes 2801672 | tf_op jit(solution)/shard_map/ppermute | solution.py:482
  46.3 4.2 %collective-permute-start.6 = (bf16[6,64,512]{2,1,0:T(8,128)(2,1)}, bf16[6,64,512]{2,1,0:T(8,128)(2,1)S(1)}, u32[]{:S(2)}, u32[]{:S(2)}) collective-permute-start(bf16[6,64,512]{2,1,0:T(8,128)(2,1)} %get-tuple-element.61), channel_id=1, source_target_pairs={{0,1},{1,0},{2,3},{3,2},{4,5},{5,4},{6,7},{7,6},{8,9},{9,8},{10,11... | collective-permute-start | bytes 1179656 | tf_op jit(solution)/shard_map/ppermute | solution.py:482
  46.7 2.2 %copy-start = (f32[33,64,512]{2,1,0:T(8,128)S(1)}, f32[33,64,512]{2,1,0:T(8,128)}, u32[]{:S(2)}) copy-start(f32[33,64,512]{2,1,0:T(8,128)} %get-tuple-element.66.rest) | copy-start | bytes 12976132
  48.9 1.0 copy-start.2
  50.5 3.9 %copy-start.1 = (bf16[3,64,2432]{2,1,0:T(8,128)(2,1)S(1)}, bf16[3,64,2432]{2,1,0:T(8,128)(2,1)}, u32[]{:S(2)}) copy-start(bf16[3,64,2432]{2,1,0:T(8,128)(2,1)} %get-tuple-element.74.far_fast) | copy-start | bytes 2801668
  50.5 3.9 %copy-start.3 = (bf16[3,64,512]{2,1,0:T(8,128)(2,1)S(1)}, bf16[3,64,512]{2,1,0:T(8,128)(2,1)}, u32[]{:S(2)}) copy-start(bf16[3,64,512]{2,1,0:T(8,128)(2,1)} %get-tuple-element.70.slow) | copy-start | bytes 589828
  50.6 7.0 %copy-start.5 = (bf16[6,64,512]{2,1,0:T(8,128)(2,1)S(1)}, bf16[6,64,512]{2,1,0:T(8,128)(2,1)}, u32[]{:S(2)}) copy-start(bf16[6,64,512]{2,1,0:T(8,128)(2,1)} %get-tuple-element.69.slow) | copy-start | bytes 1179652
  54.1 6.5 %collective-permute-start.7 = (bf16[40,64,512]{2,1,0:T(8,128)(2,1)S(1)}, bf16[40,64,512]{2,1,0:T(8,128)(2,1)S(1)}, u32[]{:S(2)}, u32[]{:S(2)}) collective-permute-start(bf16[40,64,512]{2,1,0:T(8,128)(2,1)S(1)} %slow.1.wt_slow), channel_id=1, source_target_pairs={{0,1},{1,0},{2,3},{3,2},{4,5},{5,4},{6,7},{7,6},{8,9},{9,8},{10,11... | collective-permute-start | bytes 7864328 | tf_op jit(solution)/shard_map/ppermute | solution.py:482
  54.4 3.1 %copy-start.4 = (bf16[6,64,2432]{2,1,0:T(8,128)(2,1)S(1)}, bf16[6,64,2432]{2,1,0:T(8,128)(2,1)}, u32[]{:S(2)}) copy-start(bf16[6,64,2432]{2,1,0:T(8,128)(2,1)} %get-tuple-element.76.inner) | copy-start | bytes 5603332
  54.4 22.5 %slice-start = ((s8[5242880]{0:T(1024)(128)(4,1)}), s8[4194304]{0:T(1024)(128)(4,1)S(1)}, s32[]{:S(2)}) async-start(s8[5242880]{0:T(1024)(128)(4,1)} %bitcast.9), calls=%async_computation | async-start | bytes 8388608
  56.7 6.9 %collective-permute-start.8 = (bf16[3,64,2304]{2,1,0:T(8,128)(2,1)S(1)}, bf16[3,64,2304]{2,1,0:T(8,128)(2,1)S(1)}, u32[]{:S(2)}, u32[]{:S(2)}) collective-permute-start(bf16[3,64,2304]{2,1,0:T(8,128)(2,1)S(1)} %far.1), channel_id=1, source_target_pairs={{1,2},{2,1},{5,6},{6,5},{9,10},{10,9},{13,14},{14,13},{17,18},{18,... | collective-permute-start | bytes 2654216 | tf_op jit(solution)/shard_map/ppermute | solution.py:482
  57.6 19.3 %slice-start.1 = ((s8[5242880]{0:T(1024)(128)(4,1)}), s8[1048576]{0:T(1024)(128)(4,1)S(1)}, s32[]{:S(2)}) async-start(s8[5242880]{0:T(1024)(128)(4,1)} %bitcast.9), calls=%async_computation.1 | async-start | bytes 2097152
  60.6 3.0 %copy-start.10 = (bf16[9,64,2432]{2,1,0:T(8,128)(2,1)S(1)}, bf16[9,64,2432]{2,1,0:T(8,128)(2,1)}, u32[]{:S(2)}) copy-start(bf16[9,64,2432]{2,1,0:T(8,128)(2,1)} %get-tuple-element.86) | copy-start | bytes 8404996
  60.6 10.7 %copy-start.11 = (bf16[9,64,512]{2,1,0:T(8,128)(2,1)S(1)}, bf16[9,64,512]{2,1,0:T(8,128)(2,1)}, u32[]{:S(2)}) copy-start(bf16[9,64,512]{2,1,0:T(8,128)(2,1)} %get-tuple-element.84) | copy-start | bytes 1769476
  63.6 13.4 %copy-start.6 = (bf16[9,64,1024]{2,1,0:T(8,128)(2,1)S(1)}, bf16[9,64,1024]{2,1,0:T(8,128)(2,1)}, u32[]{:S(2)}) copy-start(bf16[9,64,1024]{2,1,0:T(8,128)(2,1)} %get-tuple-element.56.fast) | copy-start | bytes 3538948
  63.6 13.4 %copy-start.7 = (bf16[9,64,512]{2,1,0:T(8,128)(2,1)S(1)}, bf16[9,64,512]{2,1,0:T(8,128)(2,1)}, u32[]{:S(2)}) copy-start(bf16[9,64,512]{2,1,0:T(8,128)(2,1)} %get-tuple-element.57.slow) | copy-start | bytes 1769476
  63.6 13.3 %collective-permute-start.10 = (bf16[9,64,2432]{2,1,0:T(8,128)(2,1)S(1)}, bf16[9,64,2432]{2,1,0:T(8,128)(2,1)S(1)}, u32[]{:S(2)}, u32[]{:S(2)}) collective-permute-start(bf16[9,64,2432]{2,1,0:T(8,128)(2,1)S(1)} %copy-done.10), channel_id=1, source_target_pairs={{0,1},{1,0},{2,3},{3,2},{4,5},{5,4},{6,7},{7,6},{8,9},{9,8},{10,11... | collective-permute-start | bytes 8405000 | tf_op jit(solution)/shard_map/ppermute | solution.py:482
  71.3 5.6 %collective-permute-start.9 = (bf16[9,64,512]{2,1,0:T(8,128)(2,1)S(1)}, bf16[9,64,512]{2,1,0:T(8,128)(2,1)S(1)}, u32[]{:S(2)}, u32[]{:S(2)}) collective-permute-start(bf16[9,64,512]{2,1,0:T(8,128)(2,1)S(1)} %copy-done.11), channel_id=1, source_target_pairs={{0,1},{1,0},{2,3},{3,2},{4,5},{5,4},{6,7},{7,6},{8,9},{9,8},{10,11... | collective-permute-start | bytes 1769480 | tf_op jit(solution)/shard_map/ppermute | solution.py:482
  71.4 23.0 %collective-permute-start.12 = (bf16[3,64,2432]{2,1,0:T(8,128)(2,1)S(1)}, bf16[3,64,2432]{2,1,0:T(8,128)(2,1)S(1)}, u32[]{:S(2)}, u32[]{:S(2)}) collective-permute-start(bf16[3,64,2432]{2,1,0:T(8,128)(2,1)S(1)} %get-tuple-element.90), channel_id=1, source_target_pairs={{0,2},{1,3},{2,0},{3,1},{4,6},{5,7},{6,4},{7,5},{8,10},{9,11},{10,... | collective-permute-start | bytes 2801672 | tf_op jit(solution)/shard_map/ppermute | solution.py:482
  73.9 44.7 %collective-permute-start.11 = (bf16[3,64,2816]{2,1,0:T(8,128)(2,1)S(1)}, bf16[3,64,2816]{2,1,0:T(8,128)(2,1)S(1)}, u32[]{:S(2)}, u32[]{:S(2)}) collective-permute-start(bf16[3,64,2816]{2,1,0:T(8,128)(2,1)S(1)} %merge_far.1), channel_id=1, source_target_pairs={{0,28},{1,29},{2,6},{3,7},{4,0},{5,1},{6,10},{7,11},{8,4},{9,5},{1... | collective-permute-start | bytes 3244040 | tf_op jit(solution)/shard_map/ppermute | solution.py:482
  94.4 22.3 %collective-permute-start.13 = (bf16[3,64,2432]{2,1,0:T(8,128)(2,1)S(1)}, bf16[3,64,2432]{2,1,0:T(8,128)(2,1)S(1)}, u32[]{:S(2)}, u32[]{:S(2)}) collective-permute-start(bf16[3,64,2432]{2,1,0:T(8,128)(2,1)S(1)} %get-tuple-element.92), channel_id=1, source_target_pairs={{0,2},{1,3},{2,0},{3,1},{4,6},{5,7},{6,4},{7,5},{8,10},{9,11},{10,... | collective-permute-start | bytes 2801672 | tf_op jit(solution)/shard_map/ppermute | solution.py:482
  96.8 27.6 %collective-permute-start.14 = (bf16[3,64,2816]{2,1,0:T(8,128)(2,1)S(1)}, bf16[3,64,2816]{2,1,0:T(8,128)(2,1)S(1)}, u32[]{:S(2)}, u32[]{:S(2)}) collective-permute-start(bf16[3,64,2816]{2,1,0:T(8,128)(2,1)S(1)} %merge.1), channel_id=1, source_target_pairs={{0,4},{1,5},{2,30},{3,31},{4,8},{5,9},{6,2},{7,3},{8,12},{9,13},{1... | collective-permute-start | bytes 3244040 | tf_op jit(solution)/shard_map/ppermute | solution.py:482
  116.7 17.0 %collective-permute-start.15 = (bf16[3,64,2304]{2,1,0:T(8,128)(2,1)S(1)}, bf16[3,64,2304]{2,1,0:T(8,128)(2,1)S(1)}, u32[]{:S(2)}, u32[]{:S(2)}) collective-permute-start(bf16[3,64,2304]{2,1,0:T(8,128)(2,1)S(1)} %far.1), channel_id=1, source_target_pairs={{0,27},{3,8},{4,31},{7,12},{8,3},{11,16},{12,7},{15,20},{16,11},{1... | collective-permute-start | bytes 2654216 | tf_op jit(solution)/shard_map/ppermute | solution.py:482

commit v14 on v13

--- a/solution.py
+++ b/solution.py
@@ -428,11 +428,12 @@
         store(frame[:, first - BS : last - BS])
 
 
-def early_kernel(core, own, direct, pair, out, frame):
+def early_kernel(core, own, direct, pair, far, out, frame):
     s, x = places(core)
     for j in range(NC):
         top = 27 - 3 * s - j
         messages = [(own, top - 12), (direct, top - 30 * x), (pair, top - 6 - 12 * x)]
+        messages.append((far, jnp.where(s == 1, 30 - j, -1 - j)))
 
         def store(value, j=j):
             out[j] = value
@@ -440,16 +441,15 @@
         in_frame(s, j, frame, messages, store)
 
 
-def total_kernel(core, early, merged, far, out, frame, buf, sems):
+def total_kernel(core, early, merged, out, frame, buf, sems):
     s, x = places(core)
     copies = []
     for j in range(NC):
-        far_start = jnp.where(s == 1, 30 - j, -1 - j)
 
         def store(value, j=j):
             buf[j] = value + early[j]
 
-        in_frame(s, j, frame, [(merged, 3 - 3 * s - j + 18 * x), (far, far_start)], store)
+        in_frame(s, j, frame, [(merged, 3 - 3 * s - j + 18 * x)], store)
         copy = pltpu.make_async_copy(buf.at[j], out.at[j], sems.at[j])
         copy.start()
         copies.append(copy)
@@ -710,7 +710,7 @@
     merged = merge_rows(merge, relay, 0, "merge")
     merged = permuted(merged, [(i, (i - 4 * x_sign[i]) % devices) for i in range(devices)])
     pair = permuted(pair, along_x)
-    pair, far = lax.optimization_barrier((pair, far))
+    direct, far = lax.optimization_barrier((direct, far))
     straight = [i for i in range(devices) if i % 4 in (0, 3)]
     far = permuted(far, [(i, (i + (5 if i % 2 else -5)) % devices) for i in straight])
 
@@ -719,17 +719,17 @@
     early = pl.pallas_call(
         early_kernel,
         out_shape=total,
-        in_specs=[smem] + [vmem] * 3,
+        in_specs=[smem] + [vmem] * 4,
         out_specs=vmem,
         scratch_shapes=[frame],
         compiler_params=params(16),
         cost_estimate=cost(10**10, 100 * 10**6),
         name="early",
-    )(core, own, direct, pair)
+    )(core, own, direct, pair, far)
     return pl.pallas_call(
         total_kernel,
         out_shape=total,
-        in_specs=[smem] + [vmem] * 3,
+        in_specs=[smem] + [vmem] * 2,
         out_specs=hbm,
         scratch_shapes=[
             frame,
@@ -739,7 +739,7 @@
         compiler_params=params(20),
         cost_estimate=cost(10**7, 10**7),
         name="total",
-    )(core, early, merged, far)
+    )(core, early, merged)
 
 
 def solution(mesh):

time: 137 us -> 142 us (1.036)
  starting transfers between devices: 25.4 us -> 28.3 us
  waiting for transfers between devices: 44.2 us -> 46.3 us
    ppermute x16, starting transfers between devices: 25.4 us -> 28.3 us  [permuted(): return lax.ppermute(block, 'dom', pairs)]
    ppermute x16, waiting for transfers between devices: 44.2 us -> 46.3 us  [permuted(): return lax.ppermute(block, 'dom', pairs)]
  transfers between devices with their start and end apart: 16 -> 16, of which waited for: 6 -> 6; matrix products, arithmetic and copies ran while one was open for 2% -> 2% of each run, Pallas kernels for 38% -> 37%
where the time goes in v14:
time: 142 us
  Pallas kernels  61.2 us (43%)
  waiting for transfers between devices  46.3 us (33%)
  starting transfers between devices  28.3 us (20%)
  local copies, waits for them, and re-layouts  3.59 us (3%)
  other arithmetic  1.91 us (1%)
    ppermute x16, waiting for transfers between devices, permuted(): return lax.ppermute(block, 'dom', pairs)  46.3 us
    pallas_call x1, Pallas kernels, body(): pl.pallas_call(fast_kernel, out_shape=outs, in_specs=[smem] * 3 + [hbm, h...  31.9 us
    ppermute x16, starting transfers between devices, permuted(): return lax.ppermute(block, 'dom', pairs)  28.3 us
    pallas_call x1, Pallas kernels, body(): pl.pallas_call(join_rest_kernel, out_shape=[block(NC, span, jnp.float32),...  8.11 us
    pallas_call x1, Pallas kernels, body(): pl.pallas_call(slow_kernel, out_shape=block(WCOLS, AW), in_specs=[smem] *...  3.53 us
    unnamed x28, local copies, waits for them, and re-layouts  3.32 us
    pallas_call x1, Pallas kernels, body(): pl.pallas_call(pick_kernel, out_shape=[edge, edge], in_specs=[smem, hbm],...  3.08 us
    pallas_call x1, Pallas kernels, body(): pl.pallas_call(mine_kernel, out_shape=block(FIRST, span, jnp.float32), in...  2.98 us
  transfers between devices with their start and end apart: 16, of which 6 were waited for; matrix products, arithmetic and copies ran while one was open for 2% of the time, Pallas kernels for 37%

profile of v14, /device:TPU:0, one launch (start us, length us, event | category | flops | bytes accessed | tf_op | source)
XLA Modules:
  0.0 141.8 jit_solution(16039293378997573964)
XLA Ops:
  0.0 3.1 %pick.1 = (bf16[8,64,1728]{2,1,0:T(8,128)(2,1)}, bf16[8,64,1728]{2,1,0:T(8,128)(2,1)}) custom-call(s32[1]{0:T(128)} %bitcast.core, bf16[24,64,1728]{2,1,0:T(8,128)(2,1)} %p_own.1), custom_call_target="tpu_custom_call" | custom-call | tf_op jit(solution)/shard_map/pick/pallas_call | solution.py:516
  3.2 6.4 %collective-permute-start.1 = (s32[8,27]{1,0:T(8,128)S(1)}, s32[8,27]{1,0:T(8,128)S(1)}, u32[]{:S(2)}, u32[]{:S(2)}) collective-permute-start(s32[8,27]{1,0:T(8,128)S(1)} %get-tuple-element.99), channel_id=1, source_target_pairs={{0,31},{1,2},{2,1},{3,4},{4,3},{5,6},{6,5},{7,8},{8,7},{9,10},{10,... | collective-permute-start | bytes 2600 | tf_op jit(solution)/shard_map/ppermute | solution.py:482
  9.6 0.0 collective-permute-start
  9.6 0.5 collective-permute-start.2
  10.1 0.3 collective-permute-start.3
  10.4 0.1 fusion.1
  10.5 0.1 copy.15
  10.6 0.2 select_reduce_fusion
  10.8 0.1 select_reduce_fusion.3
  10.9 0.6 broadcast_add_fusion.inv_a
  11.6 0.1 copy.17
  11.7 0.1 copy.16
  11.8 0.1 select_reduce_fusion.1
  11.9 0.1 select_reduce_fusion.2
  12.1 0.6 pad_add_fusion.inv_p
  12.7 1.2 collective-permute-done.2.p_fast
  13.9 31.9 %fast.1 = (bf16[3,64,2432]{2,1,0:T(8,128)(2,1)}, bf16[3,64,2432]{2,1,0:T(8,128)(2,1)}, bf16[3,64,2432]{2,1,0:T(8,128)(2,1)}, bf16[6,64,2432]{2,1,0:T(8,128)(2,1)...) custom-call(s32[1]{0:T(128)} %bitcast.core, ...), custom_call_target="tpu_custom_call" | custom-call | flops 20000000000 | bytes 30000000 | tf_op jit(solution)/shard_map/fast/pallas_call | solution.py:585
  45.7 0.5 collective-permute-start.4
  46.2 0.1 collective-permute-start.5
  46.3 0.4 collective-permute-start.6
  46.7 2.2 %copy-done = f32[33,64,512]{2,1,0:T(8,128)S(1)} copy-done((f32[33,64,512]{2,1,0:T(8,128)S(1)}, f32[33,64,512]{2,1,0:T(8,128)}, u32[]{:S(2)}) %copy-start) | copy-done | bytes 4325400
  48.9 1.0 copy-done.2
  50.0 0.5 stage.1
  50.6 3.5 %slow.1.wt_slow = bf16[40,64,512]{2,1,0:T(8,128)(2,1)S(1)} custom-call(s32[1]{0:T(128)} %bitcast.core, s32[8,33]{1,0:T(8,128)S(1)} %broadcast_add_fusion.2.inv_slow, bf16[8,64,1728]{2,1,0:T(8,128)(2,1)S(1)} %collective-permute-done.3.p_slow, bf16[8,64,512]{2,1,0:T(8,128)(2,1)S(1)} %get-tuple-element.67.at_halo, f32[33,64,512]{2,1,0:T(8,128)S(1)} %get-tuple-element.68.rest), custom_call_target="tpu_custom_call" | custom-call | flops 20000000000 | bytes 200000000 | tf_op jit(solution)/shard_map/slow/pallas_call | solution.py:629
  54.1 0.3 collective-permute-start.7
  54.5 2.2 %far.1 = bf16[3,64,2304]{2,1,0:T(8,128)(2,1)S(1)} custom-call(s32[1]{0:T(128)} %bitcast.core, bf16[3,64,512]{2,1,0:T(8,128)(2,1)S(1)} %copy-done.3, bf16[40,64,512]{2,1,0:T(8,128)(2,1)S(1)} %slow.1.wt_slow, bf16[3,64,2432]{2,1,0:T(8,128)(2,1)S(1)} %copy-done.1), custom_call_target="tpu_custom_call" | custom-call | flops 1000000000 | bytes 10000000 | tf_op jit(solution)/shard_map/far/pallas_call | solution.py:647
  56.7 0.9 collective-permute-start.8
  57.6 3.0 %mine.1 = f32[6,64,2432]{2,1,0:T(8,128)S(1)} custom-call(bf16[6,64,512]{2,1,0:T(8,128)(2,1)S(1)} %copy-done.5, bf16[40,64,512]{2,1,0:T(8,128)(2,1)S(1)} %slow.1.wt_slow, bf16[6,64,2432]{2,1,0:T(8,128)(2,1)S(1)} %copy-done.4, bf16[3,64,2432]{2,1,0:T(8,128)(2,1)S(1)} %collective-permute-done.4.low, bf16[3,64,2432]{2,1,0:T(8,128)(2,1)S(1)} %collective-permute-done.5.high), custom_call_target="tpu_custom_call" | custom-call | flops 10000000000 | bytes 100000000 | tf_op jit(solution)/shard_map/mine/pallas_call | solution.py:657
  60.6 0.0 copy-start.10
  60.6 2.9 %join_first.1 = (bf16[3,64,2432]{2,1,0:T(8,128)(2,1)S(1)}, f32[3,64,2432]{2,1,0:T(8,128)S(1)}) custom-call(bf16[6,64,512]{2,1,0:T(8,128)(2,1)S(1)} %collective-permute-done.6.other, bf16[40,64,512]{2,1,0:T(8,128)(2,1)S(1)} %collective-permute-done.7.wt_other, f32[6,64,2432]{2,1,0:T(8,128)S(1)} %mine.1), custom_call_target="tpu_custom_call" | custom-call | flops 1000000 | bytes 100000 | tf_op jit(solution)/shard_map/join_first/pallas_call | solution.py:668
  63.6 7.7 %collective-permute-start.10 = (bf16[9,64,2432]{2,1,0:T(8,128)(2,1)S(1)}, bf16[9,64,2432]{2,1,0:T(8,128)(2,1)S(1)}, u32[]{:S(2)}, u32[]{:S(2)}) collective-permute-start(bf16[9,64,2432]{2,1,0:T(8,128)(2,1)S(1)} %copy-done.10), channel_id=1, source_target_pairs={{0,1},{1,0},{2,3},{3,2},{4,5},{5,4},{6,7},{7,6},{8,9},{9,8},{10,11... | collective-permute-start | bytes 8405000 | tf_op jit(solution)/shard_map/ppermute | solution.py:482
  71.3 0.1 collective-permute-start.9
  71.4 2.0 %collective-permute-start.12 = (bf16[3,64,2432]{2,1,0:T(8,128)(2,1)S(1)}, bf16[3,64,2432]{2,1,0:T(8,128)(2,1)S(1)}, u32[]{:S(2)}, u32[]{:S(2)}) collective-permute-start(bf16[3,64,2432]{2,1,0:T(8,128)(2,1)S(1)} %get-tuple-element.91), channel_id=1, source_target_pairs={{0,2},{1,3},{2,0},{3,1},{4,6},{5,7},{6,4},{7,5},{8,10},{9,11},{10,... | collective-permute-start | bytes 2801672 | tf_op jit(solution)/shard_map/ppermute | solution.py:482
  73.3 0.6 merge_far.1
  73.9 2.6 %collective-permute-start.11 = (bf16[3,64,2816]{2,1,0:T(8,128)(2,1)S(1)}, bf16[3,64,2816]{2,1,0:T(8,128)(2,1)S(1)}, u32[]{:S(2)}, u32[]{:S(2)}) collective-permute-start(bf16[3,64,2816]{2,1,0:T(8,128)(2,1)S(1)} %merge_far.1), channel_id=1, source_target_pairs={{0,28},{1,29},{2,6},{3,7},{4,0},{5,1},{6,10},{7,11},{8,4},{9,5},{1... | collective-permute-start | bytes 3244040 | tf_op jit(solution)/shard_map/ppermute | solution.py:482
  76.5 0.4 collective-permute-done.9.other
  77.0 8.1 %join_rest.1 = (f32[3,64,2432]{2,1,0:T(8,128)S(1)}, bf16[3,64,2432]{2,1,0:T(8,128)(2,1)S(1)}, f32[3,64,2432]{2,1,0:T(8,128)S(1)}) custom-call(bf16[9,64,1024]{2,1,0:T(8,128)(2,1)S(1)} %copy-done.6, bf16[9,64,512]{2,1,0:T(8,128)(2,1)S(1)} %copy-done.7, bf16[9,64,512]{2,1,0:T(8,128)(2,1)S(1)} %collective-permute-done.9.other, ...), custom_call_target="tpu_custom_call" | custom-call | flops 40000000000 | bytes 200000000 | tf_op jit(solution)/shard_map/join_rest/pallas_call | solution.py:700
  85.1 9.3 %collective-permute-done.12.other = bf16[3,64,2432]{2,1,0:T(8,128)(2,1)S(1)} collective-permute-done((bf16[3,64,2432]{2,1,0:T(8,128)(2,1)S(1)}, bf16[3,64,2432]{2,1,0:T(8,128)(2,1)S(1)}, u32[]{:S(2)}, u32[]{:S(2)}) %collective-permute-start.12) | collective-permute-done | bytes 933920 | tf_op jit(solution)/shard_map/ppermute | solution.py:482
  94.4 1.6 %collective-permute-start.13 = (bf16[3,64,2432]{2,1,0:T(8,128)(2,1)S(1)}, bf16[3,64,2432]{2,1,0:T(8,128)(2,1)S(1)}, u32[]{:S(2)}, u32[]{:S(2)}) collective-permute-start(bf16[3,64,2432]{2,1,0:T(8,128)(2,1)S(1)} %get-tuple-element.93), channel_id=1, source_target_pairs={{0,2},{1,3},{2,0},{3,1},{4,6},{5,7},{6,4},{7,5},{8,10},{9,11},{10,... | collective-permute-start | bytes 2801672 | tf_op jit(solution)/shard_map/ppermute | solution.py:482
  96.0 3.6 %collective-permute-done.11.direct = bf16[3,64,2816]{2,1,0:T(8,128)(2,1)S(1)} collective-permute-done((bf16[3,64,2816]{2,1,0:T(8,128)(2,1)S(1)}, bf16[3,64,2816]{2,1,0:T(8,128)(2,1)S(1)}, u32[]{:S(2)}, u32[]{:S(2)}) %collective-permute-start.11) | collective-permute-done | bytes 1081376 | tf_op jit(solution)/shard_map/ppermute | solution.py:482
  99.6 3.5 %collective-permute-start.14 = (bf16[3,64,2304]{2,1,0:T(8,128)(2,1)S(1)}, bf16[3,64,2304]{2,1,0:T(8,128)(2,1)S(1)}, u32[]{:S(2)}, u32[]{:S(2)}) collective-permute-start(bf16[3,64,2304]{2,1,0:T(8,128)(2,1)S(1)} %far.1), channel_id=1, source_target_pairs={{0,27},{3,8},{4,31},{7,12},{8,3},{11,16},{12,7},{15,20},{16,11},{1... | collective-permute-start | bytes 2654216 | tf_op jit(solution)/shard_map/ppermute | solution.py:482
  103.1 0.8 merge.1
  103.9 1.4 collective-permute-start.15
  105.3 20.8 %collective-permute-done.14.far = bf16[3,64,2304]{2,1,0:T(8,128)(2,1)S(1)} collective-permute-done((bf16[3,64,2304]{2,1,0:T(8,128)(2,1)S(1)}, bf16[3,64,2304]{2,1,0:T(8,128)(2,1)S(1)}, u32[]{:S(2)}, u32[]{:S(2)}) %collective-permute-start.14) | collective-permute-done | bytes 884768 | tf_op jit(solution)/shard_map/ppermute | solution.py:482
  126.1 0.0 collective-permute-done.13.pair
  126.2 1.8 %early.1 = f32[3,64,4032]{2,1,0:T(8,128)S(1)} custom-call(s32[1]{0:T(128)} %bitcast.core, f32[3,64,2432]{2,1,0:T(8,128)S(1)} %get-tuple-element.87.own, bf16[3,64,2816]{2,1,0:T(8,128)(2,1)S(1)} %collective-permute-done.11.direct, bf16[3,64,2432]{2,1,0:T(8,128)(2,1)S(1)} %collective-permute-done.13.pair, bf16[3,64,2304]{2,1,0:T(8,128)(2,1)S(1)} %collective-permute-done.14.far), custom_call_target="tpu_custom_call" | custom-call | flops 10000000000 | bytes 100000000 | tf_op jit(solution)/shard_map/early/pallas_call | solution.py:719
  128.0 10.9 %collective-permute-done.15.merged = bf16[3,64,2816]{2,1,0:T(8,128)(2,1)S(1)} collective-permute-done((bf16[3,64,2816]{2,1,0:T(8,128)(2,1)S(1)}, bf16[3,64,2816]{2,1,0:T(8,128)(2,1)S(1)}, u32[]{:S(2)}, u32[]{:S(2)}) %collective-permute-start.15) | collective-permute-done | bytes 1081376 | tf_op jit(solution)/shard_map/ppermute | solution.py:482
  138.8 2.8 %total.1 = f32[3,64,4032]{2,1,0:T(8,128)} custom-call(s32[1]{0:T(128)} %bitcast.core, f32[3,64,4032]{2,1,0:T(8,128)S(1)} %early.1, bf16[3,64,2816]{2,1,0:T(8,128)(2,1)S(1)} %collective-permute-done.15.merged), custom_call_target="tpu_custom_call" | custom-call | flops 10000000 | bytes 10000000 | tf_op jit(solution)/shard_map/total/pallas_call | solution.py:729
  (47 shorter events, 0.2 us)
Async XLA Ops:
  0.0 3.1 %copy-start.8 = (s32[24,27]{1,0:T(8,128)S(1)}, s32[24,27]{1,0:T(8,128)}, u32[]{:S(2)}) copy-start(s32[24,27]{1,0:T(8,128)} %param.7) | copy-start | bytes 7780
  0.0 10.8 %copy-start.9 = (s32[24,7]{0,1:T(8,128)S(1)}, s32[24,7]{0,1:T(8,128)}, u32[]{:S(2)}) copy-start(s32[24,7]{0,1:T(8,128)} %param.6) | copy-start | bytes 2020
  3.2 8.4 %collective-permute-start.1 = (s32[8,27]{1,0:T(8,128)S(1)}, s32[8,27]{1,0:T(8,128)S(1)}, u32[]{:S(2)}, u32[]{:S(2)}) collective-permute-start(s32[8,27]{1,0:T(8,128)S(1)} %get-tuple-element.99), channel_id=1, source_target_pairs={{0,31},{1,2},{2,1},{3,4},{4,3},{5,6},{6,5},{7,8},{8,7},{9,10},{10,... | collective-permute-start | bytes 2600 | tf_op jit(solution)/shard_map/ppermute | solution.py:482
  9.6 2.1 %collective-permute-start = (s32[8,27]{1,0:T(8,128)S(1)}, s32[8,27]{1,0:T(8,128)S(1)}, u32[]{:S(2)}, u32[]{:S(2)}) collective-permute-start(s32[8,27]{1,0:T(8,128)S(1)} %get-tuple-element.100), channel_id=1, source_target_pairs={{0,1},{1,0},{2,3},{3,2},{4,5},{5,4},{6,7},{7,6},{8,9},{9,8},{10,11... | collective-permute-start | bytes 2600 | tf_op jit(solution)/shard_map/ppermute | solution.py:482
  9.6 4.3 %collective-permute-start.2 = (bf16[8,64,1728]{2,1,0:T(8,128)(2,1)}, bf16[8,64,1728]{2,1,0:T(8,128)(2,1)}, u32[]{:S(2)}, u32[]{:S(2)}) collective-permute-start(bf16[8,64,1728]{2,1,0:T(8,128)(2,1)} %get-tuple-element.55), channel_id=1, source_target_pairs={{0,1},{1,0},{2,3},{3,2},{4,5},{5,4},{6,7},{7,6},{8,9},{9,8},{10,11... | collective-permute-start | bytes 5308424 | tf_op jit(solution)/shard_map/ppermute | solution.py:482
  10.1 40.4 %collective-permute-start.3 = (bf16[8,64,1728]{2,1,0:T(8,128)(2,1)}, bf16[8,64,1728]{2,1,0:T(8,128)(2,1)S(1)}, u32[]{:S(2)}, u32[]{:S(2)}) collective-permute-start(bf16[8,64,1728]{2,1,0:T(8,128)(2,1)} %get-tuple-element.58), channel_id=1, source_target_pairs={{0,31},{1,2},{2,1},{3,4},{4,3},{5,6},{6,5},{7,8},{8,7},{9,10},{10,... | collective-permute-start | bytes 5308424 | tf_op jit(solution)/shard_map/ppermute | solution.py:482
  45.7 4.8 %collective-permute-start.4 = (bf16[3,64,2432]{2,1,0:T(8,128)(2,1)}, bf16[3,64,2432]{2,1,0:T(8,128)(2,1)S(1)}, u32[]{:S(2)}, u32[]{:S(2)}) collective-permute-start(bf16[3,64,2432]{2,1,0:T(8,128)(2,1)} %get-tuple-element.59), channel_id=1, source_target_pairs={{0,1},{1,0},{2,3},{3,2},{4,5},{5,4},{6,7},{7,6},{8,9},{9,8},{10,11... | collective-permute-start | bytes 2801672 | tf_op jit(solution)/shard_map/ppermute | solution.py:482
  46.2 4.3 %collective-permute-start.5 = (bf16[3,64,2432]{2,1,0:T(8,128)(2,1)}, bf16[3,64,2432]{2,1,0:T(8,128)(2,1)S(1)}, u32[]{:S(2)}, u32[]{:S(2)}) collective-permute-start(bf16[3,64,2432]{2,1,0:T(8,128)(2,1)} %get-tuple-element.60), channel_id=1, source_target_pairs={{0,1},{1,0},{2,3},{3,2},{4,5},{5,4},{6,7},{7,6},{8,9},{9,8},{10,11... | collective-permute-start | bytes 2801672 | tf_op jit(solution)/shard_map/ppermute | solution.py:482
  46.3 4.2 %collective-permute-start.6 = (bf16[6,64,512]{2,1,0:T(8,128)(2,1)}, bf16[6,64,512]{2,1,0:T(8,128)(2,1)S(1)}, u32[]{:S(2)}, u32[]{:S(2)}) collective-permute-start(bf16[6,64,512]{2,1,0:T(8,128)(2,1)} %get-tuple-element.61), channel_id=1, source_target_pairs={{0,1},{1,0},{2,3},{3,2},{4,5},{5,4},{6,7},{7,6},{8,9},{9,8},{10,11... | collective-permute-start | bytes 1179656 | tf_op jit(solution)/shard_map/ppermute | solution.py:482
  46.7 2.2 %copy-start = (f32[33,64,512]{2,1,0:T(8,128)S(1)}, f32[33,64,512]{2,1,0:T(8,128)}, u32[]{:S(2)}) copy-start(f32[33,64,512]{2,1,0:T(8,128)} %get-tuple-element.66.rest) | copy-start | bytes 12976132
  48.9 1.0 copy-start.2
  50.5 3.9 %copy-start.1 = (bf16[3,64,2432]{2,1,0:T(8,128)(2,1)S(1)}, bf16[3,64,2432]{2,1,0:T(8,128)(2,1)}, u32[]{:S(2)}) copy-start(bf16[3,64,2432]{2,1,0:T(8,128)(2,1)} %get-tuple-element.74.far_fast) | copy-start | bytes 2801668
  50.5 3.9 %copy-start.3 = (bf16[3,64,512]{2,1,0:T(8,128)(2,1)S(1)}, bf16[3,64,512]{2,1,0:T(8,128)(2,1)}, u32[]{:S(2)}) copy-start(bf16[3,64,512]{2,1,0:T(8,128)(2,1)} %get-tuple-element.70.slow) | copy-start | bytes 589828
  50.6 7.0 %copy-start.5 = (bf16[6,64,512]{2,1,0:T(8,128)(2,1)S(1)}, bf16[6,64,512]{2,1,0:T(8,128)(2,1)}, u32[]{:S(2)}) copy-start(bf16[6,64,512]{2,1,0:T(8,128)(2,1)} %get-tuple-element.69.slow) | copy-start | bytes 1179652
  54.1 6.5 %collective-permute-start.7 = (bf16[40,64,512]{2,1,0:T(8,128)(2,1)S(1)}, bf16[40,64,512]{2,1,0:T(8,128)(2,1)S(1)}, u32[]{:S(2)}, u32[]{:S(2)}) collective-permute-start(bf16[40,64,512]{2,1,0:T(8,128)(2,1)S(1)} %slow.1.wt_slow), channel_id=1, source_target_pairs={{0,1},{1,0},{2,3},{3,2},{4,5},{5,4},{6,7},{7,6},{8,9},{9,8},{10,11... | collective-permute-start | bytes 7864328 | tf_op jit(solution)/shard_map/ppermute | solution.py:482
  54.4 3.1 %copy-start.4 = (bf16[6,64,2432]{2,1,0:T(8,128)(2,1)S(1)}, bf16[6,64,2432]{2,1,0:T(8,128)(2,1)}, u32[]{:S(2)}) copy-start(bf16[6,64,2432]{2,1,0:T(8,128)(2,1)} %get-tuple-element.76.inner) | copy-start | bytes 5603332
  54.4 22.5 %slice-start = ((s8[5242880]{0:T(1024)(128)(4,1)}), s8[4194304]{0:T(1024)(128)(4,1)S(1)}, s32[]{:S(2)}) async-start(s8[5242880]{0:T(1024)(128)(4,1)} %bitcast.9), calls=%async_computation | async-start | bytes 8388608
  56.7 6.9 %collective-permute-start.8 = (bf16[3,64,2304]{2,1,0:T(8,128)(2,1)S(1)}, bf16[3,64,2304]{2,1,0:T(8,128)(2,1)S(1)}, u32[]{:S(2)}, u32[]{:S(2)}) collective-permute-start(bf16[3,64,2304]{2,1,0:T(8,128)(2,1)S(1)} %far.1), channel_id=1, source_target_pairs={{1,2},{2,1},{5,6},{6,5},{9,10},{10,9},{13,14},{14,13},{17,18},{18,... | collective-permute-start | bytes 2654216 | tf_op jit(solution)/shard_map/ppermute | solution.py:482
  57.6 19.3 %slice-start.1 = ((s8[5242880]{0:T(1024)(128)(4,1)}), s8[1048576]{0:T(1024)(128)(4,1)S(1)}, s32[]{:S(2)}) async-start(s8[5242880]{0:T(1024)(128)(4,1)} %bitcast.9), calls=%async_computation.1 | async-start | bytes 2097152
  60.6 3.0 %copy-start.10 = (bf16[9,64,2432]{2,1,0:T(8,128)(2,1)S(1)}, bf16[9,64,2432]{2,1,0:T(8,128)(2,1)}, u32[]{:S(2)}) copy-start(bf16[9,64,2432]{2,1,0:T(8,128)(2,1)} %get-tuple-element.86) | copy-start | bytes 8404996
  60.6 10.7 %copy-start.11 = (bf16[9,64,512]{2,1,0:T(8,128)(2,1)S(1)}, bf16[9,64,512]{2,1,0:T(8,128)(2,1)}, u32[]{:S(2)}) copy-start(bf16[9,64,512]{2,1,0:T(8,128)(2,1)} %get-tuple-element.84) | copy-start | bytes 1769476
  63.6 13.4 %copy-start.6 = (bf16[9,64,1024]{2,1,0:T(8,128)(2,1)S(1)}, bf16[9,64,1024]{2,1,0:T(8,128)(2,1)}, u32[]{:S(2)}) copy-start(bf16[9,64,1024]{2,1,0:T(8,128)(2,1)} %get-tuple-element.56.fast) | copy-start | bytes 3538948
  63.6 13.4 %copy-start.7 = (bf16[9,64,512]{2,1,0:T(8,128)(2,1)S(1)}, bf16[9,64,512]{2,1,0:T(8,128)(2,1)}, u32[]{:S(2)}) copy-start(bf16[9,64,512]{2,1,0:T(8,128)(2,1)} %get-tuple-element.57.slow) | copy-start | bytes 1769476
  63.6 13.3 %collective-permute-start.10 = (bf16[9,64,2432]{2,1,0:T(8,128)(2,1)S(1)}, bf16[9,64,2432]{2,1,0:T(8,128)(2,1)S(1)}, u32[]{:S(2)}, u32[]{:S(2)}) collective-permute-start(bf16[9,64,2432]{2,1,0:T(8,128)(2,1)S(1)} %copy-done.10), channel_id=1, source_target_pairs={{0,1},{1,0},{2,3},{3,2},{4,5},{5,4},{6,7},{7,6},{8,9},{9,8},{10,11... | collective-permute-start | bytes 8405000 | tf_op jit(solution)/shard_map/ppermute | solution.py:482
  71.3 5.6 %collective-permute-start.9 = (bf16[9,64,512]{2,1,0:T(8,128)(2,1)S(1)}, bf16[9,64,512]{2,1,0:T(8,128)(2,1)S(1)}, u32[]{:S(2)}, u32[]{:S(2)}) collective-permute-start(bf16[9,64,512]{2,1,0:T(8,128)(2,1)S(1)} %copy-done.11), channel_id=1, source_target_pairs={{0,1},{1,0},{2,3},{3,2},{4,5},{5,4},{6,7},{7,6},{8,9},{9,8},{10,11... | collective-permute-start | bytes 1769480 | tf_op jit(solution)/shard_map/ppermute | solution.py:482
  71.4 23.0 %collective-permute-start.12 = (bf16[3,64,2432]{2,1,0:T(8,128)(2,1)S(1)}, bf16[3,64,2432]{2,1,0:T(8,128)(2,1)S(1)}, u32[]{:S(2)}, u32[]{:S(2)}) collective-permute-start(bf16[3,64,2432]{2,1,0:T(8,128)(2,1)S(1)} %get-tuple-element.91), channel_id=1, source_target_pairs={{0,2},{1,3},{2,0},{3,1},{4,6},{5,7},{6,4},{7,5},{8,10},{9,11},{10,... | collective-permute-start | bytes 2801672 | tf_op jit(solution)/shard_map/ppermute | solution.py:482
  73.9 25.7 %collective-permute-start.11 = (bf16[3,64,2816]{2,1,0:T(8,128)(2,1)S(1)}, bf16[3,64,2816]{2,1,0:T(8,128)(2,1)S(1)}, u32[]{:S(2)}, u32[]{:S(2)}) collective-permute-start(bf16[3,64,2816]{2,1,0:T(8,128)(2,1)S(1)} %merge_far.1), channel_id=1, source_target_pairs={{0,28},{1,29},{2,6},{3,7},{4,0},{5,1},{6,10},{7,11},{8,4},{9,5},{1... | collective-permute-start | bytes 3244040 | tf_op jit(solution)/shard_map/ppermute | solution.py:482
  94.4 31.7 %collective-permute-start.13 = (bf16[3,64,2432]{2,1,0:T(8,128)(2,1)S(1)}, bf16[3,64,2432]{2,1,0:T(8,128)(2,1)S(1)}, u32[]{:S(2)}, u32[]{:S(2)}) collective-permute-start(bf16[3,64,2432]{2,1,0:T(8,128)(2,1)S(1)} %get-tuple-element.93), channel_id=1, source_target_pairs={{0,2},{1,3},{2,0},{3,1},{4,6},{5,7},{6,4},{7,5},{8,10},{9,11},{10,... | collective-permute-start | bytes 2801672 | tf_op jit(solution)/shard_map/ppermute | solution.py:482
  99.6 26.5 %collective-permute-start.14 = (bf16[3,64,2304]{2,1,0:T(8,128)(2,1)S(1)}, bf16[3,64,2304]{2,1,0:T(8,128)(2,1)S(1)}, u32[]{:S(2)}, u32[]{:S(2)}) collective-permute-start(bf16[3,64,2304]{2,1,0:T(8,128)(2,1)S(1)} %far.1), channel_id=1, source_target_pairs={{0,27},{3,8},{4,31},{7,12},{8,3},{11,16},{12,7},{15,20},{16,11},{1... | collective-permute-start | bytes 2654216 | tf_op jit(solution)/shard_map/ppermute | solution.py:482
  103.9 34.9 %collective-permute-start.15 = (bf16[3,64,2816]{2,1,0:T(8,128)(2,1)S(1)}, bf16[3,64,2816]{2,1,0:T(8,128)(2,1)S(1)}, u32[]{:S(2)}, u32[]{:S(2)}) collective-permute-start(bf16[3,64,2816]{2,1,0:T(8,128)(2,1)S(1)} %merge.1), channel_id=1, source_target_pairs={{0,4},{1,5},{2,30},{3,31},{4,8},{5,9},{6,2},{7,3},{8,12},{9,13},{1... | collective-permute-start | bytes 3244040 | tf_op jit(solution)/shard_map/ppermute | solution.py:482

commit v15 on v14

--- a/solution.py
+++ b/solution.py
@@ -428,12 +428,12 @@
         store(frame[:, first - BS : last - BS])
 
 
-def early_kernel(core, own, direct, pair, far, out, frame):
+def early_kernel(core, own, direct, pair, merged, out, frame):
     s, x = places(core)
     for j in range(NC):
         top = 27 - 3 * s - j
         messages = [(own, top - 12), (direct, top - 30 * x), (pair, top - 6 - 12 * x)]
-        messages.append((far, jnp.where(s == 1, 30 - j, -1 - j)))
+        messages.append((merged, top - 24 + 18 * x))
 
         def store(value, j=j):
             out[j] = value
@@ -441,15 +441,16 @@
         in_frame(s, j, frame, messages, store)
 
 
-def total_kernel(core, early, merged, out, frame, buf, sems):
+def total_kernel(core, early, far, out, frame, buf, sems):
     s, x = places(core)
     copies = []
     for j in range(NC):
+        far_start = jnp.where(s == 1, 30 - j, -1 - j)
 
         def store(value, j=j):
             buf[j] = value + early[j]
 
-        in_frame(s, j, frame, [(merged, 3 - 3 * s - j + 18 * x)], store)
+        in_frame(s, j, frame, [(far, far_start)], store)
         copy = pltpu.make_async_copy(buf.at[j], out.at[j], sems.at[j])
         copy.start()
         copies.append(copy)
@@ -708,9 +709,9 @@
     )(fast_rest, slow_rest, other_rest, wt_fast, wt_slow, wt_other, arrived_rest)
     relay, pair = lax.optimization_barrier((relay, pair))
     merged = merge_rows(merge, relay, 0, "merge")
+    merged, far = lax.optimization_barrier((merged, far))
     merged = permuted(merged, [(i, (i - 4 * x_sign[i]) % devices) for i in range(devices)])
     pair = permuted(pair, along_x)
-    direct, far = lax.optimization_barrier((direct, far))
     straight = [i for i in range(devices) if i % 4 in (0, 3)]
     far = permuted(far, [(i, (i + (5 if i % 2 else -5)) % devices) for i in straight])
 
@@ -725,7 +726,7 @@
         compiler_params=params(16),
         cost_estimate=cost(10**10, 100 * 10**6),
         name="early",
-    )(core, own, direct, pair, far)
+    )(core, own, direct, pair, merged)
     return pl.pallas_call(
         total_kernel,
         out_shape=total,
@@ -739,7 +740,7 @@
         compiler_params=params(20),
         cost_estimate=cost(10**7, 10**7),
         name="total",
-    )(core, early, merged)
+    )(core, early, far)
 
 
 def solution(mesh):

time: 142 us -> 135 us (0.951)
  waiting for transfers between devices: 46.3 us -> 39.5 us
    ppermute x16, waiting for transfers between devices: 46.3 us -> 39.5 us  [permuted(): return lax.ppermute(block, 'dom', pairs)]
  transfers between devices with their start and end apart: 16 -> 16, of which waited for: 6 -> 5; matrix products, arithmetic and copies ran while one was open for 2% -> 2% of each run, Pallas kernels for 37% -> 38%
where the time goes in v15:
time: 135 us
  Pallas kernels  61.2 us (45%)
  waiting for transfers between devices  39.5 us (29%)
  starting transfers between devices  28.1 us (21%)
  local copies, waits for them, and re-layouts  3.59 us (3%)
  other arithmetic  1.91 us (1%)
    ppermute x16, waiting for transfers between devices, permuted(): return lax.ppermute(block, 'dom', pairs)  39.5 us
    pallas_call x1, Pallas kernels, body(): pl.pallas_call(fast_kernel, out_shape=outs, in_specs=[smem] * 3 + [hbm, h...  31.9 us
    ppermute x16, starting transfers between devices, permuted(): return lax.ppermute(block, 'dom', pairs)  28.1 us
    pallas_call x1, Pallas kernels, body(): pl.pallas_call(join_rest_kernel, out_shape=[block(NC, span, jnp.float32),...  8.11 us
    pallas_call x1, Pallas kernels, body(): pl.pallas_call(slow_kernel, out_shape=block(WCOLS, AW), in_specs=[smem] *...  3.53 us
    unnamed x28, local copies, waits for them, and re-layouts  3.32 us
    pallas_call x1, Pallas kernels, body(): pl.pallas_call(pick_kernel, out_shape=[edge, edge], in_specs=[smem, hbm],...  3.08 us
    pallas_call x1, Pallas kernels, body(): pl.pallas_call(mine_kernel, out_shape=block(FIRST, span, jnp.float32), in...  2.98 us
  transfers between devices with their start and end apart: 16, of which 5 were waited for; matrix products, arithmetic and copies ran while one was open for 2% of the time, Pallas kernels for 38%

profile of v15, /device:TPU:0, one launch (start us, length us, event | category | flops | bytes accessed | tf_op | source)
XLA Modules:
  0.0 134.8 jit_solution(5951144395886490270)
XLA Ops:
  0.0 3.1 %pick.1 = (bf16[8,64,1728]{2,1,0:T(8,128)(2,1)}, bf16[8,64,1728]{2,1,0:T(8,128)(2,1)}) custom-call(s32[1]{0:T(128)} %bitcast.core, bf16[24,64,1728]{2,1,0:T(8,128)(2,1)} %p_own.1), custom_call_target="tpu_custom_call" | custom-call | tf_op jit(solution)/shard_map/pick/pallas_call | solution.py:517
  3.2 6.4 %collective-permute-start.1 = (s32[8,27]{1,0:T(8,128)S(1)}, s32[8,27]{1,0:T(8,128)S(1)}, u32[]{:S(2)}, u32[]{:S(2)}) collective-permute-start(s32[8,27]{1,0:T(8,128)S(1)} %get-tuple-element.99), channel_id=1, source_target_pairs={{0,31},{1,2},{2,1},{3,4},{4,3},{5,6},{6,5},{7,8},{8,7},{9,10},{10,... | collective-permute-start | bytes 2600 | tf_op jit(solution)/shard_map/ppermute | solution.py:483
  9.6 0.0 collective-permute-start
  9.6 0.5 collective-permute-start.2
  10.1 0.3 collective-permute-start.3
  10.4 0.1 fusion.1
  10.5 0.1 copy.15
  10.6 0.2 select_reduce_fusion
  10.8 0.1 select_reduce_fusion.3
  10.9 0.6 broadcast_add_fusion.inv_a
  11.6 0.0 collective-permute-done.1
  11.6 0.1 copy.17
  11.7 0.0 collective-permute-done
  11.7 0.1 copy.16
  11.8 0.1 select_reduce_fusion.1
  11.9 0.1 select_reduce_fusion.2
  12.1 0.6 pad_add_fusion.inv_p
  12.7 1.2 collective-permute-done.2.p_fast
  13.9 31.9 %fast.1 = (bf16[3,64,2432]{2,1,0:T(8,128)(2,1)}, bf16[3,64,2432]{2,1,0:T(8,128)(2,1)}, bf16[3,64,2432]{2,1,0:T(8,128)(2,1)}, bf16[6,64,2432]{2,1,0:T(8,128)(2,1)...) custom-call(s32[1]{0:T(128)} %bitcast.core, ...), custom_call_target="tpu_custom_call" | custom-call | flops 20000000000 | bytes 30000000 | tf_op jit(solution)/shard_map/fast/pallas_call | solution.py:586
  45.7 0.5 collective-permute-start.4
  46.2 0.1 collective-permute-start.5
  46.3 0.4 collective-permute-start.6
  46.7 2.2 %copy-done = f32[33,64,512]{2,1,0:T(8,128)S(1)} copy-done((f32[33,64,512]{2,1,0:T(8,128)S(1)}, f32[33,64,512]{2,1,0:T(8,128)}, u32[]{:S(2)}) %copy-start) | copy-done | bytes 4325400
  48.9 1.0 copy-done.2
  50.0 0.5 stage.1
  50.6 3.5 %slow.1.wt_slow = bf16[40,64,512]{2,1,0:T(8,128)(2,1)S(1)} custom-call(s32[1]{0:T(128)} %bitcast.core, s32[8,33]{1,0:T(8,128)S(1)} %broadcast_add_fusion.2.inv_slow, bf16[8,64,1728]{2,1,0:T(8,128)(2,1)S(1)} %collective-permute-done.3.p_slow, bf16[8,64,512]{2,1,0:T(8,128)(2,1)S(1)} %get-tuple-element.67.at_halo, f32[33,64,512]{2,1,0:T(8,128)S(1)} %get-tuple-element.68.rest), custom_call_target="tpu_custom_call" | custom-call | flops 20000000000 | bytes 200000000 | tf_op jit(solution)/shard_map/slow/pallas_call | solution.py:630
  54.1 0.3 collective-permute-start.7
  54.5 2.2 %far.1 = bf16[3,64,2304]{2,1,0:T(8,128)(2,1)S(1)} custom-call(s32[1]{0:T(128)} %bitcast.core, bf16[3,64,512]{2,1,0:T(8,128)(2,1)S(1)} %copy-done.3, bf16[40,64,512]{2,1,0:T(8,128)(2,1)S(1)} %slow.1.wt_slow, bf16[3,64,2432]{2,1,0:T(8,128)(2,1)S(1)} %copy-done.1), custom_call_target="tpu_custom_call" | custom-call | flops 1000000000 | bytes 10000000 | tf_op jit(solution)/shard_map/far/pallas_call | solution.py:648
  56.7 0.9 collective-permute-start.8
  57.6 3.0 %mine.1 = f32[6,64,2432]{2,1,0:T(8,128)S(1)} custom-call(bf16[6,64,512]{2,1,0:T(8,128)(2,1)S(1)} %copy-done.5, bf16[40,64,512]{2,1,0:T(8,128)(2,1)S(1)} %slow.1.wt_slow, bf16[6,64,2432]{2,1,0:T(8,128)(2,1)S(1)} %copy-done.4, bf16[3,64,2432]{2,1,0:T(8,128)(2,1)S(1)} %collective-permute-done.4.low, bf16[3,64,2432]{2,1,0:T(8,128)(2,1)S(1)} %collective-permute-done.5.high), custom_call_target="tpu_custom_call" | custom-call | flops 10000000000 | bytes 100000000 | tf_op jit(solution)/shard_map/mine/pallas_call | solution.py:658
  60.6 0.0 copy-start.10
  60.6 2.9 %join_first.1 = (bf16[3,64,2432]{2,1,0:T(8,128)(2,1)S(1)}, f32[3,64,2432]{2,1,0:T(8,128)S(1)}) custom-call(bf16[6,64,512]{2,1,0:T(8,128)(2,1)S(1)} %collective-permute-done.6.other, bf16[40,64,512]{2,1,0:T(8,128)(2,1)S(1)} %collective-permute-done.7.wt_other, f32[6,64,2432]{2,1,0:T(8,128)S(1)} %mine.1), custom_call_target="tpu_custom_call" | custom-call | flops 1000000 | bytes 100000 | tf_op jit(solution)/shard_map/join_first/pallas_call | solution.py:669
  63.6 7.7 %collective-permute-start.10 = (bf16[9,64,2432]{2,1,0:T(8,128)(2,1)S(1)}, bf16[9,64,2432]{2,1,0:T(8,128)(2,1)S(1)}, u32[]{:S(2)}, u32[]{:S(2)}) collective-permute-start(bf16[9,64,2432]{2,1,0:T(8,128)(2,1)S(1)} %copy-done.10), channel_id=1, source_target_pairs={{0,1},{1,0},{2,3},{3,2},{4,5},{5,4},{6,7},{7,6},{8,9},{9,8},{10,11... | collective-permute-start | bytes 8405000 | tf_op jit(solution)/shard_map/ppermute | solution.py:483
  71.3 0.1 collective-permute-start.9
  71.4 2.0 %collective-permute-start.12 = (bf16[3,64,2432]{2,1,0:T(8,128)(2,1)S(1)}, bf16[3,64,2432]{2,1,0:T(8,128)(2,1)S(1)}, u32[]{:S(2)}, u32[]{:S(2)}) collective-permute-start(bf16[3,64,2432]{2,1,0:T(8,128)(2,1)S(1)} %get-tuple-element.90), channel_id=1, source_target_pairs={{0,2},{1,3},{2,0},{3,1},{4,6},{5,7},{6,4},{7,5},{8,10},{9,11},{10,... | collective-permute-start | bytes 2801672 | tf_op jit(solution)/shard_map/ppermute | solution.py:483
  73.3 0.6 merge_far.1
  73.9 2.6 %collective-permute-start.11 = (bf16[3,64,2816]{2,1,0:T(8,128)(2,1)S(1)}, bf16[3,64,2816]{2,1,0:T(8,128)(2,1)S(1)}, u32[]{:S(2)}, u32[]{:S(2)}) collective-permute-start(bf16[3,64,2816]{2,1,0:T(8,128)(2,1)S(1)} %merge_far.1), channel_id=1, source_target_pairs={{0,28},{1,29},{2,6},{3,7},{4,0},{5,1},{6,10},{7,11},{8,4},{9,5},{1... | collective-permute-start | bytes 3244040 | tf_op jit(solution)/shard_map/ppermute | solution.py:483
  76.5 0.4 collective-permute-done.9.other
  77.0 8.1 %join_rest.1 = (f32[3,64,2432]{2,1,0:T(8,128)S(1)}, bf16[3,64,2432]{2,1,0:T(8,128)(2,1)S(1)}, f32[3,64,2432]{2,1,0:T(8,128)S(1)}) custom-call(bf16[9,64,1024]{2,1,0:T(8,128)(2,1)S(1)} %copy-done.6, bf16[9,64,512]{2,1,0:T(8,128)(2,1)S(1)} %copy-done.7, bf16[9,64,512]{2,1,0:T(8,128)(2,1)S(1)} %collective-permute-done.9.other, ...), custom_call_target="tpu_custom_call" | custom-call | flops 40000000000 | bytes 200000000 | tf_op jit(solution)/shard_map/join_rest/pallas_call | solution.py:701
  85.1 9.3 %collective-permute-done.12.other = bf16[3,64,2432]{2,1,0:T(8,128)(2,1)S(1)} collective-permute-done((bf16[3,64,2432]{2,1,0:T(8,128)(2,1)S(1)}, bf16[3,64,2432]{2,1,0:T(8,128)(2,1)S(1)}, u32[]{:S(2)}, u32[]{:S(2)}) %collective-permute-start.12) | collective-permute-done | bytes 933920 | tf_op jit(solution)/shard_map/ppermute | solution.py:483
  94.4 0.8 merge.1
  95.2 0.1 collective-permute-start.14
  95.3 4.1 %collective-permute-start.13 = (bf16[3,64,2432]{2,1,0:T(8,128)(2,1)S(1)}, bf16[3,64,2432]{2,1,0:T(8,128)(2,1)S(1)}, u32[]{:S(2)}, u32[]{:S(2)}) collective-permute-start(bf16[3,64,2432]{2,1,0:T(8,128)(2,1)S(1)} %get-tuple-element.92), channel_id=1, source_target_pairs={{0,2},{1,3},{2,0},{3,1},{4,6},{5,7},{6,4},{7,5},{8,10},{9,11},{10,... | collective-permute-start | bytes 2801672 | tf_op jit(solution)/shard_map/ppermute | solution.py:483
  99.4 2.1 %collective-permute-start.15 = (bf16[3,64,2304]{2,1,0:T(8,128)(2,1)S(1)}, bf16[3,64,2304]{2,1,0:T(8,128)(2,1)S(1)}, u32[]{:S(2)}, u32[]{:S(2)}) collective-permute-start(bf16[3,64,2304]{2,1,0:T(8,128)(2,1)S(1)} %far.1), channel_id=1, source_target_pairs={{0,27},{3,8},{4,31},{7,12},{8,3},{11,16},{12,7},{15,20},{16,11},{1... | collective-permute-start | bytes 2654216 | tf_op jit(solution)/shard_map/ppermute | solution.py:483
  101.5 26.5 %collective-permute-done.13.pair = bf16[3,64,2432]{2,1,0:T(8,128)(2,1)S(1)} collective-permute-done((bf16[3,64,2432]{2,1,0:T(8,128)(2,1)S(1)}, bf16[3,64,2432]{2,1,0:T(8,128)(2,1)S(1)}, u32[]{:S(2)}, u32[]{:S(2)}) %collective-permute-start.13) | collective-permute-done | bytes 933920 | tf_op jit(solution)/shard_map/ppermute | solution.py:483
  128.0 1.9 %early.1 = f32[3,64,4032]{2,1,0:T(8,128)S(1)} custom-call(s32[1]{0:T(128)} %bitcast.core, f32[3,64,2432]{2,1,0:T(8,128)S(1)} %get-tuple-element.87.own, bf16[3,64,2816]{2,1,0:T(8,128)(2,1)S(1)} %collective-permute-done.11.direct, bf16[3,64,2432]{2,1,0:T(8,128)(2,1)S(1)} %collective-permute-done.13.pair, bf16[3,64,2816]{2,1,0:T(8,128)(2,1)S(1)} %collective-permute-done.14.merged), custom_call_target="tpu_custom_call" | custom-call | flops 10000000000 | bytes 100000000 | tf_op jit(solution)/shard_map/early/pallas_call | solution.py:720
  129.9 2.0 %collective-permute-done.15.far = bf16[3,64,2304]{2,1,0:T(8,128)(2,1)S(1)} collective-permute-done((bf16[3,64,2304]{2,1,0:T(8,128)(2,1)S(1)}, bf16[3,64,2304]{2,1,0:T(8,128)(2,1)S(1)}, u32[]{:S(2)}, u32[]{:S(2)}) %collective-permute-start.15) | collective-permute-done | bytes 884768 | tf_op jit(solution)/shard_map/ppermute | solution.py:483
  131.9 2.7 %total.1 = f32[3,64,4032]{2,1,0:T(8,128)} custom-call(s32[1]{0:T(128)} %bitcast.core, f32[3,64,4032]{2,1,0:T(8,128)S(1)} %early.1, bf16[3,64,2304]{2,1,0:T(8,128)(2,1)S(1)} %collective-permute-done.15.far), custom_call_target="tpu_custom_call" | custom-call | flops 10000000 | bytes 10000000 | tf_op jit(solution)/shard_map/total/pallas_call | solution.py:730
  (47 shorter events, 0.2 us)
Async XLA Ops:
  0.0 3.1 %copy-start.8 = (s32[24,27]{1,0:T(8,128)S(1)}, s32[24,27]{1,0:T(8,128)}, u32[]{:S(2)}) copy-start(s32[24,27]{1,0:T(8,128)} %param.7) | copy-start | bytes 7780
  0.0 10.8 %copy-start.9 = (s32[24,7]{0,1:T(8,128)S(1)}, s32[24,7]{0,1:T(8,128)}, u32[]{:S(2)}) copy-start(s32[24,7]{0,1:T(8,128)} %param.6) | copy-start | bytes 2020
  3.2 8.4 %collective-permute-start.1 = (s32[8,27]{1,0:T(8,128)S(1)}, s32[8,27]{1,0:T(8,128)S(1)}, u32[]{:S(2)}, u32[]{:S(2)}) collective-permute-start(s32[8,27]{1,0:T(8,128)S(1)} %get-tuple-element.99), channel_id=1, source_target_pairs={{0,31},{1,2},{2,1},{3,4},{4,3},{5,6},{6,5},{7,8},{8,7},{9,10},{10,... | collective-permute-start | bytes 2600 | tf_op jit(solution)/shard_map/ppermute | solution.py:483
  9.6 2.1 %collective-permute-start = (s32[8,27]{1,0:T(8,128)S(1)}, s32[8,27]{1,0:T(8,128)S(1)}, u32[]{:S(2)}, u32[]{:S(2)}) collective-permute-start(s32[8,27]{1,0:T(8,128)S(1)} %get-tuple-element.100), channel_id=1, source_target_pairs={{0,1},{1,0},{2,3},{3,2},{4,5},{5,4},{6,7},{7,6},{8,9},{9,8},{10,11... | collective-permute-start | bytes 2600 | tf_op jit(solution)/shard_map/ppermute | solution.py:483
  9.6 4.3 %collective-permute-start.2 = (bf16[8,64,1728]{2,1,0:T(8,128)(2,1)}, bf16[8,64,1728]{2,1,0:T(8,128)(2,1)}, u32[]{:S(2)}, u32[]{:S(2)}) collective-permute-start(bf16[8,64,1728]{2,1,0:T(8,128)(2,1)} %get-tuple-element.55), channel_id=1, source_target_pairs={{0,1},{1,0},{2,3},{3,2},{4,5},{5,4},{6,7},{7,6},{8,9},{9,8},{10,11... | collective-permute-start | bytes 5308424 | tf_op jit(solution)/shard_map/ppermute | solution.py:483
  10.1 40.4 %collective-permute-start.3 = (bf16[8,64,1728]{2,1,0:T(8,128)(2,1)}, bf16[8,64,1728]{2,1,0:T(8,128)(2,1)S(1)}, u32[]{:S(2)}, u32[]{:S(2)}) collective-permute-start(bf16[8,64,1728]{2,1,0:T(8,128)(2,1)} %get-tuple-element.58), channel_id=1, source_target_pairs={{0,31},{1,2},{2,1},{3,4},{4,3},{5,6},{6,5},{7,8},{8,7},{9,10},{10,... | collective-permute-start | bytes 5308424 | tf_op jit(solution)/shard_map/ppermute | solution.py:483
  45.7 4.8 %collective-permute-start.4 = (bf16[3,64,2432]{2,1,0:T(8,128)(2,1)}, bf16[3,64,2432]{2,1,0:T(8,128)(2,1)S(1)}, u32[]{:S(2)}, u32[]{:S(2)}) collective-permute-start(bf16[3,64,2432]{2,1,0:T(8,128)(2,1)} %get-tuple-element.59), channel_id=1, source_target_pairs={{0,1},{1,0},{2,3},{3,2},{4,5},{5,4},{6,7},{7,6},{8,9},{9,8},{10,11... | collective-permute-start | bytes 2801672 | tf_op jit(solution)/shard_map/ppermute | solution.py:483
  46.2 4.3 %collective-permute-start.5 = (bf16[3,64,2432]{2,1,0:T(8,128)(2,1)}, bf16[3,64,2432]{2,1,0:T(8,128)(2,1)S(1)}, u32[]{:S(2)}, u32[]{:S(2)}) collective-permute-start(bf16[3,64,2432]{2,1,0:T(8,128)(2,1)} %get-tuple-element.60), channel_id=1, source_target_pairs={{0,1},{1,0},{2,3},{3,2},{4,5},{5,4},{6,7},{7,6},{8,9},{9,8},{10,11... | collective-permute-start | bytes 2801672 | tf_op jit(solution)/shard_map/ppermute | solution.py:483
  46.3 4.2 %collective-permute-start.6 = (bf16[6,64,512]{2,1,0:T(8,128)(2,1)}, bf16[6,64,512]{2,1,0:T(8,128)(2,1)S(1)}, u32[]{:S(2)}, u32[]{:S(2)}) collective-permute-start(bf16[6,64,512]{2,1,0:T(8,128)(2,1)} %get-tuple-element.61), channel_id=1, source_target_pairs={{0,1},{1,0},{2,3},{3,2},{4,5},{5,4},{6,7},{7,6},{8,9},{9,8},{10,11... | collective-permute-start | bytes 1179656 | tf_op jit(solution)/shard_map/ppermute | solution.py:483
  46.7 2.2 %copy-start = (f32[33,64,512]{2,1,0:T(8,128)S(1)}, f32[33,64,512]{2,1,0:T(8,128)}, u32[]{:S(2)}) copy-start(f32[33,64,512]{2,1,0:T(8,128)} %get-tuple-element.66.rest) | copy-start | bytes 12976132
  48.9 1.0 copy-start.2
  50.5 3.9 %copy-start.1 = (bf16[3,64,2432]{2,1,0:T(8,128)(2,1)S(1)}, bf16[3,64,2432]{2,1,0:T(8,128)(2,1)}, u32[]{:S(2)}) copy-start(bf16[3,64,2432]{2,1,0:T(8,128)(2,1)} %get-tuple-element.74.far_fast) | copy-start | bytes 2801668
  50.5 3.9 %copy-start.3 = (bf16[3,64,512]{2,1,0:T(8,128)(2,1)S(1)}, bf16[3,64,512]{2,1,0:T(8,128)(2,1)}, u32[]{:S(2)}) copy-start(bf16[3,64,512]{2,1,0:T(8,128)(2,1)} %get-tuple-element.70.slow) | copy-start | bytes 589828
  50.6 7.0 %copy-start.5 = (bf16[6,64,512]{2,1,0:T(8,128)(2,1)S(1)}, bf16[6,64,512]{2,1,0:T(8,128)(2,1)}, u32[]{:S(2)}) copy-start(bf16[6,64,512]{2,1,0:T(8,128)(2,1)} %get-tuple-element.69.slow) | copy-start | bytes 1179652
  54.1 6.5 %collective-permute-start.7 = (bf16[40,64,512]{2,1,0:T(8,128)(2,1)S(1)}, bf16[40,64,512]{2,1,0:T(8,128)(2,1)S(1)}, u32[]{:S(2)}, u32[]{:S(2)}) collective-permute-start(bf16[40,64,512]{2,1,0:T(8,128)(2,1)S(1)} %slow.1.wt_slow), channel_id=1, source_target_pairs={{0,1},{1,0},{2,3},{3,2},{4,5},{5,4},{6,7},{7,6},{8,9},{9,8},{10,11... | collective-permute-start | bytes 7864328 | tf_op jit(solution)/shard_map/ppermute | solution.py:483
  54.4 3.1 %copy-start.4 = (bf16[6,64,2432]{2,1,0:T(8,128)(2,1)S(1)}, bf16[6,64,2432]{2,1,0:T(8,128)(2,1)}, u32[]{:S(2)}) copy-start(bf16[6,64,2432]{2,1,0:T(8,128)(2,1)} %get-tuple-element.76.inner) | copy-start | bytes 5603332
  54.4 22.5 %slice-start = ((s8[5242880]{0:T(1024)(128)(4,1)}), s8[4194304]{0:T(1024)(128)(4,1)S(1)}, s32[]{:S(2)}) async-start(s8[5242880]{0:T(1024)(128)(4,1)} %bitcast.9), calls=%async_computation | async-start | bytes 8388608
  56.7 6.9 %collective-permute-start.8 = (bf16[3,64,2304]{2,1,0:T(8,128)(2,1)S(1)}, bf16[3,64,2304]{2,1,0:T(8,128)(2,1)S(1)}, u32[]{:S(2)}, u32[]{:S(2)}) collective-permute-start(bf16[3,64,2304]{2,1,0:T(8,128)(2,1)S(1)} %far.1), channel_id=1, source_target_pairs={{1,2},{2,1},{5,6},{6,5},{9,10},{10,9},{13,14},{14,13},{17,18},{18,... | collective-permute-start | bytes 2654216 | tf_op jit(solution)/shard_map/ppermute | solution.py:483
  57.6 19.3 %slice-start.1 = ((s8[5242880]{0:T(1024)(128)(4,1)}), s8[1048576]{0:T(1024)(128)(4,1)S(1)}, s32[]{:S(2)}) async-start(s8[5242880]{0:T(1024)(128)(4,1)} %bitcast.9), calls=%async_computation.1 | async-start | bytes 2097152
  60.6 3.0 %copy-start.10 = (bf16[9,64,2432]{2,1,0:T(8,128)(2,1)S(1)}, bf16[9,64,2432]{2,1,0:T(8,128)(2,1)}, u32[]{:S(2)}) copy-start(bf16[9,64,2432]{2,1,0:T(8,128)(2,1)} %get-tuple-element.86) | copy-start | bytes 8404996
  60.6 10.7 %copy-start.11 = (bf16[9,64,512]{2,1,0:T(8,128)(2,1)S(1)}, bf16[9,64,512]{2,1,0:T(8,128)(2,1)}, u32[]{:S(2)}) copy-start(bf16[9,64,512]{2,1,0:T(8,128)(2,1)} %get-tuple-element.84) | copy-start | bytes 1769476
  63.6 13.4 %copy-start.6 = (bf16[9,64,1024]{2,1,0:T(8,128)(2,1)S(1)}, bf16[9,64,1024]{2,1,0:T(8,128)(2,1)}, u32[]{:S(2)}) copy-start(bf16[9,64,1024]{2,1,0:T(8,128)(2,1)} %get-tuple-element.56.fast) | copy-start | bytes 3538948
  63.6 13.4 %copy-start.7 = (bf16[9,64,512]{2,1,0:T(8,128)(2,1)S(1)}, bf16[9,64,512]{2,1,0:T(8,128)(2,1)}, u32[]{:S(2)}) copy-start(bf16[9,64,512]{2,1,0:T(8,128)(2,1)} %get-tuple-element.57.slow) | copy-start | bytes 1769476
  63.6 13.3 %collective-permute-start.10 = (bf16[9,64,2432]{2,1,0:T(8,128)(2,1)S(1)}, bf16[9,64,2432]{2,1,0:T(8,128)(2,1)S(1)}, u32[]{:S(2)}, u32[]{:S(2)}) collective-permute-start(bf16[9,64,2432]{2,1,0:T(8,128)(2,1)S(1)} %copy-done.10), channel_id=1, source_target_pairs={{0,1},{1,0},{2,3},{3,2},{4,5},{5,4},{6,7},{7,6},{8,9},{9,8},{10,11... | collective-permute-start | bytes 8405000 | tf_op jit(solution)/shard_map/ppermute | solution.py:483
  71.3 5.6 %collective-permute-start.9 = (bf16[9,64,512]{2,1,0:T(8,128)(2,1)S(1)}, bf16[9,64,512]{2,1,0:T(8,128)(2,1)S(1)}, u32[]{:S(2)}, u32[]{:S(2)}) collective-permute-start(bf16[9,64,512]{2,1,0:T(8,128)(2,1)S(1)} %copy-done.11), channel_id=1, source_target_pairs={{0,1},{1,0},{2,3},{3,2},{4,5},{5,4},{6,7},{7,6},{8,9},{9,8},{10,11... | collective-permute-start | bytes 1769480 | tf_op jit(solution)/shard_map/ppermute | solution.py:483
  71.4 23.0 %collective-permute-start.12 = (bf16[3,64,2432]{2,1,0:T(8,128)(2,1)S(1)}, bf16[3,64,2432]{2,1,0:T(8,128)(2,1)S(1)}, u32[]{:S(2)}, u32[]{:S(2)}) collective-permute-start(bf16[3,64,2432]{2,1,0:T(8,128)(2,1)S(1)} %get-tuple-element.90), channel_id=1, source_target_pairs={{0,2},{1,3},{2,0},{3,1},{4,6},{5,7},{6,4},{7,5},{8,10},{9,11},{10,... | collective-permute-start | bytes 2801672 | tf_op jit(solution)/shard_map/ppermute | solution.py:483
  73.9 27.6 %collective-permute-start.11 = (bf16[3,64,2816]{2,1,0:T(8,128)(2,1)S(1)}, bf16[3,64,2816]{2,1,0:T(8,128)(2,1)S(1)}, u32[]{:S(2)}, u32[]{:S(2)}) collective-permute-start(bf16[3,64,2816]{2,1,0:T(8,128)(2,1)S(1)} %merge_far.1), channel_id=1, source_target_pairs={{0,28},{1,29},{2,6},{3,7},{4,0},{5,1},{6,10},{7,11},{8,4},{9,5},{1... | collective-permute-start | bytes 3244040 | tf_op jit(solution)/shard_map/ppermute | solution.py:483
  95.2 32.8 %collective-permute-start.14 = (bf16[3,64,2816]{2,1,0:T(8,128)(2,1)S(1)}, bf16[3,64,2816]{2,1,0:T(8,128)(2,1)S(1)}, u32[]{:S(2)}, u32[]{:S(2)}) collective-permute-start(bf16[3,64,2816]{2,1,0:T(8,128)(2,1)S(1)} %merge.1), channel_id=1, source_target_pairs={{0,4},{1,5},{2,30},{3,31},{4,8},{5,9},{6,2},{7,3},{8,12},{9,13},{1... | collective-permute-start | bytes 3244040 | tf_op jit(solution)/shard_map/ppermute | solution.py:483
  95.3 32.7 %collective-permute-start.13 = (bf16[3,64,2432]{2,1,0:T(8,128)(2,1)S(1)}, bf16[3,64,2432]{2,1,0:T(8,128)(2,1)S(1)}, u32[]{:S(2)}, u32[]{:S(2)}) collective-permute-start(bf16[3,64,2432]{2,1,0:T(8,128)(2,1)S(1)} %get-tuple-element.92), channel_id=1, source_target_pairs={{0,2},{1,3},{2,0},{3,1},{4,6},{5,7},{6,4},{7,5},{8,10},{9,11},{10,... | collective-permute-start | bytes 2801672 | tf_op jit(solution)/shard_map/ppermute | solution.py:483
  99.4 32.5 %collective-permute-start.15 = (bf16[3,64,2304]{2,1,0:T(8,128)(2,1)S(1)}, bf16[3,64,2304]{2,1,0:T(8,128)(2,1)S(1)}, u32[]{:S(2)}, u32[]{:S(2)}) collective-permute-start(bf16[3,64,2304]{2,1,0:T(8,128)(2,1)S(1)} %far.1), channel_id=1, source_target_pairs={{0,27},{3,8},{4,31},{7,12},{8,3},{11,16},{12,7},{15,20},{16,11},{1... | collective-permute-start | bytes 2654216 | tf_op jit(solution)/shard_map/ppermute | solution.py:483

commit v16 on v13

--- a/solution.py
+++ b/solution.py
@@ -428,11 +428,12 @@
         store(frame[:, first - BS : last - BS])
 
 
-def early_kernel(core, own, direct, pair, out, frame):
+def early_kernel(core, own, direct, far, out, frame):
     s, x = places(core)
     for j in range(NC):
         top = 27 - 3 * s - j
-        messages = [(own, top - 12), (direct, top - 30 * x), (pair, top - 6 - 12 * x)]
+        messages = [(own, top - 12), (direct, top - 30 * x)]
+        messages.append((far, jnp.where(s == 1, 30 - j, -1 - j)))
 
         def store(value, j=j):
             out[j] = value
@@ -440,16 +441,17 @@
         in_frame(s, j, frame, messages, store)
 
 
-def total_kernel(core, early, merged, far, out, frame, buf, sems):
+def total_kernel(core, early, pair, merged, out, frame, buf, sems):
     s, x = places(core)
     copies = []
     for j in range(NC):
-        far_start = jnp.where(s == 1, 30 - j, -1 - j)
+        top = 27 - 3 * s - j
 
         def store(value, j=j):
             buf[j] = value + early[j]
 
-        in_frame(s, j, frame, [(merged, 3 - 3 * s - j + 18 * x), (far, far_start)], store)
+        messages = [(pair, top - 6 - 12 * x), (merged, top - 24 + 18 * x)]
+        in_frame(s, j, frame, messages, store)
         copy = pltpu.make_async_copy(buf.at[j], out.at[j], sems.at[j])
         copy.start()
         copies.append(copy)
@@ -706,11 +708,11 @@
         cost_estimate=cost(40 * 10**9, 200 * 10**6),
         name="join_rest",
     )(fast_rest, slow_rest, other_rest, wt_fast, wt_slow, wt_other, arrived_rest)
+    pair, far = lax.optimization_barrier((pair, far))
     relay, pair = lax.optimization_barrier((relay, pair))
     merged = merge_rows(merge, relay, 0, "merge")
     merged = permuted(merged, [(i, (i - 4 * x_sign[i]) % devices) for i in range(devices)])
     pair = permuted(pair, along_x)
-    pair, far = lax.optimization_barrier((pair, far))
     straight = [i for i in range(devices) if i % 4 in (0, 3)]
     far = permuted(far, [(i, (i + (5 if i % 2 else -5)) % devices) for i in straight])
 
@@ -725,7 +727,7 @@
         compiler_params=params(16),
         cost_estimate=cost(10**10, 100 * 10**6),
         name="early",
-    )(core, own, direct, pair)
+    )(core, own, direct, far)
     return pl.pallas_call(
         total_kernel,
         out_shape=total,
@@ -739,7 +741,7 @@
         compiler_params=params(20),
         cost_estimate=cost(10**7, 10**7),
         name="total",
-    )(core, early, merged, far)
+    )(core, early, pair, merged)
 
 
 def solution(mesh):

time: 137 us -> 136 us (level)
  waiting for transfers between devices: 44.2 us -> 38.3 us
  starting transfers between devices: 25.4 us -> 30.5 us
    ppermute x16, waiting for transfers between devices: 44.2 us -> 38.3 us  [permuted(): return lax.ppermute(block, 'dom', pairs)]
    ppermute x16, starting transfers between devices: 25.4 us -> 30.5 us  [permuted(): return lax.ppermute(block, 'dom', pairs)]
where the time goes in v16:
time: 136 us
  Pallas kernels  61.2 us (45%)
  waiting for transfers between devices  38.3 us (28%)
  starting transfers between devices  30.5 us (22%)
  local copies, waits for them, and re-layouts  3.59 us (3%)
  other arithmetic  1.91 us (1%)
    ppermute x16, waiting for transfers between devices, permuted(): return lax.ppermute(block, 'dom', pairs)  38.3 us
    pallas_call x1, Pallas kernels, body(): pl.pallas_call(fast_kernel, out_shape=outs, in_specs=[smem] * 3 + [hbm, h...  31.9 us
    ppermute x16, starting transfers between devices, permuted(): return lax.ppermute(block, 'dom', pairs)  30.5 us
    pallas_call x1, Pallas kernels, body(): pl.pallas_call(join_rest_kernel, out_shape=[block(NC, span, jnp.float32),...  8.11 us
    pallas_call x1, Pallas kernels, body(): pl.pallas_call(slow_kernel, out_shape=block(WCOLS, AW), in_specs=[smem] *...  3.55 us
    unnamed x28, local copies, waits for them, and re-layouts  3.32 us
    pallas_call x1, Pallas kernels, body(): pl.pallas_call(pick_kernel, out_shape=[edge, edge], in_specs=[smem, hbm],...  3.08 us
    pallas_call x1, Pallas kernels, body(): pl.pallas_call(mine_kernel, out_shape=block(FIRST, span, jnp.float32), in...  2.98 us
  transfers between devices with their start and end apart: 16, of which 6 were waited for; matrix products, arithmetic and copies ran while one was open for 2% of the time, Pallas kernels for 38%

profile of v16, /device:TPU:0, one launch (start us, length us, event | category | flops | bytes accessed | tf_op | source)
XLA Modules:
  0.0 136.0 jit_solution(4864322180768235574)
XLA Ops:
  0.0 3.1 %pick.1 = (bf16[8,64,1728]{2,1,0:T(8,128)(2,1)}, bf16[8,64,1728]{2,1,0:T(8,128)(2,1)}) custom-call(s32[1]{0:T(128)} %bitcast.core, bf16[24,64,1728]{2,1,0:T(8,128)(2,1)} %p_own.1), custom_call_target="tpu_custom_call" | custom-call | tf_op jit(solution)/shard_map/pick/pallas_call | solution.py:518
  3.2 6.4 %collective-permute-start.1 = (s32[8,27]{1,0:T(8,128)S(1)}, s32[8,27]{1,0:T(8,128)S(1)}, u32[]{:S(2)}, u32[]{:S(2)}) collective-permute-start(s32[8,27]{1,0:T(8,128)S(1)} %get-tuple-element.99), channel_id=1, source_target_pairs={{0,31},{1,2},{2,1},{3,4},{4,3},{5,6},{6,5},{7,8},{8,7},{9,10},{10,... | collective-permute-start | bytes 2600 | tf_op jit(solution)/shard_map/ppermute | solution.py:484
  9.6 0.0 collective-permute-start
  9.6 0.5 collective-permute-start.2
  10.1 0.3 collective-permute-start.3
  10.4 0.1 fusion.1
  10.5 0.1 copy.15
  10.6 0.2 select_reduce_fusion
  10.8 0.1 select_reduce_fusion.3
  10.9 0.6 broadcast_add_fusion.inv_a
  11.6 0.0 collective-permute-done.1
  11.6 0.1 copy.17
  11.7 0.1 copy.16
  11.8 0.1 select_reduce_fusion.1
  11.9 0.1 select_reduce_fusion.2
  12.1 0.6 pad_add_fusion.inv_p
  12.7 1.2 collective-permute-done.2.p_fast
  13.9 31.9 %fast.1 = (bf16[3,64,2432]{2,1,0:T(8,128)(2,1)}, bf16[3,64,2432]{2,1,0:T(8,128)(2,1)}, bf16[3,64,2432]{2,1,0:T(8,128)(2,1)}, bf16[6,64,2432]{2,1,0:T(8,128)(2,1)...) custom-call(s32[1]{0:T(128)} %bitcast.core, ...), custom_call_target="tpu_custom_call" | custom-call | flops 20000000000 | bytes 30000000 | tf_op jit(solution)/shard_map/fast/pallas_call | solution.py:587
  45.7 0.5 collective-permute-start.4
  46.2 0.1 collective-permute-start.5
  46.3 0.4 collective-permute-start.6
  46.7 2.2 %copy-done = f32[33,64,512]{2,1,0:T(8,128)S(1)} copy-done((f32[33,64,512]{2,1,0:T(8,128)S(1)}, f32[33,64,512]{2,1,0:T(8,128)}, u32[]{:S(2)}) %copy-start) | copy-done | bytes 4325400
  48.9 1.0 copy-done.2
  50.0 0.5 stage.1
  50.6 3.5 %slow.1.wt_slow = bf16[40,64,512]{2,1,0:T(8,128)(2,1)S(1)} custom-call(s32[1]{0:T(128)} %bitcast.core, s32[8,33]{1,0:T(8,128)S(1)} %broadcast_add_fusion.2.inv_slow, bf16[8,64,1728]{2,1,0:T(8,128)(2,1)S(1)} %collective-permute-done.3.p_slow, bf16[8,64,512]{2,1,0:T(8,128)(2,1)S(1)} %get-tuple-element.67.at_halo, f32[33,64,512]{2,1,0:T(8,128)S(1)} %get-tuple-element.68.rest), custom_call_target="tpu_custom_call" | custom-call | flops 20000000000 | bytes 200000000 | tf_op jit(solution)/shard_map/slow/pallas_call | solution.py:631
  54.1 0.3 collective-permute-start.7
  54.5 2.2 %far.1 = bf16[3,64,2304]{2,1,0:T(8,128)(2,1)S(1)} custom-call(s32[1]{0:T(128)} %bitcast.core, bf16[3,64,512]{2,1,0:T(8,128)(2,1)S(1)} %copy-done.3, bf16[40,64,512]{2,1,0:T(8,128)(2,1)S(1)} %slow.1.wt_slow, bf16[3,64,2432]{2,1,0:T(8,128)(2,1)S(1)} %copy-done.1), custom_call_target="tpu_custom_call" | custom-call | flops 1000000000 | bytes 10000000 | tf_op jit(solution)/shard_map/far/pallas_call | solution.py:649
  56.7 0.9 collective-permute-start.8
  57.6 3.0 %mine.1 = f32[6,64,2432]{2,1,0:T(8,128)S(1)} custom-call(bf16[6,64,512]{2,1,0:T(8,128)(2,1)S(1)} %copy-done.5, bf16[40,64,512]{2,1,0:T(8,128)(2,1)S(1)} %slow.1.wt_slow, bf16[6,64,2432]{2,1,0:T(8,128)(2,1)S(1)} %copy-done.4, bf16[3,64,2432]{2,1,0:T(8,128)(2,1)S(1)} %collective-permute-done.4.low, bf16[3,64,2432]{2,1,0:T(8,128)(2,1)S(1)} %collective-permute-done.5.high), custom_call_target="tpu_custom_call" | custom-call | flops 10000000000 | bytes 100000000 | tf_op jit(solution)/shard_map/mine/pallas_call | solution.py:659
  60.6 0.0 copy-start.10
  60.6 2.9 %join_first.1 = (bf16[3,64,2432]{2,1,0:T(8,128)(2,1)S(1)}, f32[3,64,2432]{2,1,0:T(8,128)S(1)}) custom-call(bf16[6,64,512]{2,1,0:T(8,128)(2,1)S(1)} %collective-permute-done.6.other, bf16[40,64,512]{2,1,0:T(8,128)(2,1)S(1)} %collective-permute-done.7.wt_other, f32[6,64,2432]{2,1,0:T(8,128)S(1)} %mine.1), custom_call_target="tpu_custom_call" | custom-call | flops 1000000 | bytes 100000 | tf_op jit(solution)/shard_map/join_first/pallas_call | solution.py:670
  63.6 7.7 %collective-permute-start.10 = (bf16[9,64,2432]{2,1,0:T(8,128)(2,1)S(1)}, bf16[9,64,2432]{2,1,0:T(8,128)(2,1)S(1)}, u32[]{:S(2)}, u32[]{:S(2)}) collective-permute-start(bf16[9,64,2432]{2,1,0:T(8,128)(2,1)S(1)} %copy-done.10), channel_id=1, source_target_pairs={{0,1},{1,0},{2,3},{3,2},{4,5},{5,4},{6,7},{7,6},{8,9},{9,8},{10,11... | collective-permute-start | bytes 8405000 | tf_op jit(solution)/shard_map/ppermute | solution.py:484
  71.3 0.1 collective-permute-start.9
  71.4 1.9 %collective-permute-start.13 = (bf16[3,64,2432]{2,1,0:T(8,128)(2,1)S(1)}, bf16[3,64,2432]{2,1,0:T(8,128)(2,1)S(1)}, u32[]{:S(2)}, u32[]{:S(2)}) collective-permute-start(bf16[3,64,2432]{2,1,0:T(8,128)(2,1)S(1)} %get-tuple-element.92), channel_id=1, source_target_pairs={{0,2},{1,3},{2,0},{3,1},{4,6},{5,7},{6,4},{7,5},{8,10},{9,11},{10,... | collective-permute-start | bytes 2801672 | tf_op jit(solution)/shard_map/ppermute | solution.py:484
  73.3 0.6 merge_far.1
  73.9 2.6 %collective-permute-start.11 = (bf16[3,64,2816]{2,1,0:T(8,128)(2,1)S(1)}, bf16[3,64,2816]{2,1,0:T(8,128)(2,1)S(1)}, u32[]{:S(2)}, u32[]{:S(2)}) collective-permute-start(bf16[3,64,2816]{2,1,0:T(8,128)(2,1)S(1)} %merge_far.1), channel_id=1, source_target_pairs={{0,28},{1,29},{2,6},{3,7},{4,0},{5,1},{6,10},{7,11},{8,4},{9,5},{1... | collective-permute-start | bytes 3244040 | tf_op jit(solution)/shard_map/ppermute | solution.py:484
  76.6 0.4 collective-permute-done.9.other
  77.0 8.1 %join_rest.1 = (f32[3,64,2432]{2,1,0:T(8,128)S(1)}, bf16[3,64,2432]{2,1,0:T(8,128)(2,1)S(1)}, f32[3,64,2432]{2,1,0:T(8,128)S(1)}) custom-call(bf16[9,64,1024]{2,1,0:T(8,128)(2,1)S(1)} %copy-done.6, bf16[9,64,512]{2,1,0:T(8,128)(2,1)S(1)} %copy-done.7, bf16[9,64,512]{2,1,0:T(8,128)(2,1)S(1)} %collective-permute-done.9.other, ...), custom_call_target="tpu_custom_call" | custom-call | flops 40000000000 | bytes 200000000 | tf_op jit(solution)/shard_map/join_rest/pallas_call | solution.py:702
  85.1 4.4 %collective-permute-start.12 = (bf16[3,64,2304]{2,1,0:T(8,128)(2,1)S(1)}, bf16[3,64,2304]{2,1,0:T(8,128)(2,1)S(1)}, u32[]{:S(2)}, u32[]{:S(2)}) collective-permute-start(bf16[3,64,2304]{2,1,0:T(8,128)(2,1)S(1)} %far.1), channel_id=1, source_target_pairs={{0,27},{3,8},{4,31},{7,12},{8,3},{11,16},{12,7},{15,20},{16,11},{1... | collective-permute-start | bytes 2654216 | tf_op jit(solution)/shard_map/ppermute | solution.py:484
  89.5 14.4 %collective-permute-done.13.other = bf16[3,64,2432]{2,1,0:T(8,128)(2,1)S(1)} collective-permute-done((bf16[3,64,2432]{2,1,0:T(8,128)(2,1)S(1)}, bf16[3,64,2432]{2,1,0:T(8,128)(2,1)S(1)}, u32[]{:S(2)}, u32[]{:S(2)}) %collective-permute-start.13) | collective-permute-done | bytes 933920 | tf_op jit(solution)/shard_map/ppermute | solution.py:484
  103.9 0.8 merge.1
  104.7 0.1 collective-permute-start.15
  104.8 4.2 %collective-permute-start.14 = (bf16[3,64,2432]{2,1,0:T(8,128)(2,1)S(1)}, bf16[3,64,2432]{2,1,0:T(8,128)(2,1)S(1)}, u32[]{:S(2)}, u32[]{:S(2)}) collective-permute-start(bf16[3,64,2432]{2,1,0:T(8,128)(2,1)S(1)} %get-tuple-element.94), channel_id=1, source_target_pairs={{0,2},{1,3},{2,0},{3,1},{4,6},{5,7},{6,4},{7,5},{8,10},{9,11},{10,... | collective-permute-start | bytes 2801672 | tf_op jit(solution)/shard_map/ppermute | solution.py:484
  108.9 0.2 collective-permute-done.12.far
  109.1 1.6 %early.1 = f32[3,64,4032]{2,1,0:T(8,128)S(1)} custom-call(s32[1]{0:T(128)} %bitcast.core, f32[3,64,2432]{2,1,0:T(8,128)S(1)} %get-tuple-element.87.own, bf16[3,64,2816]{2,1,0:T(8,128)(2,1)S(1)} %collective-permute-done.11.direct, bf16[3,64,2304]{2,1,0:T(8,128)(2,1)S(1)} %collective-permute-done.12.far), custom_call_target="tpu_custom_call" | custom-call | flops 10000000000 | bytes 100000000 | tf_op jit(solution)/shard_map/early/pallas_call | solution.py:721
  110.7 18.0 %collective-permute-done.14.pair = bf16[3,64,2432]{2,1,0:T(8,128)(2,1)S(1)} collective-permute-done((bf16[3,64,2432]{2,1,0:T(8,128)(2,1)S(1)}, bf16[3,64,2432]{2,1,0:T(8,128)(2,1)S(1)}, u32[]{:S(2)}, u32[]{:S(2)}) %collective-permute-start.14) | collective-permute-done | bytes 933920 | tf_op jit(solution)/shard_map/ppermute | solution.py:484
  128.7 4.1 %collective-permute-done.15.merged = bf16[3,64,2816]{2,1,0:T(8,128)(2,1)S(1)} collective-permute-done((bf16[3,64,2816]{2,1,0:T(8,128)(2,1)S(1)}, bf16[3,64,2816]{2,1,0:T(8,128)(2,1)S(1)}, u32[]{:S(2)}, u32[]{:S(2)}) %collective-permute-start.15) | collective-permute-done | bytes 1081376 | tf_op jit(solution)/shard_map/ppermute | solution.py:484
  132.9 3.0 %total.1 = f32[3,64,4032]{2,1,0:T(8,128)} custom-call(s32[1]{0:T(128)} %bitcast.core, f32[3,64,4032]{2,1,0:T(8,128)S(1)} %early.1, bf16[3,64,2432]{2,1,0:T(8,128)(2,1)S(1)} %collective-permute-done.14.pair, bf16[3,64,2816]{2,1,0:T(8,128)(2,1)S(1)} %collective-permute-done.15.merged), custom_call_target="tpu_custom_call" | custom-call | flops 10000000 | bytes 10000000 | tf_op jit(solution)/shard_map/total/pallas_call | solution.py:731
  (47 shorter events, 0.2 us)
Async XLA Ops:
  0.0 3.1 %copy-start.8 = (s32[24,27]{1,0:T(8,128)S(1)}, s32[24,27]{1,0:T(8,128)}, u32[]{:S(2)}) copy-start(s32[24,27]{1,0:T(8,128)} %param.7) | copy-start | bytes 7780
  0.0 10.8 %copy-start.9 = (s32[24,7]{0,1:T(8,128)S(1)}, s32[24,7]{0,1:T(8,128)}, u32[]{:S(2)}) copy-start(s32[24,7]{0,1:T(8,128)} %param.6) | copy-start | bytes 2020
  3.2 8.4 %collective-permute-start.1 = (s32[8,27]{1,0:T(8,128)S(1)}, s32[8,27]{1,0:T(8,128)S(1)}, u32[]{:S(2)}, u32[]{:S(2)}) collective-permute-start(s32[8,27]{1,0:T(8,128)S(1)} %get-tuple-element.99), channel_id=1, source_target_pairs={{0,31},{1,2},{2,1},{3,4},{4,3},{5,6},{6,5},{7,8},{8,7},{9,10},{10,... | collective-permute-start | bytes 2600 | tf_op jit(solution)/shard_map/ppermute | solution.py:484
  9.6 2.1 %collective-permute-start = (s32[8,27]{1,0:T(8,128)S(1)}, s32[8,27]{1,0:T(8,128)S(1)}, u32[]{:S(2)}, u32[]{:S(2)}) collective-permute-start(s32[8,27]{1,0:T(8,128)S(1)} %get-tuple-element.100), channel_id=1, source_target_pairs={{0,1},{1,0},{2,3},{3,2},{4,5},{5,4},{6,7},{7,6},{8,9},{9,8},{10,11... | collective-permute-start | bytes 2600 | tf_op jit(solution)/shard_map/ppermute | solution.py:484
  9.6 4.3 %collective-permute-start.2 = (bf16[8,64,1728]{2,1,0:T(8,128)(2,1)}, bf16[8,64,1728]{2,1,0:T(8,128)(2,1)}, u32[]{:S(2)}, u32[]{:S(2)}) collective-permute-start(bf16[8,64,1728]{2,1,0:T(8,128)(2,1)} %get-tuple-element.55), channel_id=1, source_target_pairs={{0,1},{1,0},{2,3},{3,2},{4,5},{5,4},{6,7},{7,6},{8,9},{9,8},{10,11... | collective-permute-start | bytes 5308424 | tf_op jit(solution)/shard_map/ppermute | solution.py:484
  10.1 40.4 %collective-permute-start.3 = (bf16[8,64,1728]{2,1,0:T(8,128)(2,1)}, bf16[8,64,1728]{2,1,0:T(8,128)(2,1)S(1)}, u32[]{:S(2)}, u32[]{:S(2)}) collective-permute-start(bf16[8,64,1728]{2,1,0:T(8,128)(2,1)} %get-tuple-element.58), channel_id=1, source_target_pairs={{0,31},{1,2},{2,1},{3,4},{4,3},{5,6},{6,5},{7,8},{8,7},{9,10},{10,... | collective-permute-start | bytes 5308424 | tf_op jit(solution)/shard_map/ppermute | solution.py:484
  45.7 4.8 %collective-permute-start.4 = (bf16[3,64,2432]{2,1,0:T(8,128)(2,1)}, bf16[3,64,2432]{2,1,0:T(8,128)(2,1)S(1)}, u32[]{:S(2)}, u32[]{:S(2)}) collective-permute-start(bf16[3,64,2432]{2,1,0:T(8,128)(2,1)} %get-tuple-element.59), channel_id=1, source_target_pairs={{0,1},{1,0},{2,3},{3,2},{4,5},{5,4},{6,7},{7,6},{8,9},{9,8},{10,11... | collective-permute-start | bytes 2801672 | tf_op jit(solution)/shard_map/ppermute | solution.py:484
  46.2 4.3 %collective-permute-start.5 = (bf16[3,64,2432]{2,1,0:T(8,128)(2,1)}, bf16[3,64,2432]{2,1,0:T(8,128)(2,1)S(1)}, u32[]{:S(2)}, u32[]{:S(2)}) collective-permute-start(bf16[3,64,2432]{2,1,0:T(8,128)(2,1)} %get-tuple-element.60), channel_id=1, source_target_pairs={{0,1},{1,0},{2,3},{3,2},{4,5},{5,4},{6,7},{7,6},{8,9},{9,8},{10,11... | collective-permute-start | bytes 2801672 | tf_op jit(solution)/shard_map/ppermute | solution.py:484
  46.3 4.2 %collective-permute-start.6 = (bf16[6,64,512]{2,1,0:T(8,128)(2,1)}, bf16[6,64,512]{2,1,0:T(8,128)(2,1)S(1)}, u32[]{:S(2)}, u32[]{:S(2)}) collective-permute-start(bf16[6,64,512]{2,1,0:T(8,128)(2,1)} %get-tuple-element.61), channel_id=1, source_target_pairs={{0,1},{1,0},{2,3},{3,2},{4,5},{5,4},{6,7},{7,6},{8,9},{9,8},{10,11... | collective-permute-start | bytes 1179656 | tf_op jit(solution)/shard_map/ppermute | solution.py:484
  46.7 2.2 %copy-start = (f32[33,64,512]{2,1,0:T(8,128)S(1)}, f32[33,64,512]{2,1,0:T(8,128)}, u32[]{:S(2)}) copy-start(f32[33,64,512]{2,1,0:T(8,128)} %get-tuple-element.66.rest) | copy-start | bytes 12976132
  48.9 1.0 copy-start.2
  50.5 3.9 %copy-start.1 = (bf16[3,64,2432]{2,1,0:T(8,128)(2,1)S(1)}, bf16[3,64,2432]{2,1,0:T(8,128)(2,1)}, u32[]{:S(2)}) copy-start(bf16[3,64,2432]{2,1,0:T(8,128)(2,1)} %get-tuple-element.74.far_fast) | copy-start | bytes 2801668
  50.5 3.9 %copy-start.3 = (bf16[3,64,512]{2,1,0:T(8,128)(2,1)S(1)}, bf16[3,64,512]{2,1,0:T(8,128)(2,1)}, u32[]{:S(2)}) copy-start(bf16[3,64,512]{2,1,0:T(8,128)(2,1)} %get-tuple-element.70.slow) | copy-start | bytes 589828
  50.6 7.0 %copy-start.5 = (bf16[6,64,512]{2,1,0:T(8,128)(2,1)S(1)}, bf16[6,64,512]{2,1,0:T(8,128)(2,1)}, u32[]{:S(2)}) copy-start(bf16[6,64,512]{2,1,0:T(8,128)(2,1)} %get-tuple-element.69.slow) | copy-start | bytes 1179652
  54.1 6.5 %collective-permute-start.7 = (bf16[40,64,512]{2,1,0:T(8,128)(2,1)S(1)}, bf16[40,64,512]{2,1,0:T(8,128)(2,1)S(1)}, u32[]{:S(2)}, u32[]{:S(2)}) collective-permute-start(bf16[40,64,512]{2,1,0:T(8,128)(2,1)S(1)} %slow.1.wt_slow), channel_id=1, source_target_pairs={{0,1},{1,0},{2,3},{3,2},{4,5},{5,4},{6,7},{7,6},{8,9},{9,8},{10,11... | collective-permute-start | bytes 7864328 | tf_op jit(solution)/shard_map/ppermute | solution.py:484
  54.5 3.1 %copy-start.4 = (bf16[6,64,2432]{2,1,0:T(8,128)(2,1)S(1)}, bf16[6,64,2432]{2,1,0:T(8,128)(2,1)}, u32[]{:S(2)}) copy-start(bf16[6,64,2432]{2,1,0:T(8,128)(2,1)} %get-tuple-element.76.inner) | copy-start | bytes 5603332
  54.5 22.5 %slice-start = ((s8[5242880]{0:T(1024)(128)(4,1)}), s8[4194304]{0:T(1024)(128)(4,1)S(1)}, s32[]{:S(2)}) async-start(s8[5242880]{0:T(1024)(128)(4,1)} %bitcast.9), calls=%async_computation | async-start | bytes 8388608
  56.7 6.9 %collective-permute-start.8 = (bf16[3,64,2304]{2,1,0:T(8,128)(2,1)S(1)}, bf16[3,64,2304]{2,1,0:T(8,128)(2,1)S(1)}, u32[]{:S(2)}, u32[]{:S(2)}) collective-permute-start(bf16[3,64,2304]{2,1,0:T(8,128)(2,1)S(1)} %far.1), channel_id=1, source_target_pairs={{1,2},{2,1},{5,6},{6,5},{9,10},{10,9},{13,14},{14,13},{17,18},{18,... | collective-permute-start | bytes 2654216 | tf_op jit(solution)/shard_map/ppermute | solution.py:484
  57.6 19.3 %slice-start.1 = ((s8[5242880]{0:T(1024)(128)(4,1)}), s8[1048576]{0:T(1024)(128)(4,1)S(1)}, s32[]{:S(2)}) async-start(s8[5242880]{0:T(1024)(128)(4,1)} %bitcast.9), calls=%async_computation.1 | async-start | bytes 2097152
  60.6 3.0 %copy-start.10 = (bf16[9,64,2432]{2,1,0:T(8,128)(2,1)S(1)}, bf16[9,64,2432]{2,1,0:T(8,128)(2,1)}, u32[]{:S(2)}) copy-start(bf16[9,64,2432]{2,1,0:T(8,128)(2,1)} %get-tuple-element.86) | copy-start | bytes 8404996
  60.6 10.7 %copy-start.11 = (bf16[9,64,512]{2,1,0:T(8,128)(2,1)S(1)}, bf16[9,64,512]{2,1,0:T(8,128)(2,1)}, u32[]{:S(2)}) copy-start(bf16[9,64,512]{2,1,0:T(8,128)(2,1)} %get-tuple-element.84) | copy-start | bytes 1769476
  63.6 13.4 %copy-start.6 = (bf16[9,64,1024]{2,1,0:T(8,128)(2,1)S(1)}, bf16[9,64,1024]{2,1,0:T(8,128)(2,1)}, u32[]{:S(2)}) copy-start(bf16[9,64,1024]{2,1,0:T(8,128)(2,1)} %get-tuple-element.56.fast) | copy-start | bytes 3538948
  63.6 13.4 %copy-start.7 = (bf16[9,64,512]{2,1,0:T(8,128)(2,1)S(1)}, bf16[9,64,512]{2,1,0:T(8,128)(2,1)}, u32[]{:S(2)}) copy-start(bf16[9,64,512]{2,1,0:T(8,128)(2,1)} %get-tuple-element.57.slow) | copy-start | bytes 1769476
  63.6 13.3 %collective-permute-start.10 = (bf16[9,64,2432]{2,1,0:T(8,128)(2,1)S(1)}, bf16[9,64,2432]{2,1,0:T(8,128)(2,1)S(1)}, u32[]{:S(2)}, u32[]{:S(2)}) collective-permute-start(bf16[9,64,2432]{2,1,0:T(8,128)(2,1)S(1)} %copy-done.10), channel_id=1, source_target_pairs={{0,1},{1,0},{2,3},{3,2},{4,5},{5,4},{6,7},{7,6},{8,9},{9,8},{10,11... | collective-permute-start | bytes 8405000 | tf_op jit(solution)/shard_map/ppermute | solution.py:484
  71.3 5.6 %collective-permute-start.9 = (bf16[9,64,512]{2,1,0:T(8,128)(2,1)S(1)}, bf16[9,64,512]{2,1,0:T(8,128)(2,1)S(1)}, u32[]{:S(2)}, u32[]{:S(2)}) collective-permute-start(bf16[9,64,512]{2,1,0:T(8,128)(2,1)S(1)} %copy-done.11), channel_id=1, source_target_pairs={{0,1},{1,0},{2,3},{3,2},{4,5},{5,4},{6,7},{7,6},{8,9},{9,8},{10,11... | collective-permute-start | bytes 1769480 | tf_op jit(solution)/shard_map/ppermute | solution.py:484
  71.4 32.5 %collective-permute-start.13 = (bf16[3,64,2432]{2,1,0:T(8,128)(2,1)S(1)}, bf16[3,64,2432]{2,1,0:T(8,128)(2,1)S(1)}, u32[]{:S(2)}, u32[]{:S(2)}) collective-permute-start(bf16[3,64,2432]{2,1,0:T(8,128)(2,1)S(1)} %get-tuple-element.92), channel_id=1, source_target_pairs={{0,2},{1,3},{2,0},{3,1},{4,6},{5,7},{6,4},{7,5},{8,10},{9,11},{10,... | collective-permute-start | bytes 2801672 | tf_op jit(solution)/shard_map/ppermute | solution.py:484
  73.9 35.0 %collective-permute-start.11 = (bf16[3,64,2816]{2,1,0:T(8,128)(2,1)S(1)}, bf16[3,64,2816]{2,1,0:T(8,128)(2,1)S(1)}, u32[]{:S(2)}, u32[]{:S(2)}) collective-permute-start(bf16[3,64,2816]{2,1,0:T(8,128)(2,1)S(1)} %merge_far.1), channel_id=1, source_target_pairs={{0,28},{1,29},{2,6},{3,7},{4,0},{5,1},{6,10},{7,11},{8,4},{9,5},{1... | collective-permute-start | bytes 3244040 | tf_op jit(solution)/shard_map/ppermute | solution.py:484
  85.1 24.0 %collective-permute-start.12 = (bf16[3,64,2304]{2,1,0:T(8,128)(2,1)S(1)}, bf16[3,64,2304]{2,1,0:T(8,128)(2,1)S(1)}, u32[]{:S(2)}, u32[]{:S(2)}) collective-permute-start(bf16[3,64,2304]{2,1,0:T(8,128)(2,1)S(1)} %far.1), channel_id=1, source_target_pairs={{0,27},{3,8},{4,31},{7,12},{8,3},{11,16},{12,7},{15,20},{16,11},{1... | collective-permute-start | bytes 2654216 | tf_op jit(solution)/shard_map/ppermute | solution.py:484
  104.7 28.2 %collective-permute-start.15 = (bf16[3,64,2816]{2,1,0:T(8,128)(2,1)S(1)}, bf16[3,64,2816]{2,1,0:T(8,128)(2,1)S(1)}, u32[]{:S(2)}, u32[]{:S(2)}) collective-permute-start(bf16[3,64,2816]{2,1,0:T(8,128)(2,1)S(1)} %merge.1), channel_id=1, source_target_pairs={{0,4},{1,5},{2,30},{3,31},{4,8},{5,9},{6,2},{7,3},{8,12},{9,13},{1... | collective-permute-start | bytes 3244040 | tf_op jit(solution)/shard_map/ppermute | solution.py:484
  104.8 24.0 %collective-permute-start.14 = (bf16[3,64,2432]{2,1,0:T(8,128)(2,1)S(1)}, bf16[3,64,2432]{2,1,0:T(8,128)(2,1)S(1)}, u32[]{:S(2)}, u32[]{:S(2)}) collective-permute-start(bf16[3,64,2432]{2,1,0:T(8,128)(2,1)S(1)} %get-tuple-element.94), channel_id=1, source_target_pairs={{0,2},{1,3},{2,0},{3,1},{4,6},{5,7},{6,4},{7,5},{8,10},{9,11},{10,... | collective-permute-start | bytes 2801672 | tf_op jit(solution)/shard_map/ppermute | solution.py:484

commit v17 on v13

--- a/solution.py
+++ b/solution.py
@@ -708,9 +708,9 @@
     )(fast_rest, slow_rest, other_rest, wt_fast, wt_slow, wt_other, arrived_rest)
     relay, pair = lax.optimization_barrier((relay, pair))
     merged = merge_rows(merge, relay, 0, "merge")
+    merged, far = lax.optimization_barrier((merged, far))
     merged = permuted(merged, [(i, (i - 4 * x_sign[i]) % devices) for i in range(devices)])
     pair = permuted(pair, along_x)
-    pair, far = lax.optimization_barrier((pair, far))
     straight = [i for i in range(devices) if i % 4 in (0, 3)]
     far = permuted(far, [(i, (i + (5 if i % 2 else -5)) % devices) for i in straight])
 

time: 137 us -> 137 us (level)
  waiting for transfers between devices: 44.2 us -> 41.3 us
  starting transfers between devices: 25.4 us -> 28 us
    ppermute x16, waiting for transfers between devices: 44.2 us -> 41.3 us  [permuted(): return lax.ppermute(block, 'dom', pairs)]
    ppermute x16, starting transfers between devices: 25.4 us -> 28 us  [permuted(): return lax.ppermute(block, 'dom', pairs)]
  transfers between devices with their start and end apart: 16 -> 16, of which waited for: 6 -> 5; matrix products, arithmetic and copies ran while one was open for 2% -> 2% of each run, Pallas kernels for 38% -> 38%
where the time goes in v17:
time: 137 us
  Pallas kernels  61.2 us (45%)
  waiting for transfers between devices  41.3 us (30%)
  starting transfers between devices  28 us (20%)
  local copies, waits for them, and re-layouts  3.59 us (3%)
  other arithmetic  1.91 us (1%)
    ppermute x16, waiting for transfers between devices, permuted(): return lax.ppermute(block, 'dom', pairs)  41.3 us
    pallas_call x1, Pallas kernels, body(): pl.pallas_call(fast_kernel, out_shape=outs, in_specs=[smem] * 3 + [hbm, h...  31.9 us
    ppermute x16, starting transfers between devices, permuted(): return lax.ppermute(block, 'dom', pairs)  28 us
    pallas_call x1, Pallas kernels, body(): pl.pallas_call(join_rest_kernel, out_shape=[block(NC, span, jnp.float32),...  8.11 us
    pallas_call x1, Pallas kernels, body(): pl.pallas_call(slow_kernel, out_shape=block(WCOLS, AW), in_specs=[smem] *...  3.53 us
    unnamed x28, local copies, waits for them, and re-layouts  3.32 us
    pallas_call x1, Pallas kernels, body(): pl.pallas_call(pick_kernel, out_shape=[edge, edge], in_specs=[smem, hbm],...  3.08 us
    pallas_call x1, Pallas kernels, body(): pl.pallas_call(mine_kernel, out_shape=block(FIRST, span, jnp.float32), in...  2.98 us
  transfers between devices with their start and end apart: 16, of which 5 were waited for; matrix products, arithmetic and copies ran while one was open for 2% of the time, Pallas kernels for 38%

profile of v17, /device:TPU:0, one launch (start us, length us, event | category | flops | bytes accessed | tf_op | source)
XLA Modules:
  0.0 136.5 jit_solution(585721679505857)
XLA Ops:
  0.0 3.1 %pick.1 = (bf16[8,64,1728]{2,1,0:T(8,128)(2,1)}, bf16[8,64,1728]{2,1,0:T(8,128)(2,1)}) custom-call(s32[1]{0:T(128)} %bitcast.core, bf16[24,64,1728]{2,1,0:T(8,128)(2,1)} %p_own.1), custom_call_target="tpu_custom_call" | custom-call | tf_op jit(solution)/shard_map/pick/pallas_call | solution.py:516
  3.2 6.4 %collective-permute-start.1 = (s32[8,27]{1,0:T(8,128)S(1)}, s32[8,27]{1,0:T(8,128)S(1)}, u32[]{:S(2)}, u32[]{:S(2)}) collective-permute-start(s32[8,27]{1,0:T(8,128)S(1)} %get-tuple-element.99), channel_id=1, source_target_pairs={{0,31},{1,2},{2,1},{3,4},{4,3},{5,6},{6,5},{7,8},{8,7},{9,10},{10,... | collective-permute-start | bytes 2600 | tf_op jit(solution)/shard_map/ppermute | solution.py:482
  9.6 0.5 collective-permute-start.2
  10.1 0.3 collective-permute-start.3
  10.4 0.1 fusion.1
  10.5 0.1 copy.15
  10.6 0.2 select_reduce_fusion
  10.8 0.1 select_reduce_fusion.3
  10.9 0.6 broadcast_add_fusion.inv_a
  11.6 0.1 copy.17
  11.7 0.0 collective-permute-done
  11.7 0.1 copy.16
  11.8 0.1 select_reduce_fusion.1
  11.9 0.1 select_reduce_fusion.2
  12.1 0.6 pad_add_fusion.inv_p
  12.7 1.2 collective-permute-done.2.p_fast
  13.9 31.9 %fast.1 = (bf16[3,64,2432]{2,1,0:T(8,128)(2,1)}, bf16[3,64,2432]{2,1,0:T(8,128)(2,1)}, bf16[3,64,2432]{2,1,0:T(8,128)(2,1)}, bf16[6,64,2432]{2,1,0:T(8,128)(2,1)...) custom-call(s32[1]{0:T(128)} %bitcast.core, ...), custom_call_target="tpu_custom_call" | custom-call | flops 20000000000 | bytes 30000000 | tf_op jit(solution)/shard_map/fast/pallas_call | solution.py:585
  45.7 0.5 collective-permute-start.4
  46.2 0.1 collective-permute-start.5
  46.3 0.4 collective-permute-start.6
  46.7 2.2 %copy-done = f32[33,64,512]{2,1,0:T(8,128)S(1)} copy-done((f32[33,64,512]{2,1,0:T(8,128)S(1)}, f32[33,64,512]{2,1,0:T(8,128)}, u32[]{:S(2)}) %copy-start) | copy-done | bytes 4325400
  48.9 1.0 copy-done.2
  50.0 0.5 stage.1
  50.5 0.0 collective-permute-done.6.other
  50.5 0.0 collective-permute-done.4.low
  50.6 3.5 %slow.1.wt_slow = bf16[40,64,512]{2,1,0:T(8,128)(2,1)S(1)} custom-call(s32[1]{0:T(128)} %bitcast.core, s32[8,33]{1,0:T(8,128)S(1)} %broadcast_add_fusion.2.inv_slow, bf16[8,64,1728]{2,1,0:T(8,128)(2,1)S(1)} %collective-permute-done.3.p_slow, bf16[8,64,512]{2,1,0:T(8,128)(2,1)S(1)} %get-tuple-element.67.at_halo, f32[33,64,512]{2,1,0:T(8,128)S(1)} %get-tuple-element.68.rest), custom_call_target="tpu_custom_call" | custom-call | flops 20000000000 | bytes 200000000 | tf_op jit(solution)/shard_map/slow/pallas_call | solution.py:629
  54.1 0.3 collective-permute-start.7
  54.5 2.2 %far.1 = bf16[3,64,2304]{2,1,0:T(8,128)(2,1)S(1)} custom-call(s32[1]{0:T(128)} %bitcast.core, bf16[3,64,512]{2,1,0:T(8,128)(2,1)S(1)} %copy-done.3, bf16[40,64,512]{2,1,0:T(8,128)(2,1)S(1)} %slow.1.wt_slow, bf16[3,64,2432]{2,1,0:T(8,128)(2,1)S(1)} %copy-done.1), custom_call_target="tpu_custom_call" | custom-call | flops 1000000000 | bytes 10000000 | tf_op jit(solution)/shard_map/far/pallas_call | solution.py:647
  56.7 0.9 collective-permute-start.8
  57.6 3.0 %mine.1 = f32[6,64,2432]{2,1,0:T(8,128)S(1)} custom-call(bf16[6,64,512]{2,1,0:T(8,128)(2,1)S(1)} %copy-done.5, bf16[40,64,512]{2,1,0:T(8,128)(2,1)S(1)} %slow.1.wt_slow, bf16[6,64,2432]{2,1,0:T(8,128)(2,1)S(1)} %copy-done.4, bf16[3,64,2432]{2,1,0:T(8,128)(2,1)S(1)} %collective-permute-done.4.low, bf16[3,64,2432]{2,1,0:T(8,128)(2,1)S(1)} %collective-permute-done.5.high), custom_call_target="tpu_custom_call" | custom-call | flops 10000000000 | bytes 100000000 | tf_op jit(solution)/shard_map/mine/pallas_call | solution.py:657
  60.6 0.0 copy-start.10
  60.6 2.9 %join_first.1 = (bf16[3,64,2432]{2,1,0:T(8,128)(2,1)S(1)}, f32[3,64,2432]{2,1,0:T(8,128)S(1)}) custom-call(bf16[6,64,512]{2,1,0:T(8,128)(2,1)S(1)} %collective-permute-done.6.other, bf16[40,64,512]{2,1,0:T(8,128)(2,1)S(1)} %collective-permute-done.7.wt_other, f32[6,64,2432]{2,1,0:T(8,128)S(1)} %mine.1), custom_call_target="tpu_custom_call" | custom-call | flops 1000000 | bytes 100000 | tf_op jit(solution)/shard_map/join_first/pallas_call | solution.py:668
  63.6 7.7 %collective-permute-start.10 = (bf16[9,64,2432]{2,1,0:T(8,128)(2,1)S(1)}, bf16[9,64,2432]{2,1,0:T(8,128)(2,1)S(1)}, u32[]{:S(2)}, u32[]{:S(2)}) collective-permute-start(bf16[9,64,2432]{2,1,0:T(8,128)(2,1)S(1)} %copy-done.10), channel_id=1, source_target_pairs={{0,1},{1,0},{2,3},{3,2},{4,5},{5,4},{6,7},{7,6},{8,9},{9,8},{10,11... | collective-permute-start | bytes 8405000 | tf_op jit(solution)/shard_map/ppermute | solution.py:482
  71.3 0.1 collective-permute-start.9
  71.4 2.0 %collective-permute-start.12 = (bf16[3,64,2432]{2,1,0:T(8,128)(2,1)S(1)}, bf16[3,64,2432]{2,1,0:T(8,128)(2,1)S(1)}, u32[]{:S(2)}, u32[]{:S(2)}) collective-permute-start(bf16[3,64,2432]{2,1,0:T(8,128)(2,1)S(1)} %get-tuple-element.90), channel_id=1, source_target_pairs={{0,2},{1,3},{2,0},{3,1},{4,6},{5,7},{6,4},{7,5},{8,10},{9,11},{10,... | collective-permute-start | bytes 2801672 | tf_op jit(solution)/shard_map/ppermute | solution.py:482
  73.3 0.6 merge_far.1
  73.9 2.6 %collective-permute-start.11 = (bf16[3,64,2816]{2,1,0:T(8,128)(2,1)S(1)}, bf16[3,64,2816]{2,1,0:T(8,128)(2,1)S(1)}, u32[]{:S(2)}, u32[]{:S(2)}) collective-permute-start(bf16[3,64,2816]{2,1,0:T(8,128)(2,1)S(1)} %merge_far.1), channel_id=1, source_target_pairs={{0,28},{1,29},{2,6},{3,7},{4,0},{5,1},{6,10},{7,11},{8,4},{9,5},{1... | collective-permute-start | bytes 3244040 | tf_op jit(solution)/shard_map/ppermute | solution.py:482
  76.5 0.4 collective-permute-done.9.other
  77.0 8.1 %join_rest.1 = (f32[3,64,2432]{2,1,0:T(8,128)S(1)}, bf16[3,64,2432]{2,1,0:T(8,128)(2,1)S(1)}, f32[3,64,2432]{2,1,0:T(8,128)S(1)}) custom-call(bf16[9,64,1024]{2,1,0:T(8,128)(2,1)S(1)} %copy-done.6, bf16[9,64,512]{2,1,0:T(8,128)(2,1)S(1)} %copy-done.7, bf16[9,64,512]{2,1,0:T(8,128)(2,1)S(1)} %collective-permute-done.9.other, ...), custom_call_target="tpu_custom_call" | custom-call | flops 40000000000 | bytes 200000000 | tf_op jit(solution)/shard_map/join_rest/pallas_call | solution.py:700
  85.1 9.3 %collective-permute-done.12.other = bf16[3,64,2432]{2,1,0:T(8,128)(2,1)S(1)} collective-permute-done((bf16[3,64,2432]{2,1,0:T(8,128)(2,1)S(1)}, bf16[3,64,2432]{2,1,0:T(8,128)(2,1)S(1)}, u32[]{:S(2)}, u32[]{:S(2)}) %collective-permute-start.12) | collective-permute-done | bytes 933920 | tf_op jit(solution)/shard_map/ppermute | solution.py:482
  94.4 1.6 %collective-permute-start.13 = (bf16[3,64,2432]{2,1,0:T(8,128)(2,1)S(1)}, bf16[3,64,2432]{2,1,0:T(8,128)(2,1)S(1)}, u32[]{:S(2)}, u32[]{:S(2)}) collective-permute-start(bf16[3,64,2432]{2,1,0:T(8,128)(2,1)S(1)} %get-tuple-element.92), channel_id=1, source_target_pairs={{0,2},{1,3},{2,0},{3,1},{4,6},{5,7},{6,4},{7,5},{8,10},{9,11},{10,... | collective-permute-start | bytes 2801672 | tf_op jit(solution)/shard_map/ppermute | solution.py:482
  96.0 0.8 merge.1
  96.8 0.1 collective-permute-start.14
  96.9 4.5 %collective-permute-start.15 = (bf16[3,64,2304]{2,1,0:T(8,128)(2,1)S(1)}, bf16[3,64,2304]{2,1,0:T(8,128)(2,1)S(1)}, u32[]{:S(2)}, u32[]{:S(2)}) collective-permute-start(bf16[3,64,2304]{2,1,0:T(8,128)(2,1)S(1)} %far.1), channel_id=1, source_target_pairs={{0,27},{3,8},{4,31},{7,12},{8,3},{11,16},{12,7},{15,20},{16,11},{1... | collective-permute-start | bytes 2654216 | tf_op jit(solution)/shard_map/ppermute | solution.py:482
  101.4 23.5 %collective-permute-done.13.pair = bf16[3,64,2432]{2,1,0:T(8,128)(2,1)S(1)} collective-permute-done((bf16[3,64,2432]{2,1,0:T(8,128)(2,1)S(1)}, bf16[3,64,2432]{2,1,0:T(8,128)(2,1)S(1)}, u32[]{:S(2)}, u32[]{:S(2)}) %collective-permute-start.13) | collective-permute-done | bytes 933920 | tf_op jit(solution)/shard_map/ppermute | solution.py:482
  124.9 1.6 %early.1 = f32[3,64,4032]{2,1,0:T(8,128)S(1)} custom-call(s32[1]{0:T(128)} %bitcast.core, f32[3,64,2432]{2,1,0:T(8,128)S(1)} %get-tuple-element.87.own, bf16[3,64,2816]{2,1,0:T(8,128)(2,1)S(1)} %collective-permute-done.11.direct, bf16[3,64,2432]{2,1,0:T(8,128)(2,1)S(1)} %collective-permute-done.13.pair), custom_call_target="tpu_custom_call" | custom-call | flops 10000000000 | bytes 100000000 | tf_op jit(solution)/shard_map/early/pallas_call | solution.py:719
  126.5 6.9 %collective-permute-done.15.far = bf16[3,64,2304]{2,1,0:T(8,128)(2,1)S(1)} collective-permute-done((bf16[3,64,2304]{2,1,0:T(8,128)(2,1)S(1)}, bf16[3,64,2304]{2,1,0:T(8,128)(2,1)S(1)}, u32[]{:S(2)}, u32[]{:S(2)}) %collective-permute-start.15) | collective-permute-done | bytes 884768 | tf_op jit(solution)/shard_map/ppermute | solution.py:482
  133.4 3.0 %total.1 = f32[3,64,4032]{2,1,0:T(8,128)} custom-call(s32[1]{0:T(128)} %bitcast.core, f32[3,64,4032]{2,1,0:T(8,128)S(1)} %early.1, bf16[3,64,2816]{2,1,0:T(8,128)(2,1)S(1)} %collective-permute-done.14.merged, bf16[3,64,2304]{2,1,0:T(8,128)(2,1)S(1)} %collective-permute-done.15.far), custom_call_target="tpu_custom_call" | custom-call | flops 10000000 | bytes 10000000 | tf_op jit(solution)/shard_map/total/pallas_call | solution.py:729
  (47 shorter events, 0.2 us)
Async XLA Ops:
  0.0 3.1 %copy-start.8 = (s32[24,27]{1,0:T(8,128)S(1)}, s32[24,27]{1,0:T(8,128)}, u32[]{:S(2)}) copy-start(s32[24,27]{1,0:T(8,128)} %param.7) | copy-start | bytes 7780
  0.0 10.8 %copy-start.9 = (s32[24,7]{0,1:T(8,128)S(1)}, s32[24,7]{0,1:T(8,128)}, u32[]{:S(2)}) copy-start(s32[24,7]{0,1:T(8,128)} %param.6) | copy-start | bytes 2020
  3.2 8.4 %collective-permute-start.1 = (s32[8,27]{1,0:T(8,128)S(1)}, s32[8,27]{1,0:T(8,128)S(1)}, u32[]{:S(2)}, u32[]{:S(2)}) collective-permute-start(s32[8,27]{1,0:T(8,128)S(1)} %get-tuple-element.99), channel_id=1, source_target_pairs={{0,31},{1,2},{2,1},{3,4},{4,3},{5,6},{6,5},{7,8},{8,7},{9,10},{10,... | collective-permute-start | bytes 2600 | tf_op jit(solution)/shard_map/ppermute | solution.py:482
  9.6 2.1 %collective-permute-start = (s32[8,27]{1,0:T(8,128)S(1)}, s32[8,27]{1,0:T(8,128)S(1)}, u32[]{:S(2)}, u32[]{:S(2)}) collective-permute-start(s32[8,27]{1,0:T(8,128)S(1)} %get-tuple-element.100), channel_id=1, source_target_pairs={{0,1},{1,0},{2,3},{3,2},{4,5},{5,4},{6,7},{7,6},{8,9},{9,8},{10,11... | collective-permute-start | bytes 2600 | tf_op jit(solution)/shard_map/ppermute | solution.py:482
  9.6 4.3 %collective-permute-start.2 = (bf16[8,64,1728]{2,1,0:T(8,128)(2,1)}, bf16[8,64,1728]{2,1,0:T(8,128)(2,1)}, u32[]{:S(2)}, u32[]{:S(2)}) collective-permute-start(bf16[8,64,1728]{2,1,0:T(8,128)(2,1)} %get-tuple-element.55), channel_id=1, source_target_pairs={{0,1},{1,0},{2,3},{3,2},{4,5},{5,4},{6,7},{7,6},{8,9},{9,8},{10,11... | collective-permute-start | bytes 5308424 | tf_op jit(solution)/shard_map/ppermute | solution.py:482
  10.1 40.4 %collective-permute-start.3 = (bf16[8,64,1728]{2,1,0:T(8,128)(2,1)}, bf16[8,64,1728]{2,1,0:T(8,128)(2,1)S(1)}, u32[]{:S(2)}, u32[]{:S(2)}) collective-permute-start(bf16[8,64,1728]{2,1,0:T(8,128)(2,1)} %get-tuple-element.58), channel_id=1, source_target_pairs={{0,31},{1,2},{2,1},{3,4},{4,3},{5,6},{6,5},{7,8},{8,7},{9,10},{10,... | collective-permute-start | bytes 5308424 | tf_op jit(solution)/shard_map/ppermute | solution.py:482
  45.7 4.8 %collective-permute-start.4 = (bf16[3,64,2432]{2,1,0:T(8,128)(2,1)}, bf16[3,64,2432]{2,1,0:T(8,128)(2,1)S(1)}, u32[]{:S(2)}, u32[]{:S(2)}) collective-permute-start(bf16[3,64,2432]{2,1,0:T(8,128)(2,1)} %get-tuple-element.59), channel_id=1, source_target_pairs={{0,1},{1,0},{2,3},{3,2},{4,5},{5,4},{6,7},{7,6},{8,9},{9,8},{10,11... | collective-permute-start | bytes 2801672 | tf_op jit(solution)/shard_map/ppermute | solution.py:482
  46.2 4.3 %collective-permute-start.5 = (bf16[3,64,2432]{2,1,0:T(8,128)(2,1)}, bf16[3,64,2432]{2,1,0:T(8,128)(2,1)S(1)}, u32[]{:S(2)}, u32[]{:S(2)}) collective-permute-start(bf16[3,64,2432]{2,1,0:T(8,128)(2,1)} %get-tuple-element.60), channel_id=1, source_target_pairs={{0,1},{1,0},{2,3},{3,2},{4,5},{5,4},{6,7},{7,6},{8,9},{9,8},{10,11... | collective-permute-start | bytes 2801672 | tf_op jit(solution)/shard_map/ppermute | solution.py:482
  46.3 4.2 %collective-permute-start.6 = (bf16[6,64,512]{2,1,0:T(8,128)(2,1)}, bf16[6,64,512]{2,1,0:T(8,128)(2,1)S(1)}, u32[]{:S(2)}, u32[]{:S(2)}) collective-permute-start(bf16[6,64,512]{2,1,0:T(8,128)(2,1)} %get-tuple-element.61), channel_id=1, source_target_pairs={{0,1},{1,0},{2,3},{3,2},{4,5},{5,4},{6,7},{7,6},{8,9},{9,8},{10,11... | collective-permute-start | bytes 1179656 | tf_op jit(solution)/shard_map/ppermute | solution.py:482
  46.7 2.2 %copy-start = (f32[33,64,512]{2,1,0:T(8,128)S(1)}, f32[33,64,512]{2,1,0:T(8,128)}, u32[]{:S(2)}) copy-start(f32[33,64,512]{2,1,0:T(8,128)} %get-tuple-element.66.rest) | copy-start | bytes 12976132
  48.9 1.0 copy-start.2
  50.5 3.9 %copy-start.1 = (bf16[3,64,2432]{2,1,0:T(8,128)(2,1)S(1)}, bf16[3,64,2432]{2,1,0:T(8,128)(2,1)}, u32[]{:S(2)}) copy-start(bf16[3,64,2432]{2,1,0:T(8,128)(2,1)} %get-tuple-element.74.far_fast) | copy-start | bytes 2801668
  50.5 3.9 %copy-start.3 = (bf16[3,64,512]{2,1,0:T(8,128)(2,1)S(1)}, bf16[3,64,512]{2,1,0:T(8,128)(2,1)}, u32[]{:S(2)}) copy-start(bf16[3,64,512]{2,1,0:T(8,128)(2,1)} %get-tuple-element.70.slow) | copy-start | bytes 589828
  50.6 7.0 %copy-start.5 = (bf16[6,64,512]{2,1,0:T(8,128)(2,1)S(1)}, bf16[6,64,512]{2,1,0:T(8,128)(2,1)}, u32[]{:S(2)}) copy-start(bf16[6,64,512]{2,1,0:T(8,128)(2,1)} %get-tuple-element.69.slow) | copy-start | bytes 1179652
  54.1 6.5 %collective-permute-start.7 = (bf16[40,64,512]{2,1,0:T(8,128)(2,1)S(1)}, bf16[40,64,512]{2,1,0:T(8,128)(2,1)S(1)}, u32[]{:S(2)}, u32[]{:S(2)}) collective-permute-start(bf16[40,64,512]{2,1,0:T(8,128)(2,1)S(1)} %slow.1.wt_slow), channel_id=1, source_target_pairs={{0,1},{1,0},{2,3},{3,2},{4,5},{5,4},{6,7},{7,6},{8,9},{9,8},{10,11... | collective-permute-start | bytes 7864328 | tf_op jit(solution)/shard_map/ppermute | solution.py:482
  54.4 3.1 %copy-start.4 = (bf16[6,64,2432]{2,1,0:T(8,128)(2,1)S(1)}, bf16[6,64,2432]{2,1,0:T(8,128)(2,1)}, u32[]{:S(2)}) copy-start(bf16[6,64,2432]{2,1,0:T(8,128)(2,1)} %get-tuple-element.76.inner) | copy-start | bytes 5603332
  54.4 22.5 %slice-start = ((s8[5242880]{0:T(1024)(128)(4,1)}), s8[4194304]{0:T(1024)(128)(4,1)S(1)}, s32[]{:S(2)}) async-start(s8[5242880]{0:T(1024)(128)(4,1)} %bitcast.9), calls=%async_computation | async-start | bytes 8388608
  56.7 6.9 %collective-permute-start.8 = (bf16[3,64,2304]{2,1,0:T(8,128)(2,1)S(1)}, bf16[3,64,2304]{2,1,0:T(8,128)(2,1)S(1)}, u32[]{:S(2)}, u32[]{:S(2)}) collective-permute-start(bf16[3,64,2304]{2,1,0:T(8,128)(2,1)S(1)} %far.1), channel_id=1, source_target_pairs={{1,2},{2,1},{5,6},{6,5},{9,10},{10,9},{13,14},{14,13},{17,18},{18,... | collective-permute-start | bytes 2654216 | tf_op jit(solution)/shard_map/ppermute | solution.py:482
  57.6 19.3 %slice-start.1 = ((s8[5242880]{0:T(1024)(128)(4,1)}), s8[1048576]{0:T(1024)(128)(4,1)S(1)}, s32[]{:S(2)}) async-start(s8[5242880]{0:T(1024)(128)(4,1)} %bitcast.9), calls=%async_computation.1 | async-start | bytes 2097152
  60.6 3.0 %copy-start.10 = (bf16[9,64,2432]{2,1,0:T(8,128)(2,1)S(1)}, bf16[9,64,2432]{2,1,0:T(8,128)(2,1)}, u32[]{:S(2)}) copy-start(bf16[9,64,2432]{2,1,0:T(8,128)(2,1)} %get-tuple-element.86) | copy-start | bytes 8404996
  60.6 10.7 %copy-start.11 = (bf16[9,64,512]{2,1,0:T(8,128)(2,1)S(1)}, bf16[9,64,512]{2,1,0:T(8,128)(2,1)}, u32[]{:S(2)}) copy-start(bf16[9,64,512]{2,1,0:T(8,128)(2,1)} %get-tuple-element.84) | copy-start | bytes 1769476
  63.6 13.4 %copy-start.6 = (bf16[9,64,1024]{2,1,0:T(8,128)(2,1)S(1)}, bf16[9,64,1024]{2,1,0:T(8,128)(2,1)}, u32[]{:S(2)}) copy-start(bf16[9,64,1024]{2,1,0:T(8,128)(2,1)} %get-tuple-element.56.fast) | copy-start | bytes 3538948
  63.6 13.4 %copy-start.7 = (bf16[9,64,512]{2,1,0:T(8,128)(2,1)S(1)}, bf16[9,64,512]{2,1,0:T(8,128)(2,1)}, u32[]{:S(2)}) copy-start(bf16[9,64,512]{2,1,0:T(8,128)(2,1)} %get-tuple-element.57.slow) | copy-start | bytes 1769476
  63.6 13.3 %collective-permute-start.10 = (bf16[9,64,2432]{2,1,0:T(8,128)(2,1)S(1)}, bf16[9,64,2432]{2,1,0:T(8,128)(2,1)S(1)}, u32[]{:S(2)}, u32[]{:S(2)}) collective-permute-start(bf16[9,64,2432]{2,1,0:T(8,128)(2,1)S(1)} %copy-done.10), channel_id=1, source_target_pairs={{0,1},{1,0},{2,3},{3,2},{4,5},{5,4},{6,7},{7,6},{8,9},{9,8},{10,11... | collective-permute-start | bytes 8405000 | tf_op jit(solution)/shard_map/ppermute | solution.py:482
  71.3 5.6 %collective-permute-start.9 = (bf16[9,64,512]{2,1,0:T(8,128)(2,1)S(1)}, bf16[9,64,512]{2,1,0:T(8,128)(2,1)S(1)}, u32[]{:S(2)}, u32[]{:S(2)}) collective-permute-start(bf16[9,64,512]{2,1,0:T(8,128)(2,1)S(1)} %copy-done.11), channel_id=1, source_target_pairs={{0,1},{1,0},{2,3},{3,2},{4,5},{5,4},{6,7},{7,6},{8,9},{9,8},{10,11... | collective-permute-start | bytes 1769480 | tf_op jit(solution)/shard_map/ppermute | solution.py:482
  71.4 23.0 %collective-permute-start.12 = (bf16[3,64,2432]{2,1,0:T(8,128)(2,1)S(1)}, bf16[3,64,2432]{2,1,0:T(8,128)(2,1)S(1)}, u32[]{:S(2)}, u32[]{:S(2)}) collective-permute-start(bf16[3,64,2432]{2,1,0:T(8,128)(2,1)S(1)} %get-tuple-element.90), channel_id=1, source_target_pairs={{0,2},{1,3},{2,0},{3,1},{4,6},{5,7},{6,4},{7,5},{8,10},{9,11},{10,... | collective-permute-start | bytes 2801672 | tf_op jit(solution)/shard_map/ppermute | solution.py:482
  73.9 27.5 %collective-permute-start.11 = (bf16[3,64,2816]{2,1,0:T(8,128)(2,1)S(1)}, bf16[3,64,2816]{2,1,0:T(8,128)(2,1)S(1)}, u32[]{:S(2)}, u32[]{:S(2)}) collective-permute-start(bf16[3,64,2816]{2,1,0:T(8,128)(2,1)S(1)} %merge_far.1), channel_id=1, source_target_pairs={{0,28},{1,29},{2,6},{3,7},{4,0},{5,1},{6,10},{7,11},{8,4},{9,5},{1... | collective-permute-start | bytes 3244040 | tf_op jit(solution)/shard_map/ppermute | solution.py:482
  94.4 30.5 %collective-permute-start.13 = (bf16[3,64,2432]{2,1,0:T(8,128)(2,1)S(1)}, bf16[3,64,2432]{2,1,0:T(8,128)(2,1)S(1)}, u32[]{:S(2)}, u32[]{:S(2)}) collective-permute-start(bf16[3,64,2432]{2,1,0:T(8,128)(2,1)S(1)} %get-tuple-element.92), channel_id=1, source_target_pairs={{0,2},{1,3},{2,0},{3,1},{4,6},{5,7},{6,4},{7,5},{8,10},{9,11},{10,... | collective-permute-start | bytes 2801672 | tf_op jit(solution)/shard_map/ppermute | solution.py:482
  96.8 36.6 %collective-permute-start.14 = (bf16[3,64,2816]{2,1,0:T(8,128)(2,1)S(1)}, bf16[3,64,2816]{2,1,0:T(8,128)(2,1)S(1)}, u32[]{:S(2)}, u32[]{:S(2)}) collective-permute-start(bf16[3,64,2816]{2,1,0:T(8,128)(2,1)S(1)} %merge.1), channel_id=1, source_target_pairs={{0,4},{1,5},{2,30},{3,31},{4,8},{5,9},{6,2},{7,3},{8,12},{9,13},{1... | collective-permute-start | bytes 3244040 | tf_op jit(solution)/shard_map/ppermute | solution.py:482
  96.9 36.5 %collective-permute-start.15 = (bf16[3,64,2304]{2,1,0:T(8,128)(2,1)S(1)}, bf16[3,64,2304]{2,1,0:T(8,128)(2,1)S(1)}, u32[]{:S(2)}, u32[]{:S(2)}) collective-permute-start(bf16[3,64,2304]{2,1,0:T(8,128)(2,1)S(1)} %far.1), channel_id=1, source_target_pairs={{0,27},{3,8},{4,31},{7,12},{8,3},{11,16},{12,7},{15,20},{16,11},{1... | collective-permute-start | bytes 2654216 | tf_op jit(solution)/shard_map/ppermute | solution.py:482

commit v18 on v16

--- a/solution.py
+++ b/solution.py
@@ -411,12 +411,14 @@
         out[j] = frame[...].astype(jnp.bfloat16)
 
 
-def in_frame(s, j, frame, messages, store):
+def in_frame(s, j, frame, messages, store, row=None):
     odd = (j + 1 - s) % 2
     frame[...] = jnp.zeros_like(frame)
     for message, start in messages:
         lane = pl.multiple_of((start - odd + 8) * BS, 2 * BS)
-        frame[:, pl.ds(lane, message.shape[2])] += message[j].astype(jnp.float32)
+        frame[:, pl.ds(lane, message.shape[2])] += message[j if row is None else row].astype(
+            jnp.float32
+        )
     first, last = 8 * BS, (8 + BAND) * BS
 
     @pl.when(odd == 0)
@@ -428,12 +430,17 @@
         store(frame[:, first - BS : last - BS])
 
 
-def early_kernel(core, own, direct, far, out, frame):
+def far_place(s, j):
+    return jnp.where(s == 1, 30 - j, -1 - j)
+
+
+def first_kernel(core, own, direct, far, out, frame):
     s, x = places(core)
     for j in range(NC):
         top = 27 - 3 * s - j
         messages = [(own, top - 12), (direct, top - 30 * x)]
-        messages.append((far, jnp.where(s == 1, 30 - j, -1 - j)))
+        if j == 0:
+            messages.append((far, far_place(s, j)))
 
         def store(value, j=j):
             out[j] = value
@@ -441,17 +448,29 @@
         in_frame(s, j, frame, messages, store)
 
 
-def total_kernel(core, early, pair, merged, out, frame, buf, sems):
+def early_kernel(core, first, pair, merged, out, frame):
+    s, x = places(core)
+    for j in range(NC):
+        top = 27 - 3 * s - j
+
+        def store(value, j=j):
+            out[j] = value + first[j]
+
+        messages = [(pair, top - 6 - 12 * x), (merged, top - 24 + 18 * x)]
+        in_frame(s, j, frame, messages, store)
+
+
+def total_kernel(core, early, far, out, frame, buf, sems):
     s, x = places(core)
     copies = []
+    buf[0] = early[0]
     for j in range(NC):
-        top = 27 - 3 * s - j
-
-        def store(value, j=j):
-            buf[j] = value + early[j]
-
-        messages = [(pair, top - 6 - 12 * x), (merged, top - 24 + 18 * x)]
-        in_frame(s, j, frame, messages, store)
+        if j > 0:
+
+            def store(value, j=j):
+                buf[j] = value + early[j]
+
+            in_frame(s, j, frame, [(far, far_place(s, j))], store, j - 1)
         copy = pltpu.make_async_copy(buf.at[j], out.at[j], sems.at[j])
         copy.start()
         copies.append(copy)
@@ -708,30 +727,38 @@
         cost_estimate=cost(40 * 10**9, 200 * 10**6),
         name="join_rest",
     )(fast_rest, slow_rest, other_rest, wt_fast, wt_slow, wt_other, arrived_rest)
-    pair, far = lax.optimization_barrier((pair, far))
+    pair, far_head = lax.optimization_barrier((pair, far[:1]))
     relay, pair = lax.optimization_barrier((relay, pair))
     merged = merge_rows(merge, relay, 0, "merge")
+    merged, far_tail = lax.optimization_barrier((merged, far[1:]))
     merged = permuted(merged, [(i, (i - 4 * x_sign[i]) % devices) for i in range(devices)])
     pair = permuted(pair, along_x)
     straight = [i for i in range(devices) if i % 4 in (0, 3)]
-    far = permuted(far, [(i, (i + (5 if i % 2 else -5)) % devices) for i in straight])
+    reach = [(i, (i + (5 if i % 2 else -5)) % devices) for i in straight]
+    far_head = permuted(far_head, reach)
+    far_tail = permuted(far_tail, reach)
 
     total = block(NC, BAND * BS, jnp.float32)
     frame = pltpu.VMEM((BS, FRAME * BS), jnp.float32)
-    early = pl.pallas_call(
-        early_kernel,
-        out_shape=total,
-        in_specs=[smem] + [vmem] * 3,
-        out_specs=vmem,
-        scratch_shapes=[frame],
-        compiler_params=params(16),
-        cost_estimate=cost(10**10, 100 * 10**6),
-        name="early",
-    )(core, own, direct, far)
+
+    def partly(kernel, name, *terms):
+        return pl.pallas_call(
+            kernel,
+            out_shape=total,
+            in_specs=[smem] + [vmem] * len(terms),
+            out_specs=vmem,
+            scratch_shapes=[frame],
+            compiler_params=params(16),
+            cost_estimate=cost(10**10, 100 * 10**6),
+            name=name,
+        )(core, *terms)
+
+    first = partly(first_kernel, "first", own, direct, far_head)
+    early = partly(early_kernel, "early", first, pair, merged)
     return pl.pallas_call(
         total_kernel,
         out_shape=total,
-        in_specs=[smem] + [vmem] * 3,
+        in_specs=[smem] + [vmem] * 2,
         out_specs=hbm,
         scratch_shapes=[
             frame,
@@ -741,7 +768,7 @@
         compiler_params=params(20),
         cost_estimate=cost(10**7, 10**7),
         name="total",
-    )(core, early, pair, merged)
+    )(core, early, far_tail)
 
 
 def solution(mesh):

time: 136 us -> 135 us (level)
  waiting for transfers between devices: 38.3 us -> 34.7 us
    ppermute x16 -> x17, waiting for transfers between devices: 38.3 us -> 34.7 us  [permuted(): return lax.ppermute(block, 'dom', pairs)]
    pallas_call x1 -> x2, Pallas kernels: 1.61 us -> 3.46 us  [partly(): pl.pallas_call(kernel, out_shape=total, in_specs=[smem] + [vmem] * len(te...]
    ppermute x16 -> x17, starting transfers between devices: 30.5 us -> 31.3 us  [permuted(): return lax.ppermute(block, 'dom', pairs)]
  transfers between devices with their start and end apart: 16 -> 17, of which waited for: 6 -> 4; matrix products, arithmetic and copies ran while one was open for 2% -> 2% of each run, Pallas kernels for 38% -> 40%
where the time goes in v18:
time: 135 us; the launch traced here: 134 us
  Pallas kernels  62.1 us (46%)
  waiting for transfers between devices  34.7 us (26%)
  starting transfers between devices  31.3 us (23%)
  local copies, waits for them, and re-layouts  3.65 us (3%)
  other arithmetic  1.91 us (1%)
    ppermute x17, waiting for transfers between devices, permuted(): return lax.ppermute(block, 'dom', pairs)  34.7 us
    pallas_call x1, Pallas kernels, body(): pl.pallas_call(fast_kernel, out_shape=outs, in_specs=[smem] * 3 + [hbm, h...  31.9 us
    ppermute x17, starting transfers between devices, permuted(): return lax.ppermute(block, 'dom', pairs)  31.3 us
    pallas_call x1, Pallas kernels, body(): pl.pallas_call(join_rest_kernel, out_shape=[block(NC, span, jnp.float32),...  8.11 us
    pallas_call x1, Pallas kernels, body(): pl.pallas_call(slow_kernel, out_shape=block(WCOLS, AW), in_specs=[smem] *...  3.55 us
    pallas_call x2, Pallas kernels, partly(): pl.pallas_call(kernel, out_shape=total, in_specs=[smem] + [vmem] * len(te...  3.46 us
    unnamed x28, local copies, waits for them, and re-layouts  3.32 us
    pallas_call x1, Pallas kernels, body(): pl.pallas_call(pick_kernel, out_shape=[edge, edge], in_specs=[smem, hbm],...  3.08 us
  transfers between devices with their start and end apart: 17, of which 4 were waited for; matrix products, arithmetic and copies ran while one was open for 2% of the time, Pallas kernels for 40%

profile of v18, /device:TPU:0, one launch (start us, length us, event | category | flops | bytes accessed | tf_op | source)
XLA Modules:
  0.0 134.3 jit_solution(5591246816333932237)
XLA Ops:
  0.0 3.1 %pick.1 = (bf16[8,64,1728]{2,1,0:T(8,128)(2,1)}, bf16[8,64,1728]{2,1,0:T(8,128)(2,1)}) custom-call(s32[1]{0:T(128)} %bitcast.core, bf16[24,64,1728]{2,1,0:T(8,128)(2,1)} %p_own.1), custom_call_target="tpu_custom_call" | custom-call | tf_op jit(solution)/shard_map/pick/pallas_call | solution.py:537
  3.2 6.4 %collective-permute-start.1 = (s32[8,27]{1,0:T(8,128)S(1)}, s32[8,27]{1,0:T(8,128)S(1)}, u32[]{:S(2)}, u32[]{:S(2)}) collective-permute-start(s32[8,27]{1,0:T(8,128)S(1)} %get-tuple-element.103), channel_id=1, source_target_pairs={{0,31},{1,2},{2,1},{3,4},{4,3},{5,6},{6,5},{7,8},{8,7},{9,10},{10,... | collective-permute-start | bytes 2600 | tf_op jit(solution)/shard_map/ppermute | solution.py:503
  9.6 0.5 collective-permute-start.2
  10.1 0.3 collective-permute-start.3
  10.4 0.1 fusion.1
  10.5 0.1 copy.15
  10.6 0.2 select_reduce_fusion
  10.8 0.1 select_reduce_fusion.3
  10.9 0.6 broadcast_add_fusion.inv_a
  11.6 0.0 collective-permute-done.1
  11.6 0.1 copy.17
  11.7 0.1 copy.16
  11.8 0.1 select_reduce_fusion.1
  11.9 0.1 select_reduce_fusion.2
  12.1 0.6 pad_add_fusion.inv_p
  12.7 1.2 collective-permute-done.2.p_fast
  13.9 31.9 %fast.1 = (bf16[3,64,2432]{2,1,0:T(8,128)(2,1)}, bf16[3,64,2432]{2,1,0:T(8,128)(2,1)}, bf16[3,64,2432]{2,1,0:T(8,128)(2,1)}, bf16[6,64,2432]{2,1,0:T(8,128)(2,1)...) custom-call(s32[1]{0:T(128)} %bitcast.core, ...), custom_call_target="tpu_custom_call" | custom-call | flops 20000000000 | bytes 30000000 | tf_op jit(solution)/shard_map/fast/pallas_call | solution.py:606
  45.7 0.5 collective-permute-start.4
  46.2 0.1 collective-permute-start.5
  46.3 0.4 collective-permute-start.6
  46.7 2.2 %copy-done = f32[33,64,512]{2,1,0:T(8,128)S(1)} copy-done((f32[33,64,512]{2,1,0:T(8,128)S(1)}, f32[33,64,512]{2,1,0:T(8,128)}, u32[]{:S(2)}) %copy-start) | copy-done | bytes 4325400
  48.9 1.0 copy-done.2
  50.0 0.5 stage.1
  50.5 0.0 collective-permute-done.6.other
  50.6 3.5 %slow.1.wt_slow = bf16[40,64,512]{2,1,0:T(8,128)(2,1)S(1)} custom-call(s32[1]{0:T(128)} %bitcast.core, s32[8,33]{1,0:T(8,128)S(1)} %broadcast_add_fusion.2.inv_slow, bf16[8,64,1728]{2,1,0:T(8,128)(2,1)S(1)} %collective-permute-done.3.p_slow, bf16[8,64,512]{2,1,0:T(8,128)(2,1)S(1)} %get-tuple-element.69.at_halo, f32[33,64,512]{2,1,0:T(8,128)S(1)} %get-tuple-element.70.rest), custom_call_target="tpu_custom_call" | custom-call | flops 20000000000 | bytes 200000000 | tf_op jit(solution)/shard_map/slow/pallas_call | solution.py:650
  54.1 0.3 collective-permute-start.7
  54.5 2.2 %far.1 = bf16[3,64,2304]{2,1,0:T(8,128)(2,1)S(1)} custom-call(s32[1]{0:T(128)} %bitcast.core, bf16[3,64,512]{2,1,0:T(8,128)(2,1)S(1)} %copy-done.3, bf16[40,64,512]{2,1,0:T(8,128)(2,1)S(1)} %slow.1.wt_slow, bf16[3,64,2432]{2,1,0:T(8,128)(2,1)S(1)} %copy-done.1), custom_call_target="tpu_custom_call" | custom-call | flops 1000000000 | bytes 10000000 | tf_op jit(solution)/shard_map/far/pallas_call | solution.py:668
  56.7 0.9 collective-permute-start.8
  57.6 3.0 %mine.1 = f32[6,64,2432]{2,1,0:T(8,128)S(1)} custom-call(bf16[6,64,512]{2,1,0:T(8,128)(2,1)S(1)} %copy-done.5, bf16[40,64,512]{2,1,0:T(8,128)(2,1)S(1)} %slow.1.wt_slow, bf16[6,64,2432]{2,1,0:T(8,128)(2,1)S(1)} %copy-done.4, bf16[3,64,2432]{2,1,0:T(8,128)(2,1)S(1)} %collective-permute-done.4.low, bf16[3,64,2432]{2,1,0:T(8,128)(2,1)S(1)} %collective-permute-done.5.high), custom_call_target="tpu_custom_call" | custom-call | flops 10000000000 | bytes 100000000 | tf_op jit(solution)/shard_map/mine/pallas_call | solution.py:678
  60.6 0.0 copy-start.10
  60.6 2.9 %join_first.1 = (bf16[3,64,2432]{2,1,0:T(8,128)(2,1)S(1)}, f32[3,64,2432]{2,1,0:T(8,128)S(1)}) custom-call(bf16[6,64,512]{2,1,0:T(8,128)(2,1)S(1)} %collective-permute-done.6.other, bf16[40,64,512]{2,1,0:T(8,128)(2,1)S(1)} %collective-permute-done.7.wt_other, f32[6,64,2432]{2,1,0:T(8,128)S(1)} %mine.1), custom_call_target="tpu_custom_call" | custom-call | flops 1000000 | bytes 100000 | tf_op jit(solution)/shard_map/join_first/pallas_call | solution.py:689
  63.6 7.7 %collective-permute-start.10 = (bf16[9,64,2432]{2,1,0:T(8,128)(2,1)S(1)}, bf16[9,64,2432]{2,1,0:T(8,128)(2,1)S(1)}, u32[]{:S(2)}, u32[]{:S(2)}) collective-permute-start(bf16[9,64,2432]{2,1,0:T(8,128)(2,1)S(1)} %copy-done.10), channel_id=1, source_target_pairs={{0,1},{1,0},{2,3},{3,2},{4,5},{5,4},{6,7},{7,6},{8,9},{9,8},{10,11... | collective-permute-start | bytes 8405000 | tf_op jit(solution)/shard_map/ppermute | solution.py:503
  71.3 0.1 collective-permute-start.9
  71.4 2.0 %collective-permute-start.13 = (bf16[3,64,2432]{2,1,0:T(8,128)(2,1)S(1)}, bf16[3,64,2432]{2,1,0:T(8,128)(2,1)S(1)}, u32[]{:S(2)}, u32[]{:S(2)}) collective-permute-start(bf16[3,64,2432]{2,1,0:T(8,128)(2,1)S(1)} %get-tuple-element.94), channel_id=1, source_target_pairs={{0,2},{1,3},{2,0},{3,1},{4,6},{5,7},{6,4},{7,5},{8,10},{9,11},{10,... | collective-permute-start | bytes 2801672 | tf_op jit(solution)/shard_map/ppermute | solution.py:503
  73.4 0.6 merge_far.1
  74.0 2.7 %collective-permute-start.11 = (bf16[3,64,2816]{2,1,0:T(8,128)(2,1)S(1)}, bf16[3,64,2816]{2,1,0:T(8,128)(2,1)S(1)}, u32[]{:S(2)}, u32[]{:S(2)}) collective-permute-start(bf16[3,64,2816]{2,1,0:T(8,128)(2,1)S(1)} %merge_far.1), channel_id=1, source_target_pairs={{0,28},{1,29},{2,6},{3,7},{4,0},{5,1},{6,10},{7,11},{8,4},{9,5},{1... | collective-permute-start | bytes 3244040 | tf_op jit(solution)/shard_map/ppermute | solution.py:503
  76.7 0.2 collective-permute-done.9.other
  77.0 8.1 %join_rest.1 = (f32[3,64,2432]{2,1,0:T(8,128)S(1)}, bf16[3,64,2432]{2,1,0:T(8,128)(2,1)S(1)}, f32[3,64,2432]{2,1,0:T(8,128)S(1)}) custom-call(bf16[9,64,1024]{2,1,0:T(8,128)(2,1)S(1)} %copy-done.6, bf16[9,64,512]{2,1,0:T(8,128)(2,1)S(1)} %copy-done.7, bf16[9,64,512]{2,1,0:T(8,128)(2,1)S(1)} %collective-permute-done.9.other, ...), custom_call_target="tpu_custom_call" | custom-call | flops 40000000000 | bytes 200000000 | tf_op jit(solution)/shard_map/join_rest/pallas_call | solution.py:721
  85.1 4.4 %collective-permute-start.12 = (bf16[1,64,2304]{2,1,0:T(8,128)(2,1)S(1)}, bf16[1,64,2304]{2,1,0:T(8,128)(2,1)S(1)}, u32[]{:S(2)}, u32[]{:S(2)}) collective-permute-start(bf16[1,64,2304]{2,1,0:T(8,128)(2,1)S(1)} %slice.14), channel_id=1, source_target_pairs={{0,27},{3,8},{4,31},{7,12},{8,3},{11,16},{12,7},{15,20},{16,11},{1... | collective-permute-start | bytes 884744 | tf_op jit(solution)/shard_map/ppermute | solution.py:503
  89.5 8.1 %collective-permute-done.13.other = bf16[3,64,2432]{2,1,0:T(8,128)(2,1)S(1)} collective-permute-done((bf16[3,64,2432]{2,1,0:T(8,128)(2,1)S(1)}, bf16[3,64,2432]{2,1,0:T(8,128)(2,1)S(1)}, u32[]{:S(2)}, u32[]{:S(2)}) %collective-permute-start.13) | collective-permute-done | bytes 933920 | tf_op jit(solution)/shard_map/ppermute | solution.py:503
  97.7 0.8 merge.1
  98.5 0.1 collective-permute-start.15
  98.5 4.6 %collective-permute-start.16 = (bf16[2,64,2304]{2,1,0:T(8,128)(2,1)S(1)}, bf16[2,64,2304]{2,1,0:T(8,128)(2,1)S(1)}, u32[]{:S(2)}, u32[]{:S(2)}) collective-permute-start(bf16[2,64,2304]{2,1,0:T(8,128)(2,1)S(1)} %slice.15), channel_id=1, source_target_pairs={{0,27},{3,8},{4,31},{7,12},{8,3},{11,16},{12,7},{15,20},{16,11},{1... | collective-permute-start | bytes 1769480 | tf_op jit(solution)/shard_map/ppermute | solution.py:503
  103.1 0.3 collective-permute-start.14
  103.5 1.5 %first.1 = f32[3,64,4032]{2,1,0:T(8,128)S(1)} custom-call(s32[1]{0:T(128)} %bitcast.core, f32[3,64,2432]{2,1,0:T(8,128)S(1)} %get-tuple-element.89.own, bf16[3,64,2816]{2,1,0:T(8,128)(2,1)S(1)} %collective-permute-done.11.direct, bf16[1,64,2304]{2,1,0:T(8,128)(2,1)S(1)} %collective-permute-done.12.far), custom_call_target="tpu_custom_call" | custom-call | flops 10000000000 | bytes 100000000 | tf_op jit(solution)/shard_map/first/pallas_call | solution.py:745
  105.0 25.1 %collective-permute-done.14.pair = bf16[3,64,2432]{2,1,0:T(8,128)(2,1)S(1)} collective-permute-done((bf16[3,64,2432]{2,1,0:T(8,128)(2,1)S(1)}, bf16[3,64,2432]{2,1,0:T(8,128)(2,1)S(1)}, u32[]{:S(2)}, u32[]{:S(2)}) %collective-permute-start.14) | collective-permute-done | bytes 933920 | tf_op jit(solution)/shard_map/ppermute | solution.py:503
  130.1 2.0 %early.1 = f32[3,64,4032]{2,1,0:T(8,128)S(1)} custom-call(s32[1]{0:T(128)} %bitcast.core, f32[3,64,4032]{2,1,0:T(8,128)S(1)} %first.1, bf16[3,64,2432]{2,1,0:T(8,128)(2,1)S(1)} %collective-permute-done.14.pair, bf16[3,64,2816]{2,1,0:T(8,128)(2,1)S(1)} %collective-permute-done.15.merged), custom_call_target="tpu_custom_call" | custom-call | flops 10000000000 | bytes 100000000 | tf_op jit(solution)/shard_map/early/pallas_call | solution.py:745
  132.1 2.1 %total.1 = f32[3,64,4032]{2,1,0:T(8,128)} custom-call(s32[1]{0:T(128)} %bitcast.core, f32[3,64,4032]{2,1,0:T(8,128)S(1)} %early.1, bf16[2,64,2304]{2,1,0:T(8,128)(2,1)S(1)} %collective-permute-done.16.far), custom_call_target="tpu_custom_call" | custom-call | flops 10000000 | bytes 10000000 | tf_op jit(solution)/shard_map/total/pallas_call | solution.py:758
  (52 shorter events, 0.2 us)
Async XLA Ops:
  0.0 3.1 %copy-start.8 = (s32[24,27]{1,0:T(8,128)S(1)}, s32[24,27]{1,0:T(8,128)}, u32[]{:S(2)}) copy-start(s32[24,27]{1,0:T(8,128)} %param.7) | copy-start | bytes 7780
  0.0 10.8 %copy-start.9 = (s32[24,7]{0,1:T(8,128)S(1)}, s32[24,7]{0,1:T(8,128)}, u32[]{:S(2)}) copy-start(s32[24,7]{0,1:T(8,128)} %param.6) | copy-start | bytes 2020
  3.2 8.4 %collective-permute-start.1 = (s32[8,27]{1,0:T(8,128)S(1)}, s32[8,27]{1,0:T(8,128)S(1)}, u32[]{:S(2)}, u32[]{:S(2)}) collective-permute-start(s32[8,27]{1,0:T(8,128)S(1)} %get-tuple-element.103), channel_id=1, source_target_pairs={{0,31},{1,2},{2,1},{3,4},{4,3},{5,6},{6,5},{7,8},{8,7},{9,10},{10,... | collective-permute-start | bytes 2600 | tf_op jit(solution)/shard_map/ppermute | solution.py:503
  9.6 2.1 %collective-permute-start = (s32[8,27]{1,0:T(8,128)S(1)}, s32[8,27]{1,0:T(8,128)S(1)}, u32[]{:S(2)}, u32[]{:S(2)}) collective-permute-start(s32[8,27]{1,0:T(8,128)S(1)} %get-tuple-element.104), channel_id=1, source_target_pairs={{0,1},{1,0},{2,3},{3,2},{4,5},{5,4},{6,7},{7,6},{8,9},{9,8},{10,11... | collective-permute-start | bytes 2600 | tf_op jit(solution)/shard_map/ppermute | solution.py:503
  9.6 4.3 %collective-permute-start.2 = (bf16[8,64,1728]{2,1,0:T(8,128)(2,1)}, bf16[8,64,1728]{2,1,0:T(8,128)(2,1)}, u32[]{:S(2)}, u32[]{:S(2)}) collective-permute-start(bf16[8,64,1728]{2,1,0:T(8,128)(2,1)} %get-tuple-element.57), channel_id=1, source_target_pairs={{0,1},{1,0},{2,3},{3,2},{4,5},{5,4},{6,7},{7,6},{8,9},{9,8},{10,11... | collective-permute-start | bytes 5308424 | tf_op jit(solution)/shard_map/ppermute | solution.py:503
  10.1 40.4 %collective-permute-start.3 = (bf16[8,64,1728]{2,1,0:T(8,128)(2,1)}, bf16[8,64,1728]{2,1,0:T(8,128)(2,1)S(1)}, u32[]{:S(2)}, u32[]{:S(2)}) collective-permute-start(bf16[8,64,1728]{2,1,0:T(8,128)(2,1)} %get-tuple-element.60), channel_id=1, source_target_pairs={{0,31},{1,2},{2,1},{3,4},{4,3},{5,6},{6,5},{7,8},{8,7},{9,10},{10,... | collective-permute-start | bytes 5308424 | tf_op jit(solution)/shard_map/ppermute | solution.py:503
  45.7 4.8 %collective-permute-start.4 = (bf16[3,64,2432]{2,1,0:T(8,128)(2,1)}, bf16[3,64,2432]{2,1,0:T(8,128)(2,1)S(1)}, u32[]{:S(2)}, u32[]{:S(2)}) collective-permute-start(bf16[3,64,2432]{2,1,0:T(8,128)(2,1)} %get-tuple-element.61), channel_id=1, source_target_pairs={{0,1},{1,0},{2,3},{3,2},{4,5},{5,4},{6,7},{7,6},{8,9},{9,8},{10,11... | collective-permute-start | bytes 2801672 | tf_op jit(solution)/shard_map/ppermute | solution.py:503
  46.2 4.3 %collective-permute-start.5 = (bf16[3,64,2432]{2,1,0:T(8,128)(2,1)}, bf16[3,64,2432]{2,1,0:T(8,128)(2,1)S(1)}, u32[]{:S(2)}, u32[]{:S(2)}) collective-permute-start(bf16[3,64,2432]{2,1,0:T(8,128)(2,1)} %get-tuple-element.62), channel_id=1, source_target_pairs={{0,1},{1,0},{2,3},{3,2},{4,5},{5,4},{6,7},{7,6},{8,9},{9,8},{10,11... | collective-permute-start | bytes 2801672 | tf_op jit(solution)/shard_map/ppermute | solution.py:503
  46.3 4.2 %collective-permute-start.6 = (bf16[6,64,512]{2,1,0:T(8,128)(2,1)}, bf16[6,64,512]{2,1,0:T(8,128)(2,1)S(1)}, u32[]{:S(2)}, u32[]{:S(2)}) collective-permute-start(bf16[6,64,512]{2,1,0:T(8,128)(2,1)} %get-tuple-element.63), channel_id=1, source_target_pairs={{0,1},{1,0},{2,3},{3,2},{4,5},{5,4},{6,7},{7,6},{8,9},{9,8},{10,11... | collective-permute-start | bytes 1179656 | tf_op jit(solution)/shard_map/ppermute | solution.py:503
  46.7 2.2 %copy-start = (f32[33,64,512]{2,1,0:T(8,128)S(1)}, f32[33,64,512]{2,1,0:T(8,128)}, u32[]{:S(2)}) copy-start(f32[33,64,512]{2,1,0:T(8,128)} %get-tuple-element.68.rest) | copy-start | bytes 12976132
  48.9 1.0 copy-start.2
  50.5 3.9 %copy-start.1 = (bf16[3,64,2432]{2,1,0:T(8,128)(2,1)S(1)}, bf16[3,64,2432]{2,1,0:T(8,128)(2,1)}, u32[]{:S(2)}) copy-start(bf16[3,64,2432]{2,1,0:T(8,128)(2,1)} %get-tuple-element.76.far_fast) | copy-start | bytes 2801668
  50.5 3.9 %copy-start.3 = (bf16[3,64,512]{2,1,0:T(8,128)(2,1)S(1)}, bf16[3,64,512]{2,1,0:T(8,128)(2,1)}, u32[]{:S(2)}) copy-start(bf16[3,64,512]{2,1,0:T(8,128)(2,1)} %get-tuple-element.72.slow) | copy-start | bytes 589828
  50.6 7.0 %copy-start.5 = (bf16[6,64,512]{2,1,0:T(8,128)(2,1)S(1)}, bf16[6,64,512]{2,1,0:T(8,128)(2,1)}, u32[]{:S(2)}) copy-start(bf16[6,64,512]{2,1,0:T(8,128)(2,1)} %get-tuple-element.71.slow) | copy-start | bytes 1179652
  54.1 6.5 %collective-permute-start.7 = (bf16[40,64,512]{2,1,0:T(8,128)(2,1)S(1)}, bf16[40,64,512]{2,1,0:T(8,128)(2,1)S(1)}, u32[]{:S(2)}, u32[]{:S(2)}) collective-permute-start(bf16[40,64,512]{2,1,0:T(8,128)(2,1)S(1)} %slow.1.wt_slow), channel_id=1, source_target_pairs={{0,1},{1,0},{2,3},{3,2},{4,5},{5,4},{6,7},{7,6},{8,9},{9,8},{10,11... | collective-permute-start | bytes 7864328 | tf_op jit(solution)/shard_map/ppermute | solution.py:503
  54.5 3.1 %copy-start.4 = (bf16[6,64,2432]{2,1,0:T(8,128)(2,1)S(1)}, bf16[6,64,2432]{2,1,0:T(8,128)(2,1)}, u32[]{:S(2)}) copy-start(bf16[6,64,2432]{2,1,0:T(8,128)(2,1)} %get-tuple-element.78.inner) | copy-start | bytes 5603332
  54.5 22.5 %slice-start = ((s8[5242880]{0:T(1024)(128)(4,1)}), s8[4194304]{0:T(1024)(128)(4,1)S(1)}, s32[]{:S(2)}) async-start(s8[5242880]{0:T(1024)(128)(4,1)} %bitcast.9), calls=%async_computation | async-start | bytes 8388608
  56.7 6.9 %collective-permute-start.8 = (bf16[3,64,2304]{2,1,0:T(8,128)(2,1)S(1)}, bf16[3,64,2304]{2,1,0:T(8,128)(2,1)S(1)}, u32[]{:S(2)}, u32[]{:S(2)}) collective-permute-start(bf16[3,64,2304]{2,1,0:T(8,128)(2,1)S(1)} %far.1), channel_id=1, source_target_pairs={{1,2},{2,1},{5,6},{6,5},{9,10},{10,9},{13,14},{14,13},{17,18},{18,... | collective-permute-start | bytes 2654216 | tf_op jit(solution)/shard_map/ppermute | solution.py:503
  57.6 19.3 %slice-start.1 = ((s8[5242880]{0:T(1024)(128)(4,1)}), s8[1048576]{0:T(1024)(128)(4,1)S(1)}, s32[]{:S(2)}) async-start(s8[5242880]{0:T(1024)(128)(4,1)} %bitcast.9), calls=%async_computation.1 | async-start | bytes 2097152
  60.6 3.0 %copy-start.10 = (bf16[9,64,2432]{2,1,0:T(8,128)(2,1)S(1)}, bf16[9,64,2432]{2,1,0:T(8,128)(2,1)}, u32[]{:S(2)}) copy-start(bf16[9,64,2432]{2,1,0:T(8,128)(2,1)} %get-tuple-element.88) | copy-start | bytes 8404996
  60.6 10.7 %copy-start.11 = (bf16[9,64,512]{2,1,0:T(8,128)(2,1)S(1)}, bf16[9,64,512]{2,1,0:T(8,128)(2,1)}, u32[]{:S(2)}) copy-start(bf16[9,64,512]{2,1,0:T(8,128)(2,1)} %get-tuple-element.86) | copy-start | bytes 1769476
  63.6 13.4 %collective-permute-start.10 = (bf16[9,64,2432]{2,1,0:T(8,128)(2,1)S(1)}, bf16[9,64,2432]{2,1,0:T(8,128)(2,1)S(1)}, u32[]{:S(2)}, u32[]{:S(2)}) collective-permute-start(bf16[9,64,2432]{2,1,0:T(8,128)(2,1)S(1)} %copy-done.10), channel_id=1, source_target_pairs={{0,1},{1,0},{2,3},{3,2},{4,5},{5,4},{6,7},{7,6},{8,9},{9,8},{10,11... | collective-permute-start | bytes 8405000 | tf_op jit(solution)/shard_map/ppermute | solution.py:503
  71.3 5.6 %collective-permute-start.9 = (bf16[9,64,512]{2,1,0:T(8,128)(2,1)S(1)}, bf16[9,64,512]{2,1,0:T(8,128)(2,1)S(1)}, u32[]{:S(2)}, u32[]{:S(2)}) collective-permute-start(bf16[9,64,512]{2,1,0:T(8,128)(2,1)S(1)} %copy-done.11), channel_id=1, source_target_pairs={{0,1},{1,0},{2,3},{3,2},{4,5},{5,4},{6,7},{7,6},{8,9},{9,8},{10,11... | collective-permute-start | bytes 1769480 | tf_op jit(solution)/shard_map/ppermute | solution.py:503
  71.4 5.6 %copy-start.6 = (bf16[9,64,1024]{2,1,0:T(8,128)(2,1)S(1)}, bf16[9,64,1024]{2,1,0:T(8,128)(2,1)}, u32[]{:S(2)}) copy-start(bf16[9,64,1024]{2,1,0:T(8,128)(2,1)} %get-tuple-element.58.fast) | copy-start | bytes 3538948
  71.4 5.5 %copy-start.7 = (bf16[9,64,512]{2,1,0:T(8,128)(2,1)S(1)}, bf16[9,64,512]{2,1,0:T(8,128)(2,1)}, u32[]{:S(2)}) copy-start(bf16[9,64,512]{2,1,0:T(8,128)(2,1)} %get-tuple-element.59.slow) | copy-start | bytes 1769476
  71.4 26.3 %collective-permute-start.13 = (bf16[3,64,2432]{2,1,0:T(8,128)(2,1)S(1)}, bf16[3,64,2432]{2,1,0:T(8,128)(2,1)S(1)}, u32[]{:S(2)}, u32[]{:S(2)}) collective-permute-start(bf16[3,64,2432]{2,1,0:T(8,128)(2,1)S(1)} %get-tuple-element.94), channel_id=1, source_target_pairs={{0,2},{1,3},{2,0},{3,1},{4,6},{5,7},{6,4},{7,5},{8,10},{9,11},{10,... | collective-permute-start | bytes 2801672 | tf_op jit(solution)/shard_map/ppermute | solution.py:503
  74.0 29.5 %collective-permute-start.11 = (bf16[3,64,2816]{2,1,0:T(8,128)(2,1)S(1)}, bf16[3,64,2816]{2,1,0:T(8,128)(2,1)S(1)}, u32[]{:S(2)}, u32[]{:S(2)}) collective-permute-start(bf16[3,64,2816]{2,1,0:T(8,128)(2,1)S(1)} %merge_far.1), channel_id=1, source_target_pairs={{0,28},{1,29},{2,6},{3,7},{4,0},{5,1},{6,10},{7,11},{8,4},{9,5},{1... | collective-permute-start | bytes 3244040 | tf_op jit(solution)/shard_map/ppermute | solution.py:503
  85.1 18.4 %collective-permute-start.12 = (bf16[1,64,2304]{2,1,0:T(8,128)(2,1)S(1)}, bf16[1,64,2304]{2,1,0:T(8,128)(2,1)S(1)}, u32[]{:S(2)}, u32[]{:S(2)}) collective-permute-start(bf16[1,64,2304]{2,1,0:T(8,128)(2,1)S(1)} %slice.14), channel_id=1, source_target_pairs={{0,27},{3,8},{4,31},{7,12},{8,3},{11,16},{12,7},{15,20},{16,11},{1... | collective-permute-start | bytes 884744 | tf_op jit(solution)/shard_map/ppermute | solution.py:503
  98.5 31.6 %collective-permute-start.15 = (bf16[3,64,2816]{2,1,0:T(8,128)(2,1)S(1)}, bf16[3,64,2816]{2,1,0:T(8,128)(2,1)S(1)}, u32[]{:S(2)}, u32[]{:S(2)}) collective-permute-start(bf16[3,64,2816]{2,1,0:T(8,128)(2,1)S(1)} %merge.1), channel_id=1, source_target_pairs={{0,4},{1,5},{2,30},{3,31},{4,8},{5,9},{6,2},{7,3},{8,12},{9,13},{1... | collective-permute-start | bytes 3244040 | tf_op jit(solution)/shard_map/ppermute | solution.py:503
  98.5 33.6 %collective-permute-start.16 = (bf16[2,64,2304]{2,1,0:T(8,128)(2,1)S(1)}, bf16[2,64,2304]{2,1,0:T(8,128)(2,1)S(1)}, u32[]{:S(2)}, u32[]{:S(2)}) collective-permute-start(bf16[2,64,2304]{2,1,0:T(8,128)(2,1)S(1)} %slice.15), channel_id=1, source_target_pairs={{0,27},{3,8},{4,31},{7,12},{8,3},{11,16},{12,7},{15,20},{16,11},{1... | collective-permute-start | bytes 1769480 | tf_op jit(solution)/shard_map/ppermute | solution.py:503
  103.1 27.0 %collective-permute-start.14 = (bf16[3,64,2432]{2,1,0:T(8,128)(2,1)S(1)}, bf16[3,64,2432]{2,1,0:T(8,128)(2,1)S(1)}, u32[]{:S(2)}, u32[]{:S(2)}) collective-permute-start(bf16[3,64,2432]{2,1,0:T(8,128)(2,1)S(1)} %get-tuple-element.96), channel_id=1, source_target_pairs={{0,2},{1,3},{2,0},{3,1},{4,6},{5,7},{6,4},{7,5},{8,10},{9,11},{10,... | collective-permute-start | bytes 2801672 | tf_op jit(solution)/shard_map/ppermute | solution.py:503
